TPU v7x, 32 devices: a whole 2x2x4 slice. The times are simulated.
32 devices in a mesh: fsdp: 8 (over z, y), dp: 4 (over x, core).
Axes of the slice: x: 2, y: 2, z: 4, core: 2. Of those that a mesh axis runs over, the one named last changes fastest.
Arguments:
- inputs: bfloat16 [16384, 640], P(('fsdp', 'dp')), may hold values from -6 to 6
- targets: int32 [16384], P(('fsdp', 'dp')), may hold values from 0 to 24
- masked: int32 [16384], P(('fsdp', 'dp')), may hold values from 0 to 1, as said below
- lengths: int32 [128], P(('fsdp', 'dp')), may hold values from 64 to 128, as said below
- attn_weight: bfloat16 [2, 12800, 128], P(None, 'fsdp'), may hold values from -2 to 2
- up_weight: bfloat16 [2, 25600, 128], P(None, 'fsdp'), may hold values from -0.25 to 0.25
- down_weight: bfloat16 [2, 25600, 128], P(None, 'fsdp'), may hold values from -0.078125 to 0.078125
- norm_gains: float32 [2, 2, 640], replicated, may hold values from 0.5 to 1.5
- layer_biases: float32 [2, 6, 640], replicated, may hold values from -1.75 to 1.75
- up_bias: float32 [2, 5120], replicated, may hold values from -1.75 to 1.75
- head_weight: bfloat16 [640, 25], replicated, may hold values from -0.5 to 0.5
- final_gain: float32 [640], replicated, may hold values from 0.5 to 1.5
- final_shift: float32 [640], replicated, may hold values from -1.75 to 1.75
- head_bias: float32 [25], replicated, may hold values from -3 to 3
Outputs:
- activations: bfloat16 [16384, 640], P(('fsdp', 'dp'))
- input_grad: float32 [16384, 640], P(('fsdp', 'dp'))
- attn_grad: float32 [2, 12800, 128], P(None, 'fsdp')
- up_grad: float32 [2, 25600, 128], P(None, 'fsdp')
- down_grad: float32 [2, 25600, 128], P(None, 'fsdp')
- gains_grad: float32 [2, 2, 640], replicated
- biases_grad: float32 [2, 6, 640], replicated
- up_bias_grad: float32 [2, 5120], replicated
- head_weight_grad: float32 [640, 25], replicated
- final_gain_grad: float32 [640], replicated
- final_shift_grad: float32 [640], replicated
- head_bias_grad: float32 [25], replicated
- loss: float32 [], replicated
- accuracy: float32 [], replicated
- counts: int32 [], replicated
Inputs may be any that keep to these rules, and one draw needn't show every extreme that they name: `lengths`: number of valid rows of each sequence; some sequence has all 128 rows. `masked`: 1 only at rows below the sequence's length; every sequence has at least one 1.
All inputs are finite; a program needn't handle non-finite values.
Results may differ from a plain program's by a relative error of at most 0.013.
Values may be sent and summed in bfloat16 or wider, within the bound.
No kernel may reach another device: no remote copies, remote signals or barrier semaphores. Data moves between devices by JAX's collectives and lax.ppermute only.
A program may use at most 320 MiB of HBM per device.

v0:
```python
from functools import partial
import math

import jax
import jax.numpy as jnp
from jax import lax
from jax.sharding import PartitionSpec as P

D = 640
HEADS = 20
HEAD_DIM = 32
FF = 5120
VOCAB = 25
LAYERS = 2
LEN = 128
SEQ_DEV = 4


def multiply(left, right):
    return jnp.dot(left, right, preferred_element_type=jnp.float32)


def contract_rows(left, right):
    return lax.dot_general(
        left, right, (((0,), (0,)), ((), ())), preferred_element_type=jnp.float32
    )


def contract_cols(left, right):
    return lax.dot_general(
        left, right, (((1,), (1,)), ((), ())), preferred_element_type=jnp.float32
    )


def normalize(values):
    centered = values - jnp.mean(values, -1, keepdims=True)
    inverse = lax.rsqrt(jnp.mean(centered * centered, -1, keepdims=True) + 1e-05)
    return (centered * inverse, inverse)


def norm_back(grad_normed, normed, inverse):
    return inverse * (
        grad_normed
        - jnp.mean(grad_normed, -1, keepdims=True)
        - normed * jnp.mean(grad_normed * normed, -1, keepdims=True)
    )


def layer_matrices(pieces):
    attn_piece, up_piece, down_piece = pieces
    return (attn_piece.reshape(D, 4 * D), up_piece.reshape(D, FF), down_piece.reshape(FF, D))


def head_split(row_values):
    return row_values.reshape(SEQ_DEV, LEN, HEADS, HEAD_DIM)


def attention_scores(queries, key_rows, key_valid):
    scores = jnp.einsum(
        "sqhd,skhd->shqk", queries, key_rows, preferred_element_type=jnp.float32
    ) * (1.0 / math.sqrt(HEAD_DIM))
    return jnp.where(key_valid[:, None, None, :], scores, -1e30)


def layer_forward(residual, matrices, gain_rows, bias_rows, up_shift, key_valid):
    attn_matrix, up_matrix, down_matrix = matrices
    normed, inverse = normalize(residual)
    normed_in = (normed * gain_rows[0] + bias_rows[0]).astype(jnp.bfloat16)
    packed = multiply(normed_in, attn_matrix[:, : 3 * D])
    queries = (packed[:, :D] + bias_rows[2]).astype(jnp.bfloat16)
    key_rows = packed[:, D : 2 * D].astype(jnp.bfloat16)
    value_rows = (packed[:, 2 * D :] + bias_rows[3]).astype(jnp.bfloat16)
    scores = attention_scores(head_split(queries), head_split(key_rows), key_valid)
    top_score = jnp.max(scores, -1, keepdims=True)
    expos = jnp.exp(scores - top_score)
    exp_totals = jnp.sum(expos, -1, keepdims=True)
    attention = (expos / exp_totals).astype(jnp.bfloat16)
    log_total = top_score + jnp.log(exp_totals)
    mixed_rows = jnp.einsum(
        "shqk,skhd->sqhd", attention, head_split(value_rows), preferred_element_type=jnp.float32
    )
    mixed_rows = mixed_rows.reshape(SEQ_DEV * LEN, D).astype(jnp.bfloat16)
    middle = residual + multiply(mixed_rows, attn_matrix[:, 3 * D :]) + bias_rows[4]
    normed_mid, inverse_mid = normalize(middle)
    second = (normed_mid * gain_rows[1] + bias_rows[1]).astype(jnp.bfloat16)
    hidden = multiply(second, up_matrix) + up_shift
    active = jax.nn.gelu(hidden, approximate=False).astype(jnp.bfloat16)
    output = middle + multiply(active, down_matrix) + bias_rows[5]
    kept = (
        normed,
        inverse,
        normed_in,
        queries,
        key_rows,
        value_rows,
        log_total,
        mixed_rows,
        normed_mid,
        inverse_mid,
        second,
        hidden,
        active,
    )
    return (output, kept)


def layer_backward(grad_residual, kept, matrices, gain_rows, key_valid):
    (
        normed,
        inverse,
        normed_in,
        queries,
        key_rows,
        value_rows,
        log_total,
        mixed_rows,
        normed_mid,
        inverse_mid,
        second,
        hidden,
        active,
    ) = kept
    attn_matrix, up_matrix, down_matrix = matrices
    grad_out2 = grad_residual.astype(jnp.bfloat16)
    down_grad = contract_rows(active, grad_out2)
    down_shift_grad = jnp.sum(grad_out2.astype(jnp.float32), 0)
    ignored, gelu_back = jax.vjp(partial(jax.nn.gelu, approximate=False), hidden)
    grad_hidden = gelu_back(contract_cols(grad_out2, down_matrix))[0].astype(jnp.bfloat16)
    up_grad = contract_rows(second, grad_hidden)
    up_shift_grad = jnp.sum(grad_hidden.astype(jnp.float32), 0)
    grad_second = contract_cols(grad_hidden, up_matrix)
    gain_mid_grad = jnp.sum(grad_second * normed_mid, 0)
    shift_mid_grad = jnp.sum(grad_second, 0)
    grad_middle = grad_residual + norm_back(grad_second * gain_rows[1], normed_mid, inverse_mid)
    grad_out1 = grad_middle.astype(jnp.bfloat16)
    out_grad = contract_rows(mixed_rows, grad_out1)
    out_shift_grad = jnp.sum(grad_out1.astype(jnp.float32), 0)
    grad_mixed = head_split(contract_cols(grad_out1, attn_matrix[:, 3 * D :]).astype(jnp.bfloat16))
    query_heads = head_split(queries)
    key_heads = head_split(key_rows)
    value_heads = head_split(value_rows)
    attention = jnp.exp(attention_scores(query_heads, key_heads, key_valid) - log_total)
    grad_values = jnp.einsum(
        "shqk,sqhd->skhd",
        attention.astype(jnp.bfloat16),
        grad_mixed,
        preferred_element_type=jnp.float32,
    )
    grad_attention = jnp.einsum(
        "sqhd,skhd->shqk", grad_mixed, value_heads, preferred_element_type=jnp.float32
    )
    grad_scores = (
        attention * (grad_attention - jnp.sum(grad_attention * attention, -1, keepdims=True))
    ).astype(jnp.bfloat16)
    grad_queries = jnp.einsum(
        "shqk,skhd->sqhd", grad_scores, key_heads, preferred_element_type=jnp.float32
    ) * (1.0 / math.sqrt(HEAD_DIM))
    grad_keys = jnp.einsum(
        "shqk,sqhd->skhd", grad_scores, query_heads, preferred_element_type=jnp.float32
    ) * (1.0 / math.sqrt(HEAD_DIM))
    row_count = SEQ_DEV * LEN
    grad_packed = jnp.concatenate(
        [
            grad_queries.reshape(row_count, D),
            grad_keys.reshape(row_count, D),
            grad_values.reshape(row_count, D),
        ],
        1,
    ).astype(jnp.bfloat16)
    packed_grad = contract_rows(normed_in, grad_packed)
    packed_sums = jnp.sum(grad_packed.astype(jnp.float32), 0)
    grad_normed_in = contract_cols(grad_packed, attn_matrix[:, : 3 * D])
    gain_in_grad = jnp.sum(grad_normed_in * normed, 0)
    shift_in_grad = jnp.sum(grad_normed_in, 0)
    grad_input = grad_middle + norm_back(grad_normed_in * gain_rows[0], normed, inverse)
    attn_grad = jnp.concatenate([packed_grad, out_grad], 1)
    gain_grads = jnp.stack([gain_in_grad, gain_mid_grad])
    bias_grads = jnp.stack(
        [
            shift_in_grad,
            shift_mid_grad,
            packed_sums[:D],
            packed_sums[2 * D :],
            out_shift_grad,
            down_shift_grad,
        ]
    )
    return (grad_input, (attn_grad, up_grad, down_grad), gain_grads, bias_grads, up_shift_grad)


def local(
    inputs,
    targets,
    masked,
    lengths,
    attn_weight,
    up_weight,
    down_weight,
    norm_gains,
    layer_biases,
    up_bias,
    head_weight,
    final_gain,
    final_shift,
    head_bias,
):
    key_valid = jnp.arange(LEN)[None, :] < lengths[:, None]
    residual = inputs.astype(jnp.float32)
    saved = []
    gathered = []
    for layer_index in range(LAYERS):
        matrices = layer_matrices(
            (
                lax.all_gather(attn_weight[layer_index], "fsdp", axis=0, tiled=True),
                lax.all_gather(up_weight[layer_index], "fsdp", axis=0, tiled=True),
                lax.all_gather(down_weight[layer_index], "fsdp", axis=0, tiled=True),
            )
        )
        residual, kept = layer_forward(
            residual,
            matrices,
            norm_gains[layer_index],
            layer_biases[layer_index],
            up_bias[layer_index],
            key_valid,
        )
        saved.append(kept)
        gathered.append(matrices)
    final_normed, final_inverse = normalize(residual)
    final_rows = (final_normed * final_gain + final_shift).astype(jnp.bfloat16)
    logits = multiply(final_rows, head_weight) + head_bias
    top_logit = jnp.max(logits, -1, keepdims=True)
    log_total = top_logit + jnp.log(jnp.sum(jnp.exp(logits - top_logit), -1, keepdims=True))
    onehot = (targets[:, None] == jnp.arange(VOCAB)[None, :]).astype(jnp.float32)
    picked = jnp.sum(logits * onehot, -1)
    weights_mask = masked.astype(jnp.float32)
    statistics = jnp.stack(
        [
            jnp.sum(weights_mask * (log_total[:, 0] - picked)),
            jnp.sum(weights_mask * jnp.exp(picked - log_total[:, 0])),
            jnp.sum(weights_mask),
        ]
    )
    grad_logits = (weights_mask[:, None] * (jnp.exp(logits - log_total) - onehot)).astype(
        jnp.bfloat16
    )
    head_weight_grad = contract_rows(final_rows, grad_logits)
    head_bias_grad = jnp.sum(grad_logits.astype(jnp.float32), 0)
    grad_final = contract_cols(grad_logits, head_weight)
    final_gain_grad = jnp.sum(grad_final * final_normed, 0)
    final_shift_grad = jnp.sum(grad_final, 0)
    grad_residual = norm_back(grad_final * final_gain, final_normed, final_inverse)
    shard_lists = [[None] * LAYERS, [None] * LAYERS, [None] * LAYERS]
    gain_list = [None] * LAYERS
    bias_list = [None] * LAYERS
    upshift_list = [None] * LAYERS
    for layer_index in reversed(range(LAYERS)):
        matrices = layer_matrices(
            (
                lax.all_gather(attn_weight[layer_index], "fsdp", axis=0, tiled=True),
                lax.all_gather(up_weight[layer_index], "fsdp", axis=0, tiled=True),
                lax.all_gather(down_weight[layer_index], "fsdp", axis=0, tiled=True),
            )
        )
        grad_residual, matrix_grads, gain_grads, bias_grads, upshift_grad = layer_backward(
            grad_residual, saved[layer_index], matrices, norm_gains[layer_index], key_valid
        )
        flat_grads = (
            matrix_grads[0].reshape(-1, 128),
            matrix_grads[1].reshape(-1, 128),
            matrix_grads[2].reshape(-1, 128),
        )
        shares = (
            lax.psum_scatter(flat_grads[0], "fsdp", scatter_dimension=0, tiled=True),
            lax.psum_scatter(flat_grads[1], "fsdp", scatter_dimension=0, tiled=True),
            lax.psum_scatter(flat_grads[2], "fsdp", scatter_dimension=0, tiled=True),
        )
        shares = (
            lax.psum(shares[0].astype(jnp.bfloat16), "dp").astype(jnp.float32),
            lax.psum(shares[1].astype(jnp.bfloat16), "dp").astype(jnp.float32),
            lax.psum(shares[2].astype(jnp.bfloat16), "dp").astype(jnp.float32),
        )
        for member in range(3):
            shard_lists[member][layer_index] = shares[member]
        gain_list[layer_index] = gain_grads
        bias_list[layer_index] = bias_grads
        upshift_list[layer_index] = upshift_grad
    summed = lax.psum(
        (
            jnp.stack(gain_list),
            jnp.stack(bias_list),
            jnp.stack(upshift_list),
            head_weight_grad,
            final_gain_grad,
            final_shift_grad,
            head_bias_grad,
            statistics,
        ),
        ("fsdp", "dp"),
    )
    totals = summed[7]
    return (
        residual.astype(jnp.bfloat16),
        grad_residual,
        jnp.stack(shard_lists[0]),
        jnp.stack(shard_lists[1]),
        jnp.stack(shard_lists[2]),
        summed[0],
        summed[1],
        summed[2],
        summed[3],
        summed[4],
        summed[5],
        summed[6],
        totals[0] / totals[2],
        totals[1] / totals[2],
        totals[2].astype(jnp.int32),
    )


def solution(mesh):
    placed = (
        P(("fsdp", "dp"), None),
        P(("fsdp", "dp")),
        P(("fsdp", "dp")),
        P(("fsdp", "dp")),
        P(None, "fsdp", None),
        P(None, "fsdp", None),
        P(None, "fsdp", None),
        P(),
        P(),
        P(),
        P(),
        P(),
        P(),
        P(),
    )
    return jax.shard_map(
        local,
        mesh=mesh,
        in_specs=placed,
        out_specs=(
            P(("fsdp", "dp"), None),
            P(("fsdp", "dp"), None),
            P(None, "fsdp", None),
            P(None, "fsdp", None),
            P(None, "fsdp", None),
            P(),
            P(),
            P(),
            P(),
            P(),
            P(),
            P(),
            P(),
            P(),
            P(),
        ),
        check_vma=False,
    )
```

profile of v0, /device:TPU:0, one launch (start us, length us, event | category | flops | bytes accessed | tf_op | source)
XLA Modules:
  0.0 1998.0 jit_solution(17473049530344552207)
XLA Ops:
  7.3 2.2 fusion.138
  11.7 2.8 fusion.136
  17.6 57.9 %all-gather.13.cloned.1.call-done = bf16[1,12800,128]{2,1,0:T(8,128)(2,1)} async-done(((bf16[1,1600,128]{2,1,0:T(8,128)(2,1)}), bf16[1,12800,128]{2,1,0:T(8,128)(2,1)}) %all-gather.13.cloned.1.call-update) | async-done | bytes 3276816 | tf_op jit(solution)/shard_map/all_gather | solution.py:214
  75.5 7.1 reshape.318
  82.6 3.7 fusion.30
  94.7 2.3 fusion.144
  97.4 41.5 %all-gather.19.cloned.1.call-done = bf16[1,12800,128]{2,1,0:T(8,128)(2,1)} async-done(((bf16[1,1600,128]{2,1,0:T(8,128)(2,1)}), bf16[1,12800,128]{2,1,0:T(8,128)(2,1)}) %all-gather.19.cloned.1.call-update) | async-done | bytes 3276816 | tf_op jit(solution)/shard_map/all_gather | solution.py:214
  138.8 7.1 reshape.324
  145.9 96.5 %all-gather.15.cloned.1.call-done = bf16[1,25600,128]{2,1,0:T(8,128)(2,1)} async-done(((bf16[1,3200,128]{2,1,0:T(8,128)(2,1)}), bf16[1,25600,128]{2,1,0:T(8,128)(2,1)}) %all-gather.15.cloned.1.call-update) | async-done | bytes 6553616 | tf_op jit(solution)/shard_map/all_gather | solution.py:215
  242.5 10.5 reshape.322
  253.0 30.9 %multiply_convert_fusion.1 = (bf16[512,5120]{1,0:T(8,128)(2,1)}, f32[512,5120]{1,0:T(8,128)}, f32[512,5120]{1,0:T(8,128)}) fusion(f32[5120]{0:T(1024)S(1)} %bitcast.165, bf16[640,5120]{1,0:T(8,128)(2,1)} %reshape.322, f32[512,640]{1,0:T(8,128)S(1)} %get-tuple-element.123, f32[640]{0:T(1024)S(1)} %get-tuple-element.58, f32[640]{0:T(1024)S(1)} %get-tuple-element.65, ...), kind=kOutput, calls=%fused_computation.21 | convolution fusion | flops 3530096640 | bytes 34108416 | tf_op jit(solution)/shard_map/dot_general | solution.py:20
  283.9 61.0 %all-gather.17.cloned.1.call-done = bf16[1,25600,128]{2,1,0:T(8,128)(2,1)} async-done(((bf16[1,3200,128]{2,1,0:T(8,128)(2,1)}), bf16[1,25600,128]{2,1,0:T(8,128)(2,1)}) %all-gather.17.cloned.1.call-update) | async-done | bytes 6553616 | tf_op jit(solution)/shard_map/all_gather | solution.py:216
  345.0 11.8 reshape.323
  356.7 8.6 fusion.145
  375.7 72.3 %all-gather.21.cloned.1.call-done = bf16[1,25600,128]{2,1,0:T(8,128)(2,1)} async-done(((bf16[1,3200,128]{2,1,0:T(8,128)(2,1)}), bf16[1,25600,128]{2,1,0:T(8,128)(2,1)}) %all-gather.21.cloned.1.call-update) | async-done | bytes 6553616 | tf_op jit(solution)/shard_map/all_gather | solution.py:215
  448.0 10.5 reshape.328
  458.5 2.5 fusion.147
  461.4 31.3 %multiply_convert_fusion = (bf16[512,5120]{1,0:T(8,128)(2,1)}, f32[512,5120]{1,0:T(8,128)}, f32[512,5120]{1,0:T(8,128)}) fusion(f32[5120]{0:T(1024)S(1)} %bitcast.168, bf16[640,5120]{1,0:T(8,128)(2,1)} %reshape.328, f32[512,640]{1,0:T(8,128)S(1)} %get-tuple-element.130, f32[640]{0:T(1024)S(1)} %get-tuple-element.63, f32[640]{0:T(1024)S(1)} %get-tuple-element.64, ...), kind=kOutput, calls=%fused_computation.8 | convolution fusion | flops 3530096640 | bytes 34108416 | tf_op jit(solution)/shard_map/dot_general | solution.py:20
  492.7 57.8 %all-gather.23.cloned.1.call-done = bf16[1,25600,128]{2,1,0:T(8,128)(2,1)} async-done(((bf16[1,3200,128]{2,1,0:T(8,128)(2,1)}), bf16[1,25600,128]{2,1,0:T(8,128)(2,1)}) %all-gather.23.cloned.1.call-update) | async-done | bytes 6553616 | tf_op jit(solution)/shard_map/all_gather | solution.py:216
  550.5 11.7 reshape.329
  562.2 8.3 fusion.148
  574.2 1.9 convert_reduce_fusion.5
  576.1 15.3 convert_reduce_fusion
  591.5 9.1 multiply_reduce_fusion.3
  601.7 3.3 convolution_convert_fusion.1
  606.8 2.2 copy.71
  610.8 4.1 fusion.71
  615.0 4.1 multiply_reduce_fusion.1
  627.3 3.6 pad_maximum_fusion.1
  630.9 7.4 reshape.339
  639.1 5.1 multiply_reduce_fusion.4
  644.9 14.5 convert_reduce_fusion.1
  659.4 8.6 multiply_reduce_fusion.5
  669.6 2.0 convolution_convert_fusion
  674.6 4.1 fusion.68
  689.3 3.6 pad_maximum_fusion
  693.0 7.4 reshape.338
  701.0 11.4 fusion.129
  712.4 14.2 reshape.340
  727.3 11.3 fusion.132
  738.6 14.4 reshape.341
  754.3 11.5 fusion.112
  765.8 14.1 reshape.342
  781.3 11.6 fusion.120
  792.9 14.2 reshape.343
  809.0 5.7 fusion.60
  815.2 2.6 pad_maximum_fusion.5
  820.7 2.0 convert_bitcast_fusion.4
  822.7 60.5 %reduce-scatter.7.cloned.1.call-done = f32[1600,128]{1,0:T(8,128)} async-done(((f32[12800,128]{1,0:T(8,128)}), f32[1600,128]{1,0:T(8,128)}) %reduce-scatter.7.cloned.1.call-update) | async-done | bytes 819216 | tf_op jit(solution)/shard_map/reduce_scatter | solution.py:274
  883.1 1.9 convert_bitcast_fusion.5
  885.1 215.8 %reduce-scatter.11.cloned.1.call-done = f32[3200,128]{1,0:T(8,128)} async-done(((f32[25600,128]{1,0:T(8,128)}), f32[3200,128]{1,0:T(8,128)}) %reduce-scatter.11.cloned.1.call-update) | async-done | bytes 1638416 | tf_op jit(solution)/shard_map/reduce_scatter | solution.py:275
  1100.9 2.4 convert_bitcast_fusion.3
  1103.3 214.8 %reduce-scatter.13.cloned.1.call-done = f32[3200,128]{1,0:T(8,128)} async-done(((f32[25600,128]{1,0:T(8,128)}), f32[3200,128]{1,0:T(8,128)}) %reduce-scatter.13.cloned.1.call-update) | async-done | bytes 1638416 | tf_op jit(solution)/shard_map/reduce_scatter | solution.py:275
  1318.1 2.4 convert_bitcast_fusion.2
  1320.5 215.0 %reduce-scatter.15.cloned.1.call-done = f32[3200,128]{1,0:T(8,128)} async-done(((f32[25600,128]{1,0:T(8,128)}), f32[3200,128]{1,0:T(8,128)}) %reduce-scatter.15.cloned.1.call-update) | async-done | bytes 1638416 | tf_op jit(solution)/shard_map/reduce_scatter | solution.py:276
  1535.6 2.5 convert_bitcast_fusion.1
  1538.0 214.8 %reduce-scatter.17.cloned.1.call-done = f32[3200,128]{1,0:T(8,128)} async-done(((f32[25600,128]{1,0:T(8,128)}), f32[3200,128]{1,0:T(8,128)}) %reduce-scatter.17.cloned.1.call-update) | async-done | bytes 1638416 | tf_op jit(solution)/shard_map/reduce_scatter | solution.py:276
  1752.8 2.4 convert_bitcast_fusion
  1755.3 2.9 fusion.59
  1758.1 127.1 %all-reduce.5.cloned.1.call-done = (f32[2,2,640]{2,1,0:T(2,128)}, f32[2,6,640]{2,1,0:T(8,128)}, f32[2,5120]{1,0:T(2,128)}, f32[640,25]{0,1:T(8,128)}, f32[640]{0...) async-done(((f32[2,2,640]{2,1,0:T(2,128)}, f32[2,6,640]{2,1,0:T(8,128)}, f32[2,5120]{1,0:T(2,128)}, f32[640,25]{0,1:T(8,128)}, f32[640]{0:T(1024)}, ...) | async-done | bytes 151168 | tf_op jit(solution)/shard_map/psum | solution.py:288
  1891.2 85.0 %all-reduce.7.cloned.1.call-done = (bf16[1,1600,128]{2,1,0:T(8,128)(2,1)}, bf16[1,1600,128]{2,1,0:T(8,128)(2,1)}, bf16[1,3200,128]{2,1,0:T(8,128)(2,1)}, bf16[1,...) async-done(((bf16[1,1600,128]{2,1,0:T(8,128)(2,1)}, bf16[1,1600,128]{2,1,0:T(8,128)(2,1)}, bf16[1,3200,128]{2,1,0:T(8,128)(2,1)}, ...) | async-done | bytes 4096016 | tf_op jit(solution)/shard_map/psum | solution.py:279
  1976.2 2.5 maximum_convert_fusion.2
  1978.7 3.3 maximum_convert_fusion
  1982.1 1.9 maximum_convert_fusion.1
  (368 shorter events, 72.5 us)
Async XLA Ops:
  7.2 564.0 %copy-start = (bf16[640,25]{0,1:T(8,128)(2,1)S(1)}, bf16[640,25]{0,1:T(8,128)(2,1)}, u32[]{:S(2)}) copy-start(bf16[640,25]{0,1:T(8,128)(2,1)} %param.24) | copy-start | bytes 96004
  7.2 68.3 %all-gather.13.cloned.1.call-start = ((), (), s32[]{:S(2)}) async-start(), calls=%async_computation.12 | async-start | bytes 3686400 | tf_op jit(solution)/shard_map/all_gather | solution.py:214
  9.5 129.4 %all-gather.19.cloned.1.call-start = ((), (), s32[]{:S(2)}) async-start(), calls=%async_computation.15 | async-start | bytes 3686400 | tf_op jit(solution)/shard_map/all_gather | solution.py:214
  10.2 232.3 %all-gather.15.cloned.1.call-start = ((), (), s32[]{:S(2)}) async-start(), calls=%async_computation.13 | async-start | bytes 7372800 | tf_op jit(solution)/shard_map/all_gather | solution.py:215
  11.5 4.2 copy-start.85
  11.5 4.8 copy-start.22
  11.6 5.3 copy-start.77
  11.6 5.3 copy-start.60
  11.6 5.4 copy-start.62
  11.6 333.4 %all-gather.17.cloned.1.call-start = ((), (), s32[]{:S(2)}) async-start(), calls=%async_computation.14 | async-start | bytes 7372800 | tf_op jit(solution)/shard_map/all_gather | solution.py:216
  14.4 433.6 %all-gather.21.cloned.1.call-start = ((), (), s32[]{:S(2)}) async-start(), calls=%async_computation.16 | async-start | bytes 7372800 | tf_op jit(solution)/shard_map/all_gather | solution.py:215
  15.0 535.5 %all-gather.23.cloned.1.call-start = ((), (), s32[]{:S(2)}) async-start(), calls=%async_computation.17 | async-start | bytes 7372800 | tf_op jit(solution)/shard_map/all_gather | solution.py:216
  15.6 805.0 %reduce-scatter.9.cloned.1.call-start = ((), (), s32[]{:S(2)}) async-start(), calls=%async_computation.7 | async-start | bytes 7372800 | tf_op jit(solution)/shard_map/reduce_scatter | solution.py:274
  16.5 66.1 %copy-start.68 = (f32[512]{0:T(512)}, f32[512]{0:T(512)S(1)}, u32[]{:S(2)}) copy-start(f32[512]{0:T(512)S(1)} %broadcast_multiply_fusion.14) | copy-start | bytes 6148
  16.8 65.8 %copy-start.81 = (f32[512]{0:T(512)}, f32[512]{0:T(512)S(1)}, u32[]{:S(2)}) copy-start(f32[512]{0:T(512)S(1)} %add_rsqrt_fusion.4) | copy-start | bytes 6148
  16.9 65.7 %copy-start.75 = (f32[640]{0:T(1024)}, f32[640]{0:T(1024)S(1)}, u32[]{:S(2)}) copy-start(f32[640]{0:T(1024)S(1)} %get-tuple-element.66) | copy-start | bytes 7684
  16.9 236.0 %copy-start.45 = (f32[640]{0:T(1024)}, f32[640]{0:T(1024)S(1)}, u32[]{:S(2)}) copy-start(f32[640]{0:T(1024)S(1)} %get-tuple-element.65) | copy-start | bytes 7684
  16.9 348.8 %copy-start.73 = (f32[640]{0:T(1024)}, f32[640]{0:T(1024)S(1)}, u32[]{:S(2)}) copy-start(f32[640]{0:T(1024)S(1)} %get-tuple-element.67) | copy-start | bytes 7684
  17.0 236.0 %copy-start.64 = (f32[1,5120]{1,0:T(1,128)}, f32[1,5120]{1,0:T(1,128)S(1)}, u32[]{:S(2)}) copy-start(f32[1,5120]{1,0:T(1,128)S(1)} %get-tuple-element.112) | copy-start | bytes 61444
  17.6 65.0 %copy-start.88 = (f32[640]{0:T(1024)}, f32[640]{0:T(1024)S(1)}, u32[]{:S(2)}) copy-start(f32[640]{0:T(1024)S(1)} %get-tuple-element.62) | copy-start | bytes 7684
  17.6 235.3 %copy-start.51 = (f32[640]{0:T(1024)}, f32[640]{0:T(1024)S(1)}, u32[]{:S(2)}) copy-start(f32[640]{0:T(1024)S(1)} %get-tuple-element.58) | copy-start | bytes 7684
  17.6 348.1 %copy-start.90 = (f32[640]{0:T(1024)}, f32[640]{0:T(1024)S(1)}, u32[]{:S(2)}) copy-start(f32[640]{0:T(1024)S(1)} %get-tuple-element.56) | copy-start | bytes 7684
  17.6 443.7 %copy-start.49 = (f32[640]{0:T(1024)}, f32[640]{0:T(1024)S(1)}, u32[]{:S(2)}) copy-start(f32[640]{0:T(1024)S(1)} %get-tuple-element.63) | copy-start | bytes 7684
  87.9 5.3 copy-start.34
  97.0 259.7 %copy-start.11 = (f32[512,640]{1,0:T(8,128)}, f32[512,640]{1,0:T(8,128)S(1)}, u32[]{:S(2)}) copy-start(f32[512,640]{1,0:T(8,128)S(1)} %get-tuple-element.123) | copy-start | bytes 3932164
  97.0 155.9 %copy-start.53 = (f32[512]{0:T(512)}, f32[512]{0:T(512)S(1)}, u32[]{:S(2)}) copy-start(f32[512]{0:T(512)S(1)} %broadcast_multiply_fusion.13) | copy-start | bytes 6148
  97.4 155.6 %copy-start.57 = (f32[512]{0:T(512)}, f32[512]{0:T(512)S(1)}, u32[]{:S(2)}) copy-start(f32[512]{0:T(512)S(1)} %add_rsqrt_fusion.3) | copy-start | bytes 6148
  356.7 9.0 copy-start.18
  369.2 5.0 copy-start.36
  492.7 69.5 %copy-start.92 = (f32[640]{0:T(1024)S(1)}, f32[640]{0:T(1024)}, u32[]{:S(2)}) copy-start(f32[640]{0:T(1024)} %get-tuple-element.52) | copy-start | bytes 7684
  562.2 8.7 copy-start.70
  562.2 8.7 copy-start.87
  571.2 4.9 copy-start.20
  576.1 24.5 %copy-start.13 = (f32[512,640]{1,0:T(8,128)}, f32[512,640]{1,0:T(8,128)S(1)}, u32[]{:S(2)}) copy-start(f32[512,640]{1,0:T(8,128)S(1)} %get-tuple-element.93) | copy-start | bytes 3932164
  610.8 4.1 copy-start.37
  610.8 8.2 slice-start.2
  614.9 4.1 slice-start.3
  638.3 244.9 %reduce-scatter.7.cloned.1.call-start = ((), (), s32[]{:S(2)}) async-start(), calls=%async_computation.6 | async-start | bytes 7372800 | tf_op jit(solution)/shard_map/reduce_scatter | solution.py:274
  639.1 5.1 copy-start.5
  639.1 5.1 copy-start.17
  644.7 23.3 %copy-start.9 = (f32[512,640]{1,0:T(8,128)}, f32[512,640]{1,0:T(8,128)S(1)}, u32[]{:S(2)}) copy-start(f32[512,640]{1,0:T(8,128)S(1)} %get-tuple-element.89) | copy-start | bytes 3932164
  644.9 14.5 copy-start.12
  644.9 14.5 copy-start.46
  644.9 14.5 copy-start.54
  644.9 14.5 copy-start.58
  671.6 7.6 slice-start
  674.6 4.7 slice-start.1
  674.6 4.7 copy-start.35
  700.4 400.6 %reduce-scatter.11.cloned.1.call-start = ((), (), s32[]{:S(2)}) async-start(), calls=%async_computation.8 | async-start | bytes 14745600 | tf_op jit(solution)/shard_map/reduce_scatter | solution.py:275
  726.6 591.5 %reduce-scatter.13.cloned.1.call-start = ((), (), s32[]{:S(2)}) async-start(), calls=%async_computation.9 | async-start | bytes 14745600 | tf_op jit(solution)/shard_map/reduce_scatter | solution.py:275
  753.0 782.5 %reduce-scatter.15.cloned.1.call-start = ((), (), s32[]{:S(2)}) async-start(), calls=%async_computation.10 | async-start | bytes 14745600 | tf_op jit(solution)/shard_map/reduce_scatter | solution.py:276
  780.0 972.8 %reduce-scatter.17.cloned.1.call-start = ((), (), s32[]{:S(2)}) async-start(), calls=%async_computation.11 | async-start | bytes 14745600 | tf_op jit(solution)/shard_map/reduce_scatter | solution.py:276
  807.1 1078.1 %all-reduce.5.cloned.1.call-start = ((), (), s32[]{:S(2)}) async-start(), calls=%async_computation.18 | async-start | bytes 366592 | tf_op jit(solution)/shard_map/psum | solution.py:288
  809.0 5.7 copy-start.33
  809.0 10.0 copy-start.21
  809.0 10.0 copy-start.56
  809.0 10.9 copy-start.63
  820.6 1155.6 %all-reduce.7.cloned.1.call-start = ((), (), s32[]{:S(2)}) async-start(), calls=%async_computation.19 | async-start | bytes 8192000 | tf_op jit(solution)/shard_map/psum | solution.py:279
  1538.0 217.2 %copy-start.8 = (f32[512,640]{1,0:T(8,128)S(1)}, f32[512,640]{1,0:T(8,128)}, u32[]{:S(2)}) copy-start(f32[512,640]{1,0:T(8,128)} %copy-done.6) | copy-start | bytes 3932164
  1976.2 5.9 copy-start.41
  1976.2 5.9 copy-start.42
  1978.7 8.9 copy-start.1
  1982.0 4.4 copy-start.93
  1982.1 5.0 copy-start.99
  (54 other events, 94.2 us)
Sparse Core Ops, SparseCore 0:
  10.8 64.6 all-gather.12
  78.3 60.5 all-gather.18
  141.6 100.8 all-gather.14
  244.5 100.3 all-gather.16
  347.6 100.3 all-gather.20
  450.0 100.3 all-gather.22
  638.4 119.8 reduce-scatter.8
  762.3 120.7 reduce-scatter.6
  886.8 214.0 reduce-scatter.10
  1104.4 213.6 reduce-scatter.12
  1321.8 213.7 reduce-scatter.14
  1539.1 213.7 reduce-scatter.16
  1760.4 124.7 all-reduce.4
  1890.1 86.0 all-reduce.6
where the time goes:
time: 2010 us; the launch traced here: 2000 us
  waiting for transfers between devices  1520 us (76%)
  matrix products  231 us (11%)
  local copies, waits for them, and re-layouts  167 us (8%)
  other arithmetic  52.7 us (3%)
  between operations  22.9 us (1%)
    reduce_scatter x2, waiting for transfers between devices, local(): lax.psum_scatter(flat_grads[1], 'fsdp', scatter_dimension=0, tiled=True)  431 us
    reduce_scatter x2, waiting for transfers between devices, local(): lax.psum_scatter(flat_grads[2], 'fsdp', scatter_dimension=0, tiled=True)  430 us
    all_gather x2, waiting for transfers between devices, local(): lax.all_gather(up_weight[layer_index], 'fsdp', axis=0, tiled=True)  169 us
    psum x1, waiting for transfers between devices, local(): lax.psum((jnp.stack(gain_list), jnp.stack(bias_list), jnp.stack(upshift_l...  127 us
    all_gather x2, waiting for transfers between devices, local(): lax.all_gather(down_weight[layer_index], 'fsdp', axis=0, tiled=True)  119 us
    all_gather x2, waiting for transfers between devices, local(): lax.all_gather(attn_weight[layer_index], 'fsdp', axis=0, tiled=True)  99.4 us
    dot_general x9, matrix products, multiply(): return jnp.dot(left, right, preferred_element_type=jnp.float32)  89.9 us
    psum x1, waiting for transfers between devices, local(): lax.psum(shares[0].astype(jnp.bfloat16), 'dp').astype(jnp.float32)  85 us
  transfers between devices with their start and end apart: 14, of which 13 were waited for; matrix products, arithmetic and copies ran while one was open for 17% of the time, Pallas kernels for 0%

commit v1 on v0

v1 whole, which is shorter than its diff:
```python
import math

import jax
import jax.numpy as jnp
from jax import lax
from jax.experimental import pallas as pl
from jax.experimental.pallas import tpu as pltpu
from jax.sharding import Mesh
from jax.sharding import PartitionSpec as P

D = 640
HEADS = 20
HEAD_DIM = 32
FF = 5120
VOCAB = 25
LAYERS = 2
LEN = 128
SEQ_DEV = 4
ROWS = SEQ_DEV * LEN
TILE = 640
TILES = FF // TILE
GROUPS = HEADS * HEAD_DIM // 128
PER_GROUP = 128 // HEAD_DIM
CHUNK = 128
BF = jnp.bfloat16
F32 = jnp.float32
MIB = 2**20

VMEM_SPEC = pl.BlockSpec(memory_space=pltpu.VMEM)
SMEM_SPEC = pl.BlockSpec(memory_space=pltpu.SMEM)
ANY_SPEC = pl.BlockSpec(memory_space=pl.ANY)


def dot(left, right, dims):
    return lax.dot_general(left, right, (dims, ((), ())), preferred_element_type=F32)


def mul_nn(left, right):
    return dot(left, right, ((1,), (0,)))


def mul_nt(left, right):
    return dot(left, right, ((1,), (1,)))


def mul_tn(left, right):
    return dot(left, right, ((0,), (0,)))


def normalize(values):
    centered = values - jnp.mean(values, -1, keepdims=True)
    inverse = lax.rsqrt(jnp.mean(centered * centered, -1, keepdims=True) + 1e-05)
    return (centered * inverse, inverse)


def norm_back(grad_normed, normed, inverse):
    return inverse * (
        grad_normed
        - jnp.mean(grad_normed, -1, keepdims=True)
        - normed * jnp.mean(grad_normed * normed, -1, keepdims=True)
    )


def col_sum(values):
    return jnp.sum(values, 0, keepdims=True)


def sds(shape, dtype):
    return jax.ShapeDtypeStruct(shape, dtype)


def over_chunks(body, start):
    def step(index, carry):
        return body(pl.ds(pl.multiple_of(index * CHUNK, CHUNK), CHUNK), carry)

    return lax.fori_loop(0, ROWS // CHUNK, step, start)


def quarter_copies(place_ref, buffers, held, sems):
    x_at, y_at, c_at = place_ref[0], place_ref[1], place_ref[2]
    copies = []
    for number, buffer in enumerate(buffers):
        quarter = (x_at ^ (number >> 1)) * 2 + (c_at ^ (number & 1))
        for dy in range(2):
            copies.append(
                pltpu.make_async_copy(
                    buffer.at[dy], held.at[quarter, :, y_at ^ dy], sems.at[2 * number + dy]
                )
            )
    return copies


def tile_copies(place_ref, buffers, held, sems):
    x_at, y_at, c_at = place_ref[0], place_ref[1], place_ref[2]
    copies = []
    for number, buffer in enumerate(buffers):
        quarter = (x_at ^ (number >> 1)) * 2 + (c_at ^ (number & 1))
        for dy in range(2):
            for half in range(2):
                copies.append(
                    pltpu.make_async_copy(
                        buffer.at[dy, :, :, pl.ds(half * TILE, TILE)],
                        held.at[quarter * 2 + half, :, y_at ^ dy],
                        sems.at[4 * number + 2 * dy + half],
                    )
                )
    return copies


def half_copies(place_ref, buffers, held, sems):
    y_at, c_at = place_ref[1], place_ref[2]
    copies = []
    for number, buffer in enumerate(buffers):
        for dy in range(2):
            copies.append(
                pltpu.make_async_copy(
                    buffer.at[dy], held.at[:, y_at ^ dy, c_at ^ number], sems.at[2 * number + dy]
                )
            )
    return copies


def square(values):
    return values.reshape(D, values.shape[-1])


def head_masks():
    lanes = lax.broadcasted_iota(jnp.int32, (LEN, 128), 1) // HEAD_DIM
    return [(lanes == member) for member in range(PER_GROUP)]


def stack_heads(values, masks):
    zero = jnp.zeros_like(values)
    return jnp.concatenate([jnp.where(mask, values, zero) for mask in masks], 0)


def unstack_heads(values):
    parts = [
        values[HEAD_DIM * member : HEAD_DIM * (member + 1), LEN * member : LEN * (member + 1)]
        for member in range(PER_GROUP)
    ]
    return jnp.concatenate(parts, 0).T


def scores_of(keys, queries, valid):
    scores = mul_nt(keys, queries) * (1.0 / math.sqrt(HEAD_DIM))
    return jnp.where(valid, scores, -1e30)


def mix_kernel(
    place_ref,
    lengths_ref,
    residual_ref,
    w0_ref,
    w1_ref,
    w2_ref,
    w3_ref,
    gains_ref,
    biases_ref,
    packed_ref,
    log_ref,
    mixed_ref,
    middle_ref,
    second_ref,
    held,
    pre_ref,
    sems,
):
    copies = quarter_copies(place_ref, (w0_ref, w1_ref, w2_ref, w3_ref), held, sems)
    for copy in copies:
        copy.start()

    def first(rows, carry):
        normed, inverse = normalize(residual_ref[rows, :].astype(F32))
        pre_ref[rows, :] = (normed * gains_ref[0:1, :] + biases_ref[0:1, :]).astype(BF)
        return carry

    over_chunks(first, 0)
    for copy in copies:
        copy.wait()
    shifts = (biases_ref[2:3, :], None, biases_ref[3:4, :])
    for part in range(3):
        result = mul_nn(pre_ref[...], square(held[part]))
        if shifts[part] is not None:
            result = result + shifts[part]
        packed_ref[:, part * D : (part + 1) * D] = result.astype(BF)
    masks = head_masks()
    row_ids = lax.broadcasted_iota(jnp.int32, (LEN, 1), 0)

    def one_sequence(seq, carry):
        rows = pl.ds(pl.multiple_of(seq * LEN, LEN), LEN)
        valid = row_ids < lengths_ref[seq]
        for group in range(GROUPS):
            lanes = slice(group * 128, (group + 1) * 128)
            queries = stack_heads(packed_ref[rows, lanes], masks)
            key_rows = packed_ref[rows, D + group * 128 : D + (group + 1) * 128]
            value_rows = packed_ref[rows, 2 * D + group * 128 : 2 * D + (group + 1) * 128]
            scores = scores_of(key_rows, queries, valid)
            top = jnp.max(scores, 0, keepdims=True)
            expos = jnp.exp(scores - top)
            total = jnp.sum(expos, 0, keepdims=True)
            probs = (expos * (1.0 / total)).astype(BF)
            log_ref[seq * GROUPS + group] = top + jnp.log(total)
            mixed_ref[rows, lanes] = unstack_heads(mul_tn(value_rows, probs)).astype(BF)
        return carry

    lax.fori_loop(0, SEQ_DEV, one_sequence, 0)
    middle_ref[...] = mul_nn(mixed_ref[...], square(held[3])) + biases_ref[4:5, :]

    def last(rows, carry):
        middle = middle_ref[rows, :] + residual_ref[rows, :].astype(F32)
        middle_ref[rows, :] = middle
        normed, inverse = normalize(middle)
        second_ref[rows, :] = (normed * gains_ref[1:2, :] + biases_ref[1:2, :]).astype(BF)
        return carry

    over_chunks(last, 0)


def mix(place, lengths, residual, quarters, gains, biases):
    return pl.pallas_call(
        mix_kernel,
        out_shape=(
            sds((ROWS, 3 * D), BF),
            sds((SEQ_DEV * GROUPS, 1, PER_GROUP * LEN), F32),
            sds((ROWS, D), BF),
            sds((ROWS, D), F32),
            sds((ROWS, D), BF),
        ),
        in_specs=[SMEM_SPEC, SMEM_SPEC, VMEM_SPEC] + [ANY_SPEC] * 4 + [VMEM_SPEC] * 2,
        out_specs=(VMEM_SPEC,) * 5,
        scratch_shapes=[
            pltpu.VMEM((4, 4, 2, D // 8, D), BF),
            pltpu.VMEM((ROWS, D), BF),
            pltpu.SemaphoreType.DMA((8,)),
        ],
        compiler_params=pltpu.CompilerParams(vmem_limit_bytes=40 * MIB),
        cost_estimate=pl.CostEstimate(
            flops=2 * ROWS * D * 4 * D * 4, bytes_accessed=10 * MIB, transcendentals=0
        ),
    )(place, lengths, residual, *quarters, gains, biases)


def wide_kernel(
    place_ref,
    second_ref,
    middle_ref,
    u0_ref,
    u1_ref,
    u2_ref,
    u3_ref,
    d0_ref,
    d1_ref,
    shift_ref,
    biases_ref,
    active_ref,
    slope_ref,
    out_ref,
    held_up,
    held_down,
    up_sems,
    down_sems,
):
    tile = pl.program_id(0)
    up_copies = tile_copies(place_ref, (u0_ref, u1_ref, u2_ref, u3_ref), held_up, up_sems)
    down_copies = half_copies(place_ref, (d0_ref, d1_ref), held_down, down_sems)

    @pl.when(tile == 0)
    def _():
        for copy in up_copies + down_copies:
            copy.start()
        out_ref[...] = middle_ref[...] + biases_ref[5:6, :]
        for copy in up_copies + down_copies:
            copy.wait()

    up_tile = square(held_up[tile])
    down_tile = square(held_down[tile // 2, tile % 2])
    shift = shift_ref[pl.ds(tile, 1), :]
    for chunk in range(ROWS // CHUNK):
        rows = slice(chunk * CHUNK, (chunk + 1) * CHUNK)
        hidden = mul_nn(second_ref[rows, :], up_tile) + shift
        phi = 0.5 + 0.5 * lax.erf(hidden * math.sqrt(0.5))
        density = jnp.exp(hidden * hidden * -0.5) * (1.0 / math.sqrt(2.0 * math.pi))
        active = (hidden * phi).astype(BF)
        active_ref[0, rows, :] = active
        slope_ref[0, rows, :] = (phi + hidden * density).astype(BF)
        out_ref[rows, :] += mul_nn(active, down_tile)


def whole_block(shape):
    zeros = (0,) * len(shape)
    return pl.BlockSpec(shape, lambda *_: zeros)


def wide(place, second, middle, up_parts, down_parts, shift, biases):
    tile_block = pl.BlockSpec((1, ROWS, TILE), lambda tile: (tile, 0, 0))
    return pl.pallas_call(
        wide_kernel,
        grid=(TILES,),
        out_shape=(
            sds((TILES, ROWS, TILE), BF),
            sds((TILES, ROWS, TILE), BF),
            sds((ROWS, D), F32),
        ),
        in_specs=[SMEM_SPEC, whole_block((ROWS, D)), whole_block((ROWS, D))]
        + [ANY_SPEC] * 6
        + [whole_block((TILES, TILE)), whole_block((6, D))],
        out_specs=(tile_block, tile_block, whole_block((ROWS, D))),
        scratch_shapes=[
            pltpu.VMEM((TILES, 4, 2, D // 8, TILE), BF),
            pltpu.VMEM((4, 2, 2, TILE // 2, D), BF),
            pltpu.SemaphoreType.DMA((16,)),
            pltpu.SemaphoreType.DMA((4,)),
        ],
        compiler_params=pltpu.CompilerParams(vmem_limit_bytes=52 * MIB),
        cost_estimate=pl.CostEstimate(
            flops=2 * ROWS * D * FF * 6, bytes_accessed=30 * MIB, transcendentals=0
        ),
    )(place, second, middle, *up_parts, *down_parts, shift, biases)


def head_kernel(
    residual_ref,
    targets_ref,
    masked_ref,
    weight_ref,
    shift_ref,
    gain_ref,
    move_ref,
    activations_ref,
    grad_ref,
    rounded_ref,
    small_ref,
):
    small_ref[...] = jnp.zeros_like(small_ref)
    lanes = lax.broadcasted_iota(jnp.int32, (1, 128), 1)

    def body(rows, carry):
        weight_grad, gain_grad, move_grad, shift_grad, stats = carry
        residual = residual_ref[rows, :]
        activations_ref[rows, :] = residual.astype(BF)
        normed, inverse = normalize(residual)
        final = (normed * gain_ref[...] + move_ref[...]).astype(BF)
        logits = mul_nn(final, weight_ref[...]) + shift_ref[...]
        top = jnp.max(logits, -1, keepdims=True)
        log_total = top + jnp.log(jnp.sum(jnp.exp(logits - top), -1, keepdims=True))
        onehot = (targets_ref[rows, :] == lanes).astype(F32)
        picked = jnp.sum(logits * onehot, -1, keepdims=True)
        mask = masked_ref[rows, :].astype(F32)
        loss = col_sum(mask * (log_total - picked))
        hits = col_sum(mask * jnp.exp(picked - log_total))
        count = col_sum(mask)
        stats = stats + (
            jnp.where(lanes == 0, loss, 0.0)
            + jnp.where(lanes == 1, hits, 0.0)
            + jnp.where(lanes == 2, count, 0.0)
        )
        grad_logits = (mask * (jnp.exp(logits - log_total) - onehot)).astype(BF)
        weight_grad = weight_grad + mul_tn(grad_logits, final)
        shift_grad = shift_grad + col_sum(grad_logits.astype(F32))
        grad_final = mul_nt(grad_logits, weight_ref[...])
        gain_grad = gain_grad + col_sum(grad_final * normed)
        move_grad = move_grad + col_sum(grad_final)
        grad = norm_back(grad_final * gain_ref[...], normed, inverse)
        grad_ref[rows, :] = grad
        rounded_ref[rows, :] = grad.astype(BF)
        return weight_grad, gain_grad, move_grad, shift_grad, stats

    row = jnp.zeros((1, D), F32)
    narrow = jnp.zeros((1, 128), F32)
    weight_grad, gain_grad, move_grad, shift_grad, stats = over_chunks(
        body, (jnp.zeros((128, D), F32), row, row, narrow, narrow)
    )
    small_ref[0:32, :] = weight_grad[0:32, :]
    small_ref[32:33, :] = gain_grad
    small_ref[33:34, :] = move_grad
    small_ref[34:35, 0:128] = shift_grad
    small_ref[35:36, 0:128] = stats


def head(residual, targets, masked, weight, shift, gain, move):
    return pl.pallas_call(
        head_kernel,
        out_shape=(
            sds((ROWS, D), BF),
            sds((ROWS, D), F32),
            sds((ROWS, D), BF),
            sds((40, D), F32),
        ),
        in_specs=[VMEM_SPEC] * 7,
        out_specs=(VMEM_SPEC,) * 4,
        compiler_params=pltpu.CompilerParams(vmem_limit_bytes=32 * MIB),
        cost_estimate=pl.CostEstimate(
            flops=2 * ROWS * D * 128 * 8, bytes_accessed=5 * MIB, transcendentals=0
        ),
    )(residual, targets, masked, weight, shift, gain, move)


def down_back_kernel(place_ref, grad_ref, active_ref, send_ref, keep_ref, turned):
    @pl.when(pl.program_id(0) == 0)
    def _():
        for half in range(2):
            turned[half] = grad_ref[:, half * (D // 2) : (half + 1) * (D // 2)].T

    c_at = place_ref[2]
    active = active_ref[0]
    send_ref[0, 0] = mul_nn(turned[1 - c_at], active).astype(BF)
    keep_ref[0, 0] = mul_nn(turned[c_at], active).astype(BF)


def down_back(place, grad, active):
    def block_at(step, place_ref):
        return ((step % 4) * 2 + (place_ref[1] ^ (1 - step // 4)), 0, 0)

    out_block = pl.BlockSpec(
        (1, 1, D // 2, TILE), lambda step, place_ref: (1 - step // 4, step % 4, 0, 0)
    )
    out = sds((2, 4, D // 2, TILE), BF)
    return pl.pallas_call(
        down_back_kernel,
        grid_spec=pltpu.PrefetchScalarGridSpec(
            num_scalar_prefetch=1,
            grid=(TILES,),
            in_specs=[whole_block((ROWS, D)), pl.BlockSpec((1, ROWS, TILE), block_at)],
            out_specs=(out_block, out_block),
            scratch_shapes=[pltpu.VMEM((2, D // 2, ROWS), BF)],
        ),
        out_shape=(out, out),
        compiler_params=pltpu.CompilerParams(vmem_limit_bytes=32 * MIB),
        cost_estimate=pl.CostEstimate(
            flops=2 * ROWS * D * FF, bytes_accessed=13 * MIB, transcendentals=0
        ),
    )(place, grad, active)


def wide_back_kernel(
    place_ref,
    rounded_ref,
    grad_ref,
    second_ref,
    middle_ref,
    slope_ref,
    u0_ref,
    u1_ref,
    u2_ref,
    u3_ref,
    d0_ref,
    d1_ref,
    gains_ref,
    send_ref,
    keep_ref,
    shift_ref,
    middle_grad_ref,
    middle_rounded_ref,
    small_ref,
    held_up,
    held_down,
    turned,
    total,
    up_sems,
    down_sems,
):
    step = pl.program_id(0)
    up_copies = tile_copies(place_ref, (u0_ref, u1_ref, u2_ref, u3_ref), held_up, up_sems)
    down_copies = half_copies(place_ref, (d0_ref, d1_ref), held_down, down_sems)

    @pl.when(step == 0)
    def _():
        for copy in down_copies + up_copies:
            copy.start()
        turned[...] = second_ref[...].T
        total[...] = jnp.zeros_like(total)
        for copy in down_copies + up_copies:
            copy.wait()

    tile = wide_back_tile(step, place_ref)
    y_at = place_ref[1]
    grad_active = mul_nt(rounded_ref[...], square(held_down[tile // 2, tile % 2]))
    grad_hidden = (grad_active * slope_ref[0].astype(F32)).astype(BF)
    shift_ref[pl.ds(tile, 1), :] = col_sum(grad_hidden.astype(F32))
    total[...] += mul_nt(grad_hidden, square(held_up[tile]))
    up_grad = mul_nn(turned[...], grad_hidden).astype(BF).reshape(4, 2, D // 8, TILE)

    def store(out_ref):
        for side in range(2):
            out_ref[0, side ^ y_at] = up_grad[:, side]

    @pl.when(step < 4)
    def _():
        store(send_ref)

    @pl.when(step >= 4)
    def _():
        store(keep_ref)

    @pl.when(step == TILES - 1)
    def _():
        def body(rows, carry):
            gain_sum, move_sum, out_sum, down_sum = carry
            normed, inverse = normalize(middle_ref[rows, :])
            grad_second = total[rows, :]
            grad = grad_ref[rows, :] + norm_back(grad_second * gains_ref[1:2, :], normed, inverse)
            rounded = grad.astype(BF)
            middle_grad_ref[rows, :] = grad
            middle_rounded_ref[rows, :] = rounded
            return (
                gain_sum + col_sum(grad_second * normed),
                move_sum + col_sum(grad_second),
                out_sum + col_sum(rounded.astype(F32)),
                down_sum + col_sum(rounded_ref[rows, :].astype(F32)),
            )

        row = jnp.zeros((1, D), F32)
        sums = over_chunks(body, (row, row, row, row))
        small_ref[...] = jnp.zeros_like(small_ref)
        for number in range(4):
            small_ref[number : number + 1, :] = sums[number]


def wide_back_tile(step, place_ref):
    inner = step % 4
    quarter = (place_ref[0] ^ (1 - inner // 2)) * 2 + (place_ref[2] ^ (1 - step // 4))
    return quarter * 2 + inner % 2


def wide_back(place, rounded, grad, second, middle, slope, up_parts, down_parts, gains):
    def send_at(step, place_ref):
        inner = jnp.minimum(step, 3)
        return (1 - inner // 2, 0, 0, 0, inner % 2)

    def keep_at(step, place_ref):
        inner = jnp.maximum(step - 4, 0)
        return (1 - inner // 2, 0, 0, 0, inner % 2)

    out = sds((2, 2, 4, D // 8, 2 * TILE), BF)
    out_shape = (1, 2, 4, D // 8, TILE)
    full = whole_block((ROWS, D))
    return pl.pallas_call(
        wide_back_kernel,
        grid_spec=pltpu.PrefetchScalarGridSpec(
            num_scalar_prefetch=1,
            grid=(TILES,),
            in_specs=[full] * 4
            + [
                pl.BlockSpec(
                    (1, ROWS, TILE),
                    lambda step, place_ref: (wide_back_tile(step, place_ref), 0, 0),
                )
            ]
            + [ANY_SPEC] * 6
            + [whole_block((2, D))],
            out_specs=(
                pl.BlockSpec(out_shape, send_at),
                pl.BlockSpec(out_shape, keep_at),
                whole_block((TILES, TILE)),
                full,
                full,
                whole_block((8, D)),
            ),
            scratch_shapes=[
                pltpu.VMEM((TILES, 4, 2, D // 8, TILE), BF),
                pltpu.VMEM((4, 2, 2, TILE // 2, D), BF),
                pltpu.VMEM((D, ROWS), BF),
                pltpu.VMEM((ROWS, D), F32),
                pltpu.SemaphoreType.DMA((16,)),
                pltpu.SemaphoreType.DMA((4,)),
            ],
        ),
        out_shape=(
            out,
            out,
            sds((TILES, TILE), F32),
            sds((ROWS, D), F32),
            sds((ROWS, D), BF),
            sds((8, D), F32),
        ),
        compiler_params=pltpu.CompilerParams(vmem_limit_bytes=56 * MIB),
        cost_estimate=pl.CostEstimate(
            flops=2 * ROWS * D * FF * 4, bytes_accessed=30 * MIB, transcendentals=0
        ),
    )(place, rounded, grad, second, middle, slope, *up_parts, *down_parts, gains)


def mix_back_kernel(
    place_ref,
    lengths_ref,
    rounded_ref,
    middle_grad_ref,
    residual_ref,
    w0_ref,
    w1_ref,
    w2_ref,
    w3_ref,
    packed_ref,
    log_ref,
    mixed_ref,
    gains_ref,
    biases_ref,
    send_ref,
    keep_ref,
    grad_ref,
    grad_rounded_ref,
    small_ref,
    held,
    turned,
    grad_mixed,
    grad_packed,
    total,
    sems,
):
    x_at, y_at, c_at = place_ref[0], place_ref[1], place_ref[2]
    copies = quarter_copies(place_ref, (w0_ref, w1_ref, w2_ref, w3_ref), held, sems)
    for copy in copies:
        copy.start()

    def store_grad(part, value):
        value = value.astype(BF).reshape(4, 2, D // 8, D)
        dx, dc = x_at ^ (part >> 1), c_at ^ (part & 1)

        @pl.when(dc == 1)
        def _():
            for side in range(2):
                send_ref[dx, side ^ y_at] = value[:, side]

        @pl.when(dc == 0)
        def _():
            for side in range(2):
                keep_ref[dx, side ^ y_at] = value[:, side]

    turned[...] = mixed_ref[...].T
    store_grad(3, mul_nn(turned[...], rounded_ref[...]))

    def first(rows, carry):
        normed, inverse = normalize(residual_ref[rows, :].astype(F32))
        total[rows, :] = normed * gains_ref[0:1, :] + biases_ref[0:1, :]
        return carry

    over_chunks(first, 0)
    turned[...] = total[...].astype(BF).T
    for copy in copies:
        copy.wait()
    grad_mixed[...] = mul_nt(rounded_ref[...], square(held[3])).astype(BF)
    masks = head_masks()
    row_ids = lax.broadcasted_iota(jnp.int32, (LEN, 1), 0)
    scale = 1.0 / math.sqrt(HEAD_DIM)

    def one_sequence(seq, carry):
        rows = pl.ds(pl.multiple_of(seq * LEN, LEN), LEN)
        valid = row_ids < lengths_ref[seq]
        for group in range(GROUPS):
            at_query = slice(group * 128, (group + 1) * 128)
            at_key = slice(D + group * 128, D + (group + 1) * 128)
            at_value = slice(2 * D + group * 128, 2 * D + (group + 1) * 128)
            queries = stack_heads(packed_ref[rows, at_query], masks)
            key_rows = packed_ref[rows, at_key]
            value_rows = packed_ref[rows, at_value]
            grads = stack_heads(grad_mixed[rows, at_query], masks)
            scores = scores_of(key_rows, queries, valid)
            probs = jnp.exp(scores - log_ref[seq * GROUPS + group])
            grad_probs = mul_nt(value_rows, grads)
            inner = jnp.sum(grad_probs * probs, 0, keepdims=True)
            grad_scores = (probs * (grad_probs - inner)).astype(BF)
            grad_packed[rows, at_value] = mul_nn(probs.astype(BF), grads).astype(BF)
            grad_packed[rows, at_key] = (mul_nn(grad_scores, queries) * scale).astype(BF)
            grad_queries = unstack_heads(mul_tn(key_rows, grad_scores))
            grad_packed[rows, at_query] = (grad_queries * scale).astype(BF)
        return carry

    lax.fori_loop(0, SEQ_DEV, one_sequence, 0)
    for part in range(3):
        grads = grad_packed[:, part * D : (part + 1) * D]
        store_grad(part, mul_nn(turned[...], grads))
        result = mul_nt(grads, square(held[part]))
        if part == 0:
            total[...] = result
        else:
            total[...] += result

    def body(rows, carry):
        gain_sum, move_sum, query_sum, value_sum = carry
        normed, inverse = normalize(residual_ref[rows, :].astype(F32))
        grad_pre = total[rows, :]
        grad = middle_grad_ref[rows, :] + norm_back(grad_pre * gains_ref[0:1, :], normed, inverse)
        grad_ref[rows, :] = grad
        grad_rounded_ref[rows, :] = grad.astype(BF)
        return (
            gain_sum + col_sum(grad_pre * normed),
            move_sum + col_sum(grad_pre),
            query_sum + col_sum(grad_packed[rows, 0:D].astype(F32)),
            value_sum + col_sum(grad_packed[rows, 2 * D : 3 * D].astype(F32)),
        )

    row = jnp.zeros((1, D), F32)
    sums = over_chunks(body, (row, row, row, row))
    small_ref[...] = jnp.zeros_like(small_ref)
    for number in range(4):
        small_ref[number : number + 1, :] = sums[number]


def mix_back(
    place, lengths, rounded, middle_grad, residual, quarters, packed, logs, mixed, gains, biases
):
    out = sds((2, 2, 4, D // 8, D), BF)
    return pl.pallas_call(
        mix_back_kernel,
        out_shape=(out, out, sds((ROWS, D), F32), sds((ROWS, D), BF), sds((8, D), F32)),
        in_specs=[SMEM_SPEC, SMEM_SPEC] + [VMEM_SPEC] * 3 + [ANY_SPEC] * 4 + [VMEM_SPEC] * 5,
        out_specs=(VMEM_SPEC,) * 5,
        scratch_shapes=[
            pltpu.VMEM((4, 4, 2, D // 8, D), BF),
            pltpu.VMEM((D, ROWS), BF),
            pltpu.VMEM((ROWS, D), BF),
            pltpu.VMEM((ROWS, 3 * D), BF),
            pltpu.VMEM((ROWS, D), F32),
            pltpu.SemaphoreType.DMA((8,)),
        ],
        compiler_params=pltpu.CompilerParams(vmem_limit_bytes=48 * MIB),
        cost_estimate=pl.CostEstimate(
            flops=2 * ROWS * D * 4 * D * 8, bytes_accessed=18 * MIB, transcendentals=0
        ),
    )(
        place, lengths, rounded, middle_grad, residual, *quarters, packed, logs, mixed, gains, biases
    )


def swap(value, axis):
    return lax.ppermute(value, axis, [(0, 1), (1, 0)])


def as_rows(flat, width):
    return flat.reshape(-1, width // 128, 128)


class Moves:
    def __init__(self, fsdp):
        self.z_size = fsdp // 2
        self.staged = fsdp == 8
        self.x_at = lax.axis_index("x")
        self.y_at = lax.axis_index("y")
        self.c_at = lax.axis_index("c")
        self.place = jnp.stack([self.x_at, self.y_at, self.c_at]).astype(jnp.int32)

    def relative(self, value):
        value = value.swapaxes(0, 1)
        return jnp.where(self.y_at == 0, value, value[::-1])

    def natural(self, value):
        value = jnp.where(self.y_at == 0, value, value[::-1]).swapaxes(0, 1)
        return value.reshape(-1, value.shape[-1])

    def gather_quarters(self, flat, width):
        shard = as_rows(flat, width)
        rows, blocks, _ = shard.shape
        step = blocks // 4
        if not self.staged:
            whole = lax.all_gather(flat, ("z", "y"), axis=0, tiled=True).reshape(4, 2, D // 8, width)
            parts = []
            for number in range(4):
                quarter = (self.x_at ^ (number >> 1)) * 2 + (self.c_at ^ (number & 1))
                part = lax.dynamic_slice_in_dim(whole, quarter * (width // 4), width // 4, 3)
                parts.append(self.relative(part))
            return tuple(parts)
        own = lax.dynamic_slice_in_dim(shard, (self.x_at * 2 + self.c_at) * step, step, 1)
        own = own.reshape(rows, step * 128)
        line = lax.all_gather(own, "z", axis=0, tiled=False)
        plane = jnp.stack([line, swap(line, "y")])
        beside = swap(plane, "x")
        return (plane, swap(plane, "c"), beside, swap(beside, "c"))

    def gather_halves(self, flat):
        if not self.staged:
            whole = lax.all_gather(flat, ("z", "y"), axis=0, tiled=True)
            whole = whole.reshape(4, 2, 2, TILE // 2, D)
            return tuple(
                self.relative(lax.dynamic_index_in_dim(whole, self.c_at ^ number, 2, False))
                for number in range(2)
            )
        shard = as_rows(flat, D)
        half = shard.shape[0] // 2
        own = lax.dynamic_slice_in_dim(shard, self.c_at * half, half, 0).reshape(half, D)
        line = lax.all_gather(own, "z", axis=0, tiled=False)
        plane = jnp.stack([line, swap(line, "y")])
        return (plane, swap(plane, "c"))

    def reduce_quarters(self, send, keep):
        width = 4 * send.shape[-1]
        got_c = swap(send, "c").astype(F32)
        keep = keep.astype(F32)
        got_x = swap((keep[1] + got_c[1]).astype(BF), "x").astype(F32)
        if not self.staged:
            part = self.natural(keep[0] + got_c[0] + got_x).astype(BF)
            part = lax.psum_scatter(part, ("z", "y"), scatter_dimension=0, tiled=True)
        else:
            got_y = swap((keep[0, 1] + got_c[0, 1] + got_x[1]).astype(BF), "y").astype(F32)
            part = (keep[0, 0] + got_c[0, 0] + got_x[0] + got_y).astype(BF)
            part = lax.psum_scatter(part, "z", scatter_dimension=0, tiled=False)
        parts = lax.all_gather(part, ("x", "c"), axis=0, tiled=False)
        return parts.swapaxes(0, 1).reshape(-1, width).astype(F32).reshape(-1, 128)

    def reduce_halves(self, send, keep):
        got_c = swap(send, "c").astype(F32)
        keep = keep.astype(F32)
        if not self.staged:
            part = keep + got_c
            part = jnp.where(self.y_at == 0, part, part[::-1]).transpose(1, 0, 3, 2)
            part = part.reshape(FF, D // 2).astype(BF)
            part = lax.psum_scatter(part, ("z", "y"), scatter_dimension=0, tiled=True).T
        else:
            got_y = swap((keep[1] + got_c[1]).astype(BF), "y").astype(F32)
            part = (keep[0] + got_c[0] + got_y).astype(BF)
            part = lax.psum_scatter(part, "z", scatter_dimension=0, tiled=False)
        part = (part.astype(F32) + swap(part, "x").astype(F32)).astype(BF)
        parts = lax.all_gather(part, "c", axis=0, tiled=True)
        return parts.T.astype(F32).reshape(-1, 128)

    def sum_all(self, value):
        value = value + swap(value, "c")
        value = value + swap(value, "x")
        value = value + swap(value, "y")
        reach = 1
        while reach < self.z_size:
            pairs = [(at, at ^ reach) for at in range(self.z_size)]
            value = value + lax.ppermute(value, "z", pairs)
            reach *= 2
        return value


def local(
    fsdp,
    inputs,
    targets,
    masked,
    lengths,
    attn_weight,
    up_weight,
    down_weight,
    norm_gains,
    layer_biases,
    up_bias,
    head_weight,
    final_gain,
    final_shift,
    head_bias,
):
    moves = Moves(fsdp)
    place = moves.place
    targets = targets.reshape(ROWS, 1)
    masked = masked.reshape(ROWS, 1)
    head_padded = jnp.pad(head_weight, ((0, 0), (0, 128 - VOCAB)))
    bias_padded = jnp.pad(head_bias.reshape(1, VOCAB), ((0, 0), (0, 128 - VOCAB)), constant_values=-1e30)
    shifts = up_bias.reshape(LAYERS, TILES, TILE)
    residual = inputs
    saved = []
    for layer in range(LAYERS):
        quarters = moves.gather_quarters(attn_weight[layer], 4 * D)
        up_parts = moves.gather_quarters(up_weight[layer], FF)
        down_parts = moves.gather_halves(down_weight[layer])
        packed, logs, mixed, middle, second = mix(
            place, lengths, residual, quarters, norm_gains[layer], layer_biases[layer]
        )
        active, slope, output = wide(
            place, second, middle, up_parts, down_parts, shifts[layer], layer_biases[layer]
        )
        saved.append(
            (quarters, up_parts, down_parts, residual, packed, logs, mixed, middle, second, active, slope)
        )
        residual = output
    activations, grad, rounded, head_small = head(
        residual,
        targets,
        masked,
        head_padded,
        bias_padded,
        final_gain.reshape(1, D),
        final_shift.reshape(1, D),
    )
    small = [head_small]
    attn_grads = [None] * LAYERS
    up_grads = [None] * LAYERS
    down_grads = [None] * LAYERS
    for layer in reversed(range(LAYERS)):
        (quarters, up_parts, down_parts, residual, packed, logs, mixed, middle, second, active, slope) = (
            saved[layer]
        )
        send, keep = down_back(place, rounded, active)
        down_grads[layer] = moves.reduce_halves(send, keep)
        send, keep, shift_grad, middle_grad, middle_rounded, wide_small = wide_back(
            place, rounded, grad, second, middle, slope, up_parts, down_parts, norm_gains[layer]
        )
        up_grads[layer] = moves.reduce_quarters(send, keep)
        send, keep, grad, rounded, mix_small = mix_back(
            place,
            lengths,
            middle_rounded,
            middle_grad,
            residual,
            quarters,
            packed,
            logs,
            mixed,
            norm_gains[layer],
            layer_biases[layer],
        )
        attn_grads[layer] = moves.reduce_quarters(send, keep)
        small += [shift_grad, wide_small, mix_small]
    summed = moves.sum_all(jnp.concatenate(small, 0))
    gains_grad, biases_grad, shifts_grad = [], [], []
    for layer in range(LAYERS):
        base = 40 + 24 * (LAYERS - 1 - layer)
        shifts_grad.append(summed[base : base + 8].reshape(FF))
        wide_sums = summed[base + 8 : base + 16]
        mix_sums = summed[base + 16 : base + 24]
        gains_grad.append(jnp.stack([mix_sums[0], wide_sums[0]]))
        biases_grad.append(
            jnp.stack([mix_sums[1], wide_sums[1], mix_sums[2], mix_sums[3], wide_sums[2], wide_sums[3]])
        )
    totals = summed[35]
    return (
        activations,
        grad,
        jnp.stack(attn_grads),
        jnp.stack(up_grads),
        jnp.stack(down_grads),
        jnp.stack(gains_grad),
        jnp.stack(biases_grad),
        jnp.stack(shifts_grad),
        summed[:VOCAB].T,
        summed[32],
        summed[33],
        summed[34, :VOCAB],
        totals[0] / totals[2],
        totals[1] / totals[2],
        totals[2].astype(jnp.int32),
    )


def solution(mesh):
    fsdp, dp = mesh.shape["fsdp"], mesh.shape["dp"]
    fine = Mesh(mesh.devices.reshape(fsdp // 2, 2, dp // 2, 2), ("z", "y", "x", "c"))
    tokens = ("z", "y", "x", "c")
    flat = P(None, ("z", "y"), None)
    placed = (P(tokens, None), P(tokens), P(tokens), P(tokens), flat, flat, flat) + (P(),) * 7

    def run(*arrays):
        return local(fsdp, *arrays)

    return jax.shard_map(
        run,
        mesh=fine,
        in_specs=placed,
        out_specs=(P(tokens, None), P(tokens, None), flat, flat, flat) + (P(),) * 10,
        check_vma=False,
    )
```

time: 2010 us -> 745 us (0.37)
  waiting for transfers between devices: 1520 us -> 249 us
  matrix products: 231 us -> 0 us
  Pallas kernels: 0 us -> 188 us
  local copies, waits for them, and re-layouts: 167 us -> 48 us
  blocking collectives: 0 us -> 119 us
  starting transfers between devices: 1.73 us -> 35 us
  other arithmetic: 52.7 us -> 76.4 us
    reduce_scatter x6, waiting for transfers between devices: 921 us -> 0.07 us  [the longest x4 0.05 us: reduce_quarters(): part = lax.psum_scatter(part, 'z', scatter_dimension=0, tiled=False)]
    all_gather x6 -> x2, waiting for transfers between devices: 387 us -> 20.7 us  [gather_halves(): line = lax.all_gather(own, 'z', axis=0, tiled=False)]
    dot_general x39 -> x0, matrix products: 231 us -> none  [the longest x9 89.9 us: multiply(): return jnp.dot(left, right, preferred_element_type=jnp.float32)]
    ppermute x0 -> x43, waiting for transfers between devices: none -> 228 us  [the longest x41 213 us: swap(): return lax.ppermute(value, axis, [(0, 1), (1, 0)])]
    psum x2 -> x0, waiting for transfers between devices: 212 us -> none  [the longest x1 127 us: local(): lax.psum((jnp.stack(gain_list), jnp.stack(bias_list), jnp.stack(upshift_l...]
    pallas_call x0 -> x11, Pallas kernels: none -> 188 us  [the longest x2 56.3 us: wide_back(): pl.pallas_call(wide_back_kernel, grid_spec=pltpu.PrefetchScalarGridSpec(n...]
    reshape x20 -> x4, local copies, waits for them, and re-layouts: 135 us -> 0.3 us  [the longest x1 0.15 us: local(): targets = targets.reshape(ROWS, 1)]
    all_gather x0 -> x10, blocking collectives: none -> 119 us  [the longest x4 82.8 us: gather_quarters(): line = lax.all_gather(own, 'z', axis=0, tiled=False)]
  transfers between devices with their start and end apart: 14 -> 51, of which waited for: 13 -> 18; matrix products, arithmetic and copies ran while one was open for 17% -> 12% of each run, Pallas kernels for 0% -> 11%
where the time goes in v1:
time: 745 us; the launch traced here: 738 us
  waiting for transfers between devices  249 us (33%)
  Pallas kernels  188 us (25%)
  blocking collectives  119 us (16%)
  other arithmetic  76.4 us (10%)
  local copies, waits for them, and re-layouts  48 us (6%)
  starting transfers between devices  35 us (5%)
  between operations  22.6 us (3%)
    ppermute x41, waiting for transfers between devices, swap(): return lax.ppermute(value, axis, [(0, 1), (1, 0)])  213 us
    all_gather x4, blocking collectives, gather_quarters(): line = lax.all_gather(own, 'z', axis=0, tiled=False)  82.8 us
    pallas_call x2, Pallas kernels, wide_back(): pl.pallas_call(wide_back_kernel, grid_spec=pltpu.PrefetchScalarGridSpec(n...  56.3 us
    pallas_call x2, Pallas kernels, wide(): pl.pallas_call(wide_kernel, grid=(TILES,), out_shape=(sds((TILES, ROWS, T...  46.4 us
    pallas_call x2, Pallas kernels, mix_back(): pl.pallas_call(mix_back_kernel, out_shape=(out, out, sds((ROWS, D), F32),...  41.6 us
    ppermute x41, starting transfers between devices, swap(): return lax.ppermute(value, axis, [(0, 1), (1, 0)])  31.7 us
    all_gather x4, blocking collectives, reduce_quarters(): parts = lax.all_gather(part, ('x', 'c'), axis=0, tiled=False)  31.5 us
    unnamed x167, local copies, waits for them, and re-layouts  29.3 us
  transfers between devices with their start and end apart: 51, of which 18 were waited for; matrix products, arithmetic and copies ran while one was open for 12% of the time, Pallas kernels for 11%

profile of v1, /device:TPU:0, one launch (start us, length us, event | category | flops | bytes accessed | tf_op | source)
XLA Modules:
  0.0 738.5 jit_solution(13814931255913300758)
XLA Ops:
  13.4 19.3 %all_gather.39 = bf16[4,80,640]{2,1,0:T(8,128)(2,1)} all-gather(bf16[1,80,640]{2,1,0:T(8,128)(2,1)S(1)} %all_gather_reshape.21), channel_id=1, replica_groups=mesh['z'=4,'y'=2,'x'=2,'c'=2] {'z'}, dimensions={0}, use_global_device_ids=true | all-gather | bytes 512000 | tf_op jit(solution)/shard_map/all_gather | solution.py:765
  35.7 20.7 %all-gather.3.cloned.1.call-done = bf16[4,320,640]{2,1,0:T(8,128)(2,1)} async-done(((bf16[1,320,640]{2,1,0:T(8,128)(2,1)}), bf16[4,320,640]{2,1,0:T(8,128)(2,1)}) %all-gather.3.cloned.1.call-update) | async-done | bytes 1638416 | tf_op jit(solution)/shard_map/all_gather | solution.py:781
  60.2 27.0 %all_gather.37 = bf16[4,80,1280]{2,1,0:T(8,128)(2,1)} all-gather(bf16[1,80,1280]{2,1,0:T(8,128)(2,1)S(1)} %all_gather_reshape.19), channel_id=1, replica_groups=mesh['z'=4,'y'=2,'x'=2,'c'=2] {'z'}, dimensions={0}, use_global_device_ids=true | all-gather | bytes 1024000 | tf_op jit(solution)/shard_map/all_gather | solution.py:765
  87.5 18.9 %all_gather.36 = bf16[4,80,640]{2,1,0:T(8,128)(2,1)S(1)} all-gather(bf16[1,80,640]{2,1,0:T(8,128)(2,1)S(1)} %all_gather_reshape.18), channel_id=1, replica_groups=mesh['z'=4,'y'=2,'x'=2,'c'=2] {'z'}, dimensions={0}, use_global_device_ids=true | all-gather | bytes 512000 | tf_op jit(solution)/shard_map/all_gather | solution.py:765
  106.4 1.9 collective-permute-start
  108.5 17.6 %all_gather.40 = bf16[4,80,1280]{2,1,0:T(8,128)(2,1)S(1)} all-gather(bf16[1,80,1280]{2,1,0:T(8,128)(2,1)S(1)} %all_gather_reshape.22), channel_id=1, replica_groups=mesh['z'=4,'y'=2,'x'=2,'c'=2] {'z'}, dimensions={0}, use_global_device_ids=true | all-gather | bytes 1024000 | tf_op jit(solution)/shard_map/all_gather | solution.py:765
  127.9 2.7 pad_maximum_fusion.2.u0_ref
  131.1 2.0 collective-permute-start.18
  133.1 4.0 pad_maximum_fusion.d0_ref
  137.1 10.4 %collective-permute-done.14 = bf16[4,80,1280]{2,1,0:T(8,128)(2,1)} collective-permute-done((bf16[4,80,1280]{2,1,0:T(8,128)(2,1)S(1)}, bf16[4,80,1280]{2,1,0:T(8,128)(2,1)}, u32[]{:S(2)}, u32[]{:S(2)}) %collective-permute-start.14) | collective-permute-done | bytes 819232 | tf_op jit(solution)/shard_map/ppermute | solution.py:727
  151.4 2.6 pad_maximum_fusion.3.u0_ref
  154.0 40.2 %collective-permute-done.12.w2_ref = bf16[2,4,80,640]{3,2,1,0:T(8,128)(2,1)S(1)} collective-permute-done((bf16[2,4,80,640]{3,2,1,0:T(8,128)(2,1)S(1)}, bf16[2,4,80,640]{3,2,1,0:T(8,128)(2,1)S(1)}, u32[]{:S(2)}, u32[]{:S(2)}) %collective-permute-start.12) | collective-permute-done | bytes 819232 | tf_op jit(solution)/shard_map/ppermute | solution.py:727
  196.0 2.0 pad_maximum_fusion.1.d0_ref
  203.6 12.6 %shard_map.253 = (bf16[512,1920]{1,0:T(8,128)(2,1)S(1)}, f32[20,1,512]{2,1,0:T(1,128)S(1)}, bf16[512,640]{1,0:T(8,128)(2,1)S(1)}, f32[512,640]{1,0:T(8,128)S(1)}, bf16[512,640]{1,0:T(8,128)(2,1)S(1)}) custom-call(s32[3]{0:T(128)S(1)} %pad_add_fusion.place_ref, s32[4]{0:T(128)S(1)} %copy-done.17, bf16[512,640]{1,0:T(8,128)(2,1)S(1)} %copy-done.15, ...), custom_call_target="tpu_custom_call" | custom-call | flops 6710886400 | bytes 10485760 | tf_op jit(solution)/shard_map/pallas_call | solution.py:221
  218.2 14.6 %collective-permute-done.16.u2_ref = bf16[2,4,80,1280]{3,2,1,0:T(8,128)(2,1)} collective-permute-done((bf16[2,4,80,1280]{3,2,1,0:T(8,128)(2,1)}, bf16[2,4,80,1280]{3,2,1,0:T(8,128)(2,1)}, u32[]{:S(2)}, u32[]{:S(2)}) %collective-permute-start.16) | collective-permute-done | bytes 1638432 | tf_op jit(solution)/shard_map/ppermute | solution.py:727
  233.4 23.0 %shard_map.254 = (bf16[8,512,640]{2,1,0:T(8,128)(2,1)}, bf16[8,512,640]{2,1,0:T(8,128)(2,1)}, f32[512,640]{1,0:T(8,128)S(1)}) custom-call(s32[3]{0:T(128)S(1)} %pad_add_fusion.place_ref, bf16[512,640]{1,0:T(8,128)(2,1)S(1)} %get-tuple-element.60.second_ref, f32[512,640]{1,0:T(8,128)} %copy-done.27, bf16[2,4,80,1280]{3,2,1,0:T(8,128)(2,1)} %pad_maximum_fusion.2.u0_ref, ...), custom_call_target="tpu_custom_call" | custom-call | flops 20132659200 | bytes 31457280 | tf_op jit(solution)/shard_map/pallas_call | solution.py:297
  256.5 12.3 %shard_map.255 = (bf16[512,1920]{1,0:T(8,128)(2,1)S(1)}, f32[20,1,512]{2,1,0:T(1,128)S(1)}, bf16[512,640]{1,0:T(8,128)(2,1)S(1)}, f32[512,640]{1,0:T(8,128)S(1)}, bf16[512,640]{1,0:T(8,128)(2,1)S(1)}) custom-call(s32[3]{0:T(128)S(1)} %pad_add_fusion.place_ref, s32[4]{0:T(128)S(1)} %copy-done.17, f32[512,640]{1,0:T(8,128)S(1)} %get-tuple-element.62.residual_ref, ...), custom_call_target="tpu_custom_call" | custom-call | flops 6710886400 | bytes 10485760 | tf_op jit(solution)/shard_map/pallas_call | solution.py:221
  272.0 23.4 %shard_map.256 = (bf16[8,512,640]{2,1,0:T(8,128)(2,1)}, bf16[8,512,640]{2,1,0:T(8,128)(2,1)}, f32[512,640]{1,0:T(8,128)S(1)}) custom-call(s32[3]{0:T(128)S(1)} %pad_add_fusion.place_ref, bf16[512,640]{1,0:T(8,128)(2,1)S(1)} %get-tuple-element.63.second_ref, f32[512,640]{1,0:T(8,128)} %copy-done.26, bf16[2,4,80,1280]{3,2,1,0:T(8,128)(2,1)} %pad_maximum_fusion.3.u0_ref, ...), custom_call_target="tpu_custom_call" | custom-call | flops 20132659200 | bytes 31457280 | tf_op jit(solution)/shard_map/pallas_call | solution.py:297
  295.4 4.6 shard_map.257
  302.0 28.2 %shard_map.258 = (bf16[2,2,4,80,1280]{4,3,2,1,0:T(8,128)(2,1)}, bf16[2,2,4,80,1280]{4,3,2,1,0:T(8,128)(2,1)}, f32[8,640]{1,0:T(8,128)}, f32[512,640]{1,0:T(8,128...) custom-call(s32[3]{0:T(128)} %copy-done.4, bf16[512,640]{1,0:T(8,128)(2,1)} %copy-done.19, f32[512,640]{1,0:T(8,128)} %copy-done.18, ...), custom_call_target="tpu_custom_call" | custom-call | flops 13421772800 | bytes 31457280 | tf_op jit(solution)/shard_map/pallas_call | solution.py:538
  331.3 20.8 %shard_map.259 = (bf16[2,2,4,80,640]{4,3,2,1,0:T(8,128)(2,1)}, bf16[2,2,4,80,640]{4,3,2,1,0:T(8,128)(2,1)}, f32[512,640]{1,0:T(8,128)}, bf16[512,640]{1,0:T(8,128)(2,1)S(1)}, f32[8,640]{1,0:T(8,128)S(1)}) custom-call(s32[3]{0:T(128)S(1)} %copy-done.5, s32[4]{0:T(128)S(1)} %copy-done.17, bf16[512,640]{1,0:T(8,128)(2,1)S(1)} %copy-done.35, ...), custom_call_target="tpu_custom_call" | custom-call | flops 13421772800 | bytes 18874368 | tf_op jit(solution)/shard_map/pallas_call | solution.py:704
  353.0 28.2 %shard_map.260 = (bf16[2,2,4,80,1280]{4,3,2,1,0:T(8,128)(2,1)}, bf16[2,2,4,80,1280]{4,3,2,1,0:T(8,128)(2,1)}, f32[8,640]{1,0:T(8,128)}, f32[512,640]{1,0:T(8,128...) custom-call(s32[3]{0:T(128)} %copy-done.4, bf16[512,640]{1,0:T(8,128)(2,1)} %copy-done.21, ...), custom_call_target="tpu_custom_call" | custom-call | flops 13421772800 | bytes 31457280 | tf_op jit(solution)/shard_map/pallas_call | solution.py:538
  382.8 20.7 %shard_map.261 = (bf16[2,2,4,80,640]{4,3,2,1,0:T(8,128)(2,1)}, bf16[2,2,4,80,640]{4,3,2,1,0:T(8,128)(2,1)}, f32[512,640]{1,0:T(8,128)}, bf16[512,640]{1,0:T(8,128)(2,1)}, f32[8,640]{1,0:T(8,128)S(1)}) custom-call(s32[3]{0:T(128)S(1)} %copy-done.6, s32[4]{0:T(128)S(1)} %copy-done.17, bf16[512,640]{1,0:T(8,128)(2,1)S(1)} %copy-done.34, ...), custom_call_target="tpu_custom_call" | custom-call | flops 13421772800 | bytes 18874368 | tf_op jit(solution)/shard_map/pallas_call | solution.py:704
  411.2 7.2 shard_map.263
  419.3 1.9 copy-done.50
  424.8 4.2 collective-permute-done.21
  430.3 2.6 convert_element_type.243
  432.9 1.7 fusion.10
  435.9 2.1 fusion.40
  439.2 7.4 collective-permute-done.24
  450.1 2.6 convert_element_type.253
  454.2 1.8 copy-done.38
  458.3 23.4 %collective-permute-done.27 = bf16[2,4,80,1280]{3,2,1,0:T(8,128)(2,1)} collective-permute-done((bf16[2,4,80,1280]{3,2,1,0:T(8,128)(2,1)}, bf16[2,4,80,1280]{3,2,1,0:T(8,128)(2,1)}, u32[]{:S(2)}, u32[]{:S(2)}) %collective-permute-start.27) | collective-permute-done | bytes 1638432 | tf_op jit(solution)/shard_map/ppermute | solution.py:727
  481.7 1.7 convert_element_type.246
  483.5 4.3 fusion.22
  489.0 2.4 fusion.37
  491.6 24.4 %collective-permute-done.30 = bf16[2,4,80,1280]{3,2,1,0:T(8,128)(2,1)} collective-permute-done((bf16[2,4,80,1280]{3,2,1,0:T(8,128)(2,1)}, bf16[2,4,80,1280]{3,2,1,0:T(8,128)(2,1)}, u32[]{:S(2)}, u32[]{:S(2)}) %collective-permute-start.30) | collective-permute-done | bytes 1638432 | tf_op jit(solution)/shard_map/ppermute | solution.py:727
  516.0 3.4 convert_element_type.256
  519.5 3.4 fusion.26
  523.0 2.8 fusion.15
  528.6 7.2 shard_map.262
  535.8 2.4 convert_element_type.273
  539.9 2.2 copy-done.41
  542.9 2.4 collective-permute-done.31
  545.3 3.3 fusion.19
  549.9 30.7 %collective-permute-done.36 = bf16[4,320,640]{2,1,0:T(8,128)(2,1)} collective-permute-done((bf16[4,320,640]{2,1,0:T(8,128)(2,1)}, bf16[4,320,640]{2,1,0:T(8,128)(2,1)}, u32[]{:S(2)}, u32[]{:S(2)}) %collective-permute-start.36) | collective-permute-done | bytes 1638432 | tf_op jit(solution)/shard_map/ppermute | solution.py:727
  580.6 5.0 fusion.3
  593.4 2.3 convert_element_type.263
  597.5 2.2 collective-permute-done.39
  600.9 37.9 %collective-permute-done.40 = f32[88,640]{1,0:T(8,128)S(1)} collective-permute-done((f32[88,640]{1,0:T(8,128)S(1)}, f32[88,640]{1,0:T(8,128)S(1)}, u32[]{:S(2)}, u32[]{:S(2)}) %collective-permute-start.40) | collective-permute-done | bytes 225312 | tf_op jit(solution)/shard_map/ppermute | solution.py:727
  639.8 5.5 collective-permute-done.41
  645.3 1.8 collective-permute-start.42
  647.1 9.5 %collective-permute-done.42 = f32[88,640]{1,0:T(8,128)S(1)} collective-permute-done((f32[88,640]{1,0:T(8,128)S(1)}, f32[88,640]{1,0:T(8,128)S(1)}, u32[]{:S(2)}, u32[]{:S(2)}) %collective-permute-start.42) | collective-permute-done | bytes 225312 | tf_op jit(solution)/shard_map/ppermute | solution.py:823
  661.8 1.7 fusion.7
  666.1 6.4 all_gather.42
  672.8 6.9 all_gather.43
  681.3 9.1 %all_gather.44 = bf16[4,80,1280]{2,1,0:T(8,128)(2,1)S(1)} all-gather(bf16[1,80,1280]{2,1,0:T(8,128)(2,1)} %reduce-scatter.11.cloned.1.call-done), channel_id=1, replica_groups=mesh['z'=4,'y'=2,'x'=2,'c'=2] {'x','c'}, dimensions={0}, use_global_device_ids=true | all-gather | bytes 1024000 | tf_op jit(solution)/shard_map/all_gather | solution.py:797
  691.2 9.1 %all_gather.45 = bf16[4,80,1280]{2,1,0:T(8,128)(2,1)S(1)} all-gather(bf16[1,80,1280]{2,1,0:T(8,128)(2,1)} %reduce-scatter.13.cloned.1.call-done), channel_id=1, replica_groups=mesh['z'=4,'y'=2,'x'=2,'c'=2] {'x','c'}, dimensions={0}, use_global_device_ids=true | all-gather | bytes 1024000 | tf_op jit(solution)/shard_map/all_gather | solution.py:797
  702.0 1.9 maximum_convert_fusion
  705.1 8.5 %collective-permute-done.37 = bf16[320,640]{1,0:T(8,128)(2,1)S(1)} collective-permute-done((bf16[320,640]{1,0:T(8,128)(2,1)}, bf16[320,640]{1,0:T(8,128)(2,1)S(1)}, u32[]{:S(2)}, u32[]{:S(2)}) %collective-permute-start.37) | collective-permute-done | bytes 409632 | tf_op jit(solution)/shard_map/ppermute | solution.py:727
  713.7 2.4 all_gather.47
  717.7 4.2 collective-permute-done.34
  722.0 2.4 all_gather.46
  725.9 1.9 maximum_convert_fusion.1
  (341 shorter events, 93.8 us)
Async XLA Ops:
  7.2 49.2 %all-gather.3.cloned.1.call-start = ((), (), s32[]{:S(2)}) async-start(), calls=%async_computation.6 | async-start | bytes 2048000 | tf_op jit(solution)/shard_map/all_gather | solution.py:781
  13.0 118.2 %all-gather.5.cloned.1.call-start = ((), (), s32[]{:S(2)}) async-start(), calls=%async_computation.7 | async-start | bytes 2048000 | tf_op jit(solution)/shard_map/all_gather | solution.py:781
  13.3 44.6 %copy-start.54 = (bf16[2,3200,128]{2,1,0:T(8,128)(2,1)S(1)}, bf16[2,3200,128]{2,1,0:T(8,128)(2,1)}, u32[]{:S(2)}) copy-start(bf16[2,3200,128]{2,1,0:T(8,128)(2,1)} %param.19) | copy-start | bytes 4915204
  32.7 104.4 %collective-permute-start.10 = (bf16[4,80,640]{2,1,0:T(8,128)(2,1)}, bf16[4,80,640]{2,1,0:T(8,128)(2,1)}, u32[]{:S(2)}, u32[]{:S(2)}) collective-permute-start(bf16[4,80,640]{2,1,0:T(8,128)(2,1)} %all_gather.39), channel_id=1, source_target_pairs={{0,4},{4,0},{1,5},{5,1},{2,6},{6,2},{3,7},{7,3},{8,12},{12,8},{9,1... | collective-permute-start | bytes 1228808 | tf_op jit(solution)/shard_map/ppermute | solution.py:727
  35.6 630.5 %reduce-scatter.7.cloned.1.call-start = ((), (), s32[]{:S(2)}) async-start(), calls=%async_computation.8 | async-start | bytes 512000 | tf_op jit(solution)/shard_map/reduce_scatter | solution.py:796
  56.4 74.8 %collective-permute-start.8 = (bf16[4,320,640]{2,1,0:T(8,128)(2,1)}, bf16[4,320,640]{2,1,0:T(8,128)(2,1)}, u32[]{:S(2)}, u32[]{:S(2)}) collective-permute-start(bf16[4,320,640]{2,1,0:T(8,128)(2,1)} %all-gather.3.cloned.1.call-done), channel_id=1, source_target_pairs={{0,4},{4,0},{1,5},{5,1},{2,6},{6,2},{3,7},{7,3},{8,12},{12,8},{9,1... | collective-permute-start | bytes 4915208 | tf_op jit(solution)/shard_map/ppermute | solution.py:727
  87.2 40.8 %collective-permute-start.4 = (bf16[4,80,1280]{2,1,0:T(8,128)(2,1)}, bf16[4,80,1280]{2,1,0:T(8,128)(2,1)}, u32[]{:S(2)}, u32[]{:S(2)}) collective-permute-start(bf16[4,80,1280]{2,1,0:T(8,128)(2,1)} %all_gather.37), channel_id=1, source_target_pairs={{0,4},{4,0},{1,5},{5,1},{2,6},{6,2},{3,7},{7,3},{8,12},{12,8},{9,1... | collective-permute-start | bytes 2457608 | tf_op jit(solution)/shard_map/ppermute | solution.py:727
  106.4 19.9 %collective-permute-start = (bf16[4,80,640]{2,1,0:T(8,128)(2,1)S(1)}, bf16[4,80,640]{2,1,0:T(8,128)(2,1)S(1)}, u32[]{:S(2)}, u32[]{:S(2)}) collective-permute-start(bf16[4,80,640]{2,1,0:T(8,128)(2,1)S(1)} %all_gather.36), channel_id=1, source_target_pairs={{0,4},{4,0},{1,5},{5,1},{2,6},{6,2},{3,7},{7,3},{8,12},{12,8},{9,1... | collective-permute-start | bytes 1228808 | tf_op jit(solution)/shard_map/ppermute | solution.py:727
  126.2 21.3 %collective-permute-start.14 = (bf16[4,80,1280]{2,1,0:T(8,128)(2,1)S(1)}, bf16[4,80,1280]{2,1,0:T(8,128)(2,1)}, u32[]{:S(2)}, u32[]{:S(2)}) collective-permute-start(bf16[4,80,1280]{2,1,0:T(8,128)(2,1)S(1)} %all_gather.40), channel_id=1, source_target_pairs={{0,4},{4,0},{1,5},{5,1},{2,6},{6,2},{3,7},{7,3},{8,12},{12,8},{9,1... | collective-permute-start | bytes 2457608 | tf_op jit(solution)/shard_map/ppermute | solution.py:727
  126.3 22.4 %collective-permute-start.2 = (bf16[2,4,80,640]{3,2,1,0:T(8,128)(2,1)S(1)}, bf16[2,4,80,640]{3,2,1,0:T(8,128)(2,1)S(1)}, u32[]{:S(2)}, u32[]{:S(2)}) collective-permute-start(bf16[2,4,80,640]{3,2,1,0:T(8,128)(2,1)S(1)} %pad_maximum_fusion.4.w0_ref), channel_id=1, source_target_pairs={{0,2},{2,0},{1,3},{3,1},{4,6},{6,4},{5,7},{7,5},{8,10},{10,8},{9,1... | collective-permute-start | bytes 2457608 | tf_op jit(solution)/shard_map/ppermute | solution.py:727
  130.6 63.6 %collective-permute-start.6 = (bf16[2,4,80,1280]{3,2,1,0:T(8,128)(2,1)}, bf16[2,4,80,1280]{3,2,1,0:T(8,128)(2,1)}, u32[]{:S(2)}, u32[]{:S(2)}) collective-permute-start(bf16[2,4,80,1280]{3,2,1,0:T(8,128)(2,1)} %pad_maximum_fusion.2.u0_ref), channel_id=1, source_target_pairs={{0,2},{2,0},{1,3},{3,1},{4,6},{6,4},{5,7},{7,5},{8,10},{10,8},{9,1... | collective-permute-start | bytes 4915208 | tf_op jit(solution)/shard_map/ppermute | solution.py:727
  131.1 64.5 %collective-permute-start.18 = (bf16[4,320,640]{2,1,0:T(8,128)(2,1)}, bf16[4,320,640]{2,1,0:T(8,128)(2,1)S(1)}, u32[]{:S(2)}, u32[]{:S(2)}) collective-permute-start(bf16[4,320,640]{2,1,0:T(8,128)(2,1)} %all-gather.5.cloned.1.call-done), channel_id=1, source_target_pairs={{0,4},{4,0},{1,5},{5,1},{2,6},{6,2},{3,7},{7,3},{8,12},{12,8},{9,1... | collective-permute-start | bytes 4915208 | tf_op jit(solution)/shard_map/ppermute | solution.py:727
  137.1 96.2 %collective-permute-start.9 = (bf16[2,4,320,640]{3,2,1,0:T(8,128)(2,1)}, bf16[2,4,320,640]{3,2,1,0:T(8,128)(2,1)}, u32[]{:S(2)}, u32[]{:S(2)}) collective-permute-start(bf16[2,4,320,640]{3,2,1,0:T(8,128)(2,1)} %pad_maximum_fusion.d0_ref), channel_id=1, source_target_pairs={{0,1},{1,0},{2,3},{3,2},{4,5},{5,4},{6,7},{7,6},{8,9},{9,8},{10,11... | collective-permute-start | bytes 9830408 | tf_op jit(solution)/shard_map/ppermute | solution.py:727
  147.5 2.8 collective-permute-start.1
  148.7 45.6 %collective-permute-start.12 = (bf16[2,4,80,640]{3,2,1,0:T(8,128)(2,1)S(1)}, bf16[2,4,80,640]{3,2,1,0:T(8,128)(2,1)S(1)}, u32[]{:S(2)}, u32[]{:S(2)}) collective-permute-start(bf16[2,4,80,640]{3,2,1,0:T(8,128)(2,1)S(1)} %pad_maximum_fusion.5.w0_ref), channel_id=1, source_target_pairs={{0,2},{2,0},{1,3},{3,1},{4,6},{6,4},{5,7},{7,5},{8,10},{10,8},{9,1... | collective-permute-start | bytes 2457608 | tf_op jit(solution)/shard_map/ppermute | solution.py:727
  151.2 46.9 %collective-permute-start.3 = (bf16[2,4,80,640]{3,2,1,0:T(8,128)(2,1)S(1)}, bf16[2,4,80,640]{3,2,1,0:T(8,128)(2,1)S(1)}, u32[]{:S(2)}, u32[]{:S(2)}) collective-permute-start(bf16[2,4,80,640]{3,2,1,0:T(8,128)(2,1)S(1)} %collective-permute-done.2.w2_ref), channel_id=1, source_target_pairs={{0,1},{1,0},{2,3},{3,2},{4,5},{5,4},{6,7},{7,6},{8,9},{9,8},{10,11... | collective-permute-start | bytes 2457608 | tf_op jit(solution)/shard_map/ppermute | solution.py:727
  151.4 44.4 %copy-start.67 = (f32[2,2,640]{2,1,0:T(2,128)S(1)}, f32[2,2,640]{2,1,0:T(2,128)}, u32[]{:S(2)}) copy-start(f32[2,2,640]{2,1,0:T(2,128)} %param.21) | copy-start | bytes 30724
  151.4 44.4 %copy-start.62 = (f32[2,6,640]{2,0,1:T(2,128)S(1)}, f32[2,6,640]{2,0,1:T(2,128)}, u32[]{:S(2)}) copy-start(f32[2,6,640]{2,0,1:T(2,128)} %param.22) | copy-start | bytes 92164
  151.4 44.5 %copy-start.55 = (bf16[4,320,640]{2,1,0:T(8,128)(2,1)S(1)}, bf16[4,320,640]{2,1,0:T(8,128)(2,1)}, u32[]{:S(2)}) copy-start(bf16[4,320,640]{2,1,0:T(8,128)(2,1)} %all-gather.5.cloned.1.call-done) | copy-start | bytes 4915204
  194.3 23.8 %collective-permute-start.5 = (bf16[2,4,80,1280]{3,2,1,0:T(8,128)(2,1)}, bf16[2,4,80,1280]{3,2,1,0:T(8,128)(2,1)}, u32[]{:S(2)}, u32[]{:S(2)}) collective-permute-start(bf16[2,4,80,1280]{3,2,1,0:T(8,128)(2,1)} %pad_maximum_fusion.2.u0_ref), channel_id=1, source_target_pairs={{0,1},{1,0},{2,3},{3,2},{4,5},{5,4},{6,7},{7,6},{8,9},{9,8},{10,11... | collective-permute-start | bytes 4915208 | tf_op jit(solution)/shard_map/ppermute | solution.py:727
  194.3 38.5 %collective-permute-start.16 = (bf16[2,4,80,1280]{3,2,1,0:T(8,128)(2,1)}, bf16[2,4,80,1280]{3,2,1,0:T(8,128)(2,1)}, u32[]{:S(2)}, u32[]{:S(2)}) collective-permute-start(bf16[2,4,80,1280]{3,2,1,0:T(8,128)(2,1)} %pad_maximum_fusion.3.u0_ref), channel_id=1, source_target_pairs={{0,2},{2,0},{1,3},{3,1},{4,6},{6,4},{5,7},{7,5},{8,10},{10,8},{9,1... | collective-permute-start | bytes 4915208 | tf_op jit(solution)/shard_map/ppermute | solution.py:727
  195.6 37.2 %collective-permute-start.7 = (bf16[2,4,80,1280]{3,2,1,0:T(8,128)(2,1)}, bf16[2,4,80,1280]{3,2,1,0:T(8,128)(2,1)}, u32[]{:S(2)}, u32[]{:S(2)}) collective-permute-start(bf16[2,4,80,1280]{3,2,1,0:T(8,128)(2,1)} %collective-permute-done.6.u2_ref), channel_id=1, source_target_pairs={{0,1},{1,0},{2,3},{3,2},{4,5},{5,4},{6,7},{7,6},{8,9},{9,8},{10,11... | collective-permute-start | bytes 4915208 | tf_op jit(solution)/shard_map/ppermute | solution.py:727
  195.8 60.6 %copy-start.2 = (f32[2,640]{1,0:T(2,128)}, f32[2,640]{1,0:T(2,128)S(1)}, u32[]{:S(2)}) copy-start(f32[2,640]{1,0:T(2,128)S(1)} %get-tuple-element.179.gains_ref) | copy-start | bytes 15364
  199.0 73.0 %collective-permute-start.19 = (bf16[2,4,320,640]{3,2,1,0:T(8,128)(2,1)}, bf16[2,4,320,640]{3,2,1,0:T(8,128)(2,1)}, u32[]{:S(2)}, u32[]{:S(2)}) collective-permute-start(bf16[2,4,320,640]{3,2,1,0:T(8,128)(2,1)} %pad_maximum_fusion.1.d0_ref), channel_id=1, source_target_pairs={{0,1},{1,0},{2,3},{3,2},{4,5},{5,4},{6,7},{7,6},{8,9},{9,8},{10,11... | collective-permute-start | bytes 9830408 | tf_op jit(solution)/shard_map/ppermute | solution.py:727
  200.2 71.8 %copy-start.4 = (s32[3]{0:T(128)}, s32[3]{0:T(128)S(1)}, u32[]{:S(2)}) copy-start(s32[3]{0:T(128)S(1)} %pad_add_fusion.place_ref) | copy-start | bytes 40
  203.6 29.2 %copy-start.14 = (bf16[2,4,80,640]{3,2,1,0:T(8,128)(2,1)S(1)}, bf16[2,4,80,640]{3,2,1,0:T(8,128)(2,1)}, u32[]{:S(2)}) copy-start(bf16[2,4,80,640]{3,2,1,0:T(8,128)(2,1)} %copy-done.13) | copy-start | bytes 2457604
  218.1 38.3 %copy-start.24 = (bf16[512,1920]{1,0:T(8,128)(2,1)}, bf16[512,1920]{1,0:T(8,128)(2,1)S(1)}, u32[]{:S(2)}) copy-start(bf16[512,1920]{1,0:T(8,128)(2,1)S(1)} %get-tuple-element.80.packed_ref) | copy-start | bytes 5898244
  218.1 38.3 %copy-start.33 = (bf16[512,640]{1,0:T(8,128)(2,1)}, bf16[512,640]{1,0:T(8,128)(2,1)S(1)}, u32[]{:S(2)}) copy-start(bf16[512,640]{1,0:T(8,128)(2,1)S(1)} %get-tuple-element.60.second_ref) | copy-start | bytes 1966084
  218.1 38.3 %collective-permute-start.11 = (bf16[2,4,80,640]{3,2,1,0:T(8,128)(2,1)S(1)}, bf16[2,4,80,640]{3,2,1,0:T(8,128)(2,1)S(1)}, u32[]{:S(2)}, u32[]{:S(2)}) collective-permute-start(bf16[2,4,80,640]{3,2,1,0:T(8,128)(2,1)S(1)} %pad_maximum_fusion.5.w0_ref), channel_id=1, source_target_pairs={{0,1},{1,0},{2,3},{3,2},{4,5},{5,4},{6,7},{7,6},{8,9},{9,8},{10,11... | collective-permute-start | bytes 2457608 | tf_op jit(solution)/shard_map/ppermute | solution.py:727
  232.8 39.2 %collective-permute-start.15 = (bf16[2,4,80,1280]{3,2,1,0:T(8,128)(2,1)}, bf16[2,4,80,1280]{3,2,1,0:T(8,128)(2,1)}, u32[]{:S(2)}, u32[]{:S(2)}) collective-permute-start(bf16[2,4,80,1280]{3,2,1,0:T(8,128)(2,1)} %pad_maximum_fusion.3.u0_ref), channel_id=1, source_target_pairs={{0,1},{1,0},{2,3},{3,2},{4,5},{5,4},{6,7},{7,6},{8,9},{9,8},{10,11... | collective-permute-start | bytes 4915208 | tf_op jit(solution)/shard_map/ppermute | solution.py:727
  232.8 23.6 %collective-permute-start.13 = (bf16[2,4,80,640]{3,2,1,0:T(8,128)(2,1)S(1)}, bf16[2,4,80,640]{3,2,1,0:T(8,128)(2,1)S(1)}, u32[]{:S(2)}, u32[]{:S(2)}) collective-permute-start(bf16[2,4,80,640]{3,2,1,0:T(8,128)(2,1)S(1)} %copy-done.14), channel_id=1, source_target_pairs={{0,1},{1,0},{2,3},{3,2},{4,5},{5,4},{6,7},{7,6},{8,9},{9,8},{10,11... | collective-permute-start | bytes 2457608 | tf_op jit(solution)/shard_map/ppermute | solution.py:727
  233.3 38.7 %collective-permute-start.17 = (bf16[2,4,80,1280]{3,2,1,0:T(8,128)(2,1)}, bf16[2,4,80,1280]{3,2,1,0:T(8,128)(2,1)}, u32[]{:S(2)}, u32[]{:S(2)}) collective-permute-start(bf16[2,4,80,1280]{3,2,1,0:T(8,128)(2,1)} %collective-permute-done.16.u2_ref), channel_id=1, source_target_pairs={{0,1},{1,0},{2,3},{3,2},{4,5},{5,4},{6,7},{7,6},{8,9},{9,8},{10,11... | collective-permute-start | bytes 4915208 | tf_op jit(solution)/shard_map/ppermute | solution.py:727
  353.0 28.7 %copy-start.12 = (bf16[2,4,80,640]{3,2,1,0:T(8,128)(2,1)S(1)}, bf16[2,4,80,640]{3,2,1,0:T(8,128)(2,1)}, u32[]{:S(2)}) copy-start(bf16[2,4,80,640]{3,2,1,0:T(8,128)(2,1)} %copy-done.10) | copy-start | bytes 2457604
  353.0 28.7 %copy-start.16 = (bf16[512,640]{1,0:T(8,128)(2,1)S(1)}, bf16[512,640]{1,0:T(8,128)(2,1)}, u32[]{:S(2)}) copy-start(bf16[512,640]{1,0:T(8,128)(2,1)} %residual_ref.3) | copy-start | bytes 1966084
  381.2 49.1 %collective-permute-start.26 = (bf16[2,2,4,80,1280]{4,3,2,1,0:T(8,128)(2,1)}, bf16[2,2,4,80,1280]{4,3,2,1,0:T(8,128)(2,1)}, u32[]{:S(2)}, u32[]{:S(2)}) collective-permute-start(bf16[2,2,4,80,1280]{4,3,2,1,0:T(8,128)(2,1)} %get-tuple-element.89), channel_id=1, source_target_pairs={{0,1},{1,0},{2,3},{3,2},{4,5},{5,4},{6,7},{7,6},{8,9},{9,8},{10,11... | collective-permute-start | bytes 9830408 | tf_op jit(solution)/shard_map/ppermute | solution.py:727
  403.5 3.8 collective-permute-start.20
  403.7 18.2 %collective-permute-start.23 = (bf16[2,2,4,80,640]{4,3,2,1,0:T(8,128)(2,1)}, bf16[2,2,4,80,640]{4,3,2,1,0:T(8,128)(2,1)S(1)}, u32[]{:S(2)}, u32[]{:S(2)}) collective-permute-start(bf16[2,2,4,80,640]{4,3,2,1,0:T(8,128)(2,1)} %get-tuple-element.87), channel_id=1, source_target_pairs={{0,1},{1,0},{2,3},{3,2},{4,5},{5,4},{6,7},{7,6},{8,9},{9,8},{10,11... | collective-permute-start | bytes 4915208 | tf_op jit(solution)/shard_map/ppermute | solution.py:727
  404.1 46.0 %collective-permute-start.29 = (bf16[2,2,4,80,1280]{4,3,2,1,0:T(8,128)(2,1)}, bf16[2,2,4,80,1280]{4,3,2,1,0:T(8,128)(2,1)}, u32[]{:S(2)}, u32[]{:S(2)}) collective-permute-start(bf16[2,2,4,80,1280]{4,3,2,1,0:T(8,128)(2,1)} %get-tuple-element.91), channel_id=1, source_target_pairs={{0,1},{1,0},{2,3},{3,2},{4,5},{5,4},{6,7},{7,6},{8,9},{9,8},{10,11... | collective-permute-start | bytes 9830408 | tf_op jit(solution)/shard_map/ppermute | solution.py:727
  407.8 21.2 %collective-permute-start.21 = (bf16[2,4,80,640]{3,2,1,0:T(8,128)(2,1)S(1)}, bf16[2,4,80,640]{3,2,1,0:T(8,128)(2,1)S(1)}, u32[]{:S(2)}, u32[]{:S(2)}) collective-permute-start(bf16[2,4,80,640]{3,2,1,0:T(8,128)(2,1)S(1)} %fusion.30), channel_id=1, source_target_pairs={{0,2},{2,0},{1,3},{3,1},{4,6},{6,4},{5,7},{7,5},{8,10},{10,8},{9,1... | collective-permute-start | bytes 2457608 | tf_op jit(solution)/shard_map/ppermute | solution.py:727
  409.4 38.5 %copy-start.42 = (f32[2,2,4,80,640]{4,3,2,1,0:T(8,128)}, f32[2,2,4,80,640]{4,3,2,1,0:T(8,128)S(1)}, u32[]{:S(2)}) copy-start(f32[2,2,4,80,640]{4,3,2,1,0:T(8,128)S(1)} %convert_element_type.232) | copy-start | bytes 9830404
  418.4 117.5 %collective-permute-start.35 = (bf16[2,4,320,640]{3,2,1,0:T(8,128)(2,1)}, bf16[2,4,320,640]{3,2,1,0:T(8,128)(2,1)}, u32[]{:S(2)}, u32[]{:S(2)}) collective-permute-start(bf16[2,4,320,640]{3,2,1,0:T(8,128)(2,1)} %get-tuple-element.97), channel_id=1, source_target_pairs={{0,1},{1,0},{2,3},{3,2},{4,5},{5,4},{6,7},{7,6},{8,9},{9,8},{10,11... | collective-permute-start | bytes 9830408 | tf_op jit(solution)/shard_map/ppermute | solution.py:727
  421.9 30.8 %copy-start.36 = (f32[2,2,4,80,1280]{4,3,2,1,0:T(8,128)}, f32[2,2,4,80,1280]{4,3,2,1,0:T(8,128)S(1)}, u32[]{:S(2)}) copy-start(f32[2,2,4,80,1280]{4,3,2,1,0:T(8,128)S(1)} %convert_element_type.252) | copy-start | bytes 19660804
  423.4 23.2 %collective-permute-start.24 = (bf16[2,4,80,640]{3,2,1,0:T(8,128)(2,1)}, bf16[2,4,80,640]{3,2,1,0:T(8,128)(2,1)}, u32[]{:S(2)}, u32[]{:S(2)}) collective-permute-start(bf16[2,4,80,640]{3,2,1,0:T(8,128)(2,1)} %fusion.31), channel_id=1, source_target_pairs={{0,2},{2,0},{1,3},{3,1},{4,6},{6,4},{5,7},{7,5},{8,10},{10,8},{9,1... | collective-permute-start | bytes 2457608 | tf_op jit(solution)/shard_map/ppermute | solution.py:727
  434.6 47.1 %collective-permute-start.27 = (bf16[2,4,80,1280]{3,2,1,0:T(8,128)(2,1)}, bf16[2,4,80,1280]{3,2,1,0:T(8,128)(2,1)}, u32[]{:S(2)}, u32[]{:S(2)}) collective-permute-start(bf16[2,4,80,1280]{3,2,1,0:T(8,128)(2,1)} %fusion.10), channel_id=1, source_target_pairs={{0,2},{2,0},{1,3},{3,1},{4,6},{6,4},{5,7},{7,5},{8,10},{10,8},{9,1... | collective-permute-start | bytes 4915208 | tf_op jit(solution)/shard_map/ppermute | solution.py:727
  438.0 19.3 %collective-permute-start.22 = (bf16[4,80,640]{2,1,0:T(8,128)(2,1)}, bf16[4,80,640]{2,1,0:T(8,128)(2,1)S(1)}, u32[]{:S(2)}, u32[]{:S(2)}) collective-permute-start(bf16[4,80,640]{2,1,0:T(8,128)(2,1)} %fusion.40), channel_id=1, source_target_pairs={{0,4},{4,0},{1,5},{5,1},{2,6},{6,2},{3,7},{7,3},{8,12},{12,8},{9,1... | collective-permute-start | bytes 1228808 | tf_op jit(solution)/shard_map/ppermute | solution.py:727
  448.9 40.2 %collective-permute-start.25 = (bf16[4,80,640]{2,1,0:T(8,128)(2,1)}, bf16[4,80,640]{2,1,0:T(8,128)(2,1)}, u32[]{:S(2)}, u32[]{:S(2)}) collective-permute-start(bf16[4,80,640]{2,1,0:T(8,128)(2,1)} %fusion.33), channel_id=1, source_target_pairs={{0,4},{4,0},{1,5},{5,1},{2,6},{6,2},{3,7},{7,3},{8,12},{12,8},{9,1... | collective-permute-start | bytes 1228808 | tf_op jit(solution)/shard_map/ppermute | solution.py:727
  456.0 60.0 %collective-permute-start.30 = (bf16[2,4,80,1280]{3,2,1,0:T(8,128)(2,1)}, bf16[2,4,80,1280]{3,2,1,0:T(8,128)(2,1)}, u32[]{:S(2)}, u32[]{:S(2)}) collective-permute-start(bf16[2,4,80,1280]{3,2,1,0:T(8,128)(2,1)} %fusion.11), channel_id=1, source_target_pairs={{0,2},{2,0},{1,3},{3,1},{4,6},{6,4},{5,7},{7,5},{8,10},{10,8},{9,1... | collective-permute-start | bytes 4915208 | tf_op jit(solution)/shard_map/ppermute | solution.py:727
  458.2 214.6 %reduce-scatter.9.cloned.1.call-start = ((), (), s32[]{:S(2)}) async-start(), calls=%async_computation.9 | async-start | bytes 512000 | tf_op jit(solution)/shard_map/reduce_scatter | solution.py:796
  487.8 31.7 %collective-permute-start.28 = (bf16[4,80,1280]{2,1,0:T(8,128)(2,1)}, bf16[4,80,1280]{2,1,0:T(8,128)(2,1)}, u32[]{:S(2)}, u32[]{:S(2)}) collective-permute-start(bf16[4,80,1280]{2,1,0:T(8,128)(2,1)} %fusion.22), channel_id=1, source_target_pairs={{0,4},{4,0},{1,5},{5,1},{2,6},{6,2},{3,7},{7,3},{8,12},{12,8},{9,1... | collective-permute-start | bytes 2457608 | tf_op jit(solution)/shard_map/ppermute | solution.py:727
  491.5 189.8 %reduce-scatter.11.cloned.1.call-start = ((), (), s32[]{:S(2)}) async-start(), calls=%async_computation.10 | async-start | bytes 1024000 | tf_op jit(solution)/shard_map/reduce_scatter | solution.py:796
  522.9 168.3 %reduce-scatter.13.cloned.1.call-start = ((), (), s32[]{:S(2)}) async-start(), calls=%async_computation.11 | async-start | bytes 1024000 | tf_op jit(solution)/shard_map/reduce_scatter | solution.py:796
  525.8 19.5 %collective-permute-start.31 = (bf16[4,80,1280]{2,1,0:T(8,128)(2,1)S(1)}, bf16[4,80,1280]{2,1,0:T(8,128)(2,1)S(1)}, u32[]{:S(2)}, u32[]{:S(2)}) collective-permute-start(bf16[4,80,1280]{2,1,0:T(8,128)(2,1)S(1)} %fusion.15), channel_id=1, source_target_pairs={{0,4},{4,0},{1,5},{5,1},{2,6},{6,2},{3,7},{7,3},{8,12},{12,8},{9,1... | collective-permute-start | bytes 2457608 | tf_op jit(solution)/shard_map/ppermute | solution.py:727
  535.8 57.6 %collective-permute-start.32 = (bf16[2,4,320,640]{3,2,1,0:T(8,128)(2,1)}, bf16[2,4,320,640]{3,2,1,0:T(8,128)(2,1)}, u32[]{:S(2)}, u32[]{:S(2)}) collective-permute-start(bf16[2,4,320,640]{3,2,1,0:T(8,128)(2,1)} %get-tuple-element.94), channel_id=1, source_target_pairs={{0,1},{1,0},{2,3},{3,2},{4,5},{5,4},{6,7},{7,6},{8,9},{9,8},{10,11... | collective-permute-start | bytes 9830408 | tf_op jit(solution)/shard_map/ppermute | solution.py:727
  542.1 38.5 %collective-permute-start.36 = (bf16[4,320,640]{2,1,0:T(8,128)(2,1)}, bf16[4,320,640]{2,1,0:T(8,128)(2,1)}, u32[]{:S(2)}, u32[]{:S(2)}) collective-permute-start(bf16[4,320,640]{2,1,0:T(8,128)(2,1)} %fusion.13), channel_id=1, source_target_pairs={{0,4},{4,0},{1,5},{5,1},{2,6},{6,2},{3,7},{7,3},{8,12},{12,8},{9,1... | collective-permute-start | bytes 4915208 | tf_op jit(solution)/shard_map/ppermute | solution.py:727
  548.6 152.4 %reduce-scatter.17.cloned.1.call-start = ((), (), s32[]{:S(2)}) async-start(), calls=%async_computation.13 | async-start | bytes 2048000 | tf_op jit(solution)/shard_map/reduce_scatter | solution.py:811
  585.6 118.3 %reduce-scatter.15.cloned.1.call-start = ((), (), s32[]{:S(2)}) async-start(), calls=%async_computation.12 | async-start | bytes 2048000 | tf_op jit(solution)/shard_map/reduce_scatter | solution.py:811
  589.4 1.7 collective-permute-start.38
  592.1 7.6 %collective-permute-start.39 = (f32[88,640]{1,0:T(8,128)S(1)}, f32[88,640]{1,0:T(8,128)S(1)}, u32[]{:S(2)}, u32[]{:S(2)}) collective-permute-start(f32[88,640]{1,0:T(8,128)S(1)} %add.227), channel_id=1, source_target_pairs={{0,2},{2,0},{1,3},{3,1},{4,6},{6,4},{5,7},{7,5},{8,10},{10,8},{9,1... | collective-permute-start | bytes 675848 | tf_op jit(solution)/shard_map/ppermute | solution.py:727
  596.3 65.5 %collective-permute-start.33 = (bf16[4,320,640]{2,1,0:T(8,128)(2,1)S(1)}, bf16[4,320,640]{2,1,0:T(8,128)(2,1)S(1)}, u32[]{:S(2)}, u32[]{:S(2)}) collective-permute-start(bf16[4,320,640]{2,1,0:T(8,128)(2,1)S(1)} %fusion.12), channel_id=1, source_target_pairs={{0,4},{4,0},{1,5},{5,1},{2,6},{6,2},{3,7},{7,3},{8,12},{12,8},{9,1... | collective-permute-start | bytes 4915208 | tf_op jit(solution)/shard_map/ppermute | solution.py:727
  599.8 39.0 %collective-permute-start.40 = (f32[88,640]{1,0:T(8,128)S(1)}, f32[88,640]{1,0:T(8,128)S(1)}, u32[]{:S(2)}, u32[]{:S(2)}) collective-permute-start(f32[88,640]{1,0:T(8,128)S(1)} %add.228), channel_id=1, source_target_pairs={{0,4},{4,0},{1,5},{5,1},{2,6},{6,2},{3,7},{7,3},{8,12},{12,8},{9,1... | collective-permute-start | bytes 675848 | tf_op jit(solution)/shard_map/ppermute | solution.py:727
  638.8 6.5 collective-permute-start.41
  645.3 11.3 %collective-permute-start.42 = (f32[88,640]{1,0:T(8,128)S(1)}, f32[88,640]{1,0:T(8,128)S(1)}, u32[]{:S(2)}, u32[]{:S(2)}) collective-permute-start(f32[88,640]{1,0:T(8,128)S(1)} %add.230), channel_id=1, source_target_pairs={{0,16},{8,24},{16,0},{24,8},{1,17},{9,25},{17,1},{25,9},{2,18},{10... | collective-permute-start | bytes 675848 | tf_op jit(solution)/shard_map/ppermute | solution.py:823
  701.1 12.6 %collective-permute-start.37 = (bf16[320,640]{1,0:T(8,128)(2,1)}, bf16[320,640]{1,0:T(8,128)(2,1)S(1)}, u32[]{:S(2)}, u32[]{:S(2)}) collective-permute-start(bf16[320,640]{1,0:T(8,128)(2,1)} %bitcast.202), channel_id=1, source_target_pairs={{0,2},{2,0},{1,3},{3,1},{4,6},{6,4},{5,7},{7,5},{8,10},{10,8},{9,1... | collective-permute-start | bytes 1228808 | tf_op jit(solution)/shard_map/ppermute | solution.py:727
  704.0 17.9 %collective-permute-start.34 = (bf16[320,640]{1,0:T(8,128)(2,1)}, bf16[320,640]{1,0:T(8,128)(2,1)S(1)}, u32[]{:S(2)}, u32[]{:S(2)}) collective-permute-start(bf16[320,640]{1,0:T(8,128)(2,1)} %bitcast.203), channel_id=1, source_target_pairs={{0,2},{2,0},{1,3},{3,1},{4,6},{6,4},{5,7},{7,5},{8,10},{10,8},{9,1... | collective-permute-start | bytes 1228808 | tf_op jit(solution)/shard_map/ppermute | solution.py:727
  (64 other events, 477.9 us)
Sparse Core Ops, SparseCore 0:
  13.1 43.2 all-gather.2
  58.5 52.7 all-gather.4
  458.3 19.4 reduce-scatter.6
  491.6 20.2 reduce-scatter.8
  523.0 23.6 reduce-scatter.10
  548.9 24.1 reduce-scatter.12
  585.8 36.2 reduce-scatter.16
  663.7 36.0 reduce-scatter.14

commit v2 on v1

v2 whole, which is shorter than its diff:
```python
import math

import jax
import jax.numpy as jnp
from jax import lax
from jax.experimental import pallas as pl
from jax.experimental.pallas import tpu as pltpu
from jax.sharding import Mesh
from jax.sharding import PartitionSpec as P

D = 640
HEADS = 20
HEAD_DIM = 32
FF = 5120
VOCAB = 25
LAYERS = 2
LEN = 128
SEQ_DEV = 4
ROWS = SEQ_DEV * LEN
TILE = 640
TILES = FF // TILE
GROUPS = HEADS * HEAD_DIM // 128
PER_GROUP = 128 // HEAD_DIM
CHUNK = 128
BF = jnp.bfloat16
F32 = jnp.float32
MIB = 2**20

SMEM_SPEC = pl.BlockSpec(memory_space=pltpu.SMEM)
ANY_SPEC = pl.BlockSpec(memory_space=pl.ANY)


def dot(left, right, dims):
    return lax.dot_general(left, right, (dims, ((), ())), preferred_element_type=F32)


def mul_nn(left, right):
    return dot(left, right, ((1,), (0,)))


def mul_nt(left, right):
    return dot(left, right, ((1,), (1,)))


def mul_tn(left, right):
    return dot(left, right, ((0,), (0,)))


def normalize(values):
    centered = values - jnp.mean(values, -1, keepdims=True)
    inverse = lax.rsqrt(jnp.mean(centered * centered, -1, keepdims=True) + 1e-05)
    return (centered * inverse, inverse)


def norm_back(grad_normed, normed, inverse):
    return inverse * (
        grad_normed
        - jnp.mean(grad_normed, -1, keepdims=True)
        - normed * jnp.mean(grad_normed * normed, -1, keepdims=True)
    )


def col_sum(values):
    return jnp.sum(values, 0, keepdims=True)


def sds(shape, dtype):
    return jax.ShapeDtypeStruct(shape, dtype)


def whole_block(shape):
    zeros = (0,) * len(shape)
    return pl.BlockSpec(shape, lambda *_: zeros)


def over_chunks(body, start):
    def step(index, carry):
        return body(pl.ds(pl.multiple_of(index * CHUNK, CHUNK), CHUNK), carry)

    return lax.fori_loop(0, ROWS // CHUNK, step, start)


def quarter_copies(place_ref, buffers, held, sems):
    x_at, y_at, c_at = place_ref[0], place_ref[1], place_ref[2]
    copies = []
    for number, buffer in enumerate(buffers):
        quarter = (x_at ^ (number >> 1)) * 2 + (c_at ^ (number & 1))
        for dy in range(2):
            copies.append(
                pltpu.make_async_copy(
                    buffer.at[dy], held.at[quarter, :, y_at ^ dy], sems.at[2 * number + dy]
                )
            )
    return copies


def square(values):
    return values.reshape(D, values.shape[-1])


def head_masks():
    lanes = lax.broadcasted_iota(jnp.int32, (LEN, 128), 1) // HEAD_DIM
    return [(lanes == member) for member in range(PER_GROUP)]


def stack_heads(values, masks):
    zero = jnp.zeros_like(values)
    return jnp.concatenate([jnp.where(mask, values, zero) for mask in masks], 0)


def unstack_heads(values):
    parts = [
        values[HEAD_DIM * member : HEAD_DIM * (member + 1), LEN * member : LEN * (member + 1)]
        for member in range(PER_GROUP)
    ]
    return jnp.concatenate(parts, 0).T


def scores_of(keys, queries, valid):
    scores = mul_nt(keys, queries) * (1.0 / math.sqrt(HEAD_DIM))
    return jnp.where(valid, scores, -1e30)


def mix_kernel(
    place_ref,
    lengths_ref,
    residual_ref,
    w0_ref,
    w1_ref,
    w2_ref,
    w3_ref,
    gains_ref,
    biases_ref,
    packed_ref,
    log_ref,
    mixed_ref,
    middle_ref,
    second_ref,
    held,
    pre_ref,
    sems,
):
    copies = quarter_copies(place_ref, (w0_ref, w1_ref, w2_ref, w3_ref), held, sems)
    for copy in copies:
        copy.start()

    def first(rows, carry):
        normed, inverse = normalize(residual_ref[rows, :].astype(F32))
        pre_ref[rows, :] = (normed * gains_ref[0:1, :] + biases_ref[0:1, :]).astype(BF)
        return carry

    over_chunks(first, 0)
    for copy in copies:
        copy.wait()
    shifts = (biases_ref[2:3, :], None, biases_ref[3:4, :])
    for part in range(3):
        result = mul_nn(pre_ref[...], square(held[part]))
        if shifts[part] is not None:
            result = result + shifts[part]
        packed_ref[:, part * D : (part + 1) * D] = result.astype(BF)
    masks = head_masks()
    row_ids = lax.broadcasted_iota(jnp.int32, (LEN, 1), 0)

    def one_sequence(seq, carry):
        rows = pl.ds(pl.multiple_of(seq * LEN, LEN), LEN)
        valid = row_ids < lengths_ref[seq]
        for group in range(GROUPS):
            lanes = slice(group * 128, (group + 1) * 128)
            queries = stack_heads(packed_ref[rows, lanes], masks)
            key_rows = packed_ref[rows, D + group * 128 : D + (group + 1) * 128]
            value_rows = packed_ref[rows, 2 * D + group * 128 : 2 * D + (group + 1) * 128]
            scores = scores_of(key_rows, queries, valid)
            top = jnp.max(scores, 0, keepdims=True)
            expos = jnp.exp(scores - top)
            total = jnp.sum(expos, 0, keepdims=True)
            probs = (expos * (1.0 / total)).astype(BF)
            log_ref[seq * GROUPS + group] = top + jnp.log(total)
            mixed_ref[rows, lanes] = unstack_heads(mul_tn(value_rows, probs)).astype(BF)
        return carry

    lax.fori_loop(0, SEQ_DEV, one_sequence, 0)
    middle_ref[...] = mul_nn(mixed_ref[...], square(held[3])) + biases_ref[4:5, :]

    def last(rows, carry):
        middle = middle_ref[rows, :] + residual_ref[rows, :].astype(F32)
        middle_ref[rows, :] = middle
        normed, inverse = normalize(middle)
        second_ref[rows, :] = (normed * gains_ref[1:2, :] + biases_ref[1:2, :]).astype(BF)
        return carry

    over_chunks(last, 0)


def mix(place, lengths, residual, quarters, gains, biases):
    return pl.pallas_call(
        mix_kernel,
        out_shape=(
            sds((ROWS, 3 * D), BF),
            sds((SEQ_DEV * GROUPS, 1, PER_GROUP * LEN), F32),
            sds((ROWS, D), BF),
            sds((ROWS, D), F32),
            sds((ROWS, D), BF),
        ),
        grid=(1,),
        in_specs=[SMEM_SPEC, SMEM_SPEC, whole_block((ROWS, D))]
        + [ANY_SPEC] * 4
        + [whole_block((2, D)), whole_block((6, D))],
        out_specs=(
            whole_block((ROWS, 3 * D)),
            whole_block((SEQ_DEV * GROUPS, 1, PER_GROUP * LEN)),
            whole_block((ROWS, D)),
            whole_block((ROWS, D)),
            whole_block((ROWS, D)),
        ),
        scratch_shapes=[
            pltpu.VMEM((4, 4, 2, D // 8, D), BF),
            pltpu.VMEM((ROWS, D), BF),
            pltpu.SemaphoreType.DMA((8,)),
        ],
        compiler_params=pltpu.CompilerParams(vmem_limit_bytes=26 * MIB),
        cost_estimate=pl.CostEstimate(
            flops=2 * ROWS * D * 4 * D * 4, bytes_accessed=10 * MIB, transcendentals=0
        ),
    )(place, lengths, residual, *quarters, gains, biases)


def up_kernel(place_ref, second_ref, *refs):
    buffers, (shift_ref, active_ref, slope_ref, held, sems) = refs[:8], refs[8:]
    tile = pl.program_id(0)

    @pl.when(tile == 0)
    def _():
        for number, buffer in enumerate(buffers):
            dx, dc, half = number // 4, number // 2 % 2, number % 2
            at = ((place_ref[0] ^ dx) * 2 + (place_ref[2] ^ dc)) * 2 + half
            for dy in range(2):
                pltpu.make_async_copy(
                    buffer.at[dy], held.at[at, :, place_ref[1] ^ dy], sems.at[at, dy]
                ).start()

    for dy in range(2):
        pltpu.make_async_copy(buffers[0].at[dy], held.at[tile, :, dy], sems.at[tile, dy]).wait()
    up_tile = square(held[tile])
    shift = shift_ref[pl.ds(tile, 1), :]
    for chunk in range(ROWS // CHUNK):
        rows = slice(chunk * CHUNK, (chunk + 1) * CHUNK)
        hidden = mul_nn(second_ref[rows, :], up_tile) + shift
        phi = 0.5 + 0.5 * lax.erf(hidden * math.sqrt(0.5))
        density = jnp.exp(hidden * hidden * -0.5) * (1.0 / math.sqrt(2.0 * math.pi))
        active_ref[0, rows, :] = (hidden * phi).astype(BF)
        slope_ref[0, rows, :] = (phi + hidden * density).astype(BF)


def up(place, second, parts, shift):
    tile_block = pl.BlockSpec((1, ROWS, TILE), lambda tile: (tile, 0, 0))
    return pl.pallas_call(
        up_kernel,
        grid=(TILES,),
        out_shape=(sds((TILES, ROWS, TILE), BF), sds((TILES, ROWS, TILE), BF)),
        in_specs=[SMEM_SPEC, whole_block((ROWS, D))]
        + [ANY_SPEC] * 8
        + [whole_block((TILES, TILE))],
        out_specs=(tile_block, tile_block),
        scratch_shapes=[
            pltpu.VMEM((TILES, 4, 2, D // 8, TILE), BF),
            pltpu.SemaphoreType.DMA((TILES, 2)),
        ],
        compiler_params=pltpu.CompilerParams(vmem_limit_bytes=26 * MIB),
        cost_estimate=pl.CostEstimate(
            flops=2 * ROWS * D * FF * 4, bytes_accessed=20 * MIB, transcendentals=0
        ),
    )(place, second, *parts, shift)


def down_kernel(
    place_ref, middle_ref, active_ref, d0_ref, d1_ref, biases_ref, out_ref, held, rows, sems, row_sems
):
    tile = pl.program_id(0)

    @pl.when(tile == 0)
    def _():
        for at in range(TILES):
            for number, buffer in enumerate((d0_ref, d1_ref)):
                pltpu.make_async_copy(
                    buffer.at[at], held.at[at, place_ref[2] ^ number], sems.at[at, number]
                ).start()
            pltpu.make_async_copy(active_ref.at[at], rows.at[at], row_sems.at[at]).start()
        out_ref[...] = middle_ref[...] + biases_ref[5:6, :]

    for number in range(2):
        pltpu.make_async_copy(d0_ref.at[tile], held.at[tile, number], sems.at[tile, number]).wait()
    pltpu.make_async_copy(active_ref.at[0], rows.at[tile], row_sems.at[tile]).wait()
    out_ref[...] += mul_nn(rows[tile], square(held[tile]))


def down(place, middle, active, parts, biases):
    return pl.pallas_call(
        down_kernel,
        grid=(TILES,),
        out_shape=sds((ROWS, D), F32),
        in_specs=[
            SMEM_SPEC,
            whole_block((ROWS, D)),
            ANY_SPEC,
            ANY_SPEC,
            ANY_SPEC,
            whole_block((6, D)),
        ],
        out_specs=whole_block((ROWS, D)),
        scratch_shapes=[
            pltpu.VMEM((TILES, 2, TILE // 2, D), BF),
            pltpu.VMEM((TILES, ROWS, TILE), BF),
            pltpu.SemaphoreType.DMA((TILES, 2)),
            pltpu.SemaphoreType.DMA((TILES,)),
        ],
        compiler_params=pltpu.CompilerParams(vmem_limit_bytes=24 * MIB),
        cost_estimate=pl.CostEstimate(
            flops=2 * ROWS * D * FF, bytes_accessed=14 * MIB, transcendentals=0
        ),
    )(place, middle, active, *parts, biases)


def head_kernel(
    residual_ref,
    targets_ref,
    masked_ref,
    weight_ref,
    shift_ref,
    gain_ref,
    move_ref,
    activations_ref,
    grad_ref,
    rounded_ref,
    small_ref,
):
    small_ref[...] = jnp.zeros_like(small_ref)
    lanes = lax.broadcasted_iota(jnp.int32, (1, 128), 1)

    def body(rows, carry):
        weight_grad, gain_grad, move_grad, shift_grad, stats = carry
        residual = residual_ref[rows, :]
        activations_ref[rows, :] = residual.astype(BF)
        normed, inverse = normalize(residual)
        final = (normed * gain_ref[...] + move_ref[...]).astype(BF)
        logits = mul_nn(final, weight_ref[...]) + shift_ref[...]
        top = jnp.max(logits, -1, keepdims=True)
        log_total = top + jnp.log(jnp.sum(jnp.exp(logits - top), -1, keepdims=True))
        onehot = (targets_ref[rows, :] == lanes).astype(F32)
        picked = jnp.sum(logits * onehot, -1, keepdims=True)
        mask = masked_ref[rows, :].astype(F32)
        loss = col_sum(mask * (log_total - picked))
        hits = col_sum(mask * jnp.exp(picked - log_total))
        count = col_sum(mask)
        stats = stats + (
            jnp.where(lanes == 0, loss, 0.0)
            + jnp.where(lanes == 1, hits, 0.0)
            + jnp.where(lanes == 2, count, 0.0)
        )
        grad_logits = (mask * (jnp.exp(logits - log_total) - onehot)).astype(BF)
        weight_grad = weight_grad + mul_tn(grad_logits, final)
        shift_grad = shift_grad + col_sum(grad_logits.astype(F32))
        grad_final = mul_nt(grad_logits, weight_ref[...])
        gain_grad = gain_grad + col_sum(grad_final * normed)
        move_grad = move_grad + col_sum(grad_final)
        grad = norm_back(grad_final * gain_ref[...], normed, inverse)
        grad_ref[rows, :] = grad
        rounded_ref[rows, :] = grad.astype(BF)
        return weight_grad, gain_grad, move_grad, shift_grad, stats

    row = jnp.zeros((1, D), F32)
    narrow = jnp.zeros((1, 128), F32)
    weight_grad, gain_grad, move_grad, shift_grad, stats = over_chunks(
        body, (jnp.zeros((128, D), F32), row, row, narrow, narrow)
    )
    small_ref[0:32, :] = weight_grad[0:32, :]
    small_ref[32:33, :] = gain_grad
    small_ref[33:34, :] = move_grad
    small_ref[34:35, 0:128] = shift_grad
    small_ref[35:36, 0:128] = stats


def head(residual, targets, masked, weight, shift, gain, move):
    return pl.pallas_call(
        head_kernel,
        out_shape=(
            sds((ROWS, D), BF),
            sds((ROWS, D), F32),
            sds((ROWS, D), BF),
            sds((40, D), F32),
        ),
        grid=(1,),
        in_specs=[
            whole_block((ROWS, D)),
            whole_block((ROWS, 1)),
            whole_block((ROWS, 1)),
            whole_block((D, 128)),
            whole_block((1, 128)),
            whole_block((1, D)),
            whole_block((1, D)),
        ],
        out_specs=(whole_block((ROWS, D)),) * 3 + (whole_block((40, D)),),
        compiler_params=pltpu.CompilerParams(vmem_limit_bytes=16 * MIB),
        cost_estimate=pl.CostEstimate(
            flops=2 * ROWS * D * 128 * 8, bytes_accessed=5 * MIB, transcendentals=0
        ),
    )(residual, targets, masked, weight, shift, gain, move)


def down_back_kernel(place_ref, grad_ref, active_ref, send_ref, keep_ref, turned, held, sems):
    step = pl.program_id(0)

    @pl.when(step == 0)
    def _():
        for at in range(TILES):
            tile = (at % 4) * 2 + (place_ref[1] ^ (1 - at // 4))
            pltpu.make_async_copy(active_ref.at[tile], held.at[at], sems.at[at]).start()
        for half in range(2):
            turned[half] = grad_ref[:, half * (D // 2) : (half + 1) * (D // 2)].T

    pltpu.make_async_copy(active_ref.at[0], held.at[step], sems.at[step]).wait()
    c_at = place_ref[2]
    active = held[step]
    send_ref[0, 0] = mul_nn(turned[1 - c_at], active).astype(BF)
    keep_ref[0, 0] = mul_nn(turned[c_at], active).astype(BF)


def down_back(place, grad, active):
    block = pl.BlockSpec((1, 1, D // 2, TILE), lambda step: (1 - step // 4, step % 4, 0, 0))
    out = sds((2, 4, D // 2, TILE), BF)
    return pl.pallas_call(
        down_back_kernel,
        grid=(TILES,),
        in_specs=[SMEM_SPEC, whole_block((ROWS, D)), ANY_SPEC],
        out_specs=(block, block),
        scratch_shapes=[
            pltpu.VMEM((2, D // 2, ROWS), BF),
            pltpu.VMEM((TILES, ROWS, TILE), BF),
            pltpu.SemaphoreType.DMA((TILES,)),
        ],
        out_shape=(out, out),
        compiler_params=pltpu.CompilerParams(vmem_limit_bytes=20 * MIB),
        cost_estimate=pl.CostEstimate(
            flops=2 * ROWS * D * FF, bytes_accessed=13 * MIB, transcendentals=0
        ),
    )(place, grad, active)


def wide_back_tile(phase, step, place_ref):
    quarter = (place_ref[0] ^ (1 - step // 2)) * 2 + (place_ref[2] ^ (1 - phase))
    return quarter * 2 + step % 2


def wide_back_step(
    phase, step, place_ref, rounded_ref, second_ref, slope_ref, ups, downs, held_up, held_down,
    up_sems, down_sems, turned, shift_ref, store, total_ref, slopes, slope_sems
):
    y_at, c_at = place_ref[1], place_ref[2]

    @pl.when(step == 0)
    def _():
        for at in range(4):
            tile = wide_back_tile(phase, at, place_ref)
            for number, buffer in enumerate(downs):
                pltpu.make_async_copy(
                    buffer.at[tile], held_down.at[at, c_at ^ number], down_sems.at[at, number]
                ).start()
            for dy in range(2):
                pltpu.make_async_copy(
                    ups[(1 - at // 2) * 2 + at % 2].at[dy],
                    held_up.at[at, :, y_at ^ dy],
                    up_sems.at[at, dy],
                ).start()
            pltpu.make_async_copy(slope_ref.at[tile], slopes.at[at], slope_sems.at[at]).start()
        turned[...] = second_ref[...].T

    for number in range(2):
        pltpu.make_async_copy(
            downs[0].at[0], held_down.at[step, number], down_sems.at[step, number]
        ).wait()
    for dy in range(2):
        pltpu.make_async_copy(
            ups[0].at[dy], held_up.at[step, :, dy], up_sems.at[step, dy]
        ).wait()
    grad_active = mul_nt(rounded_ref[...], square(held_down[step]))
    pltpu.make_async_copy(slope_ref.at[0], slopes.at[step], slope_sems.at[step]).wait()
    grad_hidden = (grad_active * slopes[step].astype(F32)).astype(BF)
    shift_ref[pl.ds(step, 1), :] = col_sum(grad_hidden.astype(F32))
    total_ref[...] += mul_nt(grad_hidden, square(held_up[step]))
    store(mul_nn(turned[...], grad_hidden).reshape(4, 2, D // 8, TILE))


def wide_back_first_kernel(
    place_ref,
    rounded_ref,
    second_ref,
    slope_ref,
    u0_ref,
    u1_ref,
    u2_ref,
    u3_ref,
    d0_ref,
    d1_ref,
    send_ref,
    shift_ref,
    total_ref,
    held_up,
    held_down,
    turned,
    up_sems,
    down_sems,
    slopes,
    slope_sems,
):
    step = pl.program_id(0)

    @pl.when(step == 0)
    def _():
        total_ref[...] = jnp.zeros_like(total_ref)

    def store(up_grad):
        for side in range(2):
            send_ref[0, side ^ place_ref[1], :, 0] = up_grad[:, side].astype(BF)

    wide_back_step(
        0, step, place_ref, rounded_ref, second_ref, slope_ref,
        (u0_ref, u1_ref, u2_ref, u3_ref), (d0_ref, d1_ref),
        held_up, held_down, up_sems, down_sems, turned, shift_ref, store, total_ref, slopes, slope_sems
    )


def wide_back_last_kernel(
    place_ref,
    rounded_ref,
    second_ref,
    slope_ref,
    u0_ref,
    u1_ref,
    u2_ref,
    u3_ref,
    d0_ref,
    d1_ref,
    before_ref,
    grad_ref,
    middle_ref,
    gains_ref,
    got_ref,
    pass_ref,
    keep_ref,
    shift_ref,
    middle_grad_ref,
    middle_rounded_ref,
    small_ref,
    held_up,
    held_down,
    turned,
    up_sems,
    down_sems,
    slopes,
    slope_sems,
    total,
):
    step = pl.program_id(0)

    @pl.when(step == 0)
    def _():
        total[...] = before_ref[...]

    def store(up_grad):
        def into(out_ref):
            for side in range(2):
                at = side ^ place_ref[1]
                out_ref[at, :, 0] = (up_grad[:, side] + got_ref[0, at, :, 0].astype(F32)).astype(BF)

        @pl.when(step < 2)
        def _():
            into(pass_ref)

        @pl.when(step >= 2)
        def _():
            into(keep_ref)

    wide_back_step(
        1, step, place_ref, rounded_ref, second_ref, slope_ref,
        (u0_ref, u1_ref, u2_ref, u3_ref), (d0_ref, d1_ref),
        held_up, held_down, up_sems, down_sems, turned, shift_ref, store, total, slopes, slope_sems
    )

    @pl.when(step == 3)
    def _():
        def body(rows, carry):
            gain_sum, move_sum, out_sum, down_sum = carry
            normed, inverse = normalize(middle_ref[rows, :])
            grad_second = total[rows, :]
            grad = grad_ref[rows, :] + norm_back(grad_second * gains_ref[1:2, :], normed, inverse)
            rounded = grad.astype(BF)
            middle_grad_ref[rows, :] = grad
            middle_rounded_ref[rows, :] = rounded
            return (
                gain_sum + col_sum(grad_second * normed),
                move_sum + col_sum(grad_second),
                out_sum + col_sum(rounded.astype(F32)),
                down_sum + col_sum(rounded_ref[rows, :].astype(F32)),
            )

        row = jnp.zeros((1, D), F32)
        sums = over_chunks(body, (row, row, row, row))
        small_ref[...] = jnp.zeros_like(small_ref)
        for number in range(4):
            small_ref[number : number + 1, :] = sums[number]


def wide_back_call(kernel, in_specs, out_specs, out_shape, scratch, arrays):
    full = whole_block((ROWS, D))
    return pl.pallas_call(
        kernel,
        grid_spec=pltpu.PrefetchScalarGridSpec(
            num_scalar_prefetch=1,
            grid=(4,),
            in_specs=[full] * 2 + [ANY_SPEC] * 7 + in_specs,
            out_specs=out_specs,
            scratch_shapes=[
                pltpu.VMEM((4, 4, 2, D // 8, TILE), BF),
                pltpu.VMEM((4, 2, TILE // 2, D), BF),
                pltpu.VMEM((D, ROWS), BF),
                pltpu.SemaphoreType.DMA((4, 2)),
                pltpu.SemaphoreType.DMA((4, 2)),
                pltpu.VMEM((4, ROWS, TILE), BF),
                pltpu.SemaphoreType.DMA((4,)),
            ]
            + scratch,
        ),
        out_shape=out_shape,
        compiler_params=pltpu.CompilerParams(vmem_limit_bytes=32 * MIB),
        cost_estimate=pl.CostEstimate(
            flops=2 * ROWS * D * FF * 2, bytes_accessed=18 * MIB, transcendentals=0
        ),
    )(*arrays)


def wide_back_block():
    return pl.BlockSpec(
        (1, 2, 4, 1, D // 8, TILE), lambda step, place_ref: (1 - step // 2, 0, 0, step % 2, 0, 0)
    )


def wide_back_first(place, rounded, second, slope, up_parts, down_parts):
    return wide_back_call(
        wide_back_first_kernel,
        [],
        (wide_back_block(), whole_block((4, TILE)), whole_block((ROWS, D))),
        (sds((2, 2, 4, 2, D // 8, TILE), BF), sds((4, TILE), F32), sds((ROWS, D), F32)),
        [],
        (place, rounded, second, slope, *up_parts[2:4], *up_parts[6:8], *down_parts),
    )


def wide_back_last(
    place, rounded, second, slope, up_parts, down_parts, before, grad, middle, gains, got
):
    full = whole_block((ROWS, D))
    out = sds((2, 4, 2, D // 8, TILE), BF)
    block = (2, 4, 1, D // 8, TILE)
    return wide_back_call(
        wide_back_last_kernel,
        [full] * 3 + [whole_block((2, D)), wide_back_block()],
        (
            pl.BlockSpec(block, lambda step, place_ref: (0, 0, jnp.minimum(step, 1), 0, 0)),
            pl.BlockSpec(block, lambda step, place_ref: (0, 0, jnp.maximum(step - 2, 0), 0, 0)),
            whole_block((4, TILE)),
            full,
            full,
            whole_block((8, D)),
        ),
        (out, out, sds((4, TILE), F32), sds((ROWS, D), F32), sds((ROWS, D), BF), sds((8, D), F32)),
        [pltpu.VMEM((ROWS, D), F32)],
        (
            place, rounded, second, slope, *up_parts[0:2], *up_parts[4:6], *down_parts,
            before, grad, middle, gains, got
        ),
    )


def mix_back_kernel(
    place_ref,
    lengths_ref,
    rounded_ref,
    middle_grad_ref,
    residual_ref,
    w0_ref,
    w1_ref,
    w2_ref,
    w3_ref,
    packed_ref,
    log_ref,
    mixed_ref,
    gains_ref,
    biases_ref,
    send_ref,
    lefts_ref,
    rights_ref,
    grad_ref,
    grad_rounded_ref,
    small_ref,
    held,
    grad_mixed,
    total,
    sems,
):
    x_at, y_at, c_at = place_ref[0], place_ref[1], place_ref[2]
    copies = quarter_copies(place_ref, (w0_ref, w1_ref, w2_ref, w3_ref), held, sems)
    for copy in copies:
        copy.start()

    def send_grad(part):
        @pl.when(c_at ^ (part & 1) == 1)
        def _():
            left = lefts_ref[1 if part == 3 else 0]
            value = mul_nn(left, rights_ref[part]).astype(BF).reshape(4, 2, D // 8, D)
            for side in range(2):
                send_ref[x_at ^ (part >> 1), side ^ y_at] = value[:, side]

    lefts_ref[1] = mixed_ref[...].T
    rights_ref[3] = rounded_ref[...]
    send_grad(3)

    def first(rows, carry):
        normed, inverse = normalize(residual_ref[rows, :].astype(F32))
        total[rows, :] = normed * gains_ref[0:1, :] + biases_ref[0:1, :]
        return carry

    over_chunks(first, 0)
    lefts_ref[0] = total[...].astype(BF).T
    for copy in copies:
        copy.wait()
    grad_mixed[...] = mul_nt(rounded_ref[...], square(held[3])).astype(BF)
    masks = head_masks()
    row_ids = lax.broadcasted_iota(jnp.int32, (LEN, 1), 0)
    scale = 1.0 / math.sqrt(HEAD_DIM)

    def one_sequence(seq, carry):
        rows = pl.ds(pl.multiple_of(seq * LEN, LEN), LEN)
        valid = row_ids < lengths_ref[seq]
        for group in range(GROUPS):
            at_query = slice(group * 128, (group + 1) * 128)
            at_key = slice(D + group * 128, D + (group + 1) * 128)
            at_value = slice(2 * D + group * 128, 2 * D + (group + 1) * 128)
            queries = stack_heads(packed_ref[rows, at_query], masks)
            key_rows = packed_ref[rows, at_key]
            value_rows = packed_ref[rows, at_value]
            grads = stack_heads(grad_mixed[rows, at_query], masks)
            scores = scores_of(key_rows, queries, valid)
            probs = jnp.exp(scores - log_ref[seq * GROUPS + group])
            grad_probs = mul_nt(value_rows, grads)
            inner = jnp.sum(grad_probs * probs, 0, keepdims=True)
            grad_scores = (probs * (grad_probs - inner)).astype(BF)
            rights_ref[2, rows, at_query] = mul_nn(probs.astype(BF), grads).astype(BF)
            rights_ref[1, rows, at_query] = (mul_nn(grad_scores, queries) * scale).astype(BF)
            grad_queries = unstack_heads(mul_tn(key_rows, grad_scores))
            rights_ref[0, rows, at_query] = (grad_queries * scale).astype(BF)
        return carry

    lax.fori_loop(0, SEQ_DEV, one_sequence, 0)
    for part in range(3):
        send_grad(part)
        result = mul_nt(rights_ref[part], square(held[part]))
        if part == 0:
            total[...] = result
        else:
            total[...] += result

    def body(rows, carry):
        gain_sum, move_sum, query_sum, value_sum = carry
        normed, inverse = normalize(residual_ref[rows, :].astype(F32))
        grad_pre = total[rows, :]
        grad = middle_grad_ref[rows, :] + norm_back(grad_pre * gains_ref[0:1, :], normed, inverse)
        grad_ref[rows, :] = grad
        grad_rounded_ref[rows, :] = grad.astype(BF)
        return (
            gain_sum + col_sum(grad_pre * normed),
            move_sum + col_sum(grad_pre),
            query_sum + col_sum(rights_ref[0, rows, :].astype(F32)),
            value_sum + col_sum(rights_ref[2, rows, :].astype(F32)),
        )

    row = jnp.zeros((1, D), F32)
    sums = over_chunks(body, (row, row, row, row))
    small_ref[...] = jnp.zeros_like(small_ref)
    for number in range(4):
        small_ref[number : number + 1, :] = sums[number]


def mix_back(
    place, lengths, rounded, middle_grad, residual, quarters, packed, logs, mixed, gains, biases
):
    out = sds((2, 2, 4, D // 8, D), BF)
    return pl.pallas_call(
        mix_back_kernel,
        out_shape=(
            out,
            sds((2, D, ROWS), BF),
            sds((4, ROWS, D), BF),
            sds((ROWS, D), F32),
            sds((ROWS, D), BF),
            sds((8, D), F32),
        ),
        grid=(1,),
        in_specs=[SMEM_SPEC, SMEM_SPEC]
        + [whole_block((ROWS, D))] * 3
        + [ANY_SPEC] * 4
        + [
            whole_block((ROWS, 3 * D)),
            whole_block((SEQ_DEV * GROUPS, 1, PER_GROUP * LEN)),
            whole_block((ROWS, D)),
            whole_block((2, D)),
            whole_block((6, D)),
        ],
        out_specs=(
            whole_block((2, 2, 4, D // 8, D)),
            whole_block((2, D, ROWS)),
            whole_block((4, ROWS, D)),
            whole_block((ROWS, D)),
            whole_block((ROWS, D)),
            whole_block((8, D)),
        ),
        scratch_shapes=[
            pltpu.VMEM((4, 4, 2, D // 8, D), BF),
            pltpu.VMEM((ROWS, D), BF),
            pltpu.VMEM((ROWS, D), F32),
            pltpu.SemaphoreType.DMA((8,)),
        ],
        compiler_params=pltpu.CompilerParams(vmem_limit_bytes=40 * MIB),
        cost_estimate=pl.CostEstimate(
            flops=2 * ROWS * D * 4 * D * 8, bytes_accessed=18 * MIB, transcendentals=0
        ),
    )(
        place, lengths, rounded, middle_grad, residual, *quarters, packed, logs, mixed, gains, biases
    )


def mix_back_last_kernel(place_ref, left_ref, right_ref, got_ref, pass_ref, keep_ref):
    step = pl.program_id(0)
    y_at = place_ref[1]
    value = mul_nn(left_ref[0], right_ref[0]).reshape(4, 2, D // 8, D)

    def into(out_ref):
        for side in range(2):
            at = side ^ y_at
            out_ref[at] = (value[:, side] + got_ref[0, at].astype(F32)).astype(BF)

    @pl.when(step == 0)
    def _():
        into(pass_ref)

    @pl.when(step == 1)
    def _():
        into(keep_ref)


def mix_back_last(place, lefts, rights, got):
    def part(step, place_ref):
        return (place_ref[0] ^ (1 - step)) * 2 + place_ref[2]

    out = sds((2, 4, D // 8, D), BF)
    return pl.pallas_call(
        mix_back_last_kernel,
        grid_spec=pltpu.PrefetchScalarGridSpec(
            num_scalar_prefetch=1,
            grid=(2,),
            in_specs=[
                pl.BlockSpec(
                    (1, D, ROWS), lambda step, place_ref: (part(step, place_ref) // 3, 0, 0)
                ),
                pl.BlockSpec((1, ROWS, D), lambda step, place_ref: (part(step, place_ref), 0, 0)),
                pl.BlockSpec(
                    (1, 2, 4, D // 8, D), lambda step, place_ref: (1 - step, 0, 0, 0, 0)
                ),
            ],
            out_specs=(whole_block((2, 4, D // 8, D)),) * 2,
        ),
        out_shape=(out, out),
        compiler_params=pltpu.CompilerParams(vmem_limit_bytes=16 * MIB),
        cost_estimate=pl.CostEstimate(
            flops=2 * ROWS * D * 2 * D, bytes_accessed=6 * MIB, transcendentals=0
        ),
    )(place, lefts, rights, got)


def swap(value, axis):
    return lax.ppermute(value, axis, [(0, 1), (1, 0)])


def after(value, *others):
    return lax.optimization_barrier((value, others))[0]


class Order:
    def __init__(self):
        self.last = None

    def hold(self, *arrays):
        if self.last is not None:
            arrays, self.last = lax.optimization_barrier((arrays, self.last))
        return arrays

    def __call__(self, function, *arrays):
        results = function(*self.hold(*arrays))
        self.last = jax.tree.leaves(results)[0]
        return results


def wide_sum(*values):
    total = values[0].astype(F32)
    for value in values[1:]:
        total = total + value.astype(F32)
    return total


def rounded_sum(*values):
    return wide_sum(*values).astype(BF)


class Moves:
    def __init__(self, fsdp):
        self.z_size = fsdp // 2
        self.staged = fsdp == 8
        self.x_at = lax.axis_index("x")
        self.y_at = lax.axis_index("y")
        self.z_at = lax.axis_index("z")
        self.c_at = lax.axis_index("c")
        self.place = jnp.stack([self.x_at, self.y_at, self.c_at]).astype(jnp.int32)

    def hop(self, value, reach):
        return lax.ppermute(value, "z", [(at, at ^ reach) for at in range(self.z_size)])

    def ordered(self, bit, own, other):
        return jnp.where(bit == 0, jnp.stack([own, other]), jnp.stack([other, own]))

    def by_side(self, value):
        value = value.reshape(4, 2, *value.shape[1:]).swapaxes(0, 1)
        return jnp.where(self.y_at == 0, value, value[::-1])

    def by_shard(self, value):
        value = jnp.where(self.y_at == 0, value, value[::-1]).swapaxes(0, 1)
        return value.reshape(8, *value.shape[2:])

    def own_quarter(self, flat):
        shard = flat.reshape(D // 8, -1, 128)
        step = shard.shape[1] // 4
        own = lax.dynamic_slice_in_dim(shard, (self.x_at * 2 + self.c_at) * step, step, 1)
        return own.reshape(D // 8, step // 5, 5, 128).swapaxes(0, 1).reshape(-1, D // 8, D)

    def gather_quarters(self, flat):
        whole = lax.all_gather(flat, ("z", "y"), axis=0, tiled=True)
        whole = whole.reshape(8, D // 8, 4, -1, D).transpose(2, 0, 3, 1, 4)
        parts = []
        for number in range(4):
            quarter = (self.x_at ^ (number >> 1)) * 2 + (self.c_at ^ (number & 1))
            parts.append(self.by_side(lax.dynamic_index_in_dim(whole, quarter, 0, False)))
        return tuple(parts)

    def low_bit(self, own, other):
        return self.ordered(self.z_at % 2, own, other)

    def high_bit(self, own, other):
        line = self.ordered(self.z_at // 2, own, other)
        line = line.reshape(4, *own.shape[1:])
        return tuple(line[:, tile] for tile in range(line.shape[1]))

    def part_far(self, *parts):
        total = wide_sum(*parts)
        total = total.reshape(2, 2, *total.shape[1:])
        far = self.z_at // 2
        return tuple(
            lax.dynamic_index_in_dim(total, at, 0, False).astype(BF) for at in (1 - far, far)
        )

    def part_near(self, *parts):
        total = wide_sum(*parts)
        near = self.z_at % 2
        return tuple(
            lax.dynamic_index_in_dim(total, at, 0, False).astype(BF) for at in (1 - near, near)
        )

    def gather_halves(self, flat):
        if not self.staged:
            whole = lax.all_gather(flat, ("z", "y"), axis=0, tiled=True).reshape(8, 2, TILE // 2, D)
            return tuple(
                lax.dynamic_index_in_dim(whole, self.c_at ^ number, 1, False) for number in range(2)
            )
        plane = lax.all_gather(self.own_half(flat), ("z", "y"), axis=0, tiled=False)
        return (plane, swap(plane, "c"))

    def own_half(self, flat):
        own = lax.dynamic_slice_in_dim(flat, self.c_at * (TILE // 2) * 5, (TILE // 2) * 5, 0)
        return own.reshape(TILE // 2, D)

    def sum_all(self, value):
        value = value + swap(value, "c")
        value = value + swap(value, "x")
        value = value + swap(value, "y")
        reach = 1
        while reach < self.z_size:
            value = value + self.hop(value, reach)
            reach *= 2
        return value

    def along_z(self, part):
        return lax.psum_scatter(part, "z", scatter_dimension=0, tiled=False)

    def quarters_flat(self, own, beside):
        four = jnp.concatenate([own, beside])
        four = jnp.where(self.c_at == 0, four, four[jnp.array([1, 0, 3, 2])])
        four = jnp.where(self.x_at == 0, four, four[jnp.array([2, 3, 0, 1])])
        return four.transpose(2, 0, 1, 3).astype(F32).reshape(-1, 128)

    def halves_flat(self, own, other):
        both = self.ordered(self.c_at, own, other)
        return both.reshape(D, TILE).T.astype(F32).reshape(-1, 128)

    def plain_quarters(self, passed, keep):
        part = self.by_shard(rounded_sum(keep, swap(passed, "x")))
        part = part.transpose(0, 2, 1, 3).reshape(D, -1)
        part = lax.psum_scatter(part, ("z", "y"), scatter_dimension=0, tiled=True)
        parts = lax.all_gather(part, ("x", "c"), axis=0, tiled=False)
        return parts.swapaxes(0, 1).astype(F32).reshape(-1, 128)

    def plain_halves(self, part):
        part = self.by_shard(part).transpose(0, 2, 1)
        part = part.reshape(FF, D // 2)
        part = lax.psum_scatter(part, ("z", "y"), scatter_dimension=0, tiled=True).T
        part = rounded_sum(part, swap(part, "x"))
        return lax.all_gather(part, "c", axis=0, tiled=True).T.astype(F32).reshape(-1, 128)


def local(
    fsdp,
    inputs,
    targets,
    masked,
    lengths,
    attn_weight,
    up_weight,
    down_weight,
    norm_gains,
    layer_biases,
    up_bias,
    head_weight,
    final_gain,
    final_shift,
    head_bias,
):
    moves = Moves(fsdp)
    place = moves.place
    shifts = up_bias.reshape(LAYERS, TILES, TILE)
    saved = []

    def mix_on(layer, residual, quarters):
        return mix(place, lengths, residual, quarters, norm_gains[layer], layer_biases[layer])

    def prepared(targets, masked, head_weight, head_bias):
        wide_bias = head_bias.reshape(1, VOCAB)
        return (
            targets.reshape(ROWS, 1),
            masked.reshape(ROWS, 1),
            jnp.pad(head_weight, ((0, 0), (0, 128 - VOCAB))),
            jnp.pad(wide_bias, ((0, 0), (0, 128 - VOCAB)), constant_values=-1e30),
        )

    def up_on(layer, second, parts):
        return up(place, second, parts, shifts[layer])

    def down_on(layer, middle, active, parts):
        return down(place, middle, active, parts, layer_biases[layer])

    def two(own, other):
        return jnp.stack([own, other])

    run = Order()
    if moves.staged:
        a0 = run(moves.own_quarter, attn_weight[0])
        a0_near = moves.hop(a0, 1)
        u0 = run(moves.own_quarter, up_weight[0])
        u0_near = moves.hop(u0, 1)
        a0 = run(moves.low_bit, a0, a0_near)
        a0_far = moves.hop(a0, 2)
        u0 = run(moves.low_bit, u0, u0_near)
        u0_far = moves.hop(u0, 2)
        (a0,) = run(moves.high_bit, a0, a0_far)
        a0_y = swap(a0, "y")
        d0 = run(moves.own_half, down_weight[0])
        d0 = lax.all_gather(d0, ("z", "y"), axis=0, tiled=False)
        a0 = run(two, a0, a0_y)
        a0_x = swap(a0, "x")
        a0_c = swap(a0, "c")
        u00, u01 = run(moves.high_bit, u0, u0_far)
        u00_y, u01_y = swap(u00, "y"), swap(u01, "y")
        a1 = run(moves.own_quarter, attn_weight[1])
        a1_near = moves.hop(a1, 1)
        u1 = run(moves.own_quarter, up_weight[1])
        u1_near = moves.hop(u1, 1)
        u00 = run(two, u00, u00_y)
        u00_x = swap(u00, "x")
        u00_c = swap(u00, "c")
        a1 = run(moves.low_bit, a1, a1_near)
        a1_far = moves.hop(a1, 2)
        (a0_x,) = run.hold(a0_x)
        a0_xc = swap(a0_x, "c")
        u01 = run(two, u01, u01_y)
        u01_x = swap(u01, "x")
        u01_c = swap(u01, "c")
        u1 = run(moves.low_bit, u1, u1_near)
        u1_far = moves.hop(u1, 2)
        ready = run(prepared, targets, masked, head_weight, head_bias)
        quarters0 = (a0, a0_c, a0_x, a0_xc)
        mixed0 = run(lambda r, *q: mix_on(0, r, q), inputs, *quarters0)
        (a1,) = run(moves.high_bit, a1, a1_far)
        a1_y = swap(a1, "y")
        u00_x, = run.hold(u00_x)
        u00_xc = swap(u00_x, "c")
        a1 = run(two, a1, a1_y)
        a1_x = swap(a1, "x")
        a1_c = swap(a1, "c")
        u10, u11 = run(moves.high_bit, u1, u1_far)
        u10_y, u11_y = swap(u10, "y"), swap(u11, "y")
        u01_x, = run.hold(u01_x)
        u01_xc = swap(u01_x, "c")
        ups0 = (u00, u01, u00_c, u01_c, u00_x, u01_x, u00_xc, u01_xc)
        wide0 = run(lambda m, *p: up_on(0, m, p), mixed0[4], *ups0)
        (d0,) = run.hold(d0)
        d0_c = swap(d0, "c")
        d1 = run(moves.own_half, down_weight[1])
        d1 = lax.all_gather(d1, ("z", "y"), axis=0, tiled=False)
        u10 = run(two, u10, u10_y)
        u10_x = swap(u10, "x")
        u10_c = swap(u10, "c")
        u11 = run(two, u11, u11_y)
        u11_x = swap(u11, "x")
        u11_c = swap(u11, "c")
        residual1 = run(lambda m, a, *p: down_on(0, m, a, p), mixed0[3], wide0[0], d0, d0_c)
        (a1_x,) = run.hold(a1_x)
        a1_xc = swap(a1_x, "c")
        quarters1 = (a1, a1_c, a1_x, a1_xc)
        mixed1 = run(lambda r, *q: mix_on(1, r, q), residual1, *quarters1)
        u10_x, u11_x = run.hold(u10_x, u11_x)
        u10_xc, u11_xc = swap(u10_x, "c"), swap(u11_x, "c")
        ups1 = (u10, u11, u10_c, u11_c, u10_x, u11_x, u10_xc, u11_xc)
        wide1 = run(lambda m, *p: up_on(1, m, p), mixed1[4], *ups1)
        (d1,) = run.hold(d1)
        d1_c = swap(d1, "c")
        residual = run(lambda m, a, *p: down_on(1, m, a, p), mixed1[3], wide1[0], d1, d1_c)
        weights = [(quarters0, ups0, (d0, d0_c)), (quarters1, ups1, (d1, d1_c))]
        saved = [(inputs, *mixed0, *wide0), (residual1, *mixed1, *wide1)]
    else:
        weights = []
        for layer in range(LAYERS):
            attn_parts = moves.gather_quarters(attn_weight[layer])
            up_parts = moves.gather_quarters(up_weight[layer])
            weights.append(
                (
                    [part[:, :, 0] for part in attn_parts],
                    [up_parts[number][:, :, tile] for number in range(4) for tile in range(2)],
                    moves.gather_halves(down_weight[layer]),
                )
            )
        residual = inputs
        for layer in range(LAYERS):
            quarters, up_parts, down_parts = weights[layer]
            mixed = mix_on(layer, residual, quarters)
            wide = up_on(layer, mixed[4], up_parts)
            saved.append((residual, *mixed, *wide))
            residual = down_on(layer, mixed[3], wide[0], down_parts)
        ready = prepared(targets, masked, head_weight, head_bias)
    activations, grad, rounded, head_small = run(
        head, residual, *ready, final_gain.reshape(1, D), final_shift.reshape(1, D)
    )

    def down_at(layer, rounded):
        return down_back(place, rounded, saved[layer][6])

    def wide_first(layer, rounded):
        _, up_parts, down_parts = weights[layer]
        return wide_back_first(
            place, rounded, saved[layer][5], saved[layer][7], up_parts, down_parts
        )

    def wide_last(layer, rounded, before, grad, got):
        _, up_parts, down_parts = weights[layer]
        _, _, _, _, middle, second, _, slope = saved[layer]
        return wide_back_last(
            place, rounded, second, slope, up_parts, down_parts, before, grad, middle, norm_gains[layer], got
        )

    def mix_first(layer, rounded, middle_grad):
        residual, packed, logs, mixed, _, _, _, _ = saved[layer]
        return mix_back(
            place,
            lengths,
            rounded,
            middle_grad,
            residual,
            weights[layer][0],
            packed,
            logs,
            mixed,
            norm_gains[layer],
            layer_biases[layer],
        )

    def mix_last(lefts, rights, got):
        return mix_back_last(place, lefts, rights, got)

    def shift_rows(shift_send, shift_keep):
        send, keep = (part.reshape(2, 2, TILE)[::-1] for part in (shift_send, shift_keep))
        parts = moves.ordered(moves.c_at, keep, send).swapaxes(0, 1)
        return jnp.where(moves.x_at == 0, parts, parts[::-1]).reshape(TILES, TILE)

    def packed_small(head_small, *rest):
        small = [head_small]
        for layer in range(LAYERS):
            shift_send, shift_keep, wide_small, mix_small = rest[4 * layer : 4 * layer + 4]
            small += [shift_rows(shift_send, shift_keep), wide_small, mix_small]
        return jnp.concatenate(small, 0)

    def plus(own, other):
        return own + other

    if moves.staged:
        d1_send, d1_keep = run(lambda g: down_at(1, g), rounded)
        d1_c = swap(d1_send, "c")
        u1_send, *tail1 = run(lambda g: wide_first(1, g), rounded)
        u1_c = swap(u1_send, "c")
        d1_y = swap(run(rounded_sum, d1_keep[1], d1_c[1]), "y")
        u1_pass, u1_keep, shift_keep1, middle_grad, middle_rounded, wide_small1 = run(
            lambda *a: wide_last(1, *a), rounded, tail1[1], grad, u1_c
        )
        u1_x = swap(u1_pass, "x")
        a1_send, lefts, rights, grad, rounded, mix_small1 = run(
            lambda *a: mix_first(1, *a), middle_rounded, middle_grad
        )
        a1_c = swap(a1_send, "c")
        d1 = moves.along_z(run(rounded_sum, d1_keep[0], d1_c[0], d1_y))
        a1_pass, a1_keep = run(mix_last, lefts, rights, a1_c)
        a1_x = swap(a1_pass, "x")
        d0_send, d0_keep = run(lambda g: down_at(0, g), rounded)
        d0_c = swap(d0_send, "c")
        u0_send, *tail0 = run(lambda g: wide_first(0, g), rounded)
        u0_c = swap(u0_send, "c")
        u1_y = swap(run(rounded_sum, u1_keep[1], u1_x[1]), "y")
        d0_y = swap(run(rounded_sum, d0_keep[1], d0_c[1]), "y")
        u0_pass, u0_keep, shift_keep0, middle_grad, middle_rounded, wide_small0 = run(
            lambda *a: wide_last(0, *a), rounded, tail0[1], grad, u0_c
        )
        u0_x = swap(u0_pass, "x")
        u1 = moves.along_z(run(rounded_sum, u1_keep[0], u1_x[0], u1_y))
        a1_y = swap(run(rounded_sum, a1_keep[1], a1_x[1]), "y")
        (d1,) = run.hold(d1)
        d1_x = swap(d1, "x")
        a0_send, lefts, rights, grad, rounded, mix_small0 = run(
            lambda *a: mix_first(0, *a), middle_rounded, middle_grad
        )
        a0_c = swap(a0_send, "c")
        small = run(
            packed_small,
            head_small,
            *(tail0[0], shift_keep0, wide_small0, mix_small0),
            *(tail1[0], shift_keep1, wide_small1, mix_small1),
        )
        small_next = moves.hop(small, 2)
        a0_pass, a0_keep = run(mix_last, lefts, rights, a0_c)
        a0_x = swap(a0_pass, "x")
        small = run(plus, small, small_next)
        small_next = moves.hop(small, 1)
        d1 = run(rounded_sum, d1, d1_x)
        d1_c = swap(d1, "c")
        d0 = moves.along_z(run(rounded_sum, d0_keep[0], d0_c[0], d0_y))
        u0_y = swap(run(rounded_sum, u0_keep[1], u0_x[1]), "y")
        small = run(plus, small, small_next)
        small_next = swap(small, "c")
        a1_send, a1_stay = run(moves.part_far, a1_keep[0], a1_x[0], a1_y)
        a1_far = moves.hop(a1_send, 2)
        small = run(plus, small, small_next)
        a0_y = swap(run(rounded_sum, a0_keep[1], a0_x[1]), "y")
        small_next = swap(small, "x")
        down_grad1 = run(moves.halves_flat, d1, d1_c)
        a1_send, a1_stay = run(moves.part_near, a1_stay, a1_far)
        a1_near = moves.hop(a1_send, 1)
        u0_send, u0_stay = run(moves.part_far, u0_keep[0], u0_x[0], u0_y)
        u0_far = moves.hop(u0_send, 2)
        small = run(plus, small, small_next)
        small_next = swap(small, "y")
        last1 = run(lambda u, *a: jnp.concatenate([u, rounded_sum(*a)[None]]), u1, a1_stay, a1_near)
        last1_c = swap(last1, "c")
        a0_send, a0_stay = run(moves.part_far, a0_keep[0], a0_x[0], a0_y)
        a0_far = moves.hop(a0_send, 2)
        last1 = run(two, last1, last1_c)
        last1_x = swap(last1, "x")
        u0_send, u0_stay = run(moves.part_near, u0_stay, u0_far)
        u0_near = moves.hop(u0_send, 1)
        (d0,) = run.hold(d0)
        d0_x = swap(d0, "x")
        summed = run(plus, small, small_next)
        a0_send, a0_stay = run(moves.part_near, a0_stay, a0_far)
        a0_near = moves.hop(a0_send, 1)
        up_grad1 = run(moves.quarters_flat, last1[:, :2], last1_x[:, :2])
        attn_grad1 = run(moves.quarters_flat, last1[:, 2:], last1_x[:, 2:])
        d0 = run(rounded_sum, d0, d0_x)
        d0_c = swap(d0, "c")
        last0 = run(
            lambda u0, u1, a0, a1: jnp.concatenate([rounded_sum(u0, u1), rounded_sum(a0, a1)[None]]),
            *(u0_stay, u0_near, a0_stay, a0_near),
        )
        last0_c = swap(last0, "c")
        down_grad0 = run(moves.halves_flat, d0, d0_c)
        last0 = run(two, last0, last0_c)
        last0_x = swap(last0, "x")
        up_grad0 = run(moves.quarters_flat, last0[:, :2], last0_x[:, :2])
        attn_grad0 = run(moves.quarters_flat, last0[:, 2:], last0_x[:, 2:])
        attn_grads = [attn_grad0, attn_grad1]
        up_grads = [up_grad0, up_grad1]
        down_grads = [down_grad0, down_grad1]
    else:
        attn_grads, up_grads, down_grads, smalls = ([None] * LAYERS for _ in range(4))
        for layer in reversed(range(LAYERS)):
            send, keep = down_at(layer, rounded)
            down_grads[layer] = moves.plain_halves(rounded_sum(keep, swap(send, "c")))
            send, shift_send, before = wide_first(layer, rounded)
            passed, keep, shift_keep, middle_grad, middle_rounded, wide_small = wide_last(
                layer, rounded, before, grad, swap(send, "c")
            )
            up_grads[layer] = moves.plain_quarters(passed, keep)
            send, lefts, rights, grad, rounded, mix_small = mix_first(
                layer, middle_rounded, middle_grad
            )
            passed, keep = mix_last(lefts, rights, swap(send, "c"))
            attn_grads[layer] = moves.plain_quarters(passed[:, :, None], keep[:, :, None])
            smalls[layer] = (shift_send, shift_keep, wide_small, mix_small)
        summed = moves.sum_all(packed_small(head_small, *smalls[0], *smalls[1]))

    gains_grad, biases_grad, shifts_grad = [], [], []
    for layer in range(LAYERS):
        base = 40 + 24 * layer
        shifts_grad.append(summed[base : base + 8].reshape(FF))
        wide_sums = summed[base + 8 : base + 16]
        mix_sums = summed[base + 16 : base + 24]
        gains_grad.append(jnp.stack([mix_sums[0], wide_sums[0]]))
        biases_grad.append(
            jnp.stack([mix_sums[1], wide_sums[1], mix_sums[2], mix_sums[3], wide_sums[2], wide_sums[3]])
        )
    totals = summed[35]
    return (
        activations,
        grad,
        jnp.stack(attn_grads),
        jnp.stack(up_grads),
        jnp.stack(down_grads),
        jnp.stack(gains_grad),
        jnp.stack(biases_grad),
        jnp.stack(shifts_grad),
        summed[:VOCAB].T,
        summed[32],
        summed[33],
        summed[34, :VOCAB],
        totals[0] / totals[2],
        totals[1] / totals[2],
        totals[2].astype(jnp.int32),
    )


def solution(mesh):
    fsdp, dp = mesh.shape["fsdp"], mesh.shape["dp"]
    fine = Mesh(mesh.devices.reshape(fsdp // 2, 2, dp // 2, 2), ("z", "y", "x", "c"))
    tokens = ("z", "y", "x", "c")
    flat = P(None, ("z", "y"), None)
    placed = (P(tokens, None), P(tokens), P(tokens), P(tokens), flat, flat, flat) + (P(),) * 7

    def run(*arrays):
        return local(fsdp, *arrays)

    return jax.shard_map(
        run,
        mesh=fine,
        in_specs=placed,
        out_specs=(P(tokens, None), P(tokens, None), flat, flat, flat) + (P(),) * 10,
        check_vma=False,
    )
```

time: 745 us -> 660 us (0.89)
  blocking collectives: 119 us -> 0 us
  local copies, waits for them, and re-layouts: 48 us -> 130 us
  waiting for transfers between devices: 249 us -> 196 us
  starting transfers between devices: 35 us -> 60.5 us
  other arithmetic: 76.4 us -> 55.2 us
    all_gather x10 -> x0, blocking collectives: 119 us -> none  [the longest x4 82.8 us: gather_quarters(): line = lax.all_gather(own, 'z', axis=0, tiled=False)]
    ppermute x41 -> x53, waiting for transfers between devices: 213 us -> 122 us  [swap(): return lax.ppermute(value, axis, [(0, 1), (1, 0)])]
    ppermute x2 -> x16, waiting for transfers between devices: 15 us -> 74.2 us  [hop(): lax.ppermute(value, 'z', [(at, at ^ reach) for at in range(self.z_size)])]
    unnamed x167 -> x300, local copies, waits for them, and re-layouts: 29.3 us -> 70 us
    convert_element_type x34 -> x15, other arithmetic: 56 us -> 20.7 us  [the longest x12 18.6 us: rounded_sum(): return wide_sum(*values).astype(BF)]
    squeeze x3 -> x20, local copies, waits for them, and re-layouts: 0.01 us -> 25.7 us  [the longest x2 5.07 us: local(): d0 = moves.along_z(run(rounded_sum, d0_keep[0], d0_c[0], d0_y))]
    all_gather x2, waiting for transfers between devices: 20.7 us -> 0.01 us  [the longest x1 0.01 us: local(): d0 = lax.all_gather(d0, ('z', 'y'), axis=0, tiled=False)]
    ppermute x2 -> x16, starting transfers between devices: 2.74 us -> 19.7 us  [hop(): lax.ppermute(value, 'z', [(at, at ^ reach) for at in range(self.z_size)])]
  transfers between devices with their start and end apart: 51 -> 74, of which waited for: 18 -> 30; matrix products, arithmetic and copies ran while one was open for 12% -> 14% of each run, Pallas kernels for 11% -> 23%
where the time goes in v2:
time: 660 us; the launch traced here: 650 us
  waiting for transfers between devices  196 us (30%)
  Pallas kernels  184 us (28%)
  local copies, waits for them, and re-layouts  130 us (20%)
  starting transfers between devices  60.5 us (9%)
  other arithmetic  55.2 us (8%)
  between operations  22.9 us (3%)
    ppermute x53, waiting for transfers between devices, swap(): return lax.ppermute(value, axis, [(0, 1), (1, 0)])  122 us
    ppermute x16, waiting for transfers between devices, hop(): lax.ppermute(value, 'z', [(at, at ^ reach) for at in range(self.z_size)])  74.2 us
    unnamed x300, local copies, waits for them, and re-layouts  70 us
    pallas_call x4, Pallas kernels, wide_back_call(): pl.pallas_call(kernel, grid_spec=pltpu.PrefetchScalarGridSpec(num_scalar_...  58.2 us
    ppermute x53, starting transfers between devices, swap(): return lax.ppermute(value, axis, [(0, 1), (1, 0)])  40.2 us
    pallas_call x2, Pallas kernels, mix_back(): pl.pallas_call(mix_back_kernel, out_shape=(out, sds((2, D, ROWS), BF), sd...  34.7 us
    pallas_call x2, Pallas kernels, mix(): pl.pallas_call(mix_kernel, out_shape=(sds((ROWS, 3 * D), BF), sds((SEQ_DE...  24.5 us
    pallas_call x2, Pallas kernels, down(): pl.pallas_call(down_kernel, grid=(TILES,), out_shape=sds((ROWS, D), F32),...  20.9 us
  transfers between devices with their start and end apart: 74, of which 30 were waited for; matrix products, arithmetic and copies ran while one was open for 14% of the time, Pallas kernels for 23%

profile of v2, /device:TPU:0, one launch (start us, length us, event | category | flops | bytes accessed | tf_op | source)
XLA Modules:
  0.0 649.5 jit_solution(11726950194631275256)
XLA Ops:
  7.2 2.0 slice_bitcast_fusion.32
  9.6 3.1 collective-permute-start
  15.8 2.7 collective-permute-start.1
  18.5 6.2 collective-permute-done.2
  25.5 10.7 %collective-permute-done.1 = bf16[2,1,80,640]{3,2,0,1:T(8,128)(2,1)S(1)} collective-permute-done((bf16[2,1,80,640]{3,2,0,1:T(8,128)(2,1)S(1)}, bf16[2,1,80,640]{3,2,0,1:T(8,128)(2,1)S(1)}, u32[]{:S(2)}, u32[]{:S(2)}) %collective-permute-start.1) | collective-permute-done | bytes 204832 | tf_op jit(solution)/shard_map/ppermute | solution.py:933
  38.5 5.8 collective-permute-done.3
  48.9 3.2 collective-permute-start.7
  53.4 10.0 %collective-permute-done.8 = bf16[4,80,640]{2,1,0:T(8,128)(2,1)} collective-permute-done((bf16[4,80,640]{2,1,0:T(8,128)(2,1)}, bf16[4,80,640]{2,1,0:T(8,128)(2,1)}, u32[]{:S(2)}, u32[]{:S(2)}) %collective-permute-start.8) | collective-permute-done | bytes 409632 | tf_op jit(solution)/shard_map/ppermute | solution.py:889
  67.6 2.6 collective-permute-start.15
  70.3 9.0 %collective-permute-done.11 = bf16[4,80,640]{2,1,0:T(8,128)(2,1)S(1)} collective-permute-done((bf16[4,80,640]{2,1,0:T(8,128)(2,1)S(1)}, bf16[4,80,640]{2,1,0:T(8,128)(2,1)S(1)}, u32[]{:S(2)}, u32[]{:S(2)}) %collective-permute-start.11) | collective-permute-done | bytes 409632 | tf_op jit(solution)/shard_map/ppermute | solution.py:889
  83.8 12.3 %shard_map.325 = (bf16[512,1920]{1,0:T(8,128)(2,1)S(1)}, f32[20,1,512]{2,1,0:T(1,128)S(1)}, bf16[512,640]{1,0:T(8,128)(2,1)S(1)}, f32[512,640]{1,0:T(8,128)S(1)}, bf16[512,640]{1,0:T(8,128)(2,1)S(1)}) custom-call(s32[3]{0:T(128)S(1)} %pad_add_fusion.place_ref, s32[4]{0:T(128)S(1)} %copy-done.63, bf16[512,640]{1,0:T(8,128)(2,1)S(1)} %copy-done.61, ...), custom_call_target="tpu_custom_call" | custom-call | flops 6710886400 | bytes 10485760 | tf_op jit(solution)/shard_map/pallas_call | solution.py:195
  101.6 6.9 %collective-permute-done.18 = bf16[4,80,640]{2,1,0:T(8,128)(2,1)S(1)} collective-permute-done((bf16[4,80,640]{2,1,0:T(8,128)(2,1)S(1)}, bf16[4,80,640]{2,1,0:T(8,128)(2,1)S(1)}, u32[]{:S(2)}, u32[]{:S(2)}) %collective-permute-start.18) | collective-permute-done | bytes 409632 | tf_op jit(solution)/shard_map/ppermute | solution.py:889
  109.6 14.9 %collective-permute-done.17 = bf16[2,2,80,640]{3,2,1,0:T(8,128)(2,1)S(1)} collective-permute-done((bf16[2,2,80,640]{3,2,1,0:T(8,128)(2,1)S(1)}, bf16[2,2,80,640]{3,2,1,0:T(8,128)(2,1)S(1)}, u32[]{:S(2)}, u32[]{:S(2)}) %collective-permute-start.17) | collective-permute-done | bytes 409632 | tf_op jit(solution)/shard_map/ppermute | solution.py:933
  125.9 2.3 collective-permute-done.20.refs_7_.u3_ref
  128.2 9.1 %shard_map.326 = (bf16[8,512,640]{2,1,0:T(8,128)(2,1)S(1)}, bf16[8,512,640]{2,1,0:T(8,128)(2,1)S(1)}) custom-call(s32[3]{0:T(128)S(1)} %pad_add_fusion.place_ref, bf16[512,640]{1,0:T(8,128)(2,1)S(1)} %copy-done.79, bf16[2,4,80,640]{3,2,1,0:T(8,128)(2,1)S(1)} %pad_maximum_fusion.1.refs_0_.u0_ref, ...), custom_call_target="tpu_custom_call" | custom-call | flops 13421772800 | bytes 20971520 | tf_op jit(solution)/shard_map/pallas_call | solution.py:256
  137.3 2.4 copy-done
  139.7 2.3 copy-done.66
  147.6 2.3 collective-permute-start.25
  149.9 10.2 %collective-permute-done.23 = bf16[4,80,640]{2,1,0:T(8,128)(2,1)S(1)} collective-permute-done((bf16[4,80,640]{2,1,0:T(8,128)(2,1)S(1)}, bf16[4,80,640]{2,1,0:T(8,128)(2,1)S(1)}, u32[]{:S(2)}, u32[]{:S(2)}) %collective-permute-start.23) | collective-permute-done | bytes 409632 | tf_op jit(solution)/shard_map/ppermute | solution.py:889
  160.1 2.1 pad_maximum_fusion.4.refs_0_.u0_ref
  162.2 7.9 %collective-permute-done.22 = bf16[4,80,640]{2,1,0:T(8,128)(2,1)S(1)} collective-permute-done((bf16[4,80,640]{2,1,0:T(8,128)(2,1)}, bf16[4,80,640]{2,1,0:T(8,128)(2,1)S(1)}, u32[]{:S(2)}, u32[]{:S(2)}) %collective-permute-start.22) | collective-permute-done | bytes 409632 | tf_op jit(solution)/shard_map/ppermute | solution.py:889
  172.2 2.5 copy-done.1
  176.0 10.5 %shard_map.327.residual_ref = f32[512,640]{1,0:T(8,128)S(1)} custom-call(s32[3]{0:T(128)S(1)} %pad_add_fusion.place_ref, f32[512,640]{1,0:T(8,128)S(1)} %copy-done.21, bf16[8,512,640]{2,1,0:T(8,128)(2,1)S(1)} %copy-done.1, bf16[8,320,640]{2,1,0:T(8,128)(2,1)S(1)} %copy-done.6, bf16[8,320,640]{2,1,0:T(8,128)(2,1)} %collective-permute-done.21.d1_ref, ...), custom_call_target="tpu_custom_call" | custom-call | flops 3355443200 | bytes 14680064 | tf_op jit(solution)/shard_map/pallas_call | solution.py:297
  186.6 2.4 collective-permute-start.30
  189.7 12.2 %shard_map.328 = (bf16[512,1920]{1,0:T(8,128)(2,1)S(1)}, f32[20,1,512]{2,1,0:T(1,128)S(1)}, bf16[512,640]{1,0:T(8,128)(2,1)S(1)}, f32[512,640]{1,0:T(8,128)S(1)}, bf16[512,640]{1,0:T(8,128)(2,1)S(1)}) custom-call(s32[3]{0:T(128)S(1)} %pad_add_fusion.place_ref, s32[4]{0:T(128)S(1)} %copy-done.63, f32[512,640]{1,0:T(8,128)S(1)} %shard_map.327.residual_ref, ...), custom_call_target="tpu_custom_call" | custom-call | flops 6710886400 | bytes 10485760 | tf_op jit(solution)/shard_map/pallas_call | solution.py:195
  208.5 17.3 %collective-permute-done.29.refs_4_.u2_ref = bf16[2,4,80,640]{3,2,1,0:T(8,128)(2,1)} collective-permute-done((bf16[2,4,80,640]{3,2,1,0:T(8,128)(2,1)}, bf16[2,4,80,640]{3,2,1,0:T(8,128)(2,1)}, u32[]{:S(2)}, u32[]{:S(2)}) %collective-permute-start.29) | collective-permute-done | bytes 819232 | tf_op jit(solution)/shard_map/ppermute | solution.py:889
  226.3 2.1 collective-permute-done.31.refs_6_.u2_ref
  230.7 9.5 %shard_map.329 = (bf16[8,512,640]{2,1,0:T(8,128)(2,1)S(1)}, bf16[8,512,640]{2,1,0:T(8,128)(2,1)S(1)}) custom-call(s32[3]{0:T(128)S(1)} %pad_add_fusion.place_ref, bf16[512,640]{1,0:T(8,128)(2,1)S(1)} %copy-done.86, bf16[2,4,80,640]{3,2,1,0:T(8,128)(2,1)} %pad_maximum_fusion.4.refs_0_.u0_ref, bf16[2,4,80,640]{3,2,1,0:T(8,128)(2,1)} %pad_maximum_fusion.5.refs_1_.u1_ref, ...), custom_call_target="tpu_custom_call" | custom-call | flops 13421772800 | bytes 20971520 | tf_op jit(solution)/shard_map/pallas_call | solution.py:256
  240.3 2.3 copy-done.3
  242.6 2.3 copy-done.68
  247.5 3.8 collective-permute-done.33.d1_ref
  251.3 2.5 copy-done.4
  257.1 10.4 %shard_map.330.residual_ref = f32[512,640]{1,0:T(8,128)S(1)} custom-call(s32[3]{0:T(128)S(1)} %pad_add_fusion.place_ref, f32[512,640]{1,0:T(8,128)S(1)} %copy-done.26, bf16[8,512,640]{2,1,0:T(8,128)(2,1)S(1)} %copy-done.4, bf16[8,320,640]{2,1,0:T(8,128)(2,1)S(1)} %copy-done.7, bf16[8,320,640]{2,1,0:T(8,128)(2,1)} %collective-permute-done.33.d1_ref, ...), custom_call_target="tpu_custom_call" | custom-call | flops 3355443200 | bytes 14680064 | tf_op jit(solution)/shard_map/pallas_call | solution.py:297
  275.4 4.2 shard_map.331
  280.3 2.5 copy-done.5
  282.7 8.3 %shard_map.332 = (bf16[2,4,320,640]{3,2,1,0:T(8,128)(2,1)S(1)}, bf16[2,4,320,640]{3,2,1,0:T(8,128)(2,1)S(1)}) custom-call(s32[3]{0:T(128)S(1)} %pad_add_fusion.place_ref, bf16[512,640]{1,0:T(8,128)(2,1)S(1)} %get-tuple-element.370.grad_ref.rounded_ref, bf16[8,512,640]{2,1,0:T(8,128)(2,1)S(1)} %copy-done.5), custom_call_target="tpu_custom_call" | custom-call | flops 3355443200 | bytes 13631488 | tf_op jit(solution)/shard_map/pallas_call | solution.py:430
  291.5 12.9 %shard_map.333 = (bf16[2,2,4,2,80,640]{5,4,3,2,1,0:T(8,128)(2,1)S(1)}, f32[4,640]{1,0:T(4,128)S(1)}, f32[512,640]{1,0:T(8,128)S(1)}) custom-call(s32[3]{0:T(128)S(1)} %pad_add_fusion.place_ref, bf16[512,640]{1,0:T(8,128)(2,1)S(1)} %get-tuple-element.370.grad_ref.rounded_ref, bf16[512,640]{1,0:T(8,128)(2,1)S(1)} %copy-done.87, ...), custom_call_target="tpu_custom_call" | custom-call | flops 6710886400 | bytes 18874368 | tf_op jit(solution)/shard_map/pallas_call | solution.py:614
  306.0 3.4 slice_bitcast_fusion.2
  313.4 16.3 %shard_map.334 = (bf16[2,4,2,80,640]{4,3,2,1,0:T(8,128)(2,1)}, bf16[2,4,2,80,640]{4,3,2,1,0:T(8,128)(2,1)S(1)}, f32[4,640]{1,0:T(4,128)S(1)}, f32[512,640]{1,0:T...) custom-call(s32[3]{0:T(128)S(1)} %pad_add_fusion.place_ref, ...), custom_call_target="tpu_custom_call" | custom-call | flops 6710886400 | bytes 18874368 | tf_op jit(solution)/shard_map/pallas_call | solution.py:614
  332.0 17.1 %shard_map.335 = (bf16[2,2,4,80,640]{4,3,2,1,0:T(8,128)(2,1)}, bf16[2,640,512]{2,1,0:T(8,128)(2,1)S(1)}, bf16[4,512,640]{2,1,0:T(8,128)(2,1)}, f32[512,640]{1,0:...) custom-call(s32[3]{0:T(128)S(1)} %pad_add_fusion.place_ref, s32[4]{0:T(128)S(1)} %copy-done.64, ...), custom_call_target="tpu_custom_call" | custom-call | flops 13421772800 | bytes 18874368 | tf_op jit(solution)/shard_map/pallas_call | solution.py:796
  352.2 3.2 add_convert_fusion.2
  359.0 3.4 shard_map.336
  364.3 2.5 copy-done.2
  366.8 9.0 %shard_map.337 = (bf16[2,4,320,640]{3,2,1,0:T(8,128)(2,1)}, bf16[2,4,320,640]{3,2,1,0:T(8,128)(2,1)S(1)}) custom-call(s32[3]{0:T(128)S(1)} %pad_add_fusion.place_ref, bf16[512,640]{1,0:T(8,128)(2,1)S(1)} %copy-done.83, bf16[8,512,640]{2,1,0:T(8,128)(2,1)S(1)} %copy-done.2), custom_call_target="tpu_custom_call" | custom-call | flops 3355443200 | bytes 13631488 | tf_op jit(solution)/shard_map/pallas_call | solution.py:430
  377.6 2.7 collective-permute-start.40
  380.3 2.5 copy-done.67
  382.8 13.1 %shard_map.338 = (bf16[2,2,4,2,80,640]{5,4,3,2,1,0:T(8,128)(2,1)}, f32[4,640]{1,0:T(4,128)S(1)}, f32[512,640]{1,0:T(8,128)S(1)}) custom-call(s32[3]{0:T(128)S(1)} %pad_add_fusion.place_ref, bf16[512,640]{1,0:T(8,128)(2,1)S(1)} %copy-done.83, bf16[512,640]{1,0:T(8,128)(2,1)S(1)} %copy-done.80, bf16[8,512,640]{2,1,0:T(8,128)(2,1)S(1)} %copy-done.67, ...), custom_call_target="tpu_custom_call" | custom-call | flops 6710886400 | bytes 18874368 | tf_op jit(solution)/shard_map/pallas_call | solution.py:614
  400.0 17.3 %collective-permute-done.40 = bf16[2,4,2,80,640]{4,3,2,1,0:T(8,128)(2,1)} collective-permute-done((bf16[2,4,2,80,640]{4,3,2,1,0:T(8,128)(2,1)}, bf16[2,4,2,80,640]{4,3,2,1,0:T(8,128)(2,1)}, u32[]{:S(2)}, u32[]{:S(2)}) %collective-permute-start.40) | collective-permute-done | bytes 1638432 | tf_op jit(solution)/shard_map/ppermute | solution.py:889
  423.2 11.2 %collective-permute-done.43 = bf16[2,4,80,640]{3,2,1,0:T(8,128)(2,1)S(1)} collective-permute-done((bf16[2,4,80,640]{3,2,1,0:T(8,128)(2,1)S(1)}, bf16[2,4,80,640]{3,2,1,0:T(8,128)(2,1)S(1)}, u32[]{:S(2)}, u32[]{:S(2)}) %collective-permute-start.43) | collective-permute-done | bytes 819232 | tf_op jit(solution)/shard_map/ppermute | solution.py:889
  435.4 3.5 slice_bitcast_fusion
  442.1 16.0 %shard_map.339 = (bf16[2,4,2,80,640]{4,3,2,1,0:T(8,128)(2,1)}, bf16[2,4,2,80,640]{4,3,2,1,0:T(8,128)(2,1)S(1)}, f32[4,640]{1,0:T(4,128)S(1)}, f32[512,640]{1,0:T...) custom-call(s32[3]{0:T(128)S(1)} %pad_add_fusion.place_ref, bf16[512,640]{1,0:T(8,128)(2,1)S(1)} %copy-done.84, ...), custom_call_target="tpu_custom_call" | custom-call | flops 6710886400 | bytes 18874368 | tf_op jit(solution)/shard_map/pallas_call | solution.py:614
  471.9 17.6 %shard_map.340 = (bf16[2,2,4,80,640]{4,3,2,1,0:T(8,128)(2,1)}, bf16[2,640,512]{2,1,0:T(8,128)(2,1)S(1)}, bf16[4,512,640]{2,1,0:T(8,128)(2,1)}, f32[512,640]{1,0:...) custom-call(s32[3]{0:T(128)S(1)} %pad_add_fusion.place_ref, s32[4]{0:T(128)S(1)} %copy-done.64, ...), custom_call_target="tpu_custom_call" | custom-call | flops 13421772800 | bytes 18874368 | tf_op jit(solution)/shard_map/pallas_call | solution.py:796
  496.8 2.2 shard_map.341
  499.0 6.4 collective-permute-done.46
  509.4 3.2 add_convert_fusion
  518.8 2.5 collective-permute-start.51
  521.5 17.7 %collective-permute-done.51 = bf16[2,80,640]{2,1,0:T(8,128)(2,1)} collective-permute-done((bf16[2,80,640]{2,1,0:T(8,128)(2,1)}, bf16[2,80,640]{2,1,0:T(8,128)(2,1)}, u32[]{:S(2)}, u32[]{:S(2)}) %collective-permute-start.51) | collective-permute-done | bytes 204832 | tf_op jit(solution)/shard_map/ppermute | solution.py:933
  541.0 2.5 collective-permute-start.55
  545.8 3.0 collective-permute-start.52
  567.2 13.6 %collective-permute-done.52 = bf16[2,2,80,640]{3,2,1,0:T(8,128)(2,1)} collective-permute-done((bf16[2,2,80,640]{3,2,1,0:T(8,128)(2,1)}, bf16[2,2,80,640]{3,2,1,0:T(8,128)(2,1)}, u32[]{:S(2)}, u32[]{:S(2)}) %collective-permute-start.52) | collective-permute-done | bytes 409632 | tf_op jit(solution)/shard_map/ppermute | solution.py:933
  589.3 6.4 collective-permute-done.63
  614.7 6.3 collective-permute-done.65
  630.2 2.3 gather_fusion.1
  632.6 2.0 fusion.4
  (575 shorter events, 185.8 us)
Async XLA Ops:
  7.2 134.9 %all-gather.3.cloned.1.call-start = ((), (), s32[]{:S(2)}) async-start(), calls=%async_computation.3 | async-start | bytes 3686400 | tf_op jit(solution)/shard_map/all_gather | solution.py:1091
  13.9 10.8 %collective-permute-start.2 = (bf16[2,80,640]{2,1,0:T(8,128)(2,1)S(1)}, bf16[2,80,640]{2,1,0:T(8,128)(2,1)S(1)}, u32[]{:S(2)}, u32[]{:S(2)}) collective-permute-start(bf16[2,80,640]{2,1,0:T(8,128)(2,1)S(1)} %bitcast.295), channel_id=1, source_target_pairs={{0,8},{8,0},{16,24},{24,16},{1,9},{9,1},{17,25},{25,17},{2,10},{10... | collective-permute-start | bytes 614408 | tf_op jit(solution)/shard_map/ppermute | solution.py:933
  15.8 20.4 %collective-permute-start.1 = (bf16[2,1,80,640]{3,2,0,1:T(8,128)(2,1)S(1)}, bf16[2,1,80,640]{3,2,0,1:T(8,128)(2,1)S(1)}, u32[]{:S(2)}, u32[]{:S(2)}) collective-permute-start(bf16[2,1,80,640]{3,2,0,1:T(8,128)(2,1)S(1)} %fusion.27), channel_id=1, source_target_pairs={{0,16},{8,24},{16,0},{24,8},{1,17},{9,25},{17,1},{25,9},{2,18},{10... | collective-permute-start | bytes 614408 | tf_op jit(solution)/shard_map/ppermute | solution.py:933
  25.5 19.4 %collective-permute-start.6 = (bf16[2,2,80,640]{3,2,1,0:T(8,128)(2,1)}, bf16[2,2,80,640]{3,2,1,0:T(8,128)(2,1)}, u32[]{:S(2)}, u32[]{:S(2)}) collective-permute-start(bf16[2,2,80,640]{3,2,1,0:T(8,128)(2,1)} %maximum_select_fusion.4), channel_id=1, source_target_pairs={{0,16},{8,24},{16,0},{24,8},{1,17},{9,25},{17,1},{25,9},{2,18},{10... | collective-permute-start | bytes 1228808 | tf_op jit(solution)/shard_map/ppermute | solution.py:933
  36.3 8.0 %collective-permute-start.3 = (bf16[4,80,640]{2,1,0:T(8,128)(2,1)S(1)}, bf16[4,80,640]{2,1,0:T(8,128)(2,1)S(1)}, u32[]{:S(2)}, u32[]{:S(2)}) collective-permute-start(bf16[4,80,640]{2,1,0:T(8,128)(2,1)S(1)} %bitcast.285), channel_id=1, source_target_pairs={{0,4},{4,0},{1,5},{5,1},{2,6},{6,2},{3,7},{7,3},{8,12},{12,8},{9,1... | collective-permute-start | bytes 1228808 | tf_op jit(solution)/shard_map/ppermute | solution.py:889
  38.5 206.4 %all-gather.5.cloned.1.call-start = ((), (), s32[]{:S(2)}) async-start(), calls=%async_computation.4 | async-start | bytes 3686400 | tf_op jit(solution)/shard_map/all_gather | solution.py:1132
  44.4 21.1 %collective-permute-start.5 = (bf16[2,4,80,640]{3,2,1,0:T(8,128)(2,1)S(1)}, bf16[2,4,80,640]{3,2,1,0:T(8,128)(2,1)S(1)}, u32[]{:S(2)}, u32[]{:S(2)}) collective-permute-start(bf16[2,4,80,640]{3,2,1,0:T(8,128)(2,1)S(1)} %pad_maximum_fusion.w0_ref), channel_id=1, source_target_pairs={{0,2},{2,0},{1,3},{3,1},{4,6},{6,4},{5,7},{7,5},{8,10},{10,8},{9,1... | collective-permute-start | bytes 2457608 | tf_op jit(solution)/shard_map/ppermute | solution.py:889
  47.4 16.0 %collective-permute-start.8 = (bf16[4,80,640]{2,1,0:T(8,128)(2,1)}, bf16[4,80,640]{2,1,0:T(8,128)(2,1)}, u32[]{:S(2)}, u32[]{:S(2)}) collective-permute-start(bf16[4,80,640]{2,1,0:T(8,128)(2,1)} %get-tuple-element.276), channel_id=1, source_target_pairs={{0,4},{4,0},{1,5},{5,1},{2,6},{6,2},{3,7},{7,3},{8,12},{12,8},{9,1... | collective-permute-start | bytes 1228808 | tf_op jit(solution)/shard_map/ppermute | solution.py:889
  48.6 34.1 %collective-permute-start.4 = (bf16[2,4,80,640]{3,2,1,0:T(8,128)(2,1)S(1)}, bf16[2,4,80,640]{3,2,1,0:T(8,128)(2,1)}, u32[]{:S(2)}, u32[]{:S(2)}) collective-permute-start(bf16[2,4,80,640]{3,2,1,0:T(8,128)(2,1)S(1)} %pad_maximum_fusion.w0_ref), channel_id=1, source_target_pairs={{0,1},{1,0},{2,3},{3,2},{4,5},{5,4},{6,7},{7,6},{8,9},{9,8},{10,11... | collective-permute-start | bytes 2457608 | tf_op jit(solution)/shard_map/ppermute | solution.py:889
  48.9 15.8 %collective-permute-start.7 = (bf16[1,80,640]{2,1,0:T(8,128)(2,1)S(1)}, bf16[1,80,640]{2,1,0:T(8,128)(2,1)S(1)}, u32[]{:S(2)}, u32[]{:S(2)}) collective-permute-start(bf16[1,80,640]{2,1,0:T(8,128)(2,1)S(1)} %reshape_transpose_reshape.7), channel_id=1, source_target_pairs={{0,8},{8,0},{16,24},{24,16},{1,9},{9,1},{17,25},{25,17},{2,10},{10... | collective-permute-start | bytes 307208 | tf_op jit(solution)/shard_map/ppermute | solution.py:933
  65.4 17.3 %collective-permute-start.9 = (bf16[2,4,80,640]{3,2,1,0:T(8,128)(2,1)S(1)}, bf16[2,4,80,640]{3,2,1,0:T(8,128)(2,1)}, u32[]{:S(2)}, u32[]{:S(2)}) collective-permute-start(bf16[2,4,80,640]{3,2,1,0:T(8,128)(2,1)S(1)} %collective-permute-done.5.w2_ref), channel_id=1, source_target_pairs={{0,1},{1,0},{2,3},{3,2},{4,5},{5,4},{6,7},{7,6},{8,9},{9,8},{10,11... | collective-permute-start | bytes 2457608 | tf_op jit(solution)/shard_map/ppermute | solution.py:889
  65.5 13.9 %collective-permute-start.11 = (bf16[4,80,640]{2,1,0:T(8,128)(2,1)S(1)}, bf16[4,80,640]{2,1,0:T(8,128)(2,1)S(1)}, u32[]{:S(2)}, u32[]{:S(2)}) collective-permute-start(bf16[4,80,640]{2,1,0:T(8,128)(2,1)S(1)} %get-tuple-element.281), channel_id=1, source_target_pairs={{0,4},{4,0},{1,5},{5,1},{2,6},{6,2},{3,7},{7,3},{8,12},{12,8},{9,1... | collective-permute-start | bytes 1228808 | tf_op jit(solution)/shard_map/ppermute | solution.py:889
  67.6 15.0 %collective-permute-start.10 = (bf16[2,80,640]{2,1,0:T(8,128)(2,1)S(1)}, bf16[2,80,640]{2,1,0:T(8,128)(2,1)S(1)}, u32[]{:S(2)}, u32[]{:S(2)}) collective-permute-start(bf16[2,80,640]{2,1,0:T(8,128)(2,1)S(1)} %bitcast.297), channel_id=1, source_target_pairs={{0,8},{8,0},{16,24},{24,16},{1,9},{9,1},{17,25},{25,17},{2,10},{10... | collective-permute-start | bytes 614408 | tf_op jit(solution)/shard_map/ppermute | solution.py:933
  67.6 29.4 %collective-permute-start.15 = (bf16[2,1,80,640]{3,2,0,1:T(8,128)(2,1)}, bf16[2,1,80,640]{3,2,0,1:T(8,128)(2,1)S(1)}, u32[]{:S(2)}, u32[]{:S(2)}) collective-permute-start(bf16[2,1,80,640]{3,2,0,1:T(8,128)(2,1)} %maximum_select_fusion.8), channel_id=1, source_target_pairs={{0,16},{8,24},{16,0},{24,8},{1,17},{9,25},{17,1},{25,9},{2,18},{10... | collective-permute-start | bytes 614408 | tf_op jit(solution)/shard_map/ppermute | solution.py:933
  79.3 21.8 %collective-permute-start.14 = (bf16[2,4,80,640]{3,2,1,0:T(8,128)(2,1)S(1)}, bf16[2,4,80,640]{3,2,1,0:T(8,128)(2,1)}, u32[]{:S(2)}, u32[]{:S(2)}) collective-permute-start(bf16[2,4,80,640]{3,2,1,0:T(8,128)(2,1)S(1)} %pad_maximum_fusion.1.refs_0_.u0_ref), channel_id=1, source_target_pairs={{0,2},{2,0},{1,3},{3,1},{4,6},{6,4},{5,7},{7,5},{8,10},{10,8},{9,1... | collective-permute-start | bytes 2457608 | tf_op jit(solution)/shard_map/ppermute | solution.py:889
  98.7 9.9 %collective-permute-start.18 = (bf16[4,80,640]{2,1,0:T(8,128)(2,1)S(1)}, bf16[4,80,640]{2,1,0:T(8,128)(2,1)S(1)}, u32[]{:S(2)}, u32[]{:S(2)}) collective-permute-start(bf16[4,80,640]{2,1,0:T(8,128)(2,1)S(1)} %bitcast.287), channel_id=1, source_target_pairs={{0,4},{4,0},{1,5},{5,1},{2,6},{6,2},{3,7},{7,3},{8,12},{12,8},{9,1... | collective-permute-start | bytes 1228808 | tf_op jit(solution)/shard_map/ppermute | solution.py:889
  100.3 25.4 %collective-permute-start.16 = (bf16[2,4,80,640]{3,2,1,0:T(8,128)(2,1)S(1)}, bf16[2,4,80,640]{3,2,1,0:T(8,128)(2,1)S(1)}, u32[]{:S(2)}, u32[]{:S(2)}) collective-permute-start(bf16[2,4,80,640]{3,2,1,0:T(8,128)(2,1)S(1)} %pad_maximum_fusion.2.refs_1_.u1_ref), channel_id=1, source_target_pairs={{0,2},{2,0},{1,3},{3,1},{4,6},{6,4},{5,7},{7,5},{8,10},{10,8},{9,1... | collective-permute-start | bytes 2457608 | tf_op jit(solution)/shard_map/ppermute | solution.py:889
  101.1 23.4 %collective-permute-start.17 = (bf16[2,2,80,640]{3,2,1,0:T(8,128)(2,1)S(1)}, bf16[2,2,80,640]{3,2,1,0:T(8,128)(2,1)S(1)}, u32[]{:S(2)}, u32[]{:S(2)}) collective-permute-start(bf16[2,2,80,640]{3,2,1,0:T(8,128)(2,1)S(1)} %maximum_select_fusion.6), channel_id=1, source_target_pairs={{0,16},{8,24},{16,0},{24,8},{1,17},{9,25},{17,1},{25,9},{2,18},{10... | collective-permute-start | bytes 1228808 | tf_op jit(solution)/shard_map/ppermute | solution.py:933
  101.1 24.8 %collective-permute-start.13 = (bf16[2,4,80,640]{3,2,1,0:T(8,128)(2,1)S(1)}, bf16[2,4,80,640]{3,2,1,0:T(8,128)(2,1)}, u32[]{:S(2)}, u32[]{:S(2)}) collective-permute-start(bf16[2,4,80,640]{3,2,1,0:T(8,128)(2,1)S(1)} %pad_maximum_fusion.2.refs_1_.u1_ref), channel_id=1, source_target_pairs={{0,1},{1,0},{2,3},{3,2},{4,5},{5,4},{6,7},{7,6},{8,9},{9,8},{10,11... | collective-permute-start | bytes 2457608 | tf_op jit(solution)/shard_map/ppermute | solution.py:889
  101.1 24.8 %collective-permute-start.12 = (bf16[2,4,80,640]{3,2,1,0:T(8,128)(2,1)S(1)}, bf16[2,4,80,640]{3,2,1,0:T(8,128)(2,1)}, u32[]{:S(2)}, u32[]{:S(2)}) collective-permute-start(bf16[2,4,80,640]{3,2,1,0:T(8,128)(2,1)S(1)} %pad_maximum_fusion.1.refs_0_.u0_ref), channel_id=1, source_target_pairs={{0,1},{1,0},{2,3},{3,2},{4,5},{5,4},{6,7},{7,6},{8,9},{9,8},{10,11... | collective-permute-start | bytes 2457608 | tf_op jit(solution)/shard_map/ppermute | solution.py:889
  108.6 17.4 %collective-permute-start.19 = (bf16[2,4,80,640]{3,2,1,0:T(8,128)(2,1)}, bf16[2,4,80,640]{3,2,1,0:T(8,128)(2,1)}, u32[]{:S(2)}, u32[]{:S(2)}) collective-permute-start(bf16[2,4,80,640]{3,2,1,0:T(8,128)(2,1)} %collective-permute-done.14.refs_4_.u2_ref), channel_id=1, source_target_pairs={{0,1},{1,0},{2,3},{3,2},{4,5},{5,4},{6,7},{7,6},{8,9},{9,8},{10,11... | collective-permute-start | bytes 2457608 | tf_op jit(solution)/shard_map/ppermute | solution.py:889
  142.0 30.1 %collective-permute-start.21 = (bf16[8,320,640]{2,1,0:T(8,128)(2,1)}, bf16[8,320,640]{2,1,0:T(8,128)(2,1)}, u32[]{:S(2)}, u32[]{:S(2)}) collective-permute-start(bf16[8,320,640]{2,1,0:T(8,128)(2,1)} %all-gather.3.cloned.1.call-done.d0_ref), channel_id=1, source_target_pairs={{0,1},{1,0},{2,3},{3,2},{4,5},{5,4},{6,7},{7,6},{8,9},{9,8},{10,11... | collective-permute-start | bytes 9830408 | tf_op jit(solution)/shard_map/ppermute | solution.py:889
  145.2 319.9 %reduce-scatter.4.cloned.1.call-start = ((), (), s32[]{:S(2)}) async-start(), calls=%async_computation.5 | async-start | bytes 2048000 | tf_op jit(solution)/shard_map/reduce_scatter | solution.py:1008
  145.5 14.6 %collective-permute-start.23 = (bf16[4,80,640]{2,1,0:T(8,128)(2,1)S(1)}, bf16[4,80,640]{2,1,0:T(8,128)(2,1)S(1)}, u32[]{:S(2)}, u32[]{:S(2)}) collective-permute-start(bf16[4,80,640]{2,1,0:T(8,128)(2,1)S(1)} %copy-done.121), channel_id=1, source_target_pairs={{0,4},{4,0},{1,5},{5,1},{2,6},{6,2},{3,7},{7,3},{8,12},{12,8},{9,1... | collective-permute-start | bytes 1228808 | tf_op jit(solution)/shard_map/ppermute | solution.py:889
  146.3 23.8 %collective-permute-start.22 = (bf16[4,80,640]{2,1,0:T(8,128)(2,1)}, bf16[4,80,640]{2,1,0:T(8,128)(2,1)S(1)}, u32[]{:S(2)}, u32[]{:S(2)}) collective-permute-start(bf16[4,80,640]{2,1,0:T(8,128)(2,1)} %get-tuple-element.316), channel_id=1, source_target_pairs={{0,4},{4,0},{1,5},{5,1},{2,6},{6,2},{3,7},{7,3},{8,12},{12,8},{9,1... | collective-permute-start | bytes 1228808 | tf_op jit(solution)/shard_map/ppermute | solution.py:889
  147.6 38.9 %collective-permute-start.25 = (bf16[2,4,80,640]{3,2,1,0:T(8,128)(2,1)}, bf16[2,4,80,640]{3,2,1,0:T(8,128)(2,1)S(1)}, u32[]{:S(2)}, u32[]{:S(2)}) collective-permute-start(bf16[2,4,80,640]{3,2,1,0:T(8,128)(2,1)} %pad_maximum_fusion.3.w0_ref), channel_id=1, source_target_pairs={{0,2},{2,0},{1,3},{3,1},{4,6},{6,4},{5,7},{7,5},{8,10},{10,8},{9,1... | collective-permute-start | bytes 2457608 | tf_op jit(solution)/shard_map/ppermute | solution.py:889
  149.9 39.4 %collective-permute-start.24 = (bf16[2,4,80,640]{3,2,1,0:T(8,128)(2,1)}, bf16[2,4,80,640]{3,2,1,0:T(8,128)(2,1)S(1)}, u32[]{:S(2)}, u32[]{:S(2)}) collective-permute-start(bf16[2,4,80,640]{3,2,1,0:T(8,128)(2,1)} %pad_maximum_fusion.3.w0_ref), channel_id=1, source_target_pairs={{0,1},{1,0},{2,3},{3,2},{4,5},{5,4},{6,7},{7,6},{8,9},{9,8},{10,11... | collective-permute-start | bytes 2457608 | tf_op jit(solution)/shard_map/ppermute | solution.py:889
  186.6 21.8 %collective-permute-start.30 = (bf16[2,4,80,640]{3,2,1,0:T(8,128)(2,1)}, bf16[2,4,80,640]{3,2,1,0:T(8,128)(2,1)}, u32[]{:S(2)}, u32[]{:S(2)}) collective-permute-start(bf16[2,4,80,640]{3,2,1,0:T(8,128)(2,1)} %pad_maximum_fusion.5.refs_1_.u1_ref), channel_id=1, source_target_pairs={{0,2},{2,0},{1,3},{3,1},{4,6},{6,4},{5,7},{7,5},{8,10},{10,8},{9,1... | collective-permute-start | bytes 2457608 | tf_op jit(solution)/shard_map/ppermute | solution.py:889
  189.1 36.7 %collective-permute-start.29 = (bf16[2,4,80,640]{3,2,1,0:T(8,128)(2,1)}, bf16[2,4,80,640]{3,2,1,0:T(8,128)(2,1)}, u32[]{:S(2)}, u32[]{:S(2)}) collective-permute-start(bf16[2,4,80,640]{3,2,1,0:T(8,128)(2,1)} %pad_maximum_fusion.4.refs_0_.u0_ref), channel_id=1, source_target_pairs={{0,2},{2,0},{1,3},{3,1},{4,6},{6,4},{5,7},{7,5},{8,10},{10,8},{9,1... | collective-permute-start | bytes 2457608 | tf_op jit(solution)/shard_map/ppermute | solution.py:889
  189.2 37.1 %collective-permute-start.28 = (bf16[2,4,80,640]{3,2,1,0:T(8,128)(2,1)}, bf16[2,4,80,640]{3,2,1,0:T(8,128)(2,1)}, u32[]{:S(2)}, u32[]{:S(2)}) collective-permute-start(bf16[2,4,80,640]{3,2,1,0:T(8,128)(2,1)} %pad_maximum_fusion.5.refs_1_.u1_ref), channel_id=1, source_target_pairs={{0,1},{1,0},{2,3},{3,2},{4,5},{5,4},{6,7},{7,6},{8,9},{9,8},{10,11... | collective-permute-start | bytes 2457608 | tf_op jit(solution)/shard_map/ppermute | solution.py:889
  189.3 37.0 %collective-permute-start.27 = (bf16[2,4,80,640]{3,2,1,0:T(8,128)(2,1)}, bf16[2,4,80,640]{3,2,1,0:T(8,128)(2,1)}, u32[]{:S(2)}, u32[]{:S(2)}) collective-permute-start(bf16[2,4,80,640]{3,2,1,0:T(8,128)(2,1)} %pad_maximum_fusion.4.refs_0_.u0_ref), channel_id=1, source_target_pairs={{0,1},{1,0},{2,3},{3,2},{4,5},{5,4},{6,7},{7,6},{8,9},{9,8},{10,11... | collective-permute-start | bytes 2457608 | tf_op jit(solution)/shard_map/ppermute | solution.py:889
  291.0 15.0 %collective-permute-start.35 = (bf16[2,4,320,640]{3,2,1,0:T(8,128)(2,1)S(1)}, bf16[2,4,320,640]{3,2,1,0:T(8,128)(2,1)}, u32[]{:S(2)}, u32[]{:S(2)}) collective-permute-start(bf16[2,4,320,640]{3,2,1,0:T(8,128)(2,1)S(1)} %get-tuple-element.361), channel_id=1, source_target_pairs={{0,1},{1,0},{2,3},{3,2},{4,5},{5,4},{6,7},{7,6},{8,9},{9,8},{10,11... | collective-permute-start | bytes 9830408 | tf_op jit(solution)/shard_map/ppermute | solution.py:889
  304.4 7.2 %collective-permute-start.34 = (bf16[2,2,4,2,80,640]{5,4,3,2,1,0:T(8,128)(2,1)S(1)}, bf16[2,2,4,2,80,640]{5,4,3,2,1,0:T(8,128)(2,1)S(1)}, u32[]{:S(2)}, u32[]{:S(2)}) collective-permute-start(bf16[2,2,4,2,80,640]{5,4,3,2,1,0:T(8,128)(2,1)S(1)} %get-tuple-element.366), channel_id=1, source_target_pairs={{0,1},{1,0},{2,3},{3,2},{4,5},{5,4},{6,7},{7,6},{8,9},{9,8},{10,11... | collective-permute-start | bytes 9830408 | tf_op jit(solution)/shard_map/ppermute | solution.py:889
  311.0 41.2 %collective-permute-start.37 = (bf16[4,320,640]{2,1,0:T(8,128)(2,1)}, bf16[4,320,640]{2,1,0:T(8,128)(2,1)}, u32[]{:S(2)}, u32[]{:S(2)}) collective-permute-start(bf16[4,320,640]{2,1,0:T(8,128)(2,1)} %add_convert_fusion.3), channel_id=1, source_target_pairs={{0,4},{4,0},{1,5},{5,1},{2,6},{6,2},{3,7},{7,3},{8,12},{12,8},{9,1... | collective-permute-start | bytes 4915208 | tf_op jit(solution)/shard_map/ppermute | solution.py:889
  377.5 57.9 %collective-permute-start.39 = (bf16[2,4,320,640]{3,2,1,0:T(8,128)(2,1)}, bf16[2,4,320,640]{3,2,1,0:T(8,128)(2,1)}, u32[]{:S(2)}, u32[]{:S(2)}) collective-permute-start(bf16[2,4,320,640]{3,2,1,0:T(8,128)(2,1)} %get-tuple-element.393), channel_id=1, source_target_pairs={{0,1},{1,0},{2,3},{3,2},{4,5},{5,4},{6,7},{7,6},{8,9},{9,8},{10,11... | collective-permute-start | bytes 9830408 | tf_op jit(solution)/shard_map/ppermute | solution.py:889
  377.6 39.7 %collective-permute-start.40 = (bf16[2,4,2,80,640]{4,3,2,1,0:T(8,128)(2,1)}, bf16[2,4,2,80,640]{4,3,2,1,0:T(8,128)(2,1)}, u32[]{:S(2)}, u32[]{:S(2)}) collective-permute-start(bf16[2,4,2,80,640]{4,3,2,1,0:T(8,128)(2,1)} %get-tuple-element.376), channel_id=1, source_target_pairs={{0,2},{2,0},{1,3},{3,1},{4,6},{6,4},{5,7},{7,5},{8,10},{10,8},{9,1... | collective-permute-start | bytes 4915208 | tf_op jit(solution)/shard_map/ppermute | solution.py:889
  397.0 45.1 %collective-permute-start.38 = (bf16[2,2,4,2,80,640]{5,4,3,2,1,0:T(8,128)(2,1)}, bf16[2,2,4,2,80,640]{5,4,3,2,1,0:T(8,128)(2,1)}, u32[]{:S(2)}, u32[]{:S(2)}) collective-permute-start(bf16[2,2,4,2,80,640]{5,4,3,2,1,0:T(8,128)(2,1)} %get-tuple-element.398), channel_id=1, source_target_pairs={{0,1},{1,0},{2,3},{3,2},{4,5},{5,4},{6,7},{7,6},{8,9},{9,8},{10,11... | collective-permute-start | bytes 9830408 | tf_op jit(solution)/shard_map/ppermute | solution.py:889
  397.7 155.2 %reduce-scatter.6.cloned.1.call-start = ((), (), s32[]{:S(2)}) async-start(), calls=%async_computation.6 | async-start | bytes 1024000 | tf_op jit(solution)/shard_map/reduce_scatter | solution.py:1008
  399.6 34.8 %collective-permute-start.43 = (bf16[2,4,80,640]{3,2,1,0:T(8,128)(2,1)S(1)}, bf16[2,4,80,640]{3,2,1,0:T(8,128)(2,1)S(1)}, u32[]{:S(2)}, u32[]{:S(2)}) collective-permute-start(bf16[2,4,80,640]{3,2,1,0:T(8,128)(2,1)S(1)} %copy-done.60), channel_id=1, source_target_pairs={{0,2},{2,0},{1,3},{3,1},{4,6},{6,4},{5,7},{7,5},{8,10},{10,8},{9,1... | collective-permute-start | bytes 2457608 | tf_op jit(solution)/shard_map/ppermute | solution.py:889
  419.1 43.9 %collective-permute-start.44 = (bf16[4,2,80,640]{3,2,1,0:T(8,128)(2,1)S(1)}, bf16[4,2,80,640]{3,2,1,0:T(8,128)(2,1)S(1)}, u32[]{:S(2)}, u32[]{:S(2)}) collective-permute-start(bf16[4,2,80,640]{3,2,1,0:T(8,128)(2,1)S(1)} %add_convert_fusion.6), channel_id=1, source_target_pairs={{0,4},{4,0},{1,5},{5,1},{2,6},{6,2},{3,7},{7,3},{8,12},{12,8},{9,1... | collective-permute-start | bytes 2457608 | tf_op jit(solution)/shard_map/ppermute | solution.py:889
  440.5 68.8 %collective-permute-start.42 = (bf16[4,320,640]{2,1,0:T(8,128)(2,1)}, bf16[4,320,640]{2,1,0:T(8,128)(2,1)}, u32[]{:S(2)}, u32[]{:S(2)}) collective-permute-start(bf16[4,320,640]{2,1,0:T(8,128)(2,1)} %add_convert_fusion.1), channel_id=1, source_target_pairs={{0,4},{4,0},{1,5},{5,1},{2,6},{6,2},{3,7},{7,3},{8,12},{12,8},{9,1... | collective-permute-start | bytes 4915208 | tf_op jit(solution)/shard_map/ppermute | solution.py:889
  461.2 51.4 %collective-permute-start.41 = (bf16[2,4,2,80,640]{4,3,2,1,0:T(8,128)(2,1)}, bf16[2,4,2,80,640]{4,3,2,1,0:T(8,128)(2,1)}, u32[]{:S(2)}, u32[]{:S(2)}) collective-permute-start(bf16[2,4,2,80,640]{4,3,2,1,0:T(8,128)(2,1)} %get-tuple-element.417), channel_id=1, source_target_pairs={{0,2},{2,0},{1,3},{3,1},{4,6},{6,4},{5,7},{7,5},{8,10},{10,8},{9,1... | collective-permute-start | bytes 4915208 | tf_op jit(solution)/shard_map/ppermute | solution.py:889
  464.2 120.0 %reduce-scatter.8.cloned.1.call-start = ((), (), s32[]{:S(2)}) async-start(), calls=%async_computation.7 | async-start | bytes 2048000 | tf_op jit(solution)/shard_map/reduce_scatter | solution.py:1008
  465.2 42.4 %collective-permute-start.45 = (bf16[320,640]{1,0:T(8,128)(2,1)}, bf16[320,640]{1,0:T(8,128)(2,1)}, u32[]{:S(2)}, u32[]{:S(2)}) collective-permute-start(bf16[320,640]{1,0:T(8,128)(2,1)} %bitcast.304), channel_id=1, source_target_pairs={{0,2},{2,0},{1,3},{3,1},{4,6},{6,4},{5,7},{7,5},{8,10},{10,8},{9,1... | collective-permute-start | bytes 1228808 | tf_op jit(solution)/shard_map/ppermute | solution.py:889
  492.3 13.1 %collective-permute-start.46 = (f32[88,640]{1,0:T(8,128)S(1)}, f32[88,640]{1,0:T(8,128)S(1)}, u32[]{:S(2)}, u32[]{:S(2)}) collective-permute-start(f32[88,640]{1,0:T(8,128)S(1)} %constant_dynamic-update-slice_fusion), channel_id=1, source_target_pairs={{0,16},{8,24},{16,0},{24,8},{1,17},{9,25},{17,1},{25,9},{2,18},{10... | collective-permute-start | bytes 675848 | tf_op jit(solution)/shard_map/ppermute | solution.py:933
  494.3 22.5 %collective-permute-start.49 = (bf16[4,80,640]{2,1,0:T(8,128)(2,1)}, bf16[4,80,640]{2,1,0:T(8,128)(2,1)}, u32[]{:S(2)}, u32[]{:S(2)}) collective-permute-start(bf16[4,80,640]{2,1,0:T(8,128)(2,1)} %add_convert_fusion.10), channel_id=1, source_target_pairs={{0,4},{4,0},{1,5},{5,1},{2,6},{6,2},{3,7},{7,3},{8,12},{12,8},{9,1... | collective-permute-start | bytes 1228808 | tf_op jit(solution)/shard_map/ppermute | solution.py:889
  505.5 43.4 %collective-permute-start.57 = (bf16[2,4,80,640]{3,2,1,0:T(8,128)(2,1)S(1)}, bf16[2,4,80,640]{3,2,1,0:T(8,128)(2,1)}, u32[]{:S(2)}, u32[]{:S(2)}) collective-permute-start(bf16[2,4,80,640]{3,2,1,0:T(8,128)(2,1)S(1)} %get-tuple-element.449), channel_id=1, source_target_pairs={{0,2},{2,0},{1,3},{3,1},{4,6},{6,4},{5,7},{7,5},{8,10},{10,8},{9,1... | collective-permute-start | bytes 2457608 | tf_op jit(solution)/shard_map/ppermute | solution.py:889
  507.5 9.3 %collective-permute-start.50 = (f32[88,640]{1,0:T(8,128)S(1)}, f32[88,640]{1,0:T(8,128)S(1)}, u32[]{:S(2)}, u32[]{:S(2)}) collective-permute-start(f32[88,640]{1,0:T(8,128)S(1)} %add.194), channel_id=1, source_target_pairs={{0,8},{8,0},{16,24},{24,16},{1,9},{9,1},{17,25},{25,17},{2,10},{10... | collective-permute-start | bytes 675848 | tf_op jit(solution)/shard_map/ppermute | solution.py:933
  509.4 44.5 %collective-permute-start.68 = (bf16[320,640]{1,0:T(8,128)(2,1)}, bf16[320,640]{1,0:T(8,128)(2,1)}, u32[]{:S(2)}, u32[]{:S(2)}) collective-permute-start(bf16[320,640]{1,0:T(8,128)(2,1)} %add_convert_fusion.9), channel_id=1, source_target_pairs={{0,1},{1,0},{2,3},{3,2},{4,5},{5,4},{6,7},{7,6},{8,9},{9,8},{10,11... | collective-permute-start | bytes 1228808 | tf_op jit(solution)/shard_map/ppermute | solution.py:889
  515.4 28.1 %collective-permute-start.48 = (bf16[4,2,80,640]{3,2,1,0:T(8,128)(2,1)}, bf16[4,2,80,640]{3,2,1,0:T(8,128)(2,1)}, u32[]{:S(2)}, u32[]{:S(2)}) collective-permute-start(bf16[4,2,80,640]{3,2,1,0:T(8,128)(2,1)} %add_convert_fusion.4), channel_id=1, source_target_pairs={{0,4},{4,0},{1,5},{5,1},{2,6},{6,2},{3,7},{7,3},{8,12},{12,8},{9,1... | collective-permute-start | bytes 2457608 | tf_op jit(solution)/shard_map/ppermute | solution.py:889
  518.8 20.4 %collective-permute-start.51 = (bf16[2,80,640]{2,1,0:T(8,128)(2,1)}, bf16[2,80,640]{2,1,0:T(8,128)(2,1)}, u32[]{:S(2)}, u32[]{:S(2)}) collective-permute-start(bf16[2,80,640]{2,1,0:T(8,128)(2,1)} %get-tuple-element.615), channel_id=1, source_target_pairs={{0,16},{8,24},{16,0},{24,8},{1,17},{9,25},{17,1},{25,9},{2,18},{10... | collective-permute-start | bytes 614408 | tf_op jit(solution)/shard_map/ppermute | solution.py:933
  521.4 19.6 %collective-permute-start.54 = (f32[88,640]{1,0:T(8,128)S(1)}, f32[88,640]{1,0:T(8,128)S(1)}, u32[]{:S(2)}, u32[]{:S(2)}) collective-permute-start(f32[88,640]{1,0:T(8,128)S(1)} %add.199), channel_id=1, source_target_pairs={{0,1},{1,0},{2,3},{3,2},{4,5},{5,4},{6,7},{7,6},{8,9},{9,8},{10,11... | collective-permute-start | bytes 675848 | tf_op jit(solution)/shard_map/ppermute | solution.py:889
  541.0 12.0 %collective-permute-start.53 = (bf16[80,640]{1,0:T(8,128)(2,1)}, bf16[80,640]{1,0:T(8,128)(2,1)}, u32[]{:S(2)}, u32[]{:S(2)}) collective-permute-start(bf16[80,640]{1,0:T(8,128)(2,1)} %get-tuple-element.636), channel_id=1, source_target_pairs={{0,8},{8,0},{16,24},{24,16},{1,9},{9,1},{17,25},{25,17},{2,10},{10... | collective-permute-start | bytes 307208 | tf_op jit(solution)/shard_map/ppermute | solution.py:933
  541.0 7.8 %collective-permute-start.55 = (f32[88,640]{1,0:T(8,128)S(1)}, f32[88,640]{1,0:T(8,128)S(1)}, u32[]{:S(2)}, u32[]{:S(2)}) collective-permute-start(f32[88,640]{1,0:T(8,128)S(1)} %add.209), channel_id=1, source_target_pairs={{0,2},{2,0},{1,3},{3,1},{4,6},{6,4},{5,7},{7,5},{8,10},{10,8},{9,1... | collective-permute-start | bytes 675848 | tf_op jit(solution)/shard_map/ppermute | solution.py:889
  545.8 35.1 %collective-permute-start.52 = (bf16[2,2,80,640]{3,2,1,0:T(8,128)(2,1)}, bf16[2,2,80,640]{3,2,1,0:T(8,128)(2,1)}, u32[]{:S(2)}, u32[]{:S(2)}) collective-permute-start(bf16[2,2,80,640]{3,2,1,0:T(8,128)(2,1)} %get-tuple-element.596), channel_id=1, source_target_pairs={{0,16},{8,24},{16,0},{24,8},{1,17},{9,25},{17,1},{25,9},{2,18},{10... | collective-permute-start | bytes 1228808 | tf_op jit(solution)/shard_map/ppermute | solution.py:933
  550.9 12.4 %collective-permute-start.58 = (bf16[4,80,640]{2,1,0:T(8,128)(2,1)}, bf16[4,80,640]{2,1,0:T(8,128)(2,1)S(1)}, u32[]{:S(2)}, u32[]{:S(2)}) collective-permute-start(bf16[4,80,640]{2,1,0:T(8,128)(2,1)} %add_convert_fusion.8), channel_id=1, source_target_pairs={{0,4},{4,0},{1,5},{5,1},{2,6},{6,2},{3,7},{7,3},{8,12},{12,8},{9,1... | collective-permute-start | bytes 1228808 | tf_op jit(solution)/shard_map/ppermute | solution.py:889
  554.8 10.7 %collective-permute-start.56 = (bf16[3,80,640]{2,1,0:T(8,128)(2,1)S(1)}, bf16[3,80,640]{2,1,0:T(8,128)(2,1)S(1)}, u32[]{:S(2)}, u32[]{:S(2)}) collective-permute-start(bf16[3,80,640]{2,1,0:T(8,128)(2,1)S(1)} %pad_maximum_fusion.8), channel_id=1, source_target_pairs={{0,1},{1,0},{2,3},{3,2},{4,5},{5,4},{6,7},{7,6},{8,9},{9,8},{10,11... | collective-permute-start | bytes 921608 | tf_op jit(solution)/shard_map/ppermute | solution.py:889
  563.5 20.7 %collective-permute-start.60 = (bf16[2,80,640]{2,1,0:T(8,128)(2,1)S(1)}, bf16[2,80,640]{2,1,0:T(8,128)(2,1)S(1)}, u32[]{:S(2)}, u32[]{:S(2)}) collective-permute-start(bf16[2,80,640]{2,1,0:T(8,128)(2,1)S(1)} %get-tuple-element.612), channel_id=1, source_target_pairs={{0,16},{8,24},{16,0},{24,8},{1,17},{9,25},{17,1},{25,9},{2,18},{10... | collective-permute-start | bytes 614408 | tf_op jit(solution)/shard_map/ppermute | solution.py:933
  565.6 23.0 %collective-permute-start.66 = (bf16[2,3,80,640]{3,2,1,0:T(8,128)(2,1)S(1)}, bf16[2,3,80,640]{3,2,1,0:T(8,128)(2,1)S(1)}, u32[]{:S(2)}, u32[]{:S(2)}) collective-permute-start(bf16[2,3,80,640]{3,2,1,0:T(8,128)(2,1)S(1)} %pad_maximum_fusion.6), channel_id=1, source_target_pairs={{0,2},{2,0},{1,3},{3,1},{4,6},{6,4},{5,7},{7,5},{8,10},{10,8},{9,1... | collective-permute-start | bytes 1843208 | tf_op jit(solution)/shard_map/ppermute | solution.py:889
  582.6 14.9 %collective-permute-start.59 = (bf16[2,80,640]{2,1,0:T(8,128)(2,1)}, bf16[2,80,640]{2,1,0:T(8,128)(2,1)S(1)}, u32[]{:S(2)}, u32[]{:S(2)}) collective-permute-start(bf16[2,80,640]{2,1,0:T(8,128)(2,1)} %get-tuple-element.613), channel_id=1, source_target_pairs={{0,8},{8,0},{16,24},{24,16},{1,9},{9,1},{17,25},{25,17},{2,10},{10... | collective-permute-start | bytes 614408 | tf_op jit(solution)/shard_map/ppermute | solution.py:933
  584.9 10.8 %collective-permute-start.63 = (bf16[320,640]{1,0:T(8,128)(2,1)}, bf16[320,640]{1,0:T(8,128)(2,1)}, u32[]{:S(2)}, u32[]{:S(2)}) collective-permute-start(bf16[320,640]{1,0:T(8,128)(2,1)} %bitcast.302), channel_id=1, source_target_pairs={{0,2},{2,0},{1,3},{3,1},{4,6},{6,4},{5,7},{7,5},{8,10},{10,8},{9,1... | collective-permute-start | bytes 1228808 | tf_op jit(solution)/shard_map/ppermute | solution.py:889
  588.1 9.4 %collective-permute-start.62 = (bf16[80,640]{1,0:T(8,128)(2,1)}, bf16[80,640]{1,0:T(8,128)(2,1)S(1)}, u32[]{:S(2)}, u32[]{:S(2)}) collective-permute-start(bf16[80,640]{1,0:T(8,128)(2,1)} %get-tuple-element.634), channel_id=1, source_target_pairs={{0,8},{8,0},{16,24},{24,16},{1,9},{9,1},{17,25},{25,17},{2,10},{10... | collective-permute-start | bytes 307208 | tf_op jit(solution)/shard_map/ppermute | solution.py:933
  600.5 6.9 %collective-permute-start.67 = (bf16[320,640]{1,0:T(8,128)(2,1)}, bf16[320,640]{1,0:T(8,128)(2,1)S(1)}, u32[]{:S(2)}, u32[]{:S(2)}) collective-permute-start(bf16[320,640]{1,0:T(8,128)(2,1)} %add_convert_fusion.7), channel_id=1, source_target_pairs={{0,1},{1,0},{2,3},{3,2},{4,5},{5,4},{6,7},{7,6},{8,9},{9,8},{10,11... | collective-permute-start | bytes 1228808 | tf_op jit(solution)/shard_map/ppermute | solution.py:889
  604.9 16.1 %collective-permute-start.65 = (bf16[2,3,80,640]{3,2,1,0:T(8,128)(2,1)}, bf16[2,3,80,640]{3,2,1,0:T(8,128)(2,1)}, u32[]{:S(2)}, u32[]{:S(2)}) collective-permute-start(bf16[2,3,80,640]{3,2,1,0:T(8,128)(2,1)} %pad_maximum_fusion.7), channel_id=1, source_target_pairs={{0,2},{2,0},{1,3},{3,1},{4,6},{6,4},{5,7},{7,5},{8,10},{10,8},{9,1... | collective-permute-start | bytes 1843208 | tf_op jit(solution)/shard_map/ppermute | solution.py:889
  (152 other events, 1425.3 us)
Sparse Core Ops, SparseCore 0:
  38.6 80.2 all-gather.2
  145.4 64.2 all-gather.4
  397.9 35.0 reduce-scatter.3
  464.3 21.8 reduce-scatter.5
  521.5 45.1 reduce-scatter.7

commit v3 on v2

--- a/solution.py
+++ b/solution.py
@@ -217,10 +217,8 @@
             pltpu.VMEM((ROWS, D), BF),
             pltpu.SemaphoreType.DMA((8,)),
         ],
-        compiler_params=pltpu.CompilerParams(vmem_limit_bytes=26 * MIB),
-        cost_estimate=pl.CostEstimate(
-            flops=2 * ROWS * D * 4 * D * 4, bytes_accessed=10 * MIB, transcendentals=0
-        ),
+        compiler_params=pltpu.CompilerParams(vmem_limit_bytes=60 * MIB),
+        cost_estimate=pl.CostEstimate(flops=int((2 * ROWS * D * 4 * D * 4) * 0.1), bytes_accessed=int((10 * MIB) * 0.1), transcendentals=0),
     )(place, lengths, residual, *quarters, gains, biases)
 
 
@@ -265,10 +263,8 @@
             pltpu.VMEM((TILES, 4, 2, D // 8, TILE), BF),
             pltpu.SemaphoreType.DMA((TILES, 2)),
         ],
-        compiler_params=pltpu.CompilerParams(vmem_limit_bytes=26 * MIB),
-        cost_estimate=pl.CostEstimate(
-            flops=2 * ROWS * D * FF * 4, bytes_accessed=20 * MIB, transcendentals=0
-        ),
+        compiler_params=pltpu.CompilerParams(vmem_limit_bytes=60 * MIB),
+        cost_estimate=pl.CostEstimate(flops=int((2 * ROWS * D * FF * 4) * 0.1), bytes_accessed=int((20 * MIB) * 0.1), transcendentals=0),
     )(place, second, *parts, shift)
 
 
@@ -313,10 +309,8 @@
             pltpu.SemaphoreType.DMA((TILES, 2)),
             pltpu.SemaphoreType.DMA((TILES,)),
         ],
-        compiler_params=pltpu.CompilerParams(vmem_limit_bytes=24 * MIB),
-        cost_estimate=pl.CostEstimate(
-            flops=2 * ROWS * D * FF, bytes_accessed=14 * MIB, transcendentals=0
-        ),
+        compiler_params=pltpu.CompilerParams(vmem_limit_bytes=60 * MIB),
+        cost_estimate=pl.CostEstimate(flops=int((2 * ROWS * D * FF) * 0.1), bytes_accessed=int((14 * MIB) * 0.1), transcendentals=0),
     )(place, middle, active, *parts, biases)
 
 
@@ -399,14 +393,14 @@
             whole_block((1, D)),
         ],
         out_specs=(whole_block((ROWS, D)),) * 3 + (whole_block((40, D)),),
-        compiler_params=pltpu.CompilerParams(vmem_limit_bytes=16 * MIB),
-        cost_estimate=pl.CostEstimate(
-            flops=2 * ROWS * D * 128 * 8, bytes_accessed=5 * MIB, transcendentals=0
-        ),
+        compiler_params=pltpu.CompilerParams(vmem_limit_bytes=60 * MIB),
+        cost_estimate=pl.CostEstimate(flops=int((2 * ROWS * D * 128 * 8) * 0.1), bytes_accessed=int((5 * MIB) * 0.1), transcendentals=0),
     )(residual, targets, masked, weight, shift, gain, move)
 
 
-def down_back_kernel(place_ref, grad_ref, active_ref, send_ref, keep_ref, turned, held, sems):
+def down_back_kernel(
+    place_ref, grad_ref, active_ref, pass_ref, stay_ref, keep_ref, turned, held, sems
+):
     step = pl.program_id(0)
 
     @pl.when(step == 0)
@@ -420,28 +414,39 @@
     pltpu.make_async_copy(active_ref.at[0], held.at[step], sems.at[step]).wait()
     c_at = place_ref[2]
     active = held[step]
-    send_ref[0, 0] = mul_nn(turned[1 - c_at], active).astype(BF)
+    send = mul_nn(turned[1 - c_at], active).astype(BF)
+
+    @pl.when(step < 4)
+    def _():
+        pass_ref[0] = send
+
+    @pl.when(step >= 4)
+    def _():
+        stay_ref[0] = send
+
     keep_ref[0, 0] = mul_nn(turned[c_at], active).astype(BF)
 
 
 def down_back(place, grad, active):
-    block = pl.BlockSpec((1, 1, D // 2, TILE), lambda step: (1 - step // 4, step % 4, 0, 0))
-    out = sds((2, 4, D // 2, TILE), BF)
+    half = (1, D // 2, TILE)
+    out = sds((4, D // 2, TILE), BF)
     return pl.pallas_call(
         down_back_kernel,
         grid=(TILES,),
         in_specs=[SMEM_SPEC, whole_block((ROWS, D)), ANY_SPEC],
-        out_specs=(block, block),
+        out_specs=(
+            pl.BlockSpec(half, lambda step: (jnp.minimum(step, 3), 0, 0)),
+            pl.BlockSpec(half, lambda step: (jnp.maximum(step - 4, 0), 0, 0)),
+            pl.BlockSpec((1, *half), lambda step: (1 - step // 4, step % 4, 0, 0)),
+        ),
         scratch_shapes=[
             pltpu.VMEM((2, D // 2, ROWS), BF),
             pltpu.VMEM((TILES, ROWS, TILE), BF),
             pltpu.SemaphoreType.DMA((TILES,)),
         ],
-        out_shape=(out, out),
-        compiler_params=pltpu.CompilerParams(vmem_limit_bytes=20 * MIB),
-        cost_estimate=pl.CostEstimate(
-            flops=2 * ROWS * D * FF, bytes_accessed=13 * MIB, transcendentals=0
-        ),
+        out_shape=(out, out, sds((2, 4, D // 2, TILE), BF)),
+        compiler_params=pltpu.CompilerParams(vmem_limit_bytes=60 * MIB),
+        cost_estimate=pl.CostEstimate(flops=int((2 * ROWS * D * FF) * 0.1), bytes_accessed=int((13 * MIB) * 0.1), transcendentals=0),
     )(place, grad, active)
 
 
@@ -500,7 +505,8 @@
     u3_ref,
     d0_ref,
     d1_ref,
-    send_ref,
+    pass_ref,
+    stay_ref,
     shift_ref,
     total_ref,
     held_up,
@@ -518,8 +524,17 @@
         total_ref[...] = jnp.zeros_like(total_ref)
 
     def store(up_grad):
-        for side in range(2):
-            send_ref[0, side ^ place_ref[1], :, 0] = up_grad[:, side].astype(BF)
+        def into(out_ref):
+            for side in range(2):
+                out_ref[side ^ place_ref[1], :, 0] = up_grad[:, side].astype(BF)
+
+        @pl.when(step < 2)
+        def _():
+            into(pass_ref)
+
+        @pl.when(step >= 2)
+        def _():
+            into(stay_ref)
 
     wide_back_step(
         0, step, place_ref, rounded_ref, second_ref, slope_ref,
@@ -543,7 +558,8 @@
     grad_ref,
     middle_ref,
     gains_ref,
-    got_ref,
+    got_pass_ref,
+    got_keep_ref,
     pass_ref,
     keep_ref,
     shift_ref,
@@ -566,18 +582,18 @@
         total[...] = before_ref[...]
 
     def store(up_grad):
-        def into(out_ref):
+        def into(out_ref, got_ref):
             for side in range(2):
                 at = side ^ place_ref[1]
-                out_ref[at, :, 0] = (up_grad[:, side] + got_ref[0, at, :, 0].astype(F32)).astype(BF)
+                out_ref[at, :, 0] = (up_grad[:, side] + got_ref[at, :, 0].astype(F32)).astype(BF)
 
         @pl.when(step < 2)
         def _():
-            into(pass_ref)
+            into(pass_ref, got_pass_ref)
 
         @pl.when(step >= 2)
         def _():
-            into(keep_ref)
+            into(keep_ref, got_keep_ref)
 
     wide_back_step(
         1, step, place_ref, rounded_ref, second_ref, slope_ref,
@@ -630,52 +646,45 @@
             + scratch,
         ),
         out_shape=out_shape,
-        compiler_params=pltpu.CompilerParams(vmem_limit_bytes=32 * MIB),
-        cost_estimate=pl.CostEstimate(
-            flops=2 * ROWS * D * FF * 2, bytes_accessed=18 * MIB, transcendentals=0
-        ),
+        compiler_params=pltpu.CompilerParams(vmem_limit_bytes=60 * MIB),
+        cost_estimate=pl.CostEstimate(flops=int((2 * ROWS * D * FF * 2) * 0.1), bytes_accessed=int((18 * MIB) * 0.1), transcendentals=0),
     )(*arrays)
 
 
-def wide_back_block():
-    return pl.BlockSpec(
-        (1, 2, 4, 1, D // 8, TILE), lambda step, place_ref: (1 - step // 2, 0, 0, step % 2, 0, 0)
+def wide_back_blocks():
+    block = (2, 4, 1, D // 8, TILE)
+    return (
+        pl.BlockSpec(block, lambda step, place_ref: (0, 0, jnp.minimum(step, 1), 0, 0)),
+        pl.BlockSpec(block, lambda step, place_ref: (0, 0, jnp.maximum(step - 2, 0), 0, 0)),
     )
 
 
 def wide_back_first(place, rounded, second, slope, up_parts, down_parts):
+    out = sds((2, 4, 2, D // 8, TILE), BF)
     return wide_back_call(
         wide_back_first_kernel,
         [],
-        (wide_back_block(), whole_block((4, TILE)), whole_block((ROWS, D))),
-        (sds((2, 2, 4, 2, D // 8, TILE), BF), sds((4, TILE), F32), sds((ROWS, D), F32)),
+        (*wide_back_blocks(), whole_block((4, TILE)), whole_block((ROWS, D))),
+        (out, out, sds((4, TILE), F32), sds((ROWS, D), F32)),
         [],
         (place, rounded, second, slope, *up_parts[2:4], *up_parts[6:8], *down_parts),
     )
 
 
 def wide_back_last(
-    place, rounded, second, slope, up_parts, down_parts, before, grad, middle, gains, got
+    place, rounded, second, slope, up_parts, down_parts, before, grad, middle, gains, *got
 ):
     full = whole_block((ROWS, D))
     out = sds((2, 4, 2, D // 8, TILE), BF)
-    block = (2, 4, 1, D // 8, TILE)
     return wide_back_call(
         wide_back_last_kernel,
-        [full] * 3 + [whole_block((2, D)), wide_back_block()],
-        (
-            pl.BlockSpec(block, lambda step, place_ref: (0, 0, jnp.minimum(step, 1), 0, 0)),
-            pl.BlockSpec(block, lambda step, place_ref: (0, 0, jnp.maximum(step - 2, 0), 0, 0)),
-            whole_block((4, TILE)),
-            full,
-            full,
-            whole_block((8, D)),
-        ),
+        [full] * 3 + [whole_block((2, D)), *wide_back_blocks()],
+        (*wide_back_blocks(), whole_block((4, TILE)), full, full, whole_block((8, D))),
         (out, out, sds((4, TILE), F32), sds((ROWS, D), F32), sds((ROWS, D), BF), sds((8, D), F32)),
         [pltpu.VMEM((ROWS, D), F32)],
         (
             place, rounded, second, slope, *up_parts[0:2], *up_parts[4:6], *down_parts,
-            before, grad, middle, gains, got
+            before, grad, middle, gains, *got
         ),
     )
 
@@ -695,7 +704,10 @@
     mixed_ref,
     gains_ref,
     biases_ref,
-    send_ref,
+    s00_ref,
+    s01_ref,
+    s10_ref,
+    s11_ref,
     lefts_ref,
     rights_ref,
     grad_ref,
@@ -716,8 +728,12 @@
         def _():
             left = lefts_ref[1 if part == 3 else 0]
             value = mul_nn(left, rights_ref[part]).astype(BF).reshape(4, 2, D // 8, D)
-            for side in range(2):
-                send_ref[x_at ^ (part >> 1), side ^ y_at] = value[:, side]
+            for dx, out_refs in enumerate(((s00_ref, s01_ref), (s10_ref, s11_ref))):
+
+                @pl.when(x_at ^ (part >> 1) == dx)
+                def _():
+                    for dy, out_ref in enumerate(out_refs):
+                        out_ref[...] = jnp.where(y_at == dy, value[:, 0], value[:, 1])
 
     lefts_ref[1] = mixed_ref[...].T
     rights_ref[3] = rounded_ref[...]
@@ -792,11 +808,11 @@
 def mix_back(
     place, lengths, rounded, middle_grad, residual, quarters, packed, logs, mixed, gains, biases
 ):
-    out = sds((2, 2, 4, D // 8, D), BF)
+    out = sds((4, D // 8, D), BF)
     return pl.pallas_call(
         mix_back_kernel,
         out_shape=(
-            out,
+            *(out,) * 4,
             sds((2, D, ROWS), BF),
             sds((4, ROWS, D), BF),
             sds((ROWS, D), F32),
@@ -815,7 +831,7 @@
             whole_block((6, D)),
         ],
         out_specs=(
-            whole_block((2, 2, 4, D // 8, D)),
+            *(whole_block((4, D // 8, D)),) * 4,
             whole_block((2, D, ROWS)),
             whole_block((4, ROWS, D)),
             whole_block((ROWS, D)),
@@ -828,35 +844,35 @@
             pltpu.VMEM((ROWS, D), F32),
             pltpu.SemaphoreType.DMA((8,)),
         ],
-        compiler_params=pltpu.CompilerParams(vmem_limit_bytes=40 * MIB),
-        cost_estimate=pl.CostEstimate(
-            flops=2 * ROWS * D * 4 * D * 8, bytes_accessed=18 * MIB, transcendentals=0
-        ),
+        compiler_params=pltpu.CompilerParams(vmem_limit_bytes=60 * MIB),
+        cost_estimate=pl.CostEstimate(flops=int((2 * ROWS * D * 4 * D * 8) * 0.1), bytes_accessed=int((18 * MIB) * 0.1), transcendentals=0),
     )(
         place, lengths, rounded, middle_grad, residual, *quarters, packed, logs, mixed, gains, biases
     )
 
 
-def mix_back_last_kernel(place_ref, left_ref, right_ref, got_ref, pass_ref, keep_ref):
+def mix_back_last_kernel(
+    place_ref, left_ref, right_ref, g00_ref, g01_ref, g10_ref, g11_ref, pass_ref, keep_ref
+):
     step = pl.program_id(0)
     y_at = place_ref[1]
     value = mul_nn(left_ref[0], right_ref[0]).reshape(4, 2, D // 8, D)
 
-    def into(out_ref):
-        for side in range(2):
-            at = side ^ y_at
-            out_ref[at] = (value[:, side] + got_ref[0, at].astype(F32)).astype(BF)
+    def into(out_ref, *got_refs):
+        for dy, got_ref in enumerate(got_refs):
+            mine = jnp.where(y_at == dy, value[:, 0], value[:, 1])
+            out_ref[dy] = (mine + got_ref[...].astype(F32)).astype(BF)
 
     @pl.when(step == 0)
     def _():
-        into(pass_ref)
+        into(pass_ref, g10_ref, g11_ref)
 
     @pl.when(step == 1)
     def _():
-        into(keep_ref)
-
-
-def mix_back_last(place, lefts, rights, got):
+        into(keep_ref, g00_ref, g01_ref)
+
+
+def mix_back_last(place, lefts, rights, *got):
     def part(step, place_ref):
         return (place_ref[0] ^ (1 - step)) * 2 + place_ref[2]
 
@@ -871,22 +887,19 @@
                     (1, D, ROWS), lambda step, place_ref: (part(step, place_ref) // 3, 0, 0)
                 ),
                 pl.BlockSpec((1, ROWS, D), lambda step, place_ref: (part(step, place_ref), 0, 0)),
-                pl.BlockSpec(
-                    (1, 2, 4, D // 8, D), lambda step, place_ref: (1 - step, 0, 0, 0, 0)
-                ),
+                *(whole_block((4, D // 8, D)),) * 4,
             ],
             out_specs=(whole_block((2, 4, D // 8, D)),) * 2,
         ),
         out_shape=(out, out),
-        compiler_params=pltpu.CompilerParams(vmem_limit_bytes=16 * MIB),
-        cost_estimate=pl.CostEstimate(
-            flops=2 * ROWS * D * 2 * D, bytes_accessed=6 * MIB, transcendentals=0
-        ),
-    )(place, lefts, rights, got)
-
-
-def swap(value, axis):
-    return lax.ppermute(value, axis, [(0, 1), (1, 0)])
+        compiler_params=pltpu.CompilerParams(vmem_limit_bytes=60 * MIB),
+        cost_estimate=pl.CostEstimate(flops=int((2 * ROWS * D * 2 * D) * 0.1), bytes_accessed=int((6 * MIB) * 0.1), transcendentals=0),
+    )(place, lefts, rights, *got)
+
+
+def swap(value, axis, name="swap"):
+    with jax.named_scope(name):
+        return lax.ppermute(value, axis, [(0, 1), (1, 0)])
 
 
 def after(value, *others):
@@ -899,7 +912,7 @@
 
     def hold(self, *arrays):
         if self.last is not None:
-            arrays, self.last = lax.optimization_barrier((arrays, self.last))
+            arrays = lax.optimization_barrier((arrays, self.last))[0]
         return arrays
 
     def __call__(self, function, *arrays):
@@ -929,8 +942,9 @@
         self.c_at = lax.axis_index("c")
         self.place = jnp.stack([self.x_at, self.y_at, self.c_at]).astype(jnp.int32)
 
-    def hop(self, value, reach):
-        return lax.ppermute(value, "z", [(at, at ^ reach) for at in range(self.z_size)])
+    def hop(self, value, reach, name="hop"):
+        with jax.named_scope(name):
+            return lax.ppermute(value, "z", [(at, at ^ reach) for at in range(self.z_size)])
 
     def ordered(self, bit, own, other):
         return jnp.where(bit == 0, jnp.stack([own, other]), jnp.stack([other, own]))
@@ -958,27 +972,36 @@
             parts.append(self.by_side(lax.dynamic_index_in_dim(whole, quarter, 0, False)))
         return tuple(parts)
 
-    def low_bit(self, own, other):
-        return self.ordered(self.z_at % 2, own, other)
-
-    def high_bit(self, own, other):
-        line = self.ordered(self.z_at // 2, own, other)
-        line = line.reshape(4, *own.shape[1:])
+    def high(self, own, other):
+        return self.ordered(self.z_at // 2, own, other)
+
+    def low(self, pair, other):
+        return self.in_order(self.z_at % 2, pair, other)
+
+    def both(self, line, other):
+        return self.in_order(self.y_at, line, other)
+
+    def in_order(self, bit, own, other):
+        value = jnp.where(bit == 0, jnp.stack([own, other], 1), jnp.stack([other, own], 1))
+        return value.reshape(-1, *own.shape[1:])
+
+    def low_tiles(self, pair, other):
+        line = self.low(pair, other)
         return tuple(line[:, tile] for tile in range(line.shape[1]))
+
+    def part_near(self, *parts):
+        total = wide_sum(*parts)
+        total = total.reshape(2, 2, *total.shape[1:])
+        near = self.z_at % 2
+        return tuple(
+            lax.dynamic_index_in_dim(total, at, 1, False).astype(BF) for at in (1 - near, near)
+        )
 
     def part_far(self, *parts):
         total = wide_sum(*parts)
-        total = total.reshape(2, 2, *total.shape[1:])
         far = self.z_at // 2
         return tuple(
             lax.dynamic_index_in_dim(total, at, 0, False).astype(BF) for at in (1 - far, far)
-        )
-
-    def part_near(self, *parts):
-        total = wide_sum(*parts)
-        near = self.z_at % 2
-        return tuple(
-            lax.dynamic_index_in_dim(total, at, 0, False).astype(BF) for at in (1 - near, near)
         )
 
     def gather_halves(self, flat):
@@ -1007,11 +1030,11 @@
     def along_z(self, part):
         return lax.psum_scatter(part, "z", scatter_dimension=0, tiled=False)
 
-    def quarters_flat(self, own, beside):
-        four = jnp.concatenate([own, beside])
-        four = jnp.where(self.c_at == 0, four, four[jnp.array([1, 0, 3, 2])])
-        four = jnp.where(self.x_at == 0, four, four[jnp.array([2, 3, 0, 1])])
-        return four.transpose(2, 0, 1, 3).astype(F32).reshape(-1, 128)
+    def quarters_flat(self, own, other):
+        four = jnp.stack([own, other], 1)
+        four = jnp.where(self.c_at == 0, four, four[:, ::-1])
+        four = jnp.where(self.x_at == 0, four, four[::-1])
+        return four.transpose(3, 0, 1, 2, 4).astype(F32).reshape(-1, 128)
 
     def halves_flat(self, own, other):
         both = self.ordered(self.c_at, own, other)
@@ -1078,75 +1101,88 @@
     run = Order()
     if moves.staged:
         a0 = run(moves.own_quarter, attn_weight[0])
-        a0_near = moves.hop(a0, 1)
+        a0_far = moves.hop(a0, 2, "a0_far")
         u0 = run(moves.own_quarter, up_weight[0])
-        u0_near = moves.hop(u0, 1)
-        a0 = run(moves.low_bit, a0, a0_near)
-        a0_far = moves.hop(a0, 2)
-        u0 = run(moves.low_bit, u0, u0_near)
-        u0_far = moves.hop(u0, 2)
-        (a0,) = run(moves.high_bit, a0, a0_far)
-        a0_y = swap(a0, "y")
+        u0_far = moves.hop(u0, 2, "u0_far")
         d0 = run(moves.own_half, down_weight[0])
-        d0 = lax.all_gather(d0, ("z", "y"), axis=0, tiled=False)
+        a0 = run(moves.high, a0, a0_far)
+        a0_near = moves.hop(a0, 1, "a0_near")
+        (d0,) = run.hold(d0)
+        d0_far = moves.hop(d0, 2, "d0_far")
+        u0 = run(moves.high, u0, u0_far)
+        u0_near = moves.hop(u0, 1, "u0_near")
+        (a0,) = run(moves.low_tiles, a0, a0_near)
+        a0_y = swap(a0, "y", "a0_y")
+        a1 = run(moves.own_quarter, attn_weight[1])
+        a1_far = moves.hop(a1, 2, "a1_far")
+        u1 = run(moves.own_quarter, up_weight[1])
+        d1 = run(moves.own_half, down_weight[1])
         a0 = run(two, a0, a0_y)
-        a0_x = swap(a0, "x")
-        a0_c = swap(a0, "c")
-        u00, u01 = run(moves.high_bit, u0, u0_far)
-        u00_y, u01_y = swap(u00, "y"), swap(u01, "y")
-        a1 = run(moves.own_quarter, attn_weight[1])
-        a1_near = moves.hop(a1, 1)
-        u1 = run(moves.own_quarter, up_weight[1])
-        u1_near = moves.hop(u1, 1)
+        a0_x = swap(a0, "x", "a0_x")
+        a0_c = swap(a0, "c", "a0_c")
+        u00, u01 = run(moves.low_tiles, u0, u0_near)
+        u00_y, u01_y = swap(u00, "y", "u00_y"), swap(u01, "y", "u01_y")
+        d0 = run(moves.high, d0, d0_far)
+        d0_near = moves.hop(d0, 1, "d0_near")
+        a1 = run(moves.high, a1, a1_far)
+        a1_near = moves.hop(a1, 1, "a1_near")
+        ready = run(prepared, targets, masked, head_weight, head_bias)
         u00 = run(two, u00, u00_y)
-        u00_x = swap(u00, "x")
-        u00_c = swap(u00, "c")
-        a1 = run(moves.low_bit, a1, a1_near)
-        a1_far = moves.hop(a1, 2)
+        u00_x = swap(u00, "x", "u00_x")
+        u00_c = swap(u00, "c", "u00_c")
+        u01 = run(two, u01, u01_y)
+        u01_x = swap(u01, "x", "u01_x")
+        u01_c = swap(u01, "c", "u01_c")
+        (a1,) = run(moves.low_tiles, a1, a1_near)
+        a1_y = swap(a1, "y", "a1_y")
         (a0_x,) = run.hold(a0_x)
-        a0_xc = swap(a0_x, "c")
-        u01 = run(two, u01, u01_y)
-        u01_x = swap(u01, "x")
-        u01_c = swap(u01, "c")
-        u1 = run(moves.low_bit, u1, u1_near)
-        u1_far = moves.hop(u1, 2)
-        ready = run(prepared, targets, masked, head_weight, head_bias)
+        a0_xc = swap(a0_x, "c", "a0_xc")
         quarters0 = (a0, a0_c, a0_x, a0_xc)
         mixed0 = run(lambda r, *q: mix_on(0, r, q), inputs, *quarters0)
-        (a1,) = run(moves.high_bit, a1, a1_far)
-        a1_y = swap(a1, "y")
-        u00_x, = run.hold(u00_x)
-        u00_xc = swap(u00_x, "c")
+        d0 = run(moves.low, d0, d0_near)
+        d0_y = swap(d0, "y", "d0_y")
+        (u1,) = run.hold(u1)
+        u1_far = moves.hop(u1, 2, "u1_far")
         a1 = run(two, a1, a1_y)
-        a1_x = swap(a1, "x")
-        a1_c = swap(a1, "c")
-        u10, u11 = run(moves.high_bit, u1, u1_far)
-        u10_y, u11_y = swap(u10, "y"), swap(u11, "y")
-        u01_x, = run.hold(u01_x)
-        u01_xc = swap(u01_x, "c")
+        a1_x = swap(a1, "x", "a1_x")
+        a1_c = swap(a1, "c", "a1_c")
+        (u00_x,) = run.hold(u00_x)
+        u00_xc = swap(u00_x, "c", "u00_xc")
+        u1 = run(moves.high, u1, u1_far)
+        u1_near = moves.hop(u1, 1, "u1_near")
+        (d1,) = run.hold(d1)
+        d1_far = moves.hop(d1, 2, "d1_far")
+        (u01_x,) = run.hold(u01_x)
+        u01_xc = swap(u01_x, "c", "u01_xc")
         ups0 = (u00, u01, u00_c, u01_c, u00_x, u01_x, u00_xc, u01_xc)
         wide0 = run(lambda m, *p: up_on(0, m, p), mixed0[4], *ups0)
-        (d0,) = run.hold(d0)
-        d0_c = swap(d0, "c")
-        d1 = run(moves.own_half, down_weight[1])
-        d1 = lax.all_gather(d1, ("z", "y"), axis=0, tiled=False)
+        u10, u11 = run(moves.low_tiles, u1, u1_near)
+        u10_y, u11_y = swap(u10, "y", "u10_y"), swap(u11, "y", "u11_y")
+        d0 = run(moves.both, d0, d0_y)
+        d0_c = swap(d0, "c", "d0_c")
+        d1 = run(moves.high, d1, d1_far)
+        d1_near = moves.hop(d1, 1, "d1_near")
+        residual1 = run(lambda m, a, *p: down_on(0, m, a, p), mixed0[3], wide0[0], d0, d0_c)
         u10 = run(two, u10, u10_y)
-        u10_x = swap(u10, "x")
-        u10_c = swap(u10, "c")
+        u10_x = swap(u10, "x", "u10_x")
+        u10_c = swap(u10, "c", "u10_c")
         u11 = run(two, u11, u11_y)
-        u11_x = swap(u11, "x")
-        u11_c = swap(u11, "c")
-        residual1 = run(lambda m, a, *p: down_on(0, m, a, p), mixed0[3], wide0[0], d0, d0_c)
+        u11_x = swap(u11, "x", "u11_x")
+        u11_c = swap(u11, "c", "u11_c")
+        d1 = run(moves.low, d1, d1_near)
+        d1_y = swap(d1, "y", "d1_y")
         (a1_x,) = run.hold(a1_x)
-        a1_xc = swap(a1_x, "c")
+        a1_xc = swap(a1_x, "c", "a1_xc")
         quarters1 = (a1, a1_c, a1_x, a1_xc)
         mixed1 = run(lambda r, *q: mix_on(1, r, q), residual1, *quarters1)
-        u10_x, u11_x = run.hold(u10_x, u11_x)
-        u10_xc, u11_xc = swap(u10_x, "c"), swap(u11_x, "c")
+        (u10_x,) = run.hold(u10_x)
+        u10_xc = swap(u10_x, "c", "u10_xc")
+        (u11_x,) = run.hold(u11_x)
+        u11_xc = swap(u11_x, "c", "u11_xc")
         ups1 = (u10, u11, u10_c, u11_c, u10_x, u11_x, u10_xc, u11_xc)
         wide1 = run(lambda m, *p: up_on(1, m, p), mixed1[4], *ups1)
-        (d1,) = run.hold(d1)
-        d1_c = swap(d1, "c")
+        d1 = run(moves.both, d1, d1_y)
+        d1_c = swap(d1, "c", "d1_c")
         residual = run(lambda m, a, *p: down_on(1, m, a, p), mixed1[3], wide1[0], d1, d1_c)
         weights = [(quarters0, ups0, (d0, d0_c)), (quarters1, ups1, (d1, d1_c))]
         saved = [(inputs, *mixed0, *wide0), (residual1, *mixed1, *wide1)]
@@ -1183,11 +1219,11 @@
             place, rounded, saved[layer][5], saved[layer][7], up_parts, down_parts
         )
 
-    def wide_last(layer, rounded, before, grad, got):
+    def wide_last(layer, rounded, before, grad, *got):
         _, up_parts, down_parts = weights[layer]
         _, _, _, _, middle, second, _, slope = saved[layer]
         return wide_back_last(
-            place, rounded, second, slope, up_parts, down_parts, before, grad, middle, norm_gains[layer], got
+            place, rounded, second, slope, up_parts, down_parts, before, grad, middle, norm_gains[layer], *got
         )
 
     def mix_first(layer, rounded, middle_grad):
@@ -1206,8 +1242,8 @@
             layer_biases[layer],
         )
 
-    def mix_last(lefts, rights, got):
-        return mix_back_last(place, lefts, rights, got)
+    def mix_last(lefts, rights, *got):
+        return mix_back_last(place, lefts, rights, *got)
 
     def shift_rows(shift_send, shift_keep):
         send, keep = (part.reshape(2, 2, TILE)[::-1] for part in (shift_send, shift_keep))
@@ -1224,114 +1260,109 @@
     def plus(own, other):
         return own + other
 
+    def first_of(function, at):
+        return lambda *a: rounded_sum(*(v[at] if n in function else v for n, v in enumerate(a)))
+
     if moves.staged:
-        d1_send, d1_keep = run(lambda g: down_at(1, g), rounded)
-        d1_c = swap(d1_send, "c")
-        u1_send, *tail1 = run(lambda g: wide_first(1, g), rounded)
-        u1_c = swap(u1_send, "c")
-        d1_y = swap(run(rounded_sum, d1_keep[1], d1_c[1]), "y")
+        d1_pass, d1_stay, d1_keep = run(lambda g: down_at(1, g), rounded)
+        d1_c1, d1_c0 = swap(d1_pass, "c", "d1_c1"), swap(d1_stay, "c", "d1_c0")
+        u1_pass, u1_stay, *tail1 = run(lambda g: wide_first(1, g), rounded)
+        u1_c1, u1_c0 = swap(u1_pass, "c", "u1_c1"), swap(u1_stay, "c", "u1_c0")
+        d1_y = swap(run(first_of((0,), 1), d1_keep, d1_c1), "y", "d1_y")
         u1_pass, u1_keep, shift_keep1, middle_grad, middle_rounded, wide_small1 = run(
-            lambda *a: wide_last(1, *a), rounded, tail1[1], grad, u1_c
+            lambda *a: wide_last(1, *a), rounded, tail1[1], grad, u1_c1, u1_c0
         )
-        u1_x = swap(u1_pass, "x")
-        a1_send, lefts, rights, grad, rounded, mix_small1 = run(
+        u1_x = swap(u1_pass, "x", "u1_x")
+        *a1_send, lefts, rights, grad, rounded, mix_small1 = run(
             lambda *a: mix_first(1, *a), middle_rounded, middle_grad
         )
-        a1_c = swap(a1_send, "c")
-        d1 = moves.along_z(run(rounded_sum, d1_keep[0], d1_c[0], d1_y))
-        a1_pass, a1_keep = run(mix_last, lefts, rights, a1_c)
-        a1_x = swap(a1_pass, "x")
-        d0_send, d0_keep = run(lambda g: down_at(0, g), rounded)
-        d0_c = swap(d0_send, "c")
-        u0_send, *tail0 = run(lambda g: wide_first(0, g), rounded)
-        u0_c = swap(u0_send, "c")
-        u1_y = swap(run(rounded_sum, u1_keep[1], u1_x[1]), "y")
-        d0_y = swap(run(rounded_sum, d0_keep[1], d0_c[1]), "y")
+        a1_c = [swap(part, "c") for part in a1_send]
+        d1 = moves.along_z(run(first_of((0,), 0), d1_keep, d1_c0, d1_y))
+        a1_pass, a1_keep = run(mix_last, lefts, rights, *a1_c)
+        a1_x = swap(a1_pass, "x", "a1_x")
+        u1_y = swap(run(first_of((0, 1), 1), u1_keep, u1_x), "y", "u1_y")
+        d0_pass, d0_stay, d0_keep = run(lambda g: down_at(0, g), rounded)
+        d0_c1, d0_c0 = swap(d0_pass, "c", "d0_c1"), swap(d0_stay, "c", "d0_c0")
+        u0_pass, u0_stay, *tail0 = run(lambda g: wide_first(0, g), rounded)
+        u0_c1, u0_c0 = swap(u0_pass, "c", "u0_c1"), swap(u0_stay, "c", "u0_c0")
+        a1_y = swap(run(first_of((0, 1), 1), a1_keep, a1_x), "y", "a1_y")
+        d0_y = swap(run(first_of((0,), 1), d0_keep, d0_c1), "y", "d0_y")
+        u1 = moves.along_z(run(first_of((0, 1), 0), u1_keep, u1_x, u1_y))
         u0_pass, u0_keep, shift_keep0, middle_grad, middle_rounded, wide_small0 = run(
-            lambda *a: wide_last(0, *a), rounded, tail0[1], grad, u0_c
+            lambda *a: wide_last(0, *a), rounded, tail0[1], grad, u0_c1, u0_c0
         )
-        u0_x = swap(u0_pass, "x")
-        u1 = moves.along_z(run(rounded_sum, u1_keep[0], u1_x[0], u1_y))
-        a1_y = swap(run(rounded_sum, a1_keep[1], a1_x[1]), "y")
+        u0_x = swap(u0_pass, "x", "u0_x")
         (d1,) = run.hold(d1)
-        d1_x = swap(d1, "x")
-        a0_send, lefts, rights, grad, rounded, mix_small0 = run(
+        d1_x = swap(d1, "x", "d1_x")
+        a1 = moves.along_z(run(first_of((0, 1), 0), a1_keep, a1_x, a1_y))
+        *a0_send, lefts, rights, grad, rounded, mix_small0 = run(
             lambda *a: mix_first(0, *a), middle_rounded, middle_grad
         )
-        a0_c = swap(a0_send, "c")
+        a0_c = [swap(part, "c") for part in a0_send]
         small = run(
             packed_small,
             head_small,
             *(tail0[0], shift_keep0, wide_small0, mix_small0),
             *(tail1[0], shift_keep1, wide_small1, mix_small1),
         )
-        small_next = moves.hop(small, 2)
-        a0_pass, a0_keep = run(mix_last, lefts, rights, a0_c)
-        a0_x = swap(a0_pass, "x")
+        small_next = swap(small, "c", "small_next")
+        a0_pass, a0_keep = run(mix_last, lefts, rights, *a0_c)
+        a0_x = swap(a0_pass, "x", "a0_x")
+        d0 = moves.along_z(run(first_of((0,), 0), d0_keep, d0_c0, d0_y))
         small = run(plus, small, small_next)
-        small_next = moves.hop(small, 1)
+        small_next = moves.hop(small, 2, "small_next")
         d1 = run(rounded_sum, d1, d1_x)
-        d1_c = swap(d1, "c")
-        d0 = moves.along_z(run(rounded_sum, d0_keep[0], d0_c[0], d0_y))
-        u0_y = swap(run(rounded_sum, u0_keep[1], u0_x[1]), "y")
+        d1_c = swap(d1, "c", "d1_c")
+        u0_y = swap(run(first_of((0, 1), 1), u0_keep, u0_x), "y", "u0_y")
+        last1 = run(lambda u, a: jnp.concatenate([u, a[None]]), u1, a1)
+        last1_x = swap(last1, "x", "last1_x")
         small = run(plus, small, small_next)
-        small_next = swap(small, "c")
-        a1_send, a1_stay = run(moves.part_far, a1_keep[0], a1_x[0], a1_y)
-        a1_far = moves.hop(a1_send, 2)
+        small_next = moves.hop(small, 1, "small_next")
+        down_grad1 = run(moves.halves_flat, d1, d1_c)
+        a0_y = swap(run(first_of((0, 1), 1), a0_keep, a0_x), "y", "a0_y")
+        u0 = moves.along_z(run(first_of((0, 1), 0), u0_keep, u0_x, u0_y))
+        last1 = run(two, last1, last1_x)
+        last1_c = swap(last1, "c", "last1_c")
         small = run(plus, small, small_next)
-        a0_y = swap(run(rounded_sum, a0_keep[1], a0_x[1]), "y")
-        small_next = swap(small, "x")
-        down_grad1 = run(moves.halves_flat, d1, d1_c)
-        a1_send, a1_stay = run(moves.part_near, a1_stay, a1_far)
-        a1_near = moves.hop(a1_send, 1)
-        u0_send, u0_stay = run(moves.part_far, u0_keep[0], u0_x[0], u0_y)
-        u0_far = moves.hop(u0_send, 2)
+        small_next = swap(small, "x", "small_next")
+        a0_send, a0_stay = run(lambda k, x, y: moves.part_near(k[0], x[0], y), a0_keep, a0_x, a0_y)
+        a0_near = moves.hop(a0_send, 1, "a0_near")
+        up_grad1 = run(lambda *a: moves.quarters_flat(*(v[:, :2] for v in a)), last1, last1_c)
+        (d0,) = run.hold(d0)
+        d0_x = swap(d0, "x", "d0_x")
+        a0_send, a0_stay = run(moves.part_far, a0_stay, a0_near)
+        a0_far = moves.hop(a0_send, 2, "a0_far")
         small = run(plus, small, small_next)
-        small_next = swap(small, "y")
-        last1 = run(lambda u, *a: jnp.concatenate([u, rounded_sum(*a)[None]]), u1, a1_stay, a1_near)
-        last1_c = swap(last1, "c")
-        a0_send, a0_stay = run(moves.part_far, a0_keep[0], a0_x[0], a0_y)
-        a0_far = moves.hop(a0_send, 2)
-        last1 = run(two, last1, last1_c)
-        last1_x = swap(last1, "x")
-        u0_send, u0_stay = run(moves.part_near, u0_stay, u0_far)
-        u0_near = moves.hop(u0_send, 1)
-        (d0,) = run.hold(d0)
-        d0_x = swap(d0, "x")
+        small_next = swap(small, "y", "small_next")
+        attn_grad1 = run(lambda *a: moves.quarters_flat(*(v[:, 2:] for v in a)), last1, last1_c)
+        last0 = run(lambda u, *a: jnp.concatenate([u, rounded_sum(*a)[None]]), u0, a0_stay, a0_far)
+        last0_x = swap(last0, "x", "last0_x")
+        d0 = run(rounded_sum, d0, d0_x)
+        d0_c = swap(d0, "c", "d0_c")
         summed = run(plus, small, small_next)
-        a0_send, a0_stay = run(moves.part_near, a0_stay, a0_far)
-        a0_near = moves.hop(a0_send, 1)
-        up_grad1 = run(moves.quarters_flat, last1[:, :2], last1_x[:, :2])
-        attn_grad1 = run(moves.quarters_flat, last1[:, 2:], last1_x[:, 2:])
-        d0 = run(rounded_sum, d0, d0_x)
-        d0_c = swap(d0, "c")
-        last0 = run(
-            lambda u0, u1, a0, a1: jnp.concatenate([rounded_sum(u0, u1), rounded_sum(a0, a1)[None]]),
-            *(u0_stay, u0_near, a0_stay, a0_near),
-        )
-        last0_c = swap(last0, "c")
         down_grad0 = run(moves.halves_flat, d0, d0_c)
-        last0 = run(two, last0, last0_c)
-        last0_x = swap(last0, "x")
-        up_grad0 = run(moves.quarters_flat, last0[:, :2], last0_x[:, :2])
-        attn_grad0 = run(moves.quarters_flat, last0[:, 2:], last0_x[:, 2:])
+        last0 = run(two, last0, last0_x)
+        last0_c = swap(last0, "c", "last0_c")
+        up_grad0 = run(lambda *a: moves.quarters_flat(*(v[:, :2] for v in a)), last0, last0_c)
+        attn_grad0 = run(lambda *a: moves.quarters_flat(*(v[:, 2:] for v in a)), last0, last0_c)
         attn_grads = [attn_grad0, attn_grad1]
         up_grads = [up_grad0, up_grad1]
         down_grads = [down_grad0, down_grad1]
     else:
         attn_grads, up_grads, down_grads, smalls = ([None] * LAYERS for _ in range(4))
         for layer in reversed(range(LAYERS)):
-            send, keep = down_at(layer, rounded)
-            down_grads[layer] = moves.plain_halves(rounded_sum(keep, swap(send, "c")))
-            send, shift_send, before = wide_first(layer, rounded)
+            *send, keep = down_at(layer, rounded)
+            got = jnp.stack([swap(part, "c") for part in send[::-1]])
+            down_grads[layer] = moves.plain_halves(rounded_sum(keep, got))
+            *send, shift_send, before = wide_first(layer, rounded)
             passed, keep, shift_keep, middle_grad, middle_rounded, wide_small = wide_last(
-                layer, rounded, before, grad, swap(send, "c")
+                layer, rounded, before, grad, *(swap(part, "c") for part in send)
             )
             up_grads[layer] = moves.plain_quarters(passed, keep)
-            send, lefts, rights, grad, rounded, mix_small = mix_first(
+            *send, lefts, rights, grad, rounded, mix_small = mix_first(
                 layer, middle_rounded, middle_grad
             )
-            passed, keep = mix_last(lefts, rights, swap(send, "c"))
+            passed, keep = mix_last(lefts, rights, *(swap(part, "c") for part in send))
             attn_grads[layer] = moves.plain_quarters(passed[:, :, None], keep[:, :, None])
             smalls[layer] = (shift_send, shift_keep, wide_small, mix_small)
         summed = moves.sum_all(packed_small(head_small, *smalls[0], *smalls[1]))

time: 660 us -> 636 us (0.964)
  local copies, waits for them, and re-layouts: 130 us -> 54 us
  Pallas kernels: 184 us -> 226 us
  other arithmetic: 55.2 us -> 73.5 us
    unnamed x300 -> x110, local copies, waits for them, and re-layouts: 70 us -> 10.6 us
    squeeze x14 -> x2, local copies, waits for them, and re-layouts: 21 us -> 1.05 us  [low_tiles(): return tuple((line[:, tile] for tile in range(line.shape[1])))]
    ppermute x53 -> x65, waiting for transfers between devices: 122 us -> 106 us  [swap(): return lax.ppermute(value, axis, [(0, 1), (1, 0)])]
    select_n x3 -> x11, other arithmetic: 1.05 us -> 14.8 us  [the longest x8 13.6 us: in_order(): jnp.where(bit == 0, jnp.stack([own, other], 1), jnp.stack([other, own], 1))]
    reduce_scatter x3 -> x5, waiting for transfers between devices: 0.01 us -> 13.1 us  [along_z(): return lax.psum_scatter(part, 'z', scatter_dimension=0, tiled=False)]
    convert_element_type x12 -> x13, other arithmetic: 18.6 us -> 29.8 us  [rounded_sum(): return wide_sum(*values).astype(BF)]
    pallas_call x4, Pallas kernels: 58.2 us -> 68.4 us  [wide_back_call(): pl.pallas_call(kernel, grid_spec=pltpu.PrefetchScalarGridSpec(num_scalar_...]
    gather x8 -> x0, local copies, waits for them, and re-layouts: 9.42 us -> none  [the longest x4 5.1 us: quarters_flat(): four = jnp.where(self.x_at == 0, four, four[jnp.array([2, 3, 0, 1])])]
  transfers between devices with their start and end apart: 74 -> 86, of which waited for: 30 -> 31; matrix products, arithmetic and copies ran while one was open for 14% -> 17% of each run, Pallas kernels for 23% -> 31%
where the time goes in v3:
time: 636 us; the launch traced here: 629 us
  Pallas kernels  226 us (36%)
  waiting for transfers between devices  190 us (30%)
  other arithmetic  73.5 us (12%)
  starting transfers between devices  63.8 us (10%)
  local copies, waits for them, and re-layouts  54 us (8%)
  between operations  22 us (3%)
    ppermute x65, waiting for transfers between devices, swap(): return lax.ppermute(value, axis, [(0, 1), (1, 0)])  106 us
    ppermute x16, waiting for transfers between devices, hop(): lax.ppermute(value, 'z', [(at, at ^ reach) for at in range(self.z_size)])  70.9 us
    pallas_call x4, Pallas kernels, wide_back_call(): pl.pallas_call(kernel, grid_spec=pltpu.PrefetchScalarGridSpec(num_scalar_...  68.4 us
    pallas_call x2, Pallas kernels, mix_back(): pl.pallas_call(mix_back_kernel, out_shape=(*(out,) * 4, sds((2, D, ROWS),...  39.9 us
    ppermute x65, starting transfers between devices, swap(): return lax.ppermute(value, axis, [(0, 1), (1, 0)])  38.6 us
    pallas_call x2, Pallas kernels, mix(): pl.pallas_call(mix_kernel, out_shape=(sds((ROWS, 3 * D), BF), sds((SEQ_DE...  31.3 us
    convert_element_type x13, other arithmetic, rounded_sum(): return wide_sum(*values).astype(BF)  29.8 us
    ppermute x16, starting transfers between devices, hop(): lax.ppermute(value, 'z', [(at, at ^ reach) for at in range(self.z_size)])  24.4 us
  transfers between devices with their start and end apart: 86, of which 31 were waited for; matrix products, arithmetic and copies ran while one was open for 17% of the time, Pallas kernels for 31%

profile of v3, /device:TPU:0, one launch (start us, length us, event | category | flops | bytes accessed | tf_op | source)
XLA Modules:
  0.0 629.5 jit_solution(17860909710389896311)
XLA Ops:
  8.7 4.1 collective-permute-start
  17.9 5.3 collective-permute-start.1
  23.2 3.4 collective-permute-start.7
  29.0 6.7 %collective-permute-done.1 = bf16[2,1,80,640]{3,2,0,1:T(8,128)(2,1)S(1)} collective-permute-done((bf16[2,1,80,640]{3,2,0,1:T(8,128)(2,1)S(1)}, bf16[2,1,80,640]{3,2,0,1:T(8,128)(2,1)S(1)}, u32[]{:S(2)}, u32[]{:S(2)}) %collective-permute-start.1) | collective-permute-done | bytes 204832 | tf_op jit(solution)/shard_map/a0_near/ppermute | solution.py:947
  41.4 5.9 collective-permute-done.3
  53.8 2.2 maximum_select_fusion.5
  56.0 4.2 collective-permute-done.6
  60.3 3.7 collective-permute-done.11
  64.1 6.9 %collective-permute-done.10 = bf16[4,80,640]{2,1,0:T(8,128)(2,1)S(1)} collective-permute-done((bf16[4,80,640]{2,1,0:T(8,128)(2,1)S(1)}, bf16[4,80,640]{2,1,0:T(8,128)(2,1)S(1)}, u32[]{:S(2)}, u32[]{:S(2)}) %collective-permute-start.10) | collective-permute-done | bytes 409632 | tf_op jit(solution)/shard_map/u01_y/ppermute | solution.py:902
  78.2 15.3 %shard_map.253 = (bf16[512,1920]{1,0:T(8,128)(2,1)}, f32[20,1,512]{2,1,0:T(1,128)}, bf16[512,640]{1,0:T(8,128)(2,1)}, f32[512,640]{1,0:T(8,128)}, bf16[512,640]{1,0:T(8,128)(2,1)}) custom-call(s32[3]{0:T(128)} %pad_add_fusion.place_ref, s32[4]{0:T(128)} %lengths_ref.7, bf16[512,640]{1,0:T(8,128)(2,1)} %residual_ref.2, bf16[2,4,80,640]{3,2,1,0:T(8,128)(2,1)} %copy-done.3, ...), custom_call_target="tpu_custom_call" | custom-call | flops 671088640 | bytes 1048576 | tf_op jit(solution)/shard_map/pallas_call | solution.py:195
  93.5 2.2 maximum_select_fusion.2
  95.8 3.5 collective-permute-start.19
  99.8 2.1 pad_maximum_fusion.4.w0_ref
  102.4 5.9 collective-permute-done.19
  113.8 11.6 %shard_map.254 = (bf16[8,512,640]{2,1,0:T(8,128)(2,1)}, bf16[8,512,640]{2,1,0:T(8,128)(2,1)}) custom-call(s32[3]{0:T(128)} %pad_add_fusion.place_ref, bf16[512,640]{1,0:T(8,128)(2,1)} %get-tuple-element.334.second_ref, bf16[2,4,80,640]{3,2,1,0:T(8,128)(2,1)} %copy-done.4, bf16[2,4,80,640]{3,2,1,0:T(8,128)(2,1)} %copy-done.5, ...), custom_call_target="tpu_custom_call" | custom-call | flops 1342177280 | bytes 2097152 | tf_op jit(solution)/shard_map/pallas_call | solution.py:254
  127.9 8.3 %collective-permute-done.22 = bf16[4,320,640]{2,1,0:T(8,128)(2,1)} collective-permute-done((bf16[4,320,640]{2,1,0:T(8,128)(2,1)S(1)}, bf16[4,320,640]{2,1,0:T(8,128)(2,1)}, u32[]{:S(2)}, u32[]{:S(2)}) %collective-permute-start.22) | collective-permute-done | bytes 1638432 | tf_op jit(solution)/shard_map/d0_y/ppermute | solution.py:902
  136.2 2.7 maximum_select_fusion
  139.4 20.8 %collective-permute-done.25 = bf16[320,640]{1,0:T(8,128)(2,1)S(1)} collective-permute-done((bf16[320,640]{1,0:T(8,128)(2,1)S(1)}, bf16[320,640]{1,0:T(8,128)(2,1)S(1)}, u32[]{:S(2)}, u32[]{:S(2)}) %collective-permute-start.25) | collective-permute-done | bytes 409632 | tf_op jit(solution)/shard_map/d1_far/ppermute | solution.py:947
  166.5 10.9 %shard_map.255.residual_ref = f32[512,640]{1,0:T(8,128)} custom-call(s32[3]{0:T(128)} %pad_add_fusion.place_ref, f32[512,640]{1,0:T(8,128)} %get-tuple-element.351.middle_ref, bf16[8,512,640]{2,1,0:T(8,128)(2,1)} %get-tuple-element.352.active_ref, bf16[8,320,640]{2,1,0:T(8,128)(2,1)} %bitcast.247, bf16[8,320,640]{2,1,0:T(8,128)(2,1)} %copy-done.2, ...), custom_call_target="tpu_custom_call" | custom-call | flops 335544320 | bytes 1468006 | tf_op jit(solution)/shard_map/pallas_call | solution.py:293
  178.5 3.3 collective-permute-done.29
  183.8 2.5 maximum_select_fusion.3
  190.6 16.0 %shard_map.256 = (bf16[512,1920]{1,0:T(8,128)(2,1)}, f32[20,1,512]{2,1,0:T(1,128)}, bf16[512,640]{1,0:T(8,128)(2,1)}, f32[512,640]{1,0:T(8,128)}, bf16[512,640]{1,0:T(8,128)(2,1)}) custom-call(s32[3]{0:T(128)} %pad_add_fusion.place_ref, s32[4]{0:T(128)} %lengths_ref.7, f32[512,640]{1,0:T(8,128)} %shard_map.255.residual_ref, ...), custom_call_target="tpu_custom_call" | custom-call | flops 671088640 | bytes 1048576 | tf_op jit(solution)/shard_map/pallas_call | solution.py:195
  207.7 17.1 %collective-permute-done.34.refs_4_.u2_ref = bf16[2,4,80,640]{3,2,1,0:T(8,128)(2,1)} collective-permute-done((bf16[2,4,80,640]{3,2,1,0:T(8,128)(2,1)S(1)}, bf16[2,4,80,640]{3,2,1,0:T(8,128)(2,1)}, u32[]{:S(2)}, u32[]{:S(2)}) %collective-permute-start.34) | collective-permute-done | bytes 819232 | tf_op jit(solution)/shard_map/u10_x/ppermute | solution.py:902
  225.4 2.0 collective-permute-done.36.refs_6_.u2_ref
  227.5 11.4 %shard_map.257 = (bf16[8,512,640]{2,1,0:T(8,128)(2,1)}, bf16[8,512,640]{2,1,0:T(8,128)(2,1)}) custom-call(s32[3]{0:T(128)} %pad_add_fusion.place_ref, bf16[512,640]{1,0:T(8,128)(2,1)} %get-tuple-element.372.second_ref, bf16[2,4,80,640]{3,2,1,0:T(8,128)(2,1)} %copy-done.6, bf16[2,4,80,640]{3,2,1,0:T(8,128)(2,1)} %copy-done.7, ...), custom_call_target="tpu_custom_call" | custom-call | flops 1342177280 | bytes 2097152 | tf_op jit(solution)/shard_map/pallas_call | solution.py:254
  239.0 3.5 maximum_select_fusion.1
  246.1 2.7 collective-permute-done.39.d1_ref
  248.8 10.9 %shard_map.258.residual_ref = f32[512,640]{1,0:T(8,128)} custom-call(s32[3]{0:T(128)} %pad_add_fusion.place_ref, f32[512,640]{1,0:T(8,128)} %get-tuple-element.384.middle_ref, bf16[8,512,640]{2,1,0:T(8,128)(2,1)} %get-tuple-element.385.active_ref, bf16[8,320,640]{2,1,0:T(8,128)(2,1)} %bitcast.251, bf16[8,320,640]{2,1,0:T(8,128)(2,1)} %collective-permute-done.39.d1_ref, ...), custom_call_target="tpu_custom_call" | custom-call | flops 335544320 | bytes 1468006 | tf_op jit(solution)/shard_map/pallas_call | solution.py:293
  261.5 6.7 %shard_map.259 = (bf16[512,640]{1,0:T(8,128)(2,1)}, f32[512,640]{1,0:T(8,128)}, bf16[512,640]{1,0:T(8,128)(2,1)}, f32[40,640]{1,0:T(8,128)}) custom-call(f32[512,640]{1,0:T(8,128)} %shard_map.258.residual_ref, s32[512,1]{1,0:T(8,128)} %copy.99.targets_ref, s32[512,1]{1,0:T(8,128)} %copy.100.masked_ref, bf16[640,128]{1,0:T(8,128)(2,1)} %pad.8.weight_ref, ...), custom_call_target="tpu_custom_call" | custom-call | flops 67108864 | bytes 524288 | tf_op jit(solution)/shard_map/pallas_call | solution.py:377
  268.2 11.8 %shard_map.260 = (bf16[4,320,640]{2,1,0:T(8,128)(2,1)}, bf16[4,320,640]{2,1,0:T(8,128)(2,1)}, bf16[2,4,320,640]{3,2,1,0:T(8,128)(2,1)}) custom-call(s32[3]{0:T(128)} %pad_add_fusion.place_ref, bf16[512,640]{1,0:T(8,128)(2,1)} %get-tuple-element.411.grad_ref.rounded_ref, bf16[8,512,640]{2,1,0:T(8,128)(2,1)} %get-tuple-element.385.active_ref), custom_call_target="tpu_custom_call" | custom-call | flops 335544320 | bytes 1363148 | tf_op jit(solution)/shard_map/pallas_call | solution.py:433
  280.4 15.2 %shard_map.261 = (bf16[2,4,2,80,640]{4,3,2,1,0:T(8,128)(2,1)}, bf16[2,4,2,80,640]{4,3,2,1,0:T(8,128)(2,1)}, f32[4,640]{1,0:T(4,128)}, f32[512,640]{1,0:T(8,128)}) custom-call(s32[3]{0:T(128)} %pad_add_fusion.place_ref, bf16[512,640]{1,0:T(8,128)(2,1)} %get-tuple-element.411.grad_ref.rounded_ref, bf16[512,640]{1,0:T(8,128)(2,1)} %get-tuple-element.372.second_ref, ...), custom_call_target="tpu_custom_call" | custom-call | flops 671088640 | bytes 1887436 | tf_op jit(solution)/shard_map/pallas_call | solution.py:630
  296.3 3.0 fusion.5
  299.8 2.0 collective-permute-done.41.got_keep_ref
  301.9 19.0 %shard_map.262 = (bf16[2,4,2,80,640]{4,3,2,1,0:T(8,128)(2,1)}, bf16[2,4,2,80,640]{4,3,2,1,0:T(8,128)(2,1)}, f32[4,640]{1,0:T(4,128)}, f32[512,640]{1,0:T(8,128)}...) custom-call(s32[3]{0:T(128)} %pad_add_fusion.place_ref, bf16[512,640]{1,0:T(8,128)(2,1)} %get-tuple-element.411.grad_ref.rounded_ref, ...), custom_call_target="tpu_custom_call" | custom-call | flops 671088640 | bytes 1887436 | tf_op jit(solution)/shard_map/pallas_call | solution.py:630
  320.9 2.5 collective-permute-start.43
  323.3 20.0 %shard_map.263 = (bf16[4,80,640]{2,1,0:T(8,128)(2,1)}, bf16[4,80,640]{2,1,0:T(8,128)(2,1)}, bf16[4,80,640]{2,1,0:T(8,128)(2,1)}, bf16[4,80,640]{2,1,0:T(8,128)(2...) custom-call(s32[3]{0:T(128)} %pad_add_fusion.place_ref, ...), custom_call_target="tpu_custom_call" | custom-call | flops 1342177280 | bytes 1887436 | tf_op jit(solution)/shard_map/pallas_call | solution.py:812
  344.4 3.7 fusion.4
  349.3 5.7 shard_map.264
  355.0 4.7 collective-permute-done.43
  359.8 2.2 fusion.8
  362.0 11.8 %shard_map.265 = (bf16[4,320,640]{2,1,0:T(8,128)(2,1)}, bf16[4,320,640]{2,1,0:T(8,128)(2,1)}, bf16[2,4,320,640]{3,2,1,0:T(8,128)(2,1)}) custom-call(s32[3]{0:T(128)} %pad_add_fusion.place_ref, bf16[512,640]{1,0:T(8,128)(2,1)} %get-tuple-element.461.grad_ref.rounded_ref, bf16[8,512,640]{2,1,0:T(8,128)(2,1)} %get-tuple-element.352.active_ref), custom_call_target="tpu_custom_call" | custom-call | flops 335544320 | bytes 1363148 | tf_op jit(solution)/shard_map/pallas_call | solution.py:433
  375.7 15.2 %shard_map.266 = (bf16[2,4,2,80,640]{4,3,2,1,0:T(8,128)(2,1)}, bf16[2,4,2,80,640]{4,3,2,1,0:T(8,128)(2,1)}, f32[4,640]{1,0:T(4,128)}, f32[512,640]{1,0:T(8,128)}) custom-call(s32[3]{0:T(128)} %pad_add_fusion.place_ref, bf16[512,640]{1,0:T(8,128)(2,1)} %get-tuple-element.461.grad_ref.rounded_ref, bf16[512,640]{1,0:T(8,128)(2,1)} %get-tuple-element.334.second_ref, ...), custom_call_target="tpu_custom_call" | custom-call | flops 671088640 | bytes 1887436 | tf_op jit(solution)/shard_map/pallas_call | solution.py:630
  391.9 2.9 collective-permute-done.54
  397.2 3.2 fusion.2
  400.4 12.5 %collective-permute-done.52 = bf16[4,2,80,640]{3,2,1,0:T(8,128)(2,1)} collective-permute-done((bf16[4,2,80,640]{3,2,1,0:T(8,128)(2,1)}, bf16[4,2,80,640]{3,2,1,0:T(8,128)(2,1)}, u32[]{:S(2)}, u32[]{:S(2)}) %collective-permute-start.52) | collective-permute-done | bytes 819232 | tf_op jit(solution)/shard_map/u1_y/ppermute | solution.py:902
  413.4 2.7 fusion.7
  416.0 19.0 %shard_map.267 = (bf16[2,4,2,80,640]{4,3,2,1,0:T(8,128)(2,1)}, bf16[2,4,2,80,640]{4,3,2,1,0:T(8,128)(2,1)}, f32[4,640]{1,0:T(4,128)}, f32[512,640]{1,0:T(8,128)}...) custom-call(s32[3]{0:T(128)} %pad_add_fusion.place_ref, bf16[512,640]{1,0:T(8,128)(2,1)} %get-tuple-element.461.grad_ref.rounded_ref, ...), custom_call_target="tpu_custom_call" | custom-call | flops 671088640 | bytes 1887436 | tf_op jit(solution)/shard_map/pallas_call | solution.py:630
  435.3 2.2 fusion.10
  437.5 19.9 %shard_map.268 = (bf16[4,80,640]{2,1,0:T(8,128)(2,1)}, bf16[4,80,640]{2,1,0:T(8,128)(2,1)}, bf16[4,80,640]{2,1,0:T(8,128)(2,1)}, bf16[4,80,640]{2,1,0:T(8,128)(2...) custom-call(s32[3]{0:T(128)} %pad_add_fusion.place_ref, ...), custom_call_target="tpu_custom_call" | custom-call | flops 1342177280 | bytes 1887436 | tf_op jit(solution)/shard_map/pallas_call | solution.py:812
  464.9 5.4 shard_map.269
  470.6 3.7 fusion.1
  475.4 7.5 %collective-permute-done.57 = bf16[320,640]{1,0:T(8,128)(2,1)} collective-permute-done((bf16[320,640]{1,0:T(8,128)(2,1)}, bf16[320,640]{1,0:T(8,128)(2,1)}, u32[]{:S(2)}, u32[]{:S(2)}) %collective-permute-start.57) | collective-permute-done | bytes 409632 | tf_op jit(solution)/shard_map/d1_x/ppermute | solution.py:902
  487.3 10.3 %collective-permute-done.66 = bf16[2,4,80,640]{3,2,1,0:T(8,128)(2,1)} collective-permute-done((bf16[2,4,80,640]{3,2,1,0:T(8,128)(2,1)}, bf16[2,4,80,640]{3,2,1,0:T(8,128)(2,1)}, u32[]{:S(2)}, u32[]{:S(2)}) %collective-permute-start.66) | collective-permute-done | bytes 819232 | tf_op jit(solution)/shard_map/a0_x/ppermute | solution.py:902
  500.5 2.4 fusion.6
  507.8 4.7 collective-permute-done.70
  513.5 10.5 %collective-permute-done.68 = f32[88,640]{1,0:T(8,128)S(1)} collective-permute-done((f32[88,640]{1,0:T(8,128)S(1)}, f32[88,640]{1,0:T(8,128)S(1)}, u32[]{:S(2)}, u32[]{:S(2)}) %collective-permute-start.68) | collective-permute-done | bytes 225312 | tf_op jit(solution)/shard_map/small_next/ppermute | solution.py:947
  525.9 8.8 %collective-permute-done.69 = f32[88,640]{1,0:T(8,128)S(1)} collective-permute-done((f32[88,640]{1,0:T(8,128)S(1)}, f32[88,640]{1,0:T(8,128)S(1)}, u32[]{:S(2)}, u32[]{:S(2)}) %collective-permute-start.69) | collective-permute-done | bytes 225312 | tf_op jit(solution)/shard_map/small_next/ppermute | solution.py:947
  539.0 4.1 collective-permute-done.71
  543.8 2.0 collective-permute-start.73
  550.3 8.3 %collective-permute-done.73 = bf16[80,640]{1,0:T(8,128)(2,1)} collective-permute-done((bf16[80,640]{1,0:T(8,128)(2,1)}, bf16[80,640]{1,0:T(8,128)(2,1)}, u32[]{:S(2)}, u32[]{:S(2)}) %collective-permute-start.73) | collective-permute-done | bytes 102432 | tf_op jit(solution)/shard_map/a0_far/ppermute | solution.py:947
  562.1 13.0 %reduce-scatter.14.cloned.1.call-done = bf16[1,320,640]{2,1,0:T(8,128)(2,1)} async-done(((bf16[4,320,640]{2,1,0:T(8,128)(2,1)}), bf16[1,320,640]{2,1,0:T(8,128)(2,1)}) %reduce-scatter.14.cloned.1.call-update) | async-done | bytes 409616 | tf_op jit(solution)/shard_map/reduce_scatter | solution.py:1031
  579.6 7.2 %collective-permute-done.77 = bf16[320,640]{1,0:T(8,128)(2,1)S(1)} collective-permute-done((bf16[320,640]{1,0:T(8,128)(2,1)}, bf16[320,640]{1,0:T(8,128)(2,1)S(1)}, u32[]{:S(2)}, u32[]{:S(2)}) %collective-permute-start.77) | collective-permute-done | bytes 409632 | tf_op jit(solution)/shard_map/d0_x/ppermute | solution.py:902
  599.3 2.7 reshape.402
  606.1 2.0 stack_reshape.31
  (389 shorter events, 133.9 us)
Async XLA Ops:
  7.2 455.1 %reduce-scatter.6.cloned.1.call-start = ((), (), s32[]{:S(2)}) async-start(), calls=%async_computation.5 | async-start | bytes 2048000 | tf_op jit(solution)/shard_map/reduce_scatter | solution.py:1031
  15.2 12.3 %collective-permute-start.2 = (bf16[2,80,640]{2,1,0:T(8,128)(2,1)}, bf16[2,80,640]{2,1,0:T(8,128)(2,1)}, u32[]{:S(2)}, u32[]{:S(2)}) collective-permute-start(bf16[2,80,640]{2,1,0:T(8,128)(2,1)} %bitcast.243), channel_id=1, source_target_pairs={{0,16},{8,24},{16,0},{24,8},{1,17},{9,25},{17,1},{25,9},{2,18},{10... | collective-permute-start | bytes 614408 | tf_op jit(solution)/shard_map/u0_far/ppermute | solution.py:947
  17.9 17.8 %collective-permute-start.1 = (bf16[2,1,80,640]{3,2,0,1:T(8,128)(2,1)S(1)}, bf16[2,1,80,640]{3,2,0,1:T(8,128)(2,1)S(1)}, u32[]{:S(2)}, u32[]{:S(2)}) collective-permute-start(bf16[2,1,80,640]{3,2,0,1:T(8,128)(2,1)S(1)} %fusion.25), channel_id=1, source_target_pairs={{0,8},{8,0},{16,24},{24,16},{1,9},{9,1},{17,25},{25,17},{2,10},{10... | collective-permute-start | bytes 614408 | tf_op jit(solution)/shard_map/a0_near/ppermute | solution.py:947
  23.2 30.6 %collective-permute-start.7 = (bf16[320,640]{1,0:T(8,128)(2,1)S(1)}, bf16[320,640]{1,0:T(8,128)(2,1)}, u32[]{:S(2)}, u32[]{:S(2)}) collective-permute-start(bf16[320,640]{1,0:T(8,128)(2,1)S(1)} %reshape.379), channel_id=1, source_target_pairs={{0,16},{8,24},{16,0},{24,8},{1,17},{9,25},{17,1},{25,9},{2,18},{10... | collective-permute-start | bytes 1228808 | tf_op jit(solution)/shard_map/d0_far/ppermute | solution.py:947
  28.9 21.2 %collective-permute-start.8 = (bf16[2,2,80,640]{3,2,1,0:T(8,128)(2,1)S(1)}, bf16[2,2,80,640]{3,2,1,0:T(8,128)(2,1)}, u32[]{:S(2)}, u32[]{:S(2)}) collective-permute-start(bf16[2,2,80,640]{3,2,1,0:T(8,128)(2,1)S(1)} %maximum_select_fusion.10), channel_id=1, source_target_pairs={{0,8},{8,0},{16,24},{24,16},{1,9},{9,1},{17,25},{25,17},{2,10},{10... | collective-permute-start | bytes 1228808 | tf_op jit(solution)/shard_map/u0_near/ppermute | solution.py:947
  35.9 11.5 %collective-permute-start.3 = (bf16[4,80,640]{2,1,0:T(8,128)(2,1)S(1)}, bf16[4,80,640]{2,1,0:T(8,128)(2,1)}, u32[]{:S(2)}, u32[]{:S(2)}) collective-permute-start(bf16[4,80,640]{2,1,0:T(8,128)(2,1)S(1)} %bitcast.267), channel_id=1, source_target_pairs={{0,4},{4,0},{1,5},{5,1},{2,6},{6,2},{3,7},{7,3},{8,12},{12,8},{9,1... | collective-permute-start | bytes 1228808 | tf_op jit(solution)/shard_map/a0_y/ppermute | solution.py:902
  48.5 23.6 %collective-permute-start.5 = (bf16[2,4,80,640]{3,2,1,0:T(8,128)(2,1)S(1)}, bf16[2,4,80,640]{3,2,1,0:T(8,128)(2,1)S(1)}, u32[]{:S(2)}, u32[]{:S(2)}) collective-permute-start(bf16[2,4,80,640]{3,2,1,0:T(8,128)(2,1)S(1)} %pad_maximum_fusion.1.w0_ref), channel_id=1, source_target_pairs={{0,2},{2,0},{1,3},{3,1},{4,6},{6,4},{5,7},{7,5},{8,10},{10,8},{9,1... | collective-permute-start | bytes 2457608 | tf_op jit(solution)/shard_map/a0_x/ppermute | solution.py:902
  51.5 12.5 %collective-permute-start.11 = (bf16[4,80,640]{2,1,0:T(8,128)(2,1)S(1)}, bf16[4,80,640]{2,1,0:T(8,128)(2,1)S(1)}, u32[]{:S(2)}, u32[]{:S(2)}) collective-permute-start(bf16[4,80,640]{2,1,0:T(8,128)(2,1)S(1)} %get-tuple-element.310), channel_id=1, source_target_pairs={{0,4},{4,0},{1,5},{5,1},{2,6},{6,2},{3,7},{7,3},{8,12},{12,8},{9,1... | collective-permute-start | bytes 1228808 | tf_op jit(solution)/shard_map/u00_y/ppermute | solution.py:902
  53.1 17.9 %collective-permute-start.10 = (bf16[4,80,640]{2,1,0:T(8,128)(2,1)S(1)}, bf16[4,80,640]{2,1,0:T(8,128)(2,1)S(1)}, u32[]{:S(2)}, u32[]{:S(2)}) collective-permute-start(bf16[4,80,640]{2,1,0:T(8,128)(2,1)S(1)} %get-tuple-element.312), channel_id=1, source_target_pairs={{0,4},{4,0},{1,5},{5,1},{2,6},{6,2},{3,7},{7,3},{8,12},{12,8},{9,1... | collective-permute-start | bytes 1228808 | tf_op jit(solution)/shard_map/u01_y/ppermute | solution.py:902
  53.8 22.1 %collective-permute-start.4 = (bf16[2,4,80,640]{3,2,1,0:T(8,128)(2,1)S(1)}, bf16[2,4,80,640]{3,2,1,0:T(8,128)(2,1)S(1)}, u32[]{:S(2)}, u32[]{:S(2)}) collective-permute-start(bf16[2,4,80,640]{3,2,1,0:T(8,128)(2,1)S(1)} %pad_maximum_fusion.1.w0_ref), channel_id=1, source_target_pairs={{0,1},{1,0},{2,3},{3,2},{4,5},{5,4},{6,7},{7,6},{8,9},{9,8},{10,11... | collective-permute-start | bytes 2457608 | tf_op jit(solution)/shard_map/a0_c/ppermute | solution.py:902
  60.2 10.9 %collective-permute-start.9 = (bf16[2,1,80,640]{3,2,0,1:T(8,128)(2,1)S(1)}, bf16[2,1,80,640]{3,2,0,1:T(8,128)(2,1)S(1)}, u32[]{:S(2)}, u32[]{:S(2)}) collective-permute-start(bf16[2,1,80,640]{3,2,0,1:T(8,128)(2,1)S(1)} %maximum_select_fusion.14), channel_id=1, source_target_pairs={{0,8},{8,0},{16,24},{24,16},{1,9},{9,1},{17,25},{25,17},{2,10},{10... | collective-permute-start | bytes 614408 | tf_op jit(solution)/shard_map/a1_near/ppermute | solution.py:947
  72.1 21.4 %collective-permute-start.17 = (bf16[2,320,640]{2,1,0:T(8,128)(2,1)}, bf16[2,320,640]{2,1,0:T(8,128)(2,1)}, u32[]{:S(2)}, u32[]{:S(2)}) collective-permute-start(bf16[2,320,640]{2,1,0:T(8,128)(2,1)} %maximum_select_fusion.5), channel_id=1, source_target_pairs={{0,8},{8,0},{16,24},{24,16},{1,9},{9,1},{17,25},{25,17},{2,10},{10... | collective-permute-start | bytes 2457608 | tf_op jit(solution)/shard_map/d0_near/ppermute | solution.py:947
  72.2 29.8 %collective-permute-start.15 = (bf16[2,4,80,640]{3,2,1,0:T(8,128)(2,1)S(1)}, bf16[2,4,80,640]{3,2,1,0:T(8,128)(2,1)}, u32[]{:S(2)}, u32[]{:S(2)}) collective-permute-start(bf16[2,4,80,640]{3,2,1,0:T(8,128)(2,1)S(1)} %pad_maximum_fusion.2.refs_0_.u0_ref), channel_id=1, source_target_pairs={{0,2},{2,0},{1,3},{3,1},{4,6},{6,4},{5,7},{7,5},{8,10},{10,8},{9,1... | collective-permute-start | bytes 2457608 | tf_op jit(solution)/shard_map/u00_x/ppermute | solution.py:902
  74.4 25.4 %collective-permute-start.16 = (bf16[4,80,640]{2,1,0:T(8,128)(2,1)}, bf16[4,80,640]{2,1,0:T(8,128)(2,1)}, u32[]{:S(2)}, u32[]{:S(2)}) collective-permute-start(bf16[4,80,640]{2,1,0:T(8,128)(2,1)} %bitcast.41), channel_id=1, source_target_pairs={{0,4},{4,0},{1,5},{5,1},{2,6},{6,2},{3,7},{7,3},{8,12},{12,8},{9,1... | collective-permute-start | bytes 1228808 | tf_op jit(solution)/shard_map/a1_y/ppermute | solution.py:902
  75.9 34.5 %collective-permute-start.18 = (bf16[2,4,80,640]{3,2,1,0:T(8,128)(2,1)S(1)}, bf16[2,4,80,640]{3,2,1,0:T(8,128)(2,1)}, u32[]{:S(2)}, u32[]{:S(2)}) collective-permute-start(bf16[2,4,80,640]{3,2,1,0:T(8,128)(2,1)S(1)} %pad_maximum_fusion.3.refs_1_.u1_ref), channel_id=1, source_target_pairs={{0,2},{2,0},{1,3},{3,1},{4,6},{6,4},{5,7},{7,5},{8,10},{10,8},{9,1... | collective-permute-start | bytes 2457608 | tf_op jit(solution)/shard_map/u01_x/ppermute | solution.py:902
  95.8 12.6 %collective-permute-start.19 = (bf16[2,80,640]{2,1,0:T(8,128)(2,1)S(1)}, bf16[2,80,640]{2,1,0:T(8,128)(2,1)S(1)}, u32[]{:S(2)}, u32[]{:S(2)}) collective-permute-start(bf16[2,80,640]{2,1,0:T(8,128)(2,1)S(1)} %bitcast.277), channel_id=1, source_target_pairs={{0,16},{8,24},{16,0},{24,8},{1,17},{9,25},{17,1},{25,9},{2,18},{10... | collective-permute-start | bytes 614408 | tf_op jit(solution)/shard_map/u1_far/ppermute | solution.py:947
  99.3 36.9 %collective-permute-start.22 = (bf16[4,320,640]{2,1,0:T(8,128)(2,1)S(1)}, bf16[4,320,640]{2,1,0:T(8,128)(2,1)}, u32[]{:S(2)}, u32[]{:S(2)}) collective-permute-start(bf16[4,320,640]{2,1,0:T(8,128)(2,1)S(1)} %bitcast.256), channel_id=1, source_target_pairs={{0,4},{4,0},{1,5},{5,1},{2,6},{6,2},{3,7},{7,3},{8,12},{12,8},{9,1... | collective-permute-start | bytes 4915208 | tf_op jit(solution)/shard_map/d0_y/ppermute | solution.py:902
  101.9 11.9 %collective-permute-start.13 = (bf16[2,4,80,640]{3,2,1,0:T(8,128)(2,1)S(1)}, bf16[2,4,80,640]{3,2,1,0:T(8,128)(2,1)}, u32[]{:S(2)}, u32[]{:S(2)}) collective-permute-start(bf16[2,4,80,640]{3,2,1,0:T(8,128)(2,1)S(1)} %pad_maximum_fusion.2.refs_0_.u0_ref), channel_id=1, source_target_pairs={{0,1},{1,0},{2,3},{3,2},{4,5},{5,4},{6,7},{7,6},{8,9},{9,8},{10,11... | collective-permute-start | bytes 2457608 | tf_op jit(solution)/shard_map/u00_c/ppermute | solution.py:902
  111.4 14.1 %collective-permute-start.23 = (bf16[2,2,80,640]{3,2,1,0:T(8,128)(2,1)}, bf16[2,2,80,640]{3,2,1,0:T(8,128)(2,1)S(1)}, u32[]{:S(2)}, u32[]{:S(2)}) collective-permute-start(bf16[2,2,80,640]{3,2,1,0:T(8,128)(2,1)} %maximum_select_fusion.13), channel_id=1, source_target_pairs={{0,8},{8,0},{16,24},{24,16},{1,9},{9,1},{17,25},{25,17},{2,10},{10... | collective-permute-start | bytes 1228808 | tf_op jit(solution)/shard_map/u1_near/ppermute | solution.py:947
  138.9 25.9 %collective-permute-start.24 = (bf16[8,320,640]{2,1,0:T(8,128)(2,1)S(1)}, bf16[8,320,640]{2,1,0:T(8,128)(2,1)S(1)}, u32[]{:S(2)}, u32[]{:S(2)}) collective-permute-start(bf16[8,320,640]{2,1,0:T(8,128)(2,1)S(1)} %bitcast.246), channel_id=1, source_target_pairs={{0,1},{1,0},{2,3},{3,2},{4,5},{5,4},{6,7},{7,6},{8,9},{9,8},{10,11... | collective-permute-start | bytes 9830408 | tf_op jit(solution)/shard_map/d0_c/ppermute | solution.py:902
  139.0 21.3 %collective-permute-start.25 = (bf16[320,640]{1,0:T(8,128)(2,1)S(1)}, bf16[320,640]{1,0:T(8,128)(2,1)S(1)}, u32[]{:S(2)}, u32[]{:S(2)}) collective-permute-start(bf16[320,640]{1,0:T(8,128)(2,1)S(1)} %copy-done.23), channel_id=1, source_target_pairs={{0,16},{8,24},{16,0},{24,8},{1,17},{9,25},{17,1},{25,9},{2,18},{10... | collective-permute-start | bytes 1228808 | tf_op jit(solution)/shard_map/d1_far/ppermute | solution.py:947
  161.3 22.4 %collective-permute-start.28 = (bf16[2,320,640]{2,1,0:T(8,128)(2,1)}, bf16[2,320,640]{2,1,0:T(8,128)(2,1)}, u32[]{:S(2)}, u32[]{:S(2)}) collective-permute-start(bf16[2,320,640]{2,1,0:T(8,128)(2,1)} %maximum_select_fusion.7), channel_id=1, source_target_pairs={{0,8},{8,0},{16,24},{24,16},{1,9},{9,1},{17,25},{25,17},{2,10},{10... | collective-permute-start | bytes 2457608 | tf_op jit(solution)/shard_map/d1_near/ppermute | solution.py:947
  161.3 16.1 %collective-permute-start.30 = (bf16[4,80,640]{2,1,0:T(8,128)(2,1)}, bf16[4,80,640]{2,1,0:T(8,128)(2,1)S(1)}, u32[]{:S(2)}, u32[]{:S(2)}) collective-permute-start(bf16[4,80,640]{2,1,0:T(8,128)(2,1)} %get-tuple-element.355), channel_id=1, source_target_pairs={{0,4},{4,0},{1,5},{5,1},{2,6},{6,2},{3,7},{7,3},{8,12},{12,8},{9,1... | collective-permute-start | bytes 1228808 | tf_op jit(solution)/shard_map/u10_y/ppermute | solution.py:902
  162.1 24.3 %collective-permute-start.27 = (bf16[2,4,80,640]{3,2,1,0:T(8,128)(2,1)}, bf16[2,4,80,640]{3,2,1,0:T(8,128)(2,1)}, u32[]{:S(2)}, u32[]{:S(2)}) collective-permute-start(bf16[2,4,80,640]{3,2,1,0:T(8,128)(2,1)} %pad_maximum_fusion.4.w0_ref), channel_id=1, source_target_pairs={{0,2},{2,0},{1,3},{3,1},{4,6},{6,4},{5,7},{7,5},{8,10},{10,8},{9,1... | collective-permute-start | bytes 2457608 | tf_op jit(solution)/shard_map/a1_x/ppermute | solution.py:902
  163.5 18.2 %collective-permute-start.29 = (bf16[4,80,640]{2,1,0:T(8,128)(2,1)}, bf16[4,80,640]{2,1,0:T(8,128)(2,1)S(1)}, u32[]{:S(2)}, u32[]{:S(2)}) collective-permute-start(bf16[4,80,640]{2,1,0:T(8,128)(2,1)} %get-tuple-element.357), channel_id=1, source_target_pairs={{0,4},{4,0},{1,5},{5,1},{2,6},{6,2},{3,7},{7,3},{8,12},{12,8},{9,1... | collective-permute-start | bytes 1228808 | tf_op jit(solution)/shard_map/u11_y/ppermute | solution.py:902
  166.5 23.2 %collective-permute-start.26 = (bf16[2,4,80,640]{3,2,1,0:T(8,128)(2,1)}, bf16[2,4,80,640]{3,2,1,0:T(8,128)(2,1)}, u32[]{:S(2)}, u32[]{:S(2)}) collective-permute-start(bf16[2,4,80,640]{3,2,1,0:T(8,128)(2,1)} %pad_maximum_fusion.4.w0_ref), channel_id=1, source_target_pairs={{0,1},{1,0},{2,3},{3,2},{4,5},{5,4},{6,7},{7,6},{8,9},{9,8},{10,11... | collective-permute-start | bytes 2457608 | tf_op jit(solution)/shard_map/a1_c/ppermute | solution.py:902
  186.5 21.2 %collective-permute-start.35 = (bf16[2,4,80,640]{3,2,1,0:T(8,128)(2,1)S(1)}, bf16[2,4,80,640]{3,2,1,0:T(8,128)(2,1)}, u32[]{:S(2)}, u32[]{:S(2)}) collective-permute-start(bf16[2,4,80,640]{3,2,1,0:T(8,128)(2,1)S(1)} %pad_maximum_fusion.6.refs_1_.u1_ref), channel_id=1, source_target_pairs={{0,2},{2,0},{1,3},{3,1},{4,6},{6,4},{5,7},{7,5},{8,10},{10,8},{9,1... | collective-permute-start | bytes 2457608 | tf_op jit(solution)/shard_map/u11_x/ppermute | solution.py:902
  188.0 36.9 %collective-permute-start.34 = (bf16[2,4,80,640]{3,2,1,0:T(8,128)(2,1)S(1)}, bf16[2,4,80,640]{3,2,1,0:T(8,128)(2,1)}, u32[]{:S(2)}, u32[]{:S(2)}) collective-permute-start(bf16[2,4,80,640]{3,2,1,0:T(8,128)(2,1)S(1)} %pad_maximum_fusion.5.refs_0_.u0_ref), channel_id=1, source_target_pairs={{0,2},{2,0},{1,3},{3,1},{4,6},{6,4},{5,7},{7,5},{8,10},{10,8},{9,1... | collective-permute-start | bytes 2457608 | tf_op jit(solution)/shard_map/u10_x/ppermute | solution.py:902
  188.6 50.4 %collective-permute-start.38 = (bf16[4,320,640]{2,1,0:T(8,128)(2,1)S(1)}, bf16[4,320,640]{2,1,0:T(8,128)(2,1)}, u32[]{:S(2)}, u32[]{:S(2)}) collective-permute-start(bf16[4,320,640]{2,1,0:T(8,128)(2,1)S(1)} %bitcast.254), channel_id=1, source_target_pairs={{0,4},{4,0},{1,5},{5,1},{2,6},{6,2},{3,7},{7,3},{8,12},{12,8},{9,1... | collective-permute-start | bytes 4915208 | tf_op jit(solution)/shard_map/d1_y/ppermute | solution.py:902
  189.7 35.7 %collective-permute-start.33 = (bf16[2,4,80,640]{3,2,1,0:T(8,128)(2,1)S(1)}, bf16[2,4,80,640]{3,2,1,0:T(8,128)(2,1)}, u32[]{:S(2)}, u32[]{:S(2)}) collective-permute-start(bf16[2,4,80,640]{3,2,1,0:T(8,128)(2,1)S(1)} %pad_maximum_fusion.6.refs_1_.u1_ref), channel_id=1, source_target_pairs={{0,1},{1,0},{2,3},{3,2},{4,5},{5,4},{6,7},{7,6},{8,9},{9,8},{10,11... | collective-permute-start | bytes 2457608 | tf_op jit(solution)/shard_map/u11_c/ppermute | solution.py:902
  189.7 35.7 %collective-permute-start.32 = (bf16[2,4,80,640]{3,2,1,0:T(8,128)(2,1)S(1)}, bf16[2,4,80,640]{3,2,1,0:T(8,128)(2,1)}, u32[]{:S(2)}, u32[]{:S(2)}) collective-permute-start(bf16[2,4,80,640]{3,2,1,0:T(8,128)(2,1)S(1)} %pad_maximum_fusion.5.refs_0_.u0_ref), channel_id=1, source_target_pairs={{0,1},{1,0},{2,3},{3,2},{4,5},{5,4},{6,7},{7,6},{8,9},{9,8},{10,11... | collective-permute-start | bytes 2457608 | tf_op jit(solution)/shard_map/u10_c/ppermute | solution.py:902
  207.7 17.7 %collective-permute-start.37 = (bf16[2,4,80,640]{3,2,1,0:T(8,128)(2,1)}, bf16[2,4,80,640]{3,2,1,0:T(8,128)(2,1)}, u32[]{:S(2)}, u32[]{:S(2)}) collective-permute-start(bf16[2,4,80,640]{3,2,1,0:T(8,128)(2,1)} %collective-permute-done.35.refs_5_.u3_ref), channel_id=1, source_target_pairs={{0,1},{1,0},{2,3},{3,2},{4,5},{5,4},{6,7},{7,6},{8,9},{9,8},{10,11... | collective-permute-start | bytes 2457608 | tf_op jit(solution)/shard_map/u11_xc/ppermute | solution.py:902
  280.0 16.4 %collective-permute-start.42 = (bf16[4,320,640]{2,1,0:T(8,128)(2,1)}, bf16[4,320,640]{2,1,0:T(8,128)(2,1)}, u32[]{:S(2)}, u32[]{:S(2)}) collective-permute-start(bf16[4,320,640]{2,1,0:T(8,128)(2,1)} %get-tuple-element.401), channel_id=1, source_target_pairs={{0,1},{1,0},{2,3},{3,2},{4,5},{5,4},{6,7},{7,6},{8,9},{9,8},{10,11... | collective-permute-start | bytes 4915208 | tf_op jit(solution)/shard_map/d1_c1/ppermute | solution.py:902
  296.2 47.7 %collective-permute-start.48 = (bf16[4,320,640]{2,1,0:T(8,128)(2,1)}, bf16[4,320,640]{2,1,0:T(8,128)(2,1)}, u32[]{:S(2)}, u32[]{:S(2)}) collective-permute-start(bf16[4,320,640]{2,1,0:T(8,128)(2,1)} %get-tuple-element.431), channel_id=1, source_target_pairs={{0,1},{1,0},{2,3},{3,2},{4,5},{5,4},{6,7},{7,6},{8,9},{9,8},{10,11... | collective-permute-start | bytes 4915208 | tf_op jit(solution)/shard_map/d1_c0/ppermute | solution.py:902
  299.3 44.8 %collective-permute-start.49 = (bf16[4,320,640]{2,1,0:T(8,128)(2,1)}, bf16[4,320,640]{2,1,0:T(8,128)(2,1)}, u32[]{:S(2)}, u32[]{:S(2)}) collective-permute-start(bf16[4,320,640]{2,1,0:T(8,128)(2,1)} %fusion.5), channel_id=1, source_target_pairs={{0,4},{4,0},{1,5},{5,1},{2,6},{6,2},{3,7},{7,3},{8,12},{12,8},{9,1... | collective-permute-start | bytes 4915208 | tf_op jit(solution)/shard_map/d1_y/ppermute | solution.py:902
  320.9 38.9 %collective-permute-start.43 = (bf16[2,4,2,80,640]{4,3,2,1,0:T(8,128)(2,1)}, bf16[2,4,2,80,640]{4,3,2,1,0:T(8,128)(2,1)}, u32[]{:S(2)}, u32[]{:S(2)}) collective-permute-start(bf16[2,4,2,80,640]{4,3,2,1,0:T(8,128)(2,1)} %get-tuple-element.418), channel_id=1, source_target_pairs={{0,2},{2,0},{1,3},{3,1},{4,6},{6,4},{5,7},{7,5},{8,10},{10,8},{9,1... | collective-permute-start | bytes 4915208 | tf_op jit(solution)/shard_map/u1_x/ppermute | solution.py:902
  348.1 155.3 %reduce-scatter.12.cloned.1.call-start = ((), (), s32[]{:S(2)}) async-start(), calls=%async_computation.8 | async-start | bytes 512000 | tf_op jit(solution)/shard_map/reduce_scatter | solution.py:1031
  373.8 23.0 %collective-permute-start.53 = (bf16[4,320,640]{2,1,0:T(8,128)(2,1)}, bf16[4,320,640]{2,1,0:T(8,128)(2,1)}, u32[]{:S(2)}, u32[]{:S(2)}) collective-permute-start(bf16[4,320,640]{2,1,0:T(8,128)(2,1)} %get-tuple-element.445), channel_id=1, source_target_pairs={{0,1},{1,0},{2,3},{3,2},{4,5},{5,4},{6,7},{7,6},{8,9},{9,8},{10,11... | collective-permute-start | bytes 4915208 | tf_op jit(solution)/shard_map/d0_c1/ppermute | solution.py:902
  373.9 21.0 %collective-permute-start.54 = (bf16[2,4,80,640]{3,2,1,0:T(8,128)(2,1)}, bf16[2,4,80,640]{3,2,1,0:T(8,128)(2,1)}, u32[]{:S(2)}, u32[]{:S(2)}) collective-permute-start(bf16[2,4,80,640]{3,2,1,0:T(8,128)(2,1)} %get-tuple-element.441), channel_id=1, source_target_pairs={{0,2},{2,0},{1,3},{3,1},{4,6},{6,4},{5,7},{7,5},{8,10},{10,8},{9,1... | collective-permute-start | bytes 2457608 | tf_op jit(solution)/shard_map/a1_x/ppermute | solution.py:902
  390.9 25.1 %collective-permute-start.50 = (bf16[2,4,2,80,640]{4,3,2,1,0:T(8,128)(2,1)}, bf16[2,4,2,80,640]{4,3,2,1,0:T(8,128)(2,1)}, u32[]{:S(2)}, u32[]{:S(2)}) collective-permute-start(bf16[2,4,2,80,640]{4,3,2,1,0:T(8,128)(2,1)} %get-tuple-element.450), channel_id=1, source_target_pairs={{0,1},{1,0},{2,3},{3,2},{4,5},{5,4},{6,7},{7,6},{8,9},{9,8},{10,11... | collective-permute-start | bytes 4915208 | tf_op jit(solution)/shard_map/u0_c1/ppermute | solution.py:902
  391.2 24.8 %collective-permute-start.51 = (bf16[2,4,2,80,640]{4,3,2,1,0:T(8,128)(2,1)}, bf16[2,4,2,80,640]{4,3,2,1,0:T(8,128)(2,1)}, u32[]{:S(2)}, u32[]{:S(2)}) collective-permute-start(bf16[2,4,2,80,640]{4,3,2,1,0:T(8,128)(2,1)} %get-tuple-element.451), channel_id=1, source_target_pairs={{0,1},{1,0},{2,3},{3,2},{4,5},{5,4},{6,7},{7,6},{8,9},{9,8},{10,11... | collective-permute-start | bytes 4915208 | tf_op jit(solution)/shard_map/u0_c0/ppermute | solution.py:902
  391.5 21.4 %collective-permute-start.52 = (bf16[4,2,80,640]{3,2,1,0:T(8,128)(2,1)}, bf16[4,2,80,640]{3,2,1,0:T(8,128)(2,1)}, u32[]{:S(2)}, u32[]{:S(2)}) collective-permute-start(bf16[4,2,80,640]{3,2,1,0:T(8,128)(2,1)} %fusion.8), channel_id=1, source_target_pairs={{0,4},{4,0},{1,5},{5,1},{2,6},{6,2},{3,7},{7,3},{8,12},{12,8},{9,1... | collective-permute-start | bytes 2457608 | tf_op jit(solution)/shard_map/u1_y/ppermute | solution.py:902
  394.9 75.4 %collective-permute-start.59 = (bf16[4,320,640]{2,1,0:T(8,128)(2,1)}, bf16[4,320,640]{2,1,0:T(8,128)(2,1)}, u32[]{:S(2)}, u32[]{:S(2)}) collective-permute-start(bf16[4,320,640]{2,1,0:T(8,128)(2,1)} %get-tuple-element.498), channel_id=1, source_target_pairs={{0,1},{1,0},{2,3},{3,2},{4,5},{5,4},{6,7},{7,6},{8,9},{9,8},{10,11... | collective-permute-start | bytes 4915208 | tf_op jit(solution)/shard_map/d0_c0/ppermute | solution.py:902
  396.9 38.4 %collective-permute-start.55 = (bf16[4,80,640]{2,1,0:T(8,128)(2,1)}, bf16[4,80,640]{2,1,0:T(8,128)(2,1)}, u32[]{:S(2)}, u32[]{:S(2)}) collective-permute-start(bf16[4,80,640]{2,1,0:T(8,128)(2,1)} %fusion.13), channel_id=1, source_target_pairs={{0,4},{4,0},{1,5},{5,1},{2,6},{6,2},{3,7},{7,3},{8,12},{12,8},{9,1... | collective-permute-start | bytes 1228808 | tf_op jit(solution)/shard_map/a1_y/ppermute | solution.py:902
  412.9 57.7 %collective-permute-start.60 = (bf16[4,320,640]{2,1,0:T(8,128)(2,1)}, bf16[4,320,640]{2,1,0:T(8,128)(2,1)}, u32[]{:S(2)}, u32[]{:S(2)}) collective-permute-start(bf16[4,320,640]{2,1,0:T(8,128)(2,1)} %fusion.2), channel_id=1, source_target_pairs={{0,4},{4,0},{1,5},{5,1},{2,6},{6,2},{3,7},{7,3},{8,12},{12,8},{9,1... | collective-permute-start | bytes 4915208 | tf_op jit(solution)/shard_map/d0_y/ppermute | solution.py:902
  435.0 49.1 %collective-permute-start.56 = (bf16[2,4,2,80,640]{4,3,2,1,0:T(8,128)(2,1)}, bf16[2,4,2,80,640]{4,3,2,1,0:T(8,128)(2,1)}, u32[]{:S(2)}, u32[]{:S(2)}) collective-permute-start(bf16[2,4,2,80,640]{4,3,2,1,0:T(8,128)(2,1)} %get-tuple-element.468), channel_id=1, source_target_pairs={{0,2},{2,0},{1,3},{3,1},{4,6},{6,4},{5,7},{7,5},{8,10},{10,8},{9,1... | collective-permute-start | bytes 4915208 | tf_op jit(solution)/shard_map/u0_x/ppermute | solution.py:902
  457.6 45.9 %reduce-scatter.10.cloned.1.call-start = ((), (), s32[]{:S(2)}) async-start(), calls=%async_computation.7 | async-start | bytes 1024000 | tf_op jit(solution)/shard_map/reduce_scatter | solution.py:1031
  458.4 100.2 %reduce-scatter.8.cloned.1.call-start = ((), (), s32[]{:S(2)}) async-start(), calls=%async_computation.6 | async-start | bytes 1024000 | tf_op jit(solution)/shard_map/reduce_scatter | solution.py:1031
  462.2 20.7 %collective-permute-start.57 = (bf16[320,640]{1,0:T(8,128)(2,1)}, bf16[320,640]{1,0:T(8,128)(2,1)}, u32[]{:S(2)}, u32[]{:S(2)}) collective-permute-start(bf16[320,640]{1,0:T(8,128)(2,1)} %bitcast.283), channel_id=1, source_target_pairs={{0,2},{2,0},{1,3},{3,1},{4,6},{6,4},{5,7},{7,5},{8,10},{10,8},{9,1... | collective-permute-start | bytes 1228808 | tf_op jit(solution)/shard_map/d1_x/ppermute | solution.py:902
  470.3 27.3 %collective-permute-start.66 = (bf16[2,4,80,640]{3,2,1,0:T(8,128)(2,1)}, bf16[2,4,80,640]{3,2,1,0:T(8,128)(2,1)}, u32[]{:S(2)}, u32[]{:S(2)}) collective-permute-start(bf16[2,4,80,640]{3,2,1,0:T(8,128)(2,1)} %get-tuple-element.510), channel_id=1, source_target_pairs={{0,2},{2,0},{1,3},{3,1},{4,6},{6,4},{5,7},{7,5},{8,10},{10,8},{9,1... | collective-permute-start | bytes 2457608 | tf_op jit(solution)/shard_map/a0_x/ppermute | solution.py:902
  485.8 14.7 %collective-permute-start.65 = (bf16[4,2,80,640]{3,2,1,0:T(8,128)(2,1)S(1)}, bf16[4,2,80,640]{3,2,1,0:T(8,128)(2,1)S(1)}, u32[]{:S(2)}, u32[]{:S(2)}) collective-permute-start(bf16[4,2,80,640]{3,2,1,0:T(8,128)(2,1)S(1)} %fusion.9), channel_id=1, source_target_pairs={{0,4},{4,0},{1,5},{5,1},{2,6},{6,2},{3,7},{7,3},{8,12},{12,8},{9,1... | collective-permute-start | bytes 2457608 | tf_op jit(solution)/shard_map/u0_y/ppermute | solution.py:902
  502.9 72.2 %reduce-scatter.14.cloned.1.call-start = ((), (), s32[]{:S(2)}) async-start(), calls=%async_computation.9 | async-start | bytes 2048000 | tf_op jit(solution)/shard_map/reduce_scatter | solution.py:1031
  505.4 18.5 %collective-permute-start.68 = (f32[88,640]{1,0:T(8,128)S(1)}, f32[88,640]{1,0:T(8,128)S(1)}, u32[]{:S(2)}, u32[]{:S(2)}) collective-permute-start(f32[88,640]{1,0:T(8,128)S(1)} %add.175), channel_id=1, source_target_pairs={{0,16},{8,24},{16,0},{24,8},{1,17},{9,25},{17,1},{25,9},{2,18},{10... | collective-permute-start | bytes 675848 | tf_op jit(solution)/shard_map/small_next/ppermute | solution.py:947
  506.3 19.6 %collective-permute-start.80 = (bf16[320,640]{1,0:T(8,128)(2,1)S(1)}, bf16[320,640]{1,0:T(8,128)(2,1)}, u32[]{:S(2)}, u32[]{:S(2)}) collective-permute-start(bf16[320,640]{1,0:T(8,128)(2,1)S(1)} %add_convert_fusion.4), channel_id=1, source_target_pairs={{0,1},{1,0},{2,3},{3,2},{4,5},{5,4},{6,7},{7,6},{8,9},{9,8},{10,11... | collective-permute-start | bytes 1228808 | tf_op jit(solution)/shard_map/d1_c/ppermute | solution.py:902
  506.3 28.7 %collective-permute-start.67 = (bf16[4,80,640]{2,1,0:T(8,128)(2,1)S(1)}, bf16[4,80,640]{2,1,0:T(8,128)(2,1)S(1)}, u32[]{:S(2)}, u32[]{:S(2)}) collective-permute-start(bf16[4,80,640]{2,1,0:T(8,128)(2,1)S(1)} %fusion.14), channel_id=1, source_target_pairs={{0,4},{4,0},{1,5},{5,1},{2,6},{6,2},{3,7},{7,3},{8,12},{12,8},{9,1... | collective-permute-start | bytes 1228808 | tf_op jit(solution)/shard_map/a0_y/ppermute | solution.py:902
  513.5 23.3 %collective-permute-start.72 = (bf16[2,3,80,640]{3,2,1,0:T(8,128)(2,1)}, bf16[2,3,80,640]{3,2,1,0:T(8,128)(2,1)}, u32[]{:S(2)}, u32[]{:S(2)}) collective-permute-start(bf16[2,3,80,640]{3,2,1,0:T(8,128)(2,1)} %copy.106), channel_id=1, source_target_pairs={{0,1},{1,0},{2,3},{3,2},{4,5},{5,4},{6,7},{7,6},{8,9},{9,8},{10,11... | collective-permute-start | bytes 1843208 | tf_op jit(solution)/shard_map/last1_c/ppermute | solution.py:902
  524.0 10.7 %collective-permute-start.69 = (f32[88,640]{1,0:T(8,128)S(1)}, f32[88,640]{1,0:T(8,128)S(1)}, u32[]{:S(2)}, u32[]{:S(2)}) collective-permute-start(f32[88,640]{1,0:T(8,128)S(1)} %add.182), channel_id=1, source_target_pairs={{0,8},{8,0},{16,24},{24,16},{1,9},{9,1},{17,25},{25,17},{2,10},{10... | collective-permute-start | bytes 675848 | tf_op jit(solution)/shard_map/small_next/ppermute | solution.py:947
  534.7 11.1 %collective-permute-start.76 = (f32[88,640]{1,0:T(8,128)S(1)}, f32[88,640]{1,0:T(8,128)S(1)}, u32[]{:S(2)}, u32[]{:S(2)}) collective-permute-start(f32[88,640]{1,0:T(8,128)S(1)} %add.183), channel_id=1, source_target_pairs={{0,2},{2,0},{1,3},{3,1},{4,6},{6,4},{5,7},{7,5},{8,10},{10,8},{9,1... | collective-permute-start | bytes 675848 | tf_op jit(solution)/shard_map/small_next/ppermute | solution.py:902
  543.8 14.8 %collective-permute-start.73 = (bf16[80,640]{1,0:T(8,128)(2,1)}, bf16[80,640]{1,0:T(8,128)(2,1)}, u32[]{:S(2)}, u32[]{:S(2)}) collective-permute-start(bf16[80,640]{1,0:T(8,128)(2,1)} %get-tuple-element.642), channel_id=1, source_target_pairs={{0,16},{8,24},{16,0},{24,8},{1,17},{9,25},{17,1},{25,9},{2,18},{10... | collective-permute-start | bytes 307208 | tf_op jit(solution)/shard_map/a0_far/ppermute | solution.py:947
  545.9 41.8 %collective-permute-start.79 = (f32[88,640]{1,0:T(8,128)S(1)}, f32[88,640]{1,0:T(8,128)}, u32[]{:S(2)}, u32[]{:S(2)}) collective-permute-start(f32[88,640]{1,0:T(8,128)S(1)} %add.193), channel_id=1, source_target_pairs={{0,4},{4,0},{1,5},{5,1},{2,6},{6,2},{3,7},{7,3},{8,12},{12,8},{9,1... | collective-permute-start | bytes 675848 | tf_op jit(solution)/shard_map/small_next/ppermute | solution.py:902
  560.5 18.8 %collective-permute-start.74 = (bf16[3,80,640]{2,1,0:T(8,128)(2,1)S(1)}, bf16[3,80,640]{2,1,0:T(8,128)(2,1)S(1)}, u32[]{:S(2)}, u32[]{:S(2)}) collective-permute-start(bf16[3,80,640]{2,1,0:T(8,128)(2,1)S(1)} %pad_maximum_fusion.14), channel_id=1, source_target_pairs={{0,2},{2,0},{1,3},{3,1},{4,6},{6,4},{5,7},{7,5},{8,10},{10,8},{9,1... | collective-permute-start | bytes 921608 | tf_op jit(solution)/shard_map/last0_x/ppermute | solution.py:902
  575.1 11.6 %collective-permute-start.77 = (bf16[320,640]{1,0:T(8,128)(2,1)}, bf16[320,640]{1,0:T(8,128)(2,1)S(1)}, u32[]{:S(2)}, u32[]{:S(2)}) collective-permute-start(bf16[320,640]{1,0:T(8,128)(2,1)} %bitcast.285), channel_id=1, source_target_pairs={{0,2},{2,0},{1,3},{3,1},{4,6},{6,4},{5,7},{7,5},{8,10},{10,8},{9,1... | collective-permute-start | bytes 1228808 | tf_op jit(solution)/shard_map/d0_x/ppermute | solution.py:902
  579.5 16.9 %collective-permute-start.75 = (bf16[2,3,80,640]{3,2,0,1:T(8,128)(2,1)S(1)}, bf16[2,3,80,640]{3,2,0,1:T(8,128)(2,1)S(1)}, u32[]{:S(2)}, u32[]{:S(2)}) collective-permute-start(bf16[2,3,80,640]{3,2,0,1:T(8,128)(2,1)S(1)} %copy.109), channel_id=1, source_target_pairs={{0,1},{1,0},{2,3},{3,2},{4,5},{5,4},{6,7},{7,6},{8,9},{9,8},{10,11... | collective-permute-start | bytes 1843208 | tf_op jit(solution)/shard_map/last0_c/ppermute | solution.py:902
  589.8 22.6 %collective-permute-start.78 = (bf16[320,640]{1,0:T(8,128)(2,1)}, bf16[320,640]{1,0:T(8,128)(2,1)}, u32[]{:S(2)}, u32[]{:S(2)}) collective-permute-start(bf16[320,640]{1,0:T(8,128)(2,1)} %add_convert_fusion.2), channel_id=1, source_target_pairs={{0,1},{1,0},{2,3},{3,2},{4,5},{5,4},{6,7},{7,6},{8,9},{9,8},{10,11... | collective-permute-start | bytes 1228808 | tf_op jit(solution)/shard_map/d0_c/ppermute | solution.py:902
  (71 other events, 651.1 us)
Sparse Core Ops, SparseCore 0:
  348.3 33.8 reduce-scatter.5
  457.7 20.8 reduce-scatter.11
  480.9 21.9 reduce-scatter.9
  505.6 27.0 reduce-scatter.7
  535.5 39.5 reduce-scatter.13

commit v4 on v1

v4 whole, which is shorter than its diff:
```python
import math

import jax
import jax.numpy as jnp
from jax import lax
from jax.experimental import pallas as pl
from jax.experimental.pallas import tpu as pltpu
from jax.sharding import Mesh
from jax.sharding import PartitionSpec as P

D = 640
HEADS = 20
HEAD_DIM = 32
FF = 5120
VOCAB = 25
LAYERS = 2
LEN = 128
SEQ_DEV = 4
ROWS = SEQ_DEV * LEN
TILE = 640
TILES = FF // TILE
WIDE = 2 * TILE
STEPS = FF // WIDE
GROUPS = HEADS * HEAD_DIM // 128
PER_GROUP = 128 // HEAD_DIM
CHUNK = 128
CHUNKS = ROWS // CHUNK
SHARD = D // 8
HALF = TILE // 2
BF = jnp.bfloat16
F32 = jnp.float32
MIB = 2**20

SMEM_SPEC = pl.BlockSpec(memory_space=pltpu.SMEM)
ANY_SPEC = pl.BlockSpec(memory_space=pl.ANY)
KERNEL = dict(
    compiler_params=pltpu.CompilerParams(vmem_limit_bytes=60 * MIB),
    cost_estimate=pl.CostEstimate(flops=4 * 10**8, bytes_accessed=2 * MIB, transcendentals=0),
)


def dot(left, right, dims):
    return lax.dot_general(left, right, (dims, ((), ())), preferred_element_type=F32)


def mul_nn(left, right):
    return dot(left, right, ((1,), (0,)))


def mul_nt(left, right):
    return dot(left, right, ((1,), (1,)))


def mul_tn(left, right):
    return dot(left, right, ((0,), (0,)))


def normalize(values):
    centered = values - jnp.mean(values, -1, keepdims=True)
    inverse = lax.rsqrt(jnp.mean(centered * centered, -1, keepdims=True) + 1e-05)
    return (centered * inverse, inverse)


def norm_back(grad_normed, normed, inverse):
    return inverse * (
        grad_normed
        - jnp.mean(grad_normed, -1, keepdims=True)
        - normed * jnp.mean(grad_normed * normed, -1, keepdims=True)
    )


def col_sum(values):
    return jnp.sum(values, 0, keepdims=True)


def sds(shape, dtype):
    return jax.ShapeDtypeStruct(shape, dtype)


def whole_block(shape):
    zeros = (0,) * len(shape)
    return pl.BlockSpec(shape, lambda *_: zeros)


def semaphores(*shape):
    return pltpu.SemaphoreType.DMA(shape)


def copy(source, target, semaphore):
    return pltpu.make_async_copy(source, target, semaphore)


def chunk_rows(index):
    return slice(index * CHUNK, (index + 1) * CHUNK)


def over_chunks(body, start):
    def step(index, carry):
        return body(pl.ds(pl.multiple_of(index * CHUNK, CHUNK), CHUNK), carry)

    return lax.fori_loop(0, CHUNKS, step, start)


def quarter_copies(place_ref, buffers, held, sems):
    x_at, y_at, c_at = place_ref[0], place_ref[1], place_ref[2]
    copies = []
    for number, buffer in enumerate(buffers):
        dx, dc, dy = number // 4, number // 2 % 2, number % 2
        quarter = (x_at ^ dx) * 2 + (c_at ^ dc)
        lanes = pl.ds(pl.multiple_of(quarter * D, 128), D)
        copies.append(copy(buffer.at[:, 0], held.at[:, y_at ^ dy, :, lanes], sems.at[number]))
    return copies


def square(values):
    return values.reshape(D, values.shape[-1])


def head_masks():
    lanes = lax.broadcasted_iota(jnp.int32, (LEN, 128), 1) // HEAD_DIM
    return [(lanes == member) for member in range(PER_GROUP)]


def stack_heads(values, masks):
    zero = jnp.zeros_like(values)
    return jnp.concatenate([jnp.where(mask, values, zero) for mask in masks], 0)


def unstack_heads(values):
    parts = [
        values[HEAD_DIM * member : HEAD_DIM * (member + 1), LEN * member : LEN * (member + 1)]
        for member in range(PER_GROUP)
    ]
    return jnp.concatenate(parts, 0).T


def scores_of(keys, queries, valid):
    scores = mul_nt(keys, queries) * (1.0 / math.sqrt(HEAD_DIM))
    return jnp.where(valid, scores, -1e30)


def mix_kernel(place_ref, lengths_ref, residual_ref, *refs):
    buffers, refs = refs[:8], refs[8:]
    gains_ref, biases_ref, packed_out, log_ref, mixed_out, middle_out, second_out, *refs = refs
    held, pre, packed, mixed, middles, seconds, sems, out_sems, row_sems = refs
    copies = quarter_copies(place_ref, buffers, held, sems)
    for one in copies:
        one.start()

    def first(rows, carry):
        normed, inverse = normalize(residual_ref[rows, :].astype(F32))
        pre[rows, :] = (normed * gains_ref[0:1, :] + biases_ref[0:1, :]).astype(BF)
        return carry

    over_chunks(first, 0)
    for one in copies:
        one.wait()
    shifts = (biases_ref[2:3, :], 0.0, biases_ref[3:4, :])
    sent = []
    result = mul_nn(pre[...], square(held[:, :, :, : 3 * D]))
    for part in range(3):
        lanes = slice(part * D, (part + 1) * D)
        packed[:, lanes] = (result[:, lanes] + shifts[part]).astype(BF)
        sent.append(copy(packed.at[:, lanes], packed_out.at[:, lanes], out_sems.at[part]))
        sent[-1].start()
    masks = head_masks()
    row_ids = lax.broadcasted_iota(jnp.int32, (LEN, 1), 0)

    def one_sequence(seq, carry):
        rows = pl.ds(pl.multiple_of(seq * LEN, LEN), LEN)
        valid = row_ids < lengths_ref[seq]
        for group in range(GROUPS):
            lanes = slice(group * 128, (group + 1) * 128)
            queries = stack_heads(packed[rows, lanes], masks)
            key_rows = packed[rows, D + group * 128 : D + (group + 1) * 128]
            value_rows = packed[rows, 2 * D + group * 128 : 2 * D + (group + 1) * 128]
            scores = scores_of(key_rows, queries, valid)
            top = jnp.max(scores, 0, keepdims=True)
            expos = jnp.exp(scores - top)
            total = jnp.sum(expos, 0, keepdims=True)
            probs = (expos * (1.0 / total)).astype(BF)
            log_ref[seq * GROUPS + group] = top + jnp.log(total)
            mixed[rows, lanes] = unstack_heads(mul_tn(value_rows, probs)).astype(BF)
        return carry

    lax.fori_loop(0, SEQ_DEV, one_sequence, 0)
    sent.append(copy(mixed, mixed_out, out_sems.at[3]))
    sent[-1].start()
    middles[...] = mul_nn(mixed[...], square(held[:, :, :, 3 * D :])) + biases_ref[4:5, :]
    for index in range(CHUNKS):
        rows = chunk_rows(index)
        middle = middles[rows, :] + residual_ref[rows, :].astype(F32)
        middles[rows, :] = middle
        normed, inverse = normalize(middle)
        seconds[rows, :] = (normed * gains_ref[1:2, :] + biases_ref[1:2, :]).astype(BF)
        sent.append(copy(middles.at[rows, :], middle_out.at[rows, :], row_sems.at[index, 0]))
        sent[-1].start()
        sent.append(copy(seconds.at[rows, :], second_out.at[rows, :], row_sems.at[index, 1]))
        sent[-1].start()
    for one in sent:
        one.wait()


def mix(place, lengths, residual, quarters, gains, biases):
    logs = (SEQ_DEV * GROUPS, 1, PER_GROUP * LEN)
    return pl.pallas_call(
        mix_kernel,
        grid=(1,),
        out_shape=(
            sds((ROWS, 3 * D), BF),
            sds(logs, F32),
            sds((ROWS, D), BF),
            sds((ROWS, D), F32),
            sds((ROWS, D), BF),
        ),
        in_specs=[SMEM_SPEC, SMEM_SPEC, whole_block((ROWS, D))]
        + [ANY_SPEC] * 8
        + [whole_block((2, D)), whole_block((6, D))],
        out_specs=(ANY_SPEC, whole_block(logs), ANY_SPEC, ANY_SPEC, ANY_SPEC),
        scratch_shapes=[
            pltpu.VMEM((4, 2, SHARD, 4 * D), BF),
            pltpu.VMEM((ROWS, D), BF),
            pltpu.VMEM((ROWS, 3 * D), BF),
            pltpu.VMEM((ROWS, D), BF),
            pltpu.VMEM((ROWS, D), F32),
            pltpu.VMEM((ROWS, D), BF),
            semaphores(8),
            semaphores(4),
            semaphores(CHUNKS, 2),
        ],
        **KERNEL,
    )(place, lengths, residual, *quarters, gains, biases)


def up_kernel(place_ref, second_ref, *refs):
    buffers, refs = refs[:8], refs[8:]
    shift_ref, active_out, slope_out, held, actives, slopes, sems, out_sems = refs
    step = pl.program_id(0)

    @pl.when(step == 0)
    def _():
        for number, buffer in enumerate(buffers):
            dx, dc, dy = number // 4, number // 2 % 2, number % 2
            at = (place_ref[0] ^ dx) * 2 + (place_ref[2] ^ dc)
            for half in range(2):
                target = held.at[at, :, place_ref[1] ^ dy, :, half * TILE : (half + 1) * TILE]
                copy(buffer.at[:, half], target, sems.at[at, dy, half]).start()

    for dy in range(2):
        for half in range(2):
            target = held.at[step, :, dy, :, half * TILE : (half + 1) * TILE]
            copy(buffers[0].at[:, 0], target, sems.at[step, dy, half]).wait()
    up_tile = square(held[step])
    shift = shift_ref[pl.ds(step, 1), :]
    for index in range(2):
        rows = slice(index * 2 * CHUNK, (index + 1) * 2 * CHUNK)
        hidden = mul_nn(second_ref[rows, :], up_tile) + shift
        phi = 0.5 + 0.5 * lax.erf(hidden * math.sqrt(0.5))
        density = jnp.exp(hidden * hidden * -0.5) * (1.0 / math.sqrt(2.0 * math.pi))
        actives[step, rows, :] = (hidden * phi).astype(BF)
        slopes[step, rows, :] = (phi + hidden * density).astype(BF)
    copy(actives.at[step], active_out.at[step], out_sems.at[step, 0]).start()
    copy(slopes.at[step], slope_out.at[step], out_sems.at[step, 1]).start()

    @pl.when(step == STEPS - 1)
    def _():
        for at in range(STEPS):
            copy(actives.at[at], active_out.at[at], out_sems.at[at, 0]).wait()
            copy(slopes.at[at], slope_out.at[at], out_sems.at[at, 1]).wait()


def up(place, second, parts, shift):
    out = sds((STEPS, ROWS, WIDE), BF)
    return pl.pallas_call(
        up_kernel,
        grid=(STEPS,),
        out_shape=(out, out),
        in_specs=[SMEM_SPEC, whole_block((ROWS, D))]
        + [ANY_SPEC] * 8
        + [whole_block((STEPS, WIDE))],
        out_specs=(ANY_SPEC, ANY_SPEC),
        scratch_shapes=[
            pltpu.VMEM((STEPS, 4, 2, SHARD, WIDE), BF),
            pltpu.VMEM((STEPS, ROWS, WIDE), BF),
            pltpu.VMEM((STEPS, ROWS, WIDE), BF),
            semaphores(STEPS, 2, 2),
            semaphores(STEPS, 2),
        ],
        **KERNEL,
    )(place, second, *parts, shift)


def down_kernel(place_ref, middle_ref, active_ref, *refs):
    buffers, (biases_ref, out_ref, held, rows, sems, row_sems) = refs[:8], refs[8:]
    step = pl.program_id(0)

    @pl.when(step == 0)
    def _():
        for z_at in range(4):
            for number in range(4):
                dc, dy = number // 2, number % 2
                y_at, c_at = place_ref[1] ^ dy, place_ref[2] ^ dc
                buffer = buffers[dc * 4 + dy * 2 + z_at // 2].at[z_at % 2]
                copy(buffer, held.at[z_at, y_at, c_at], sems.at[z_at, y_at, c_at]).start()
            copy(active_ref.at[z_at], rows.at[z_at], row_sems.at[z_at]).start()
        out_ref[...] = middle_ref[...] + biases_ref[5:6, :]

    for y_at in range(2):
        for c_at in range(2):
            copy(buffers[0].at[0], held.at[step, y_at, c_at], sems.at[step, y_at, c_at]).wait()
    copy(active_ref.at[0], rows.at[step], row_sems.at[step]).wait()
    out_ref[...] += mul_nn(rows[step], held[step].reshape(WIDE, D))


def down(place, middle, active, parts, biases):
    return pl.pallas_call(
        down_kernel,
        grid=(STEPS,),
        out_shape=sds((ROWS, D), F32),
        in_specs=[SMEM_SPEC, whole_block((ROWS, D))] + [ANY_SPEC] * 9 + [whole_block((6, D))],
        out_specs=whole_block((ROWS, D)),
        scratch_shapes=[
            pltpu.VMEM((4, 2, 2, HALF, D), BF),
            pltpu.VMEM((STEPS, ROWS, WIDE), BF),
            semaphores(4, 2, 2),
            semaphores(STEPS),
        ],
        **KERNEL,
    )(place, middle, active, *parts, biases)


def head_kernel(
    residual_ref,
    targets_ref,
    masked_ref,
    weight_ref,
    shift_ref,
    gain_ref,
    move_ref,
    activations_ref,
    grad_ref,
    rounded_ref,
    small_ref,
):
    small_ref[...] = jnp.zeros_like(small_ref)
    lanes = lax.broadcasted_iota(jnp.int32, (1, 128), 1)

    def body(rows, carry):
        weight_grad, gain_grad, move_grad, shift_grad, stats = carry
        residual = residual_ref[rows, :]
        activations_ref[rows, :] = residual.astype(BF)
        normed, inverse = normalize(residual)
        final = (normed * gain_ref[...] + move_ref[...]).astype(BF)
        logits = mul_nn(final, weight_ref[...]) + shift_ref[...]
        top = jnp.max(logits, -1, keepdims=True)
        log_total = top + jnp.log(jnp.sum(jnp.exp(logits - top), -1, keepdims=True))
        onehot = (targets_ref[rows, :] == lanes).astype(F32)
        picked = jnp.sum(logits * onehot, -1, keepdims=True)
        mask = masked_ref[rows, :].astype(F32)
        loss = col_sum(mask * (log_total - picked))
        hits = col_sum(mask * jnp.exp(picked - log_total))
        count = col_sum(mask)
        stats = stats + (
            jnp.where(lanes == 0, loss, 0.0)
            + jnp.where(lanes == 1, hits, 0.0)
            + jnp.where(lanes == 2, count, 0.0)
        )
        grad_logits = (mask * (jnp.exp(logits - log_total) - onehot)).astype(BF)
        weight_grad = weight_grad + mul_tn(grad_logits, final)
        shift_grad = shift_grad + col_sum(grad_logits.astype(F32))
        grad_final = mul_nt(grad_logits, weight_ref[...])
        gain_grad = gain_grad + col_sum(grad_final * normed)
        move_grad = move_grad + col_sum(grad_final)
        grad = norm_back(grad_final * gain_ref[...], normed, inverse)
        grad_ref[rows, :] = grad
        rounded_ref[rows, :] = grad.astype(BF)
        return weight_grad, gain_grad, move_grad, shift_grad, stats

    row = jnp.zeros((1, D), F32)
    narrow = jnp.zeros((1, 128), F32)
    weight_grad, gain_grad, move_grad, shift_grad, stats = over_chunks(
        body, (jnp.zeros((128, D), F32), row, row, narrow, narrow)
    )
    small_ref[0:32, :] = weight_grad[0:32, :]
    small_ref[32:33, :] = gain_grad
    small_ref[33:34, :] = move_grad
    small_ref[34:35, 0:128] = shift_grad
    small_ref[35:36, 0:128] = stats


def head(residual, targets, masked, weight, shift, gain, move):
    full = whole_block((ROWS, D))
    return pl.pallas_call(
        head_kernel,
        out_shape=(
            sds((ROWS, D), BF),
            sds((ROWS, D), F32),
            sds((ROWS, D), BF),
            sds((40, D), F32),
        ),
        grid=(1,),
        in_specs=[full, whole_block((ROWS, 1)), whole_block((ROWS, 1)), whole_block((D, 128))]
        + [whole_block((1, 128)), whole_block((1, D)), whole_block((1, D))],
        out_specs=(full, full, full, whole_block((40, D))),
        **KERNEL,
    )(residual, targets, masked, weight, shift, gain, move)


def down_back_kernel(place_ref, grad_ref, active_ref, *refs):
    sends, (keep_out, held, grads, sems, out_sems) = refs[:8], refs[8:]
    step = pl.program_id(0)
    c_at = place_ref[2]

    @pl.when(step == 0)
    def _():
        for at in range(TILES):
            z_at, y_at = at % 4, place_ref[1] ^ (1 - at // 4)
            source = active_ref.at[z_at, :, pl.ds(pl.multiple_of(y_at * TILE, 128), TILE)]
            target = held.at[at // 2, :, at % 2 * TILE : (at % 2 + 1) * TILE]
            copy(source, target, sems.at[at]).start()

    for part in range(2):
        target = held.at[step, :, part * TILE : (part + 1) * TILE]
        copy(active_ref.at[0, :, :TILE], target, sems.at[2 * step + part]).wait()
    grads[step] = mul_tn(grad_ref[...], held[step]).astype(BF).reshape(2, HALF, WIDE)
    for at in range(TILES):

        @pl.when(step == at // 2)
        def _():
            lanes = slice(at % 2 * TILE, (at % 2 + 1) * TILE)
            copy(grads.at[at // 2, 1 - c_at, :, lanes], sends[at], out_sems.at[at, 0]).start()
            kept = grads.at[at // 2, c_at, :, lanes]
            copy(kept, keep_out.at[1 - at // 4, at % 4], out_sems.at[at, 1]).start()

    @pl.when(step == STEPS - 1)
    def _():
        for at in range(TILES):
            one = grads.at[0, 0, :, :TILE]
            copy(one, sends[at], out_sems.at[at, 0]).wait()
            copy(one, keep_out.at[0, 0], out_sems.at[at, 1]).wait()


def down_back(place, grad, active):
    part = sds((HALF, TILE), BF)
    return pl.pallas_call(
        down_back_kernel,
        grid=(STEPS,),
        in_specs=[SMEM_SPEC, whole_block((ROWS, D)), ANY_SPEC],
        out_specs=(ANY_SPEC,) * 9,
        out_shape=(part,) * 8 + (sds((2, 4, HALF, TILE), BF),),
        scratch_shapes=[
            pltpu.VMEM((STEPS, ROWS, WIDE), BF),
            pltpu.VMEM((STEPS, 2, HALF, WIDE), BF),
            semaphores(TILES),
            semaphores(TILES, 2),
        ],
        **KERNEL,
    )(place, grad, active)


def down_sum_kernel(side, others, keep_ref, *refs):
    parts, refs = refs[:4], refs[4:]
    other_refs, refs = refs[:others], refs[others:]
    out_ref, kept, got, other, total, sems, other_sems, out_sems = refs
    copies = []
    for at in range(4):
        copies.append(
            [
                copy(keep_ref.at[side, at], kept.at[at], sems.at[at, 0]),
                copy(parts[at], got.at[at], sems.at[at, 1]),
            ]
            + [copy(ref.at[at], other.at[at], other_sems.at[at]) for ref in other_refs]
        )
        for one in copies[-1]:
            one.start()
    for at in range(4):
        for one in copies[at]:
            one.wait()
        value = kept[at].astype(F32) + got[at].astype(F32)
        if others:
            value = value + other[at].astype(F32)
        total[at] = value.astype(BF)
        copy(total.at[at], out_ref.at[at], out_sems.at[at]).start()
    for at in range(4):
        copy(total.at[at], out_ref.at[at], out_sems.at[at]).wait()


def down_sum(side, keep, parts, *other):
    shape = (4, HALF, TILE)

    def kernel(*refs):
        down_sum_kernel(side, len(other), *refs)

    return pl.pallas_call(
        kernel,
        grid=(1,),
        in_specs=[ANY_SPEC] * (5 + len(other)),
        out_specs=ANY_SPEC,
        out_shape=sds(shape, BF),
        scratch_shapes=[pltpu.VMEM(shape, BF)] * 4
        + [semaphores(4, 2), semaphores(4), semaphores(4)],
        **KERNEL,
    )(keep, *parts, *other)


def wide_back_start(phase, place_ref, slope_ref, ups, downs, held, sems):
    x_at, y_at, c_at = place_ref[0], place_ref[1], place_ref[2]
    held_up, held_down, slopes = held
    up_sems, down_sems, slope_sems = sems
    for step in range(2):
        dx = 1 - step
        for number, buffer in enumerate(downs):
            dc, dy, z_high = number // 4, number // 2 % 2, number % 2

            @pl.when(x_at ^ dx == z_high)
            def _():
                y_to, c_to = y_at ^ dy, c_at ^ dc
                target = held_down.at[step, y_to, c_to]
                source = buffer.at[c_at ^ (1 - phase)]
                copy(source, target, down_sems.at[step, y_to, c_to]).start()

        quarter = (x_at ^ dx) * 2 + (c_at ^ (1 - phase))
        copy(slope_ref.at[quarter], slopes.at[step], slope_sems.at[step]).start()
        for dy in range(2):
            for half in range(2):
                target = held_up.at[step, :, y_at ^ dy, :, half * TILE : (half + 1) * TILE]
                source = ups[2 * dx + dy].at[:, half]
                copy(source, target, up_sems.at[step, dy, half]).start()


def wide_back_step(step, rounded_ref, second_ref, slope_ref, ups, downs, held, sems, shift_ref, total):
    held_up, held_down, slopes = held
    up_sems, down_sems, slope_sems = sems
    for y_at in range(2):
        for c_at in range(2):
            target = held_down.at[step, y_at, c_at]
            copy(downs[0].at[0], target, down_sems.at[step, y_at, c_at]).wait()
    grad_active = mul_nt(rounded_ref[...], held_down[step].reshape(WIDE, D))
    copy(slope_ref.at[0], slopes.at[step], slope_sems.at[step]).wait()
    grad_hidden = (grad_active * slopes[step].astype(F32)).astype(BF)
    shift_ref[pl.ds(step, 1), :] = col_sum(grad_hidden.astype(F32))
    for dy in range(2):
        for half in range(2):
            target = held_up.at[step, :, dy, :, half * TILE : (half + 1) * TILE]
            copy(ups[0].at[:, 0], target, up_sems.at[step, dy, half]).wait()
    total[...] += mul_nt(grad_hidden, square(held_up[step]))
    return mul_tn(second_ref[...], grad_hidden).reshape(4, 2, SHARD, WIDE)


def wide_back_scratch():
    return [
        pltpu.VMEM((2, 4, 2, SHARD, WIDE), BF),
        pltpu.VMEM((2, 2, 2, HALF, D), BF),
        pltpu.VMEM((2, ROWS, WIDE), BF),
        semaphores(2, 2, 2),
        semaphores(2, 2, 2),
        semaphores(2),
    ]


def wide_back_first_kernel(place_ref, rounded_ref, second_ref, slope_ref, *refs):
    ups, downs, refs = refs[:4], refs[4:12], refs[12:]
    sends, (shift_ref, total_ref, *refs) = refs[:8], refs[8:]
    held, sems, sent, out_sems = refs[:3], refs[3:6], refs[6], refs[7]
    step = pl.program_id(0)

    @pl.when(step == 0)
    def _():
        wide_back_start(0, place_ref, slope_ref, ups, downs, held, sems)
        total_ref[...] = jnp.zeros_like(total_ref)

    up_grad = wide_back_step(
        step, rounded_ref, second_ref, slope_ref, ups, downs, held, sems, shift_ref, total_ref
    )
    for side in range(2):
        sent[step, side ^ place_ref[1]] = up_grad[:, side].astype(BF)

    def out_copy(at, half, dy):
        lanes = slice(half * TILE, (half + 1) * TILE)
        number = 4 * at + 2 * half + dy
        return copy(sent.at[at, dy, :, :, lanes], sends[number], out_sems.at[at, half, dy])

    pieces = [(half, dy) for half in range(2) for dy in range(2)]
    for at in range(2):

        @pl.when(step == at)
        def _():
            for half, dy in pieces:
                out_copy(at, half, dy).start()

    @pl.when(step == 1)
    def _():
        for at in range(2):
            for half, dy in pieces:
                out_copy(at, half, dy).wait()


def wide_back_first(place, rounded, second, slope, up_parts, down_parts):
    full = whole_block((ROWS, D))
    return pl.pallas_call(
        wide_back_first_kernel,
        grid=(2,),
        in_specs=[SMEM_SPEC, full, full] + [ANY_SPEC] * 13,
        out_specs=(ANY_SPEC,) * 8 + (whole_block((2, WIDE)), full),
        out_shape=(sds((4, SHARD, TILE), BF),) * 8 + (sds((2, WIDE), F32), sds((ROWS, D), F32)),
        scratch_shapes=wide_back_scratch()
        + [pltpu.VMEM((2, 2, 4, SHARD, WIDE), BF), semaphores(2, 2, 2)],
        **KERNEL,
    )(place, rounded, second, slope, *up_parts[2:4], *up_parts[6:8], *down_parts)


def wide_back_last_kernel(place_ref, rounded_ref, second_ref, slope_ref, *refs):
    ups, downs, refs = refs[:4], refs[4:12], refs[12:]
    before_ref, grad_ref, middle_ref, gains_ref, *refs = refs
    gots, refs = refs[:8], refs[8:]
    outs, (shift_ref, grad_out, rounded_out, small_ref, *refs) = refs[:2], refs[2:]
    held, sems, refs = refs[:3], refs[3:6], refs[6:]
    kept, got, total, grads, middles, roundeds, got_sems, out_sems, in_sems, row_sems = refs
    step = pl.program_id(0)
    fetched = (
        copy(before_ref, total, in_sems.at[0]),
        copy(grad_ref, grads, in_sems.at[1]),
        copy(middle_ref, middles, in_sems.at[2]),
    )

    pieces = [(half, dy) for half in range(2) for dy in range(2)]

    def got_copy(at, half, dy):
        lanes = slice(half * TILE, (half + 1) * TILE)
        target = got.at[at, dy, :, :, lanes]
        return copy(gots[4 * at + 2 * half + dy], target, got_sems.at[at, half, dy])

    @pl.when(step == 0)
    def _():
        fetched[0].start()
        wide_back_start(1, place_ref, slope_ref, ups, downs, held, sems)
        for at in range(2):
            for half, dy in pieces:
                got_copy(at, half, dy).start()
        fetched[1].start()
        fetched[2].start()
        fetched[0].wait()

    up_grad = wide_back_step(
        step, rounded_ref, second_ref, slope_ref, ups, downs, held, sems, shift_ref, total
    )
    for half, dy in pieces:
        lanes = slice(half * TILE, (half + 1) * TILE)
        copy(gots[0], got.at[step, dy, :, :, lanes], got_sems.at[step, half, dy]).wait()
    for side in range(2):
        at_side = side ^ place_ref[1]
        kept[step, at_side] = (up_grad[:, side] + got[step, at_side].astype(F32)).astype(BF)

    def out_copy(at, half, dy):
        lanes = slice(half * TILE, (half + 1) * TILE)
        target = outs[at].at[dy, :, half]
        return copy(kept.at[at, dy, :, :, lanes], target, out_sems.at[at, half, dy])

    for at in range(2):

        @pl.when(step == at)
        def _():
            for half, dy in pieces:
                out_copy(at, half, dy).start()

    @pl.when(step == 1)
    def _():
        fetched[1].wait()
        fetched[2].wait()
        sums = [jnp.zeros((1, D), F32)] * 4
        sent = []
        for index in range(CHUNKS):
            rows = chunk_rows(index)
            normed, inverse = normalize(middles[rows, :])
            grad_second = total[rows, :]
            grad = grads[rows, :] + norm_back(grad_second * gains_ref[1:2, :], normed, inverse)
            rounded = grad.astype(BF)
            grads[rows, :] = grad
            roundeds[rows, :] = rounded
            sent.append(copy(grads.at[rows, :], grad_out.at[rows, :], row_sems.at[index, 0]))
            sent.append(copy(roundeds.at[rows, :], rounded_out.at[rows, :], row_sems.at[index, 1]))
            sent[-2].start()
            sent[-1].start()
            terms = (
                grad_second * normed,
                grad_second,
                rounded.astype(F32),
                rounded_ref[rows, :].astype(F32),
            )
            sums = [old + col_sum(term) for old, term in zip(sums, terms)]
        small_ref[...] = jnp.zeros_like(small_ref)
        for number in range(4):
            small_ref[number : number + 1, :] = sums[number]
        for at in range(2):
            for half, dy in pieces:
                out_copy(at, half, dy).wait()
        for one in sent:
            one.wait()


def wide_back_last(
    place, rounded, second, slope, up_parts, down_parts, before, grad, middle, gains, *got
):
    full = whole_block((ROWS, D))
    out = sds((2, 4, 2, SHARD, TILE), BF)
    return pl.pallas_call(
        wide_back_last_kernel,
        grid=(2,),
        in_specs=[SMEM_SPEC, full, full]
        + [ANY_SPEC] * 16
        + [whole_block((2, D))]
        + [ANY_SPEC] * 8,
        out_specs=(ANY_SPEC, ANY_SPEC, whole_block((2, WIDE)), ANY_SPEC, ANY_SPEC, whole_block((8, D))),
        out_shape=(
            out,
            out,
            sds((2, WIDE), F32),
            sds((ROWS, D), F32),
            sds((ROWS, D), BF),
            sds((8, D), F32),
        ),
        scratch_shapes=wide_back_scratch()
        + [
            pltpu.VMEM((2, 2, 4, SHARD, WIDE), BF),
            pltpu.VMEM((2, 2, 4, SHARD, WIDE), BF),
            pltpu.VMEM((ROWS, D), F32),
            pltpu.VMEM((ROWS, D), F32),
            pltpu.VMEM((ROWS, D), F32),
            pltpu.VMEM((ROWS, D), BF),
            semaphores(2, 2, 2),
            semaphores(2, 2, 2),
            semaphores(3),
            semaphores(CHUNKS, 2),
        ],
        **KERNEL,
    )(
        place, rounded, second, slope, *up_parts[0:2], *up_parts[4:6], *down_parts,
        before, grad, middle, gains, *got
    )


def mix_back_kernel(place_ref, lengths_ref, rounded_ref, grad_ref, residual_ref, *refs):
    buffers, (packed_ref, log_ref, mixed_ref, gains_ref, biases_ref, *refs) = refs[:8], refs[8:]
    sends, (pre_out, rights_out, grad_out, rounded_out, small_ref, *refs) = refs[:4], refs[4:]
    held, packed, sent, pre, rights, grad_mixed, total, grads, roundeds, *refs = refs
    sems, in_sems, send_sems, pre_sem, right_sems, row_sems = refs
    x_at, y_at, c_at = place_ref[0], place_ref[1], place_ref[2]
    copies = quarter_copies(place_ref, buffers, held, sems)
    for one in copies:
        one.start()
    fetched = [
        copy(packed_ref.at[chunk_rows(at), :], packed.at[chunk_rows(at), :], in_sems.at[at])
        for at in range(SEQ_DEV)
    ]
    fetched.append(copy(grad_ref, grads, in_sems.at[SEQ_DEV]))
    for one in fetched:
        one.start()

    def send_grad(part, right):
        @pl.when(c_at ^ (part & 1) == 1)
        def _():
            left = mixed_ref[...] if part == 3 else pre[...]
            value = mul_tn(left, right).astype(BF).reshape(4, 2, SHARD, D)
            for side in range(2):
                sent[x_at ^ (part >> 1), side ^ y_at] = value[:, side]

    send_grad(3, rounded_ref[...])

    def first(rows, carry):
        normed, inverse = normalize(residual_ref[rows, :].astype(F32))
        pre[rows, :] = (normed * gains_ref[0:1, :] + biases_ref[0:1, :]).astype(BF)
        return carry

    over_chunks(first, 0)
    pre_copy = copy(pre, pre_out, pre_sem.at[0])
    pre_copy.start()
    for one in copies:
        one.wait()
    grad_mixed[...] = mul_nt(rounded_ref[...], square(held[:, :, :, 3 * D :])).astype(BF)
    masks = head_masks()
    row_ids = lax.broadcasted_iota(jnp.int32, (LEN, 1), 0)
    scale = 1.0 / math.sqrt(HEAD_DIM)

    def right_copy(seq, part):
        rows = pl.ds(pl.multiple_of(seq * LEN, LEN), LEN)
        lanes = slice(part * D, (part + 1) * D)
        return copy(rights.at[rows, lanes], rights_out.at[part, rows, :], right_sems.at[seq, part])

    def one_sequence(seq, carry):
        rows = pl.ds(pl.multiple_of(seq * LEN, LEN), LEN)
        copy(packed_ref.at[chunk_rows(0), :], packed.at[rows, :], in_sems.at[seq]).wait()
        valid = row_ids < lengths_ref[seq]
        for group in range(GROUPS):
            at_query = slice(group * 128, (group + 1) * 128)
            queries = stack_heads(packed[rows, at_query], masks)
            key_rows = packed[rows, D + group * 128 : D + (group + 1) * 128]
            value_rows = packed[rows, 2 * D + group * 128 : 2 * D + (group + 1) * 128]
            mixed_grads = stack_heads(grad_mixed[rows, at_query], masks)
            scores = scores_of(key_rows, queries, valid)
            probs = jnp.exp(scores - log_ref[seq * GROUPS + group])
            grad_probs = mul_nt(value_rows, mixed_grads)
            inner = jnp.sum(grad_probs * probs, 0, keepdims=True)
            grad_scores = (probs * (grad_probs - inner)).astype(BF)
            rights[rows, 2 * D + group * 128 : 2 * D + (group + 1) * 128] = mul_nn(probs.astype(BF), mixed_grads).astype(BF)
            rights[rows, D + group * 128 : D + (group + 1) * 128] = (mul_nn(grad_scores, queries) * scale).astype(BF)
            grad_queries = unstack_heads(mul_tn(key_rows, grad_scores))
            rights[rows, at_query] = (grad_queries * scale).astype(BF)
        for part in range(3):
            right_copy(seq, part).start()
        return carry

    lax.fori_loop(0, SEQ_DEV, one_sequence, 0)
    for part in range(3):
        send_grad(part, rights[:, part * D : (part + 1) * D])
    for dx in range(2):
        for dy in range(2):
            copy(sent.at[dx, dy], sends[2 * dx + dy], send_sems.at[dx, dy]).start()
    total[...] = mul_nt(rights[...], square(held[:, :, :, : 3 * D]))
    fetched[-1].wait()
    sums = [jnp.zeros((1, D), F32)] * 4
    out_copies = []
    for index in range(CHUNKS):
        rows = chunk_rows(index)
        normed, inverse = normalize(residual_ref[rows, :].astype(F32))
        grad_pre = total[rows, :]
        grad = grads[rows, :] + norm_back(grad_pre * gains_ref[0:1, :], normed, inverse)
        grads[rows, :] = grad
        roundeds[rows, :] = grad.astype(BF)
        out_copies.append(copy(grads.at[rows, :], grad_out.at[rows, :], row_sems.at[index, 0]))
        out_copies.append(copy(roundeds.at[rows, :], rounded_out.at[rows, :], row_sems.at[index, 1]))
        out_copies[-2].start()
        out_copies[-1].start()
        terms = (
            grad_pre * normed,
            grad_pre,
            rights[rows, 0:D].astype(F32),
            rights[rows, 2 * D : 3 * D].astype(F32),
        )
        sums = [old + col_sum(term) for old, term in zip(sums, terms)]
    small_ref[...] = jnp.zeros_like(small_ref)
    for number in range(4):
        small_ref[number : number + 1, :] = sums[number]
    for seq in range(SEQ_DEV):
        for part in range(3):
            right_copy(seq, part).wait()
    for dx in range(2):
        for dy in range(2):
            copy(sent.at[dx, dy], sends[2 * dx + dy], send_sems.at[dx, dy]).wait()
    for one in [pre_copy] + out_copies:
        one.wait()


def mix_back(
    place, lengths, rounded, middle_grad, residual, quarters, packed, logs, mixed, gains, biases
):
    part = sds((4, SHARD, D), BF)
    full = whole_block((ROWS, D))
    return pl.pallas_call(
        mix_back_kernel,
        out_shape=(part,) * 4
        + (
            sds((ROWS, D), BF),
            sds((3, ROWS, D), BF),
            sds((ROWS, D), F32),
            sds((ROWS, D), BF),
            sds((8, D), F32),
        ),
        grid=(1,),
        in_specs=[SMEM_SPEC, SMEM_SPEC, full, ANY_SPEC, full]
        + [ANY_SPEC] * 9
        + [whole_block((SEQ_DEV * GROUPS, 1, PER_GROUP * LEN)), full]
        + [whole_block((2, D)), whole_block((6, D))],
        out_specs=(ANY_SPEC,) * 8 + (whole_block((8, D)),),
        scratch_shapes=[
            pltpu.VMEM((4, 2, SHARD, 4 * D), BF),
            pltpu.VMEM((ROWS, 3 * D), BF),
            pltpu.VMEM((2, 2, 4, SHARD, D), BF),
            pltpu.VMEM((ROWS, D), BF),
            pltpu.VMEM((ROWS, 3 * D), BF),
            pltpu.VMEM((ROWS, D), BF),
            pltpu.VMEM((ROWS, D), F32),
            pltpu.VMEM((ROWS, D), F32),
            pltpu.VMEM((ROWS, D), BF),
            semaphores(8),
            semaphores(SEQ_DEV + 1),
            semaphores(2, 2),
            semaphores(1),
            semaphores(SEQ_DEV, 3),
            semaphores(CHUNKS, 2),
        ],
        **KERNEL,
    )(
        place, lengths, rounded, middle_grad, residual, *quarters, packed, logs, mixed, gains, biases
    )


def mix_back_last_kernel(place_ref, pre_ref, mixed_ref, rights_ref, rounded_ref, *refs):
    gots, outs, (lefts, rights, got, kept, sems, out_sems) = refs[:4], refs[4:6], refs[6:]
    y_at, c_at = place_ref[1], place_ref[2]
    parts = [(place_ref[0] ^ dx) * 2 + c_at for dx in range(2)]
    for dx in (1, 0):

        @pl.when(parts[dx] == 3)
        def _():
            copy(mixed_ref, lefts.at[dx], sems.at[dx, 3]).start()
            copy(rounded_ref, rights.at[dx], sems.at[dx, 0]).start()

        @pl.when(parts[dx] != 3)
        def _():
            copy(pre_ref, lefts.at[dx], sems.at[dx, 3]).start()
            copy(rights_ref.at[jnp.minimum(parts[dx], 2)], rights.at[dx], sems.at[dx, 0]).start()

        for dy in range(2):
            copy(gots[2 * dx + dy], got.at[dx, dy], sems.at[dx, 1 + dy]).start()
    for dx in (1, 0):
        copy(pre_ref, lefts.at[dx], sems.at[dx, 3]).wait()
        copy(rounded_ref, rights.at[dx], sems.at[dx, 0]).wait()
        value = mul_tn(lefts[dx], rights[dx]).reshape(4, 2, SHARD, D)
        for dy in range(2):
            copy(gots[0], got.at[dx, dy], sems.at[dx, 1 + dy]).wait()
        for side in range(2):
            at = side ^ y_at
            kept[dx, at] = (value[:, side] + got[dx, at].astype(F32)).astype(BF)
        copy(kept.at[dx], outs[1 - dx], out_sems.at[dx]).start()
    for dx in range(2):
        copy(kept.at[dx], outs[1 - dx], out_sems.at[dx]).wait()


def mix_back_last(place, pre, mixed, rights, rounded, *got):
    out = sds((2, 4, SHARD, D), BF)
    return pl.pallas_call(
        mix_back_last_kernel,
        grid=(1,),
        in_specs=[SMEM_SPEC] + [ANY_SPEC] * 8,
        out_specs=(ANY_SPEC,) * 2,
        out_shape=(out, out),
        scratch_shapes=[
            pltpu.VMEM((2, ROWS, D), BF),
            pltpu.VMEM((2, ROWS, D), BF),
            pltpu.VMEM((2, 2, 4, SHARD, D), BF),
            pltpu.VMEM((2, 2, 4, SHARD, D), BF),
            semaphores(2, 4),
            semaphores(2),
        ],
        **KERNEL,
    )(place, pre, mixed, rights, rounded, *got)


def finish_kernel(layer, olds, place_ref, *refs):
    quarters, halves, outs = refs[:4], refs[4:8], refs[8 + olds : 11 + olds]
    attn, ups, downs, sems = refs[11 + olds :]
    x_at, c_at = place_ref[0], place_ref[2]
    values = [ref[...] for ref in quarters]
    pairs = [
        (jnp.where(c_at == 0, own, other), jnp.where(c_at == 0, other, own))
        for own, other in (values[:2], values[2:])
    ]
    ordered = [jnp.where(x_at == 0, own, other) for own, other in zip(*pairs)]
    ordered += [jnp.where(x_at == 0, other, own) for own, other in zip(*pairs)]
    for quarter, value in enumerate(ordered):
        for tile in range(3):
            target, first, stride = (
                (attn, quarter * 5, 20) if tile == 2 else (ups, quarter * 10 + tile * 5, 40)
            )
            for block in range(5):
                target[pl.ds(first + block, SHARD, stride=stride), :] = value[
                    tile, :, block * 128 : (block + 1) * 128
                ].astype(F32)
    copies = [
        copy(target, out.at[layer], sems.at[number])
        for number, (target, out) in enumerate(zip((attn, ups, downs), outs))
    ]
    copies[0].start()
    copies[1].start()
    own, other = (
        halves[at][...].astype(F32) + halves[at + 2][...].astype(F32) for at in range(2)
    )
    turned = jnp.concatenate(
        [jnp.where(c_at == 0, own, other), jnp.where(c_at == 0, other, own)], 0
    ).T
    for block in range(5):
        downs[pl.ds(block, TILE, stride=5), :] = turned[:, block * 128 : (block + 1) * 128]
    copies[2].start()
    for one in copies:
        one.wait()


def finish(layer, place, quarters, halves, *old):
    attn, wide = (D * 4 * D // 8 // 128, 128), (D * FF // 8 // 128, 128)

    def kernel(*refs):
        finish_kernel(layer, len(old), *refs)

    return pl.pallas_call(
        kernel,
        grid=(1,),
        in_specs=[SMEM_SPEC]
        + [whole_block((3, SHARD, D))] * 4
        + [whole_block((HALF, TILE))] * 4
        + [ANY_SPEC] * len(old),
        out_specs=(ANY_SPEC,) * 3,
        out_shape=tuple(sds((LAYERS, *shape), F32) for shape in (attn, wide, wide)),
        scratch_shapes=[pltpu.VMEM(shape, F32) for shape in (attn, wide, wide)] + [semaphores(3)],
        input_output_aliases={9 + number: number for number in range(len(old))},
        **KERNEL,
    )(place, *quarters, *halves, *old)


def swap(value, axis, name):
    with jax.named_scope(name):
        return lax.ppermute(value, axis, [(0, 1), (1, 0)])


def swaps(values, axis, name):
    return [swap(value, axis, name) for value in values]


class Order:
    def __init__(self):
        self.last = None

    def hold(self, *arrays):
        if self.last is not None:
            arrays = lax.optimization_barrier((arrays, self.last))[0]
        return arrays

    def __call__(self, function, *arrays):
        results = function(*self.hold(*arrays))
        self.last = jax.tree.leaves(results)[0]
        return results


def wide_sum(*values):
    total = values[0].astype(F32)
    for value in values[1:]:
        total = total + value.astype(F32)
    return total


def rounded_sum(*values):
    return wide_sum(*values).astype(BF)


def plus(own, other):
    return own + other


class Moves:
    def __init__(self, fsdp):
        self.z_size = fsdp // 2
        self.staged = fsdp == 8
        self.x_at = lax.axis_index("x")
        self.y_at = lax.axis_index("y")
        self.z_at = lax.axis_index("z")
        self.c_at = lax.axis_index("c")
        self.place = jnp.stack([self.x_at, self.y_at, self.c_at]).astype(jnp.int32)

    def hop(self, value, reach, name):
        with jax.named_scope(name):
            return lax.ppermute(value, "z", [(at, at ^ reach) for at in range(self.z_size)])

    def ordered(self, bit, own, other):
        return jnp.where(bit == 0, jnp.stack([own, other]), jnp.stack([other, own]))

    def by_side(self, value):
        value = value.reshape(4, 2, *value.shape[1:]).swapaxes(0, 1)
        return jnp.where(self.y_at == 0, value, value[::-1])

    def by_shard(self, value):
        value = jnp.where(self.y_at == 0, value, value[::-1]).swapaxes(0, 1)
        return value.reshape(8, *value.shape[2:])

    def own_quarter(self, flat):
        shard = flat.reshape(SHARD, -1, 128)
        step = shard.shape[1] // 4
        own = lax.dynamic_slice_in_dim(shard, (self.x_at * 2 + self.c_at) * step, step, 1)
        return own.reshape(SHARD, step // 5, 5, 128).swapaxes(0, 1).reshape(-1, SHARD, D)

    def own_half(self, flat):
        own = lax.dynamic_slice_in_dim(flat, self.c_at * HALF * 5, HALF * 5, 0)
        return own.reshape(1, HALF, D)

    def high(self, own, other):
        return self.ordered(self.z_at // 2, own, other)

    def low(self, pair, other):
        bit = self.z_at % 2
        line = jnp.where(bit == 0, jnp.stack([pair, other], 1), jnp.stack([other, pair], 1))
        return (line.reshape(4, *pair.shape[1:]),)

    def low_halves(self, pair, other):
        line = self.low(pair, other)[0][:, 0]
        return line[:2], line[2:]

    def part_near(self, *parts):
        total = wide_sum(*parts)
        total = total.reshape(2, 2, *total.shape[1:])
        near = self.z_at % 2
        return tuple(
            lax.dynamic_index_in_dim(total, at, 1, False).astype(BF) for at in (1 - near, near)
        )

    def part_far(self, *parts):
        total = wide_sum(*parts)
        far = self.z_at // 2
        return tuple(
            lax.dynamic_index_in_dim(total, at, 0, False).astype(BF) for at in (1 - far, far)
        )

    def along_z(self, part):
        return lax.psum_scatter(part, "z", scatter_dimension=0, tiled=False)

    def plain_quarters(self, flat):
        whole = lax.all_gather(flat, ("z", "y"), axis=0, tiled=True)
        whole = whole.reshape(8, SHARD, 4, -1, D).transpose(2, 0, 3, 1, 4)
        lines = []
        for number in range(4):
            quarter = (self.x_at ^ (number >> 1)) * 2 + (self.c_at ^ (number & 1))
            part = self.by_side(lax.dynamic_index_in_dim(whole, quarter, 0, False))
            lines += [part[dy] for dy in range(2)]
        return lines

    def plain_halves(self, flat):
        whole = lax.all_gather(flat, ("z", "y"), axis=0, tiled=True).reshape(8, 2, HALF, D)
        pairs = []
        for number in range(2):
            part = self.by_side(lax.dynamic_index_in_dim(whole, self.c_at ^ number, 1, False))
            pairs += [part[dy, 2 * at : 2 * at + 2] for dy in range(2) for at in range(2)]
        return pairs

    def plain_quarters_back(self, passed, keep):
        part = self.by_shard(rounded_sum(keep, swap(passed, "x", "quarters")))
        part = part.transpose(0, 2, 1, 3).reshape(D, -1)
        part = lax.psum_scatter(part, ("z", "y"), scatter_dimension=0, tiled=True)
        parts = lax.all_gather(part, ("x", "c"), axis=0, tiled=False)
        return parts.swapaxes(0, 1).astype(F32).reshape(-1, 128)

    def plain_halves_back(self, part):
        part = self.by_shard(part).transpose(0, 2, 1).reshape(FF, HALF)
        part = lax.psum_scatter(part, ("z", "y"), scatter_dimension=0, tiled=True).T
        part = rounded_sum(part, swap(part, "x", "halves"))
        return lax.all_gather(part, "c", axis=0, tiled=True).T.astype(F32).reshape(-1, 128)

    def sum_all(self, value):
        for axis in ("c", "x", "y"):
            value = value + swap(value, axis, "small")
        reach = 1
        while reach < self.z_size:
            value = value + self.hop(value, reach, "small")
            reach *= 2
        return value


def local(
    fsdp,
    inputs,
    targets,
    masked,
    lengths,
    attn_weight,
    up_weight,
    down_weight,
    norm_gains,
    layer_biases,
    up_bias,
    head_weight,
    final_gain,
    final_shift,
    head_bias,
):
    moves = Moves(fsdp)
    place = moves.place
    shifts = up_bias.reshape(LAYERS, STEPS, WIDE)
    run = Order()

    def mix_on(layer):
        return lambda r, *q: mix(place, lengths, r, q, norm_gains[layer], layer_biases[layer])

    def up_on(layer):
        return lambda second, *parts: up(place, second, parts, shifts[layer])

    def down_on(layer):
        return lambda m, active, *parts: down(place, m, active, parts, layer_biases[layer])

    def prepared(targets, masked, head_weight, head_bias):
        wide_bias = head_bias.reshape(1, VOCAB)
        return (
            targets.reshape(ROWS, 1),
            masked.reshape(ROWS, 1),
            jnp.pad(head_weight, ((0, 0), (0, 128 - VOCAB))),
            jnp.pad(wide_bias, ((0, 0), (0, 128 - VOCAB)), constant_values=-1e30),
        )

    def fan(lines, name):
        return [swaps(lines, axis, name + "_" + axis) for axis in "yxc"]

    def fan_y(y, name):
        return [swaps(y, axis, name + "_y" + axis) for axis in "xc"]

    def fan_x(x, yx, name):
        return swaps(x, "c", name + "_xc"), swaps(yx, "c", name + "_yxc")

    def in_place(own, y, x, c, yx, yc, xc, yxc):
        return [part[0] for part in (own, y, c, yc, x, yx, xc, yxc)]

    if moves.staged:
        a0 = run(moves.own_quarter, attn_weight[0])
        a0_far = moves.hop(a0, 2, "a0_far")
        u0 = run(moves.own_quarter, up_weight[0])
        u0_far = moves.hop(u0, 2, "u0_far")
        d0 = run(moves.own_half, down_weight[0])
        a0 = run(moves.high, a0, a0_far)
        a0_near = moves.hop(a0, 1, "a0_near")
        u0 = run(moves.high, u0, u0_far)
        u0_near = moves.hop(u0, 1, "u0_near")
        (d0,) = run.hold(d0)
        d0_far = moves.hop(d0, 2, "d0_far")
        a1 = run(moves.own_quarter, attn_weight[1])
        a0 = run(moves.low, a0, a0_near)
        a0_y, a0_x, a0_c = fan(a0, "a0")
        u1 = run(moves.own_quarter, up_weight[1])
        d1 = run(moves.own_half, down_weight[1])
        a0_y = run.hold(*a0_y)
        a0_yx, a0_yc = fan_y(a0_y, "a0")
        u0 = run(moves.low, u0, u0_near)
        u0_y, u0_x, u0_c = fan(u0, "u0")
        d0 = run(moves.high, d0, d0_far)
        d0_near = moves.hop(d0, 1, "d0_near")
        ready = run(prepared, targets, masked, head_weight, head_bias)
        a0_x, a0_yx = run.hold(a0_x, a0_yx)
        a0_xc, a0_yxc = fan_x(a0_x, a0_yx, "a0")
        quarters0 = in_place(a0, a0_y, a0_x, a0_c, a0_yx, a0_yc, a0_xc, a0_yxc)
        mixed0 = run(mix_on(0), inputs, *quarters0)
        u0_y = run.hold(*u0_y)
        u0_yx, u0_yc = fan_y(u0_y, "u0")
        d0 = run(moves.low_halves, d0, d0_near)
        d0_y, d0_c = swaps(d0, "y", "d0_y"), swaps(d0, "c", "d0_c")
        a1, u1, d1 = run.hold(a1, u1, d1)
        a1_far = moves.hop(a1, 2, "a1_far")
        u1_far = moves.hop(u1, 2, "u1_far")
        a1 = run(moves.high, a1, a1_far)
        a1_near = moves.hop(a1, 1, "a1_near")
        u1 = run(moves.high, u1, u1_far)
        u1_near = moves.hop(u1, 1, "u1_near")
        u0_x, u0_yx = run.hold(u0_x, u0_yx)
        u0_xc, u0_yxc = fan_x(u0_x, u0_yx, "u0")
        a1 = run(moves.low, a1, a1_near)
        a1_y, a1_x, a1_c = fan(a1, "a1")
        d1_far = moves.hop(d1, 2, "d1_far")
        ups0 = in_place(u0, u0_y, u0_x, u0_c, u0_yx, u0_yc, u0_xc, u0_yxc)
        wide0 = run(up_on(0), mixed0[4], *ups0)
        u1 = run(moves.low, u1, u1_near)
        u1_y, u1_x, u1_c = fan(u1, "u1")
        d1 = run(moves.high, d1, d1_far)
        d1_near = moves.hop(d1, 1, "d1_near")
        d0_y = run.hold(*d0_y)
        d0_yc = swaps(d0_y, "c", "d0_yc")
        downs0 = (*d0, *d0_y, *d0_c, *d0_yc)
        residual1 = run(down_on(0), mixed0[3], wide0[0], *downs0)
        a1_y = run.hold(*a1_y)
        a1_yx, a1_yc = fan_y(a1_y, "a1")
        d1 = run(moves.low_halves, d1, d1_near)
        d1_y, d1_c = swaps(d1, "y", "d1_y"), swaps(d1, "c", "d1_c")
        a1_x, a1_yx = run.hold(a1_x, a1_yx)
        a1_xc, a1_yxc = fan_x(a1_x, a1_yx, "a1")
        u1_y = run.hold(*u1_y)
        u1_yx, u1_yc = fan_y(u1_y, "u1")
        quarters1 = in_place(a1, a1_y, a1_x, a1_c, a1_yx, a1_yc, a1_xc, a1_yxc)
        mixed1 = run(mix_on(1), residual1, *quarters1)
        u1_x, u1_yx = run.hold(u1_x, u1_yx)
        u1_xc, u1_yxc = fan_x(u1_x, u1_yx, "u1")
        ups1 = in_place(u1, u1_y, u1_x, u1_c, u1_yx, u1_yc, u1_xc, u1_yxc)
        wide1 = run(up_on(1), mixed1[4], *ups1)
        d1_y = run.hold(*d1_y)
        d1_yc = swaps(d1_y, "c", "d1_yc")
        downs1 = (*d1, *d1_y, *d1_c, *d1_yc)
        residual = run(down_on(1), mixed1[3], wide1[0], *downs1)
        weights = [(quarters0, ups0, downs0), (quarters1, ups1, downs1)]
        saved = [(inputs, *mixed0, *wide0), (residual1, *mixed1, *wide1)]
    else:
        weights, saved = [], []
        residual = inputs
        for layer in range(LAYERS):
            quarters = moves.plain_quarters(attn_weight[layer])
            ups = moves.plain_quarters(up_weight[layer])
            downs = moves.plain_halves(down_weight[layer])
            weights.append((quarters, ups, downs))
            mixed = mix_on(layer)(residual, *quarters)
            wide = up_on(layer)(mixed[4], *ups)
            saved.append((residual, *mixed, *wide))
            residual = down_on(layer)(mixed[3], wide[0], *downs)
        ready = prepared(targets, masked, head_weight, head_bias)
    activations, grad, rounded, head_small = run(
        head, residual, *ready, final_gain.reshape(1, D), final_shift.reshape(1, D)
    )

    def down_at(layer):
        return lambda rounded: down_back(place, rounded, saved[layer][6])

    def wide_first(layer):
        _, ups, downs = weights[layer]
        _, _, _, _, _, second, _, slope = saved[layer]
        return lambda rounded: wide_back_first(place, rounded, second, slope, ups, downs)

    def wide_last(layer):
        _, ups, downs = weights[layer]
        _, _, _, _, middle, second, _, slope = saved[layer]
        return lambda rounded, before, grad, *got: wide_back_last(
            place, rounded, second, slope, ups, downs, before, grad, middle, norm_gains[layer], *got
        )

    def mix_first(layer):
        residual, packed, logs, mixed, _, _, _, _ = saved[layer]
        quarters = weights[layer][0]
        gains, biases = norm_gains[layer], layer_biases[layer]
        return lambda rounded, grad: mix_back(
            place, lengths, rounded, grad, residual, quarters, packed, logs, mixed, gains, biases
        )

    def mix_last(*arrays):
        return mix_back_last(place, *arrays)

    def shift_rows(shift_send, shift_keep):
        send, keep = (part.reshape(2, 2, TILE)[::-1] for part in (shift_send, shift_keep))
        parts = moves.ordered(moves.c_at, keep, send).swapaxes(0, 1)
        return jnp.where(moves.x_at == 0, parts, parts[::-1]).reshape(TILES, TILE)

    def packed_small(head_small, *rest):
        small = [head_small]
        for layer in range(LAYERS):
            shift_send, shift_keep, wide_small, mix_small = rest[4 * layer : 4 * layer + 4]
            small += [shift_rows(shift_send, shift_keep), wide_small, mix_small]
        return jnp.concatenate(small, 0)

    def sum_at(at):
        return lambda keep, got, *rest: rounded_sum(keep[at], got[at], *rest)

    if moves.staged:
        *d1_send, d1_keep = run(down_at(1), rounded)
        d1_c = swaps(d1_send, "c", "d1_c")
        *u1_send, shift_send1, before = run(wide_first(1), rounded)
        u1_c = swaps(u1_send, "c", "u1_c")
        d1_y = swap(run(lambda k, *c: down_sum(1, k, c), d1_keep, *d1_c[:4]), "y", "d1_y")
        u1_pass, u1_keep, shift_keep1, grad, rounded1, wide_small1 = run(
            wide_last(1), rounded, before, grad, *u1_c
        )
        u1_x = swap(u1_pass, "x", "u1_x")
        *a1_send, pre1, rights1, grad, rounded, mix_small1 = run(mix_first(1), rounded1, grad)
        a1_c = swaps(a1_send, "c", "a1_c")
        *d0_send, d0_keep = run(down_at(0), rounded)
        d0_c = swaps(d0_send, "c", "d0_c")
        a1_pass, a1_keep = run(mix_last, pre1, saved[1][3], rights1, rounded1, *a1_c)
        a1_x = swap(a1_pass, "x", "a1_x")
        d1 = run(lambda k, y, *c: down_sum(0, k, c, y), d1_keep, d1_y, *d1_c[4:])
        d1 = moves.along_z(d1)
        d0_y = swap(run(lambda k, *c: down_sum(1, k, c), d0_keep, *d0_c[:4]), "y", "d0_y")
        *u0_send, shift_send0, before = run(wide_first(0), rounded)
        u0_c = swaps(u0_send, "c", "u0_c")
        u1_y = swap(run(sum_at(1), u1_keep, u1_x), "y", "u1_y")
        a1_y = swap(run(sum_at(1), a1_keep, a1_x), "y", "a1_y")
        u0_pass, u0_keep, shift_keep0, grad, rounded0, wide_small0 = run(
            wide_last(0), rounded, before, grad, *u0_c
        )
        u0_x = swap(u0_pass, "x", "u0_x")
        d0 = run(lambda k, y, *c: down_sum(0, k, c, y), d0_keep, d0_y, *d0_c[4:])
        d0 = moves.along_z(d0)
        (d1,) = run.hold(d1)
        d1_x, d1_c = swap(d1, "x", "d1_x"), swap(d1, "c", "d1_c")

        def last_sums(u, ux, uy, a, ax, ay):
            both = (wide_sum(u[0], ux[0], uy), wide_sum(a[0], ax[0], ay)[:, None])
            return moves.part_near(jnp.concatenate(both, 1))

        *a0_send, pre0, rights0, grad, rounded, mix_small0 = run(mix_first(0), rounded0, grad)
        a0_c = swaps(a0_send, "c", "a0_c")
        j1_send, j1_stay = run(last_sums, u1_keep, u1_x, u1_y, a1_keep, a1_x, a1_y)
        j1_near = moves.hop(j1_send, 1, "j1_near")
        a0_pass, a0_keep = run(mix_last, pre0, saved[0][3], rights0, rounded0, *a0_c)
        a0_x = swap(a0_pass, "x", "a0_x")
        small = run(
            packed_small,
            head_small,
            *(shift_send0, shift_keep0, wide_small0, mix_small0),
            *(shift_send1, shift_keep1, wide_small1, mix_small1),
        )
        small_c = swap(small, "c", "small_c")
        (d1_x,) = run.hold(d1_x)
        d1_xc = swap(d1_x, "c", "d1_xc")
        u0_y = swap(run(sum_at(1), u0_keep, u0_x), "y", "u0_y")
        small = run(plus, small, small_c)
        small_far = moves.hop(small, 2, "small_far")
        j1_send, j1_stay = run(moves.part_far, j1_stay, j1_near)
        j1_far = moves.hop(j1_send, 2, "j1_far")
        (d0,) = run.hold(d0)
        d0_x, d0_c = swap(d0, "x", "d0_x"), swap(d0, "c", "d0_c")
        small = run(plus, small, small_far)
        small_near = moves.hop(small, 1, "small_near")
        a0_y = swap(run(sum_at(1), a0_keep, a0_x), "y", "a0_y")
        u0 = moves.along_z(run(sum_at(0), u0_keep, u0_x, u0_y))
        j1 = run(rounded_sum, j1_stay, j1_far)
        j1_x, j1_c = swap(j1, "x", "j1_x"), swap(j1, "c", "j1_c")
        small = run(plus, small, small_near)
        small_x = swap(small, "x", "small_x")
        (d0_x,) = run.hold(d0_x)
        d0_xc = swap(d0_x, "c", "d0_xc")
        a0_send, a0_stay = run(lambda k, x, y: moves.part_near(k[0], x[0], y), a0_keep, a0_x, a0_y)
        a0_near = moves.hop(a0_send, 1, "a0_near")
        small = run(plus, small, small_x)
        small_y = swap(small, "y", "small_y")
        (j1_x,) = run.hold(j1_x)
        j1_xc = swap(j1_x, "c", "j1_xc")
        a0_send, a0_stay = run(moves.part_far, a0_stay, a0_near)
        a0_far = moves.hop(a0_send, 2, "a0_far")
        summed = run(plus, small, small_y)
        j0 = run(lambda u, *a: jnp.concatenate([u, rounded_sum(*a)[None]]), u0, a0_stay, a0_far)
        j0_x, j0_c = swap(j0, "x", "j0_x"), swap(j0, "c", "j0_c")
        done = run(
            lambda *v: finish(1, place, v[:4], v[4:]),
            *(j1, j1_c, j1_x, j1_xc, d1, d1_c, d1_x, d1_xc),
        )
        (j0_x,) = run.hold(j0_x)
        j0_xc = swap(j0_x, "c", "j0_xc")
        matrix_grads = run(
            lambda *v: finish(0, place, v[:4], v[4:8], *v[8:]),
            *(j0, j0_c, j0_x, j0_xc, d0, d0_c, d0_x, d0_xc, *done),
        )
    else:
        flats, smalls = [None] * LAYERS, [None] * LAYERS
        for layer in reversed(range(LAYERS)):
            *send, keep = down_at(layer)(rounded)
            got = swaps(send, "c", "down")
            got = jnp.stack([jnp.stack(got[4:]), jnp.stack(got[:4])])
            down_grad = moves.plain_halves_back(rounded_sum(keep, got))
            *send, shift_send, before = wide_first(layer)(rounded)
            passed, keep, shift_keep, grad, rounded, wide_small = wide_last(layer)(
                rounded, before, grad, *swaps(send, "c", "up")
            )
            up_grad = moves.plain_quarters_back(passed, keep)
            middle_rounded = rounded
            *send, pre, rights, grad, rounded, mix_small = mix_first(layer)(rounded, grad)
            got = swaps(send, "c", "attn")
            passed, keep = mix_last(pre, saved[layer][3], rights, middle_rounded, *got)
            attn_grad = moves.plain_quarters_back(passed[:, :, None], keep[:, :, None])
            flats[layer] = (attn_grad, up_grad, down_grad)
            smalls[layer] = (shift_send, shift_keep, wide_small, mix_small)
        summed = moves.sum_all(packed_small(head_small, *smalls[0], *smalls[1]))
        matrix_grads = [jnp.stack(pair) for pair in zip(*flats)]

    gains_grad, biases_grad, shifts_grad = [], [], []
    for layer in range(LAYERS):
        base = 40 + 24 * layer
        shifts_grad.append(summed[base : base + 8].reshape(FF))
        wide_sums = summed[base + 8 : base + 16]
        mix_sums = summed[base + 16 : base + 24]
        gains_grad.append(jnp.stack([mix_sums[0], wide_sums[0]]))
        biases_grad.append(
            jnp.stack([mix_sums[1], wide_sums[1], mix_sums[2], mix_sums[3], wide_sums[2], wide_sums[3]])
        )
    totals = summed[35]
    return (
        activations,
        grad,
        *matrix_grads,
        jnp.stack(gains_grad),
        jnp.stack(biases_grad),
        jnp.stack(shifts_grad),
        summed[:VOCAB].T,
        summed[32],
        summed[33],
        summed[34, :VOCAB],
        totals[0] / totals[2],
        totals[1] / totals[2],
        totals[2].astype(jnp.int32),
    )


def solution(mesh):
    fsdp, dp = mesh.shape["fsdp"], mesh.shape["dp"]
    fine = Mesh(mesh.devices.reshape(fsdp // 2, 2, dp // 2, 2), ("z", "y", "x", "c"))
    tokens = ("z", "y", "x", "c")
    flat = P(None, ("z", "y"), None)
    placed = (P(tokens, None), P(tokens), P(tokens), P(tokens), flat, flat, flat) + (P(),) * 7

    def run(*arrays):
        return local(fsdp, *arrays)

    return jax.shard_map(
        run,
        mesh=fine,
        in_specs=placed,
        out_specs=(P(tokens, None), P(tokens, None), flat, flat, flat) + (P(),) * 10,
        check_vma=False,
    )
```

time: 745 us -> 591 us (0.79)
  blocking collectives: 119 us -> 0 us
  other arithmetic: 76.4 us -> 31 us
  waiting for transfers between devices: 249 us -> 207 us
  starting transfers between devices: 35 us -> 71.7 us
  Pallas kernels: 188 us -> 220 us
  local copies, waits for them, and re-layouts: 48 us -> 33.6 us
    all_gather x10 -> x0, blocking collectives: 119 us -> none  [the longest x4 82.8 us: gather_quarters(): line = lax.all_gather(own, 'z', axis=0, tiled=False)]
    ppermute x41 -> x105, waiting for transfers between devices: 213 us -> 110 us  [swap(): return lax.ppermute(value, axis, [(0, 1), (1, 0)])]
    ppermute x2 -> x18, waiting for transfers between devices: 15 us -> 96.4 us  [hop(): lax.ppermute(value, 'z', [(at, at ^ reach) for at in range(self.z_size)])]
    convert_element_type x34 -> x6, other arithmetic: 56 us -> 10.7 us  [rounded_sum(): return wide_sum(*values).astype(BF)]
    pallas_call x10 -> x22, Pallas kernels: 184 us -> 213 us  [the longest x2 33.9 us: mix_back(): pl.pallas_call(mix_back_kernel, out_shape=(part,) * 4 + (sds((ROWS, D), B...]
    all_gather x2 -> x0, waiting for transfers between devices: 20.7 us -> none  [gather_halves(): line = lax.all_gather(own, 'z', axis=0, tiled=False)]
    ppermute x2 -> x18, starting transfers between devices: 2.74 us -> 21.4 us  [hop(): lax.ppermute(value, 'z', [(at, at ^ reach) for at in range(self.z_size)])]
    ppermute x41 -> x105, starting transfers between devices: 31.7 us -> 49.9 us  [swap(): return lax.ppermute(value, axis, [(0, 1), (1, 0)])]
  transfers between devices with their start and end apart: 51 -> 126, of which waited for: 18 -> 45; matrix products, arithmetic and copies ran while one was open for 12% -> 8% of each run, Pallas kernels for 11% -> 32%
where the time goes in v4:
time: 591 us; the launch traced here: 586 us
  Pallas kernels  220 us (37%)
  waiting for transfers between devices  207 us (35%)
  starting transfers between devices  71.7 us (12%)
  local copies, waits for them, and re-layouts  33.6 us (6%)
  other arithmetic  31 us (5%)
  between operations  22.4 us (4%)
    ppermute x105, waiting for transfers between devices, swap(): return lax.ppermute(value, axis, [(0, 1), (1, 0)])  110 us
    ppermute x18, waiting for transfers between devices, hop(): lax.ppermute(value, 'z', [(at, at ^ reach) for at in range(self.z_size)])  96.4 us
    ppermute x105, starting transfers between devices, swap(): return lax.ppermute(value, axis, [(0, 1), (1, 0)])  49.9 us
    pallas_call x2, Pallas kernels, mix_back(): pl.pallas_call(mix_back_kernel, out_shape=(part,) * 4 + (sds((ROWS, D), B...  33.9 us
    pallas_call x2, Pallas kernels, wide_back_last(): pl.pallas_call(wide_back_last_kernel, grid=(2,), in_specs=[SMEM_SPEC, ful...  31.3 us
    pallas_call x2, Pallas kernels, mix(): pl.pallas_call(mix_kernel, grid=(1,), out_shape=(sds((ROWS, 3 * D), BF),...  28.9 us
    pallas_call x2, Pallas kernels, wide_back_first(): pl.pallas_call(wide_back_first_kernel, grid=(2,), in_specs=[SMEM_SPEC, fu...  28.6 us
    pallas_call x2, Pallas kernels, up(): pl.pallas_call(up_kernel, grid=(STEPS,), out_shape=(out, out), in_specs=[...  22.3 us
  transfers between devices with their start and end apart: 126, of which 45 were waited for; matrix products, arithmetic and copies ran while one was open for 8% of the time, Pallas kernels for 32%

profile of v4, /device:TPU:0, one launch (start us, length us, event | category | flops | bytes accessed | tf_op | source)
XLA Modules:
  0.0 586.1 jit_solution(16125995471849658901)
XLA Ops:
  8.8 4.1 collective-permute-start
  16.2 6.9 %collective-permute-done = bf16[1,80,640]{2,1,0:T(8,128)(2,1)S(1)} collective-permute-done((bf16[1,80,640]{2,1,0:T(8,128)(2,1)S(1)}, bf16[1,80,640]{2,1,0:T(8,128)(2,1)S(1)}, u32[]{:S(2)}, u32[]{:S(2)}) %collective-permute-start) | collective-permute-done | bytes 102432 | tf_op jit(solution)/shard_map/a0_far/ppermute | solution.py:1060
  24.0 2.9 collective-permute-done.2
  28.6 3.4 collective-permute-done.1
  32.1 1.8 collective-permute-start.3
  39.0 6.7 %collective-permute-done.9 = bf16[2,2,80,640]{3,2,1,0:T(8,128)(2,1)} collective-permute-done((bf16[2,2,80,640]{3,2,1,0:T(8,128)(2,1)S(1)}, bf16[2,2,80,640]{3,2,1,0:T(8,128)(2,1)}, u32[]{:S(2)}, u32[]{:S(2)}) %collective-permute-start.9) | collective-permute-done | bytes 409632 | tf_op jit(solution)/shard_map/u0_near/ppermute | solution.py:1060
  48.7 2.6 collective-permute-start.12
  51.2 1.8 collective-permute-done.8
  61.1 14.3 %shard_map.253 = (bf16[512,1920]{1,0:T(8,128)(2,1)}, f32[20,1,512]{2,1,0:T(1,128)}, bf16[512,640]{1,0:T(8,128)(2,1)}, f32[512,640]{1,0:T(8,128)}, bf16[512,640]{1,0:T(8,128)(2,1)}) custom-call(s32[3]{0:T(128)} %pad_add_fusion.place_ref.refs_0_, s32[4]{0:T(128)} %lengths_ref.7, bf16[512,640]{1,0:T(8,128)(2,1)} %residual_ref.2, ...), custom_call_target="tpu_custom_call" | custom-call | flops 400000000 | bytes 2097152 | tf_op jit(solution)/shard_map/pallas_call | solution.py:206
  78.7 3.0 collective-permute-start.19
  81.7 9.6 %collective-permute-done.19 = bf16[1,80,640]{2,1,0:T(8,128)(2,1)S(1)} collective-permute-done((bf16[1,80,640]{2,1,0:T(8,128)(2,1)S(1)}, bf16[1,80,640]{2,1,0:T(8,128)(2,1)S(1)}, u32[]{:S(2)}, u32[]{:S(2)}) %collective-permute-start.19) | collective-permute-done | bytes 102432 | tf_op jit(solution)/shard_map/a1_far/ppermute | solution.py:1060
  91.4 4.2 collective-permute-done.18
  99.2 13.7 %collective-permute-done.22 = bf16[2,1,80,640]{3,2,0,1:T(8,128)(2,1)S(1)} collective-permute-done((bf16[2,1,80,640]{3,2,0,1:T(8,128)(2,1)S(1)}, bf16[2,1,80,640]{3,2,0,1:T(8,128)(2,1)S(1)}, u32[]{:S(2)}, u32[]{:S(2)}) %collective-permute-start.22) | collective-permute-done | bytes 204832 | tf_op jit(solution)/shard_map/a1_near/ppermute | solution.py:1060
  113.0 2.4 collective-permute-start.23
  116.1 2.3 collective-permute-start.25
  120.8 11.2 %shard_map.254 = (bf16[4,512,1280]{2,1,0:T(8,128)(2,1)}, bf16[4,512,1280]{2,1,0:T(8,128)(2,1)}) custom-call(s32[3]{0:T(128)} %pad_add_fusion.place_ref.refs_0_, bf16[512,640]{1,0:T(8,128)(2,1)} %get-tuple-element.412.second_ref, bf16[4,2,80,640]{3,2,1,0:T(8,128)(2,1)} %bitcast.172, bf16[4,2,80,640]{3,2,1,0:T(8,128)(2,1)} %collective-permute-done.12.refs_1_, ...), custom_call_target="tpu_custom_call" | custom-call | flops 400000000 | bytes 2097152 | tf_op jit(solution)/shard_map/pallas_call | solution.py:274
  132.3 4.0 collective-permute-done.25
  136.4 2.4 maximum_select_fusion.5
  138.8 11.8 %collective-permute-done.24.refs_3_.refs_7_ = bf16[2,320,640]{2,1,0:T(8,128)(2,1)} collective-permute-done((bf16[2,320,640]{2,1,0:T(8,128)(2,1)S(1)}, bf16[2,320,640]{2,1,0:T(8,128)(2,1)}, u32[]{:S(2)}, u32[]{:S(2)}) %collective-permute-start.24) | collective-permute-done | bytes 819232 | tf_op jit(solution)/shard_map/d0_y/ppermute | solution.py:1011
  151.7 1.7 collective-permute-start.31
  156.5 10.4 %shard_map.255.residual_ref = f32[512,640]{1,0:T(8,128)} custom-call(s32[3]{0:T(128)} %pad_add_fusion.place_ref.refs_0_, f32[512,640]{1,0:T(8,128)} %get-tuple-element.429.middle_ref.refs_14_, bf16[4,512,1280]{2,1,0:T(8,128)(2,1)} %get-tuple-element.430.active_ref, bf16[2,320,640]{2,1,0:T(8,128)(2,1)} %copy-done.1, bf16[2,320,640]{2,1,0:T(8,128)(2,1)} %copy-done, ...), custom_call_target="tpu_custom_call" | custom-call | flops 400000000 | bytes 2097152 | tf_op jit(solution)/shard_map/pallas_call | solution.py:316
  167.4 4.1 collective-permute-done.36
  171.6 2.2 maximum_select_fusion.1
  173.9 6.5 %collective-permute-done.39.refs_1_ = bf16[4,2,80,640]{3,2,1,0:T(8,128)(2,1)} collective-permute-done((bf16[4,2,80,640]{3,2,1,0:T(8,128)(2,1)S(1)}, bf16[4,2,80,640]{3,2,1,0:T(8,128)(2,1)}, u32[]{:S(2)}, u32[]{:S(2)}) %collective-permute-start.39) | collective-permute-done | bytes 819232 | tf_op jit(solution)/shard_map/u1_y/ppermute | solution.py:1011
  183.8 2.2 collective-permute-done.37.refs_6_
  187.0 14.6 %shard_map.256 = (bf16[512,1920]{1,0:T(8,128)(2,1)}, f32[20,1,512]{2,1,0:T(1,128)}, bf16[512,640]{1,0:T(8,128)(2,1)}, f32[512,640]{1,0:T(8,128)}, bf16[512,640]{1,0:T(8,128)(2,1)}) custom-call(s32[3]{0:T(128)} %pad_add_fusion.place_ref.refs_0_, s32[4]{0:T(128)} %lengths_ref.7, f32[512,640]{1,0:T(8,128)} %shard_map.255.residual_ref, ...), custom_call_target="tpu_custom_call" | custom-call | flops 400000000 | bytes 2097152 | tf_op jit(solution)/shard_map/pallas_call | solution.py:206
  201.7 15.4 %collective-permute-done.43.refs_5_.refs_3_ = bf16[4,2,80,640]{3,2,1,0:T(8,128)(2,1)} collective-permute-done((bf16[4,2,80,640]{3,2,1,0:T(8,128)(2,1)}, bf16[4,2,80,640]{3,2,1,0:T(8,128)(2,1)}, u32[]{:S(2)}, u32[]{:S(2)}) %collective-permute-start.43) | collective-permute-done | bytes 819232 | tf_op jit(solution)/shard_map/u1_yx/ppermute | solution.py:1011
  220.9 11.0 %shard_map.257 = (bf16[4,512,1280]{2,1,0:T(8,128)(2,1)}, bf16[4,512,1280]{2,1,0:T(8,128)(2,1)}) custom-call(s32[3]{0:T(128)} %pad_add_fusion.place_ref.refs_0_, bf16[512,640]{1,0:T(8,128)(2,1)} %get-tuple-element.459.second_ref, bf16[4,2,80,640]{3,2,1,0:T(8,128)(2,1)} %bitcast.177, bf16[4,2,80,640]{3,2,1,0:T(8,128)(2,1)} %collective-permute-done.39.refs_1_, ...), custom_call_target="tpu_custom_call" | custom-call | flops 400000000 | bytes 2097152 | tf_op jit(solution)/shard_map/pallas_call | solution.py:274
  232.0 6.7 %collective-permute-done.46.refs_2_.refs_6_ = bf16[2,320,640]{2,1,0:T(8,128)(2,1)S(1)} collective-permute-done((bf16[2,320,640]{2,1,0:T(8,128)(2,1)S(1)}, bf16[2,320,640]{2,1,0:T(8,128)(2,1)S(1)}, u32[]{:S(2)}, u32[]{:S(2)}) %collective-permute-start.46) | collective-permute-done | bytes 819232 | tf_op jit(solution)/shard_map/d1_y/ppermute | solution.py:1011
  238.7 16.6 %collective-permute-done.47.refs_3_.refs_7_ = bf16[2,320,640]{2,1,0:T(8,128)(2,1)S(1)} collective-permute-done((bf16[2,320,640]{2,1,0:T(8,128)(2,1)S(1)}, bf16[2,320,640]{2,1,0:T(8,128)(2,1)S(1)}, u32[]{:S(2)}, u32[]{:S(2)}) %collective-permute-start.47) | collective-permute-done | bytes 819232 | tf_op jit(solution)/shard_map/d1_y/ppermute | solution.py:1011
  259.0 10.4 %shard_map.258.residual_ref = f32[512,640]{1,0:T(8,128)} custom-call(s32[3]{0:T(128)} %pad_add_fusion.place_ref.refs_0_, f32[512,640]{1,0:T(8,128)} %get-tuple-element.471.middle_ref.refs_14_, bf16[4,512,1280]{2,1,0:T(8,128)(2,1)} %get-tuple-element.472.active_ref, bf16[2,320,640]{2,1,0:T(8,128)(2,1)} %copy-done.3, bf16[2,320,640]{2,1,0:T(8,128)(2,1)} %copy-done.2, ...), custom_call_target="tpu_custom_call" | custom-call | flops 400000000 | bytes 2097152 | tf_op jit(solution)/shard_map/pallas_call | solution.py:316
  271.1 6.7 %shard_map.259 = (bf16[512,640]{1,0:T(8,128)(2,1)}, f32[512,640]{1,0:T(8,128)}, bf16[512,640]{1,0:T(8,128)(2,1)}, f32[40,640]{1,0:T(8,128)}) custom-call(f32[512,640]{1,0:T(8,128)} %shard_map.258.residual_ref, s32[512,1]{1,0:T(8,128)} %copy.78.targets_ref, s32[512,1]{1,0:T(8,128)} %copy.79.masked_ref, bf16[640,128]{1,0:T(8,128)(2,1)} %pad.8.weight_ref, ...), custom_call_target="tpu_custom_call" | custom-call | flops 400000000 | bytes 2097152 | tf_op jit(solution)/shard_map/pallas_call | solution.py:393
  277.8 8.2 %shard_map.260 = (bf16[320,640]{1,0:T(8,128)(2,1)}, bf16[320,640]{1,0:T(8,128)(2,1)}, bf16[320,640]{1,0:T(8,128)(2,1)}, bf16[320,640]{1,0:T(8,128)(2,1)}, bf16[3...) custom-call(s32[3]{0:T(128)} %pad_add_fusion.place_ref.refs_0_, ...), custom_call_target="tpu_custom_call" | custom-call | flops 400000000 | bytes 2097152 | tf_op jit(solution)/shard_map/pallas_call | solution.py:445
  287.1 14.3 %shard_map.261 = (bf16[4,80,640]{2,1,0:T(8,128)(2,1)}, bf16[4,80,640]{2,1,0:T(8,128)(2,1)}, bf16[4,80,640]{2,1,0:T(8,128)(2,1)}, bf16[4,80,640]{2,1,0:T(8,128)(2...) custom-call(s32[3]{0:T(128)} %pad_add_fusion.place_ref.refs_0_, ...), custom_call_target="tpu_custom_call" | custom-call | flops 400000000 | bytes 2097152 | tf_op jit(solution)/shard_map/pallas_call | solution.py:600
  303.2 2.9 shard_map.262
  306.1 1.8 collective-permute-start.68
  312.5 15.7 %shard_map.263 = (bf16[2,4,2,80,640]{4,3,2,1,0:T(8,128)(2,1)}, bf16[2,4,2,80,640]{4,3,2,1,0:T(8,128)(2,1)}, f32[2,1280]{1,0:T(2,128)}, f32[512,640]{1,0:T(8,128)...) custom-call(s32[3]{0:T(128)} %pad_add_fusion.place_ref.refs_0_, bf16[512,640]{1,0:T(8,128)(2,1)} %get-tuple-element.516.grad_ref.rounded_ref, ...), custom_call_target="tpu_custom_call" | custom-call | flops 400000000 | bytes 2097152 | tf_op jit(solution)/shard_map/pallas_call | solution.py:706
  328.2 17.1 %shard_map.264 = (bf16[4,80,640]{2,1,0:T(8,128)(2,1)}, bf16[4,80,640]{2,1,0:T(8,128)(2,1)}, bf16[4,80,640]{2,1,0:T(8,128)(2,1)}, bf16[4,80,640]{2,1,0:T(8,128)(2...) custom-call(s32[3]{0:T(128)} %pad_add_fusion.place_ref.refs_0_, ...), custom_call_target="tpu_custom_call" | custom-call | flops 400000000 | bytes 2097152 | tf_op jit(solution)/shard_map/pallas_call | solution.py:858
  351.1 8.2 %shard_map.265 = (bf16[320,640]{1,0:T(8,128)(2,1)}, bf16[320,640]{1,0:T(8,128)(2,1)}, bf16[320,640]{1,0:T(8,128)(2,1)}, bf16[320,640]{1,0:T(8,128)(2,1)}, bf16[3...) custom-call(s32[3]{0:T(128)} %pad_add_fusion.place_ref.refs_0_, ...), custom_call_target="tpu_custom_call" | custom-call | flops 400000000 | bytes 2097152 | tf_op jit(solution)/shard_map/pallas_call | solution.py:445
  359.3 4.6 shard_map.266
  365.2 3.4 shard_map.267
  373.9 2.9 shard_map.268
  377.3 14.3 %shard_map.269 = (bf16[4,80,640]{2,1,0:T(8,128)(2,1)}, bf16[4,80,640]{2,1,0:T(8,128)(2,1)}, bf16[4,80,640]{2,1,0:T(8,128)(2,1)}, bf16[4,80,640]{2,1,0:T(8,128)(2...) custom-call(s32[3]{0:T(128)} %pad_add_fusion.place_ref.refs_0_, ...), custom_call_target="tpu_custom_call" | custom-call | flops 400000000 | bytes 2097152 | tf_op jit(solution)/shard_map/pallas_call | solution.py:600
  392.2 13.3 %collective-permute-done.85 = bf16[2,4,80,640]{3,2,1,0:T(8,128)(2,1)} collective-permute-done((bf16[2,4,80,640]{3,2,1,0:T(8,128)(2,1)}, bf16[2,4,80,640]{3,2,1,0:T(8,128)(2,1)}, u32[]{:S(2)}, u32[]{:S(2)}) %collective-permute-start.85) | collective-permute-done | bytes 819232 | tf_op jit(solution)/shard_map/a1_x/ppermute | solution.py:1011
  410.6 1.9 fusion.5
  413.2 1.8 collective-permute-start.98
  415.0 15.6 %shard_map.270 = (bf16[2,4,2,80,640]{4,3,2,1,0:T(8,128)(2,1)}, bf16[2,4,2,80,640]{4,3,2,1,0:T(8,128)(2,1)}, f32[2,1280]{1,0:T(2,128)}, f32[512,640]{1,0:T(8,128)...) custom-call(s32[3]{0:T(128)} %pad_add_fusion.place_ref.refs_0_, bf16[512,640]{1,0:T(8,128)(2,1)} %get-tuple-element.589.grad_ref.rounded_ref, ...), custom_call_target="tpu_custom_call" | custom-call | flops 400000000 | bytes 2097152 | tf_op jit(solution)/shard_map/pallas_call | solution.py:706
  432.2 3.4 shard_map.271
  435.6 16.8 %shard_map.272 = (bf16[4,80,640]{2,1,0:T(8,128)(2,1)}, bf16[4,80,640]{2,1,0:T(8,128)(2,1)}, bf16[4,80,640]{2,1,0:T(8,128)(2,1)}, bf16[4,80,640]{2,1,0:T(8,128)(2...) custom-call(s32[3]{0:T(128)} %pad_add_fusion.place_ref.refs_0_, ...), custom_call_target="tpu_custom_call" | custom-call | flops 400000000 | bytes 2097152 | tf_op jit(solution)/shard_map/pallas_call | solution.py:858
  459.9 4.8 shard_map.273
  466.0 3.4 collective-permute-done.92
  469.4 2.2 fusion.2
  472.8 2.6 collective-permute-start.102
  475.4 30.3 %collective-permute-done.103 = bf16[2,3,80,640]{3,2,1,0:T(8,128)(2,1)S(1)} collective-permute-done((bf16[2,3,80,640]{3,2,1,0:T(8,128)(2,1)}, bf16[2,3,80,640]{3,2,1,0:T(8,128)(2,1)S(1)}, u32[]{:S(2)}, u32[]{:S(2)}) %collective-permute-start.103) | collective-permute-done | bytes 614432 | tf_op jit(solution)/shard_map/j1_near/ppermute | solution.py:1060
  508.4 1.9 fusion.6
  511.9 2.6 fusion
  514.5 4.6 collective-permute-done.106
  522.0 2.0 collective-permute-start.108
  525.7 10.3 %collective-permute-done.108 = f32[88,640]{1,0:T(8,128)S(1)} collective-permute-done((f32[88,640]{1,0:T(8,128)S(1)}, f32[88,640]{1,0:T(8,128)S(1)}, u32[]{:S(2)}, u32[]{:S(2)}) %collective-permute-start.108) | collective-permute-done | bytes 225312 | tf_op jit(solution)/shard_map/small_x/ppermute | solution.py:1011
  536.4 7.7 %collective-permute-done.110 = f32[88,640]{1,0:T(8,128)S(1)} collective-permute-done((f32[88,640]{1,0:T(8,128)S(1)}, f32[88,640]{1,0:T(8,128)S(1)}, u32[]{:S(2)}, u32[]{:S(2)}) %collective-permute-start.110) | collective-permute-done | bytes 225312 | tf_op jit(solution)/shard_map/small_y/ppermute | solution.py:1011
  546.7 4.0 collective-permute-done.109
  552.1 5.2 collective-permute-done.121.refs_7_
  563.8 4.6 shard_map.274
  571.2 4.6 shard_map.275
  (513 shorter events, 109.0 us)
Async XLA Ops:
  7.2 518.4 %reduce-scatter.6.cloned.1.call-start = ((), (), s32[]{:S(2)}) async-start(), calls=%async_computation.4 | async-start | bytes 2048000 | tf_op jit(solution)/shard_map/reduce_scatter | solution.py:1111
  27.0 18.7 %collective-permute-start.9 = (bf16[2,2,80,640]{3,2,1,0:T(8,128)(2,1)S(1)}, bf16[2,2,80,640]{3,2,1,0:T(8,128)(2,1)}, u32[]{:S(2)}, u32[]{:S(2)}) collective-permute-start(bf16[2,2,80,640]{3,2,1,0:T(8,128)(2,1)S(1)} %maximum_select_fusion.6), channel_id=1, source_target_pairs={{0,8},{8,0},{16,24},{24,16},{1,9},{9,1},{17,25},{25,17},{2,10},{10... | collective-permute-start | bytes 1228808 | tf_op jit(solution)/shard_map/u0_near/ppermute | solution.py:1060
  33.9 19.2 %collective-permute-start.8 = (bf16[1,320,640]{2,1,0:T(8,128)(2,1)S(1)}, bf16[1,320,640]{2,1,0:T(8,128)(2,1)}, u32[]{:S(2)}, u32[]{:S(2)}) collective-permute-start(bf16[1,320,640]{2,1,0:T(8,128)(2,1)S(1)} %reshape.646), channel_id=1, source_target_pairs={{0,16},{8,24},{16,0},{24,8},{1,17},{9,25},{17,1},{25,9},{2,18},{10... | collective-permute-start | bytes 1228808 | tf_op jit(solution)/shard_map/d0_far/ppermute | solution.py:1060
  35.1 20.6 %collective-permute-start.6 = (bf16[4,1,80,640]{3,2,1,0:T(8,128)(2,1)S(1)}, bf16[4,1,80,640]{3,2,1,0:T(8,128)(2,1)S(1)}, u32[]{:S(2)}, u32[]{:S(2)}) collective-permute-start(bf16[4,1,80,640]{3,2,1,0:T(8,128)(2,1)S(1)} %bitcast.180), channel_id=1, source_target_pairs={{0,2},{2,0},{1,3},{3,1},{4,6},{6,4},{5,7},{7,5},{8,10},{10,8},{9,1... | collective-permute-start | bytes 1228808 | tf_op jit(solution)/shard_map/a0_x/ppermute | solution.py:1011
  36.6 19.9 %collective-permute-start.4 = (bf16[4,1,80,640]{3,2,1,0:T(8,128)(2,1)S(1)}, bf16[4,1,80,640]{3,2,1,0:T(8,128)(2,1)}, u32[]{:S(2)}, u32[]{:S(2)}) collective-permute-start(bf16[4,1,80,640]{3,2,1,0:T(8,128)(2,1)S(1)} %bitcast.181), channel_id=1, source_target_pairs={{0,1},{1,0},{2,3},{3,2},{4,5},{5,4},{6,7},{7,6},{8,9},{9,8},{10,11... | collective-permute-start | bytes 1228808 | tf_op jit(solution)/shard_map/a0_c/ppermute | solution.py:1011
  48.7 26.7 %collective-permute-start.12 = (bf16[4,2,80,640]{3,2,1,0:T(8,128)(2,1)S(1)}, bf16[4,2,80,640]{3,2,1,0:T(8,128)(2,1)}, u32[]{:S(2)}, u32[]{:S(2)}) collective-permute-start(bf16[4,2,80,640]{3,2,1,0:T(8,128)(2,1)S(1)} %bitcast.169), channel_id=1, source_target_pairs={{0,4},{4,0},{1,5},{5,1},{2,6},{6,2},{3,7},{7,3},{8,12},{12,8},{9,1... | collective-permute-start | bytes 2457608 | tf_op jit(solution)/shard_map/u0_y/ppermute | solution.py:1011
  54.3 21.7 %collective-permute-start.17 = (bf16[2,1,320,640]{3,2,0,1:T(8,128)(2,1)S(1)}, bf16[2,1,320,640]{3,2,0,1:T(8,128)(2,1)}, u32[]{:S(2)}, u32[]{:S(2)}) collective-permute-start(bf16[2,1,320,640]{3,2,0,1:T(8,128)(2,1)S(1)} %maximum_select_fusion.3), channel_id=1, source_target_pairs={{0,8},{8,0},{16,24},{24,16},{1,9},{9,1},{17,25},{25,17},{2,10},{10... | collective-permute-start | bytes 2457608 | tf_op jit(solution)/shard_map/d0_near/ppermute | solution.py:1060
  58.9 36.9 %collective-permute-start.15 = (bf16[4,2,80,640]{3,2,1,0:T(8,128)(2,1)S(1)}, bf16[4,2,80,640]{3,2,1,0:T(8,128)(2,1)}, u32[]{:S(2)}, u32[]{:S(2)}) collective-permute-start(bf16[4,2,80,640]{3,2,1,0:T(8,128)(2,1)S(1)} %bitcast.170), channel_id=1, source_target_pairs={{0,2},{2,0},{1,3},{3,1},{4,6},{6,4},{5,7},{7,5},{8,10},{10,8},{9,1... | collective-permute-start | bytes 2457608 | tf_op jit(solution)/shard_map/u0_x/ppermute | solution.py:1011
  75.4 21.3 %collective-permute-start.16 = (bf16[4,2,80,640]{3,2,1,0:T(8,128)(2,1)}, bf16[4,2,80,640]{3,2,1,0:T(8,128)(2,1)}, u32[]{:S(2)}, u32[]{:S(2)}) collective-permute-start(bf16[4,2,80,640]{3,2,1,0:T(8,128)(2,1)} %collective-permute-done.12.refs_1_), channel_id=1, source_target_pairs={{0,2},{2,0},{1,3},{3,1},{4,6},{6,4},{5,7},{7,5},{8,10},{10,8},{9,1... | collective-permute-start | bytes 2457608 | tf_op jit(solution)/shard_map/u0_yx/ppermute | solution.py:1011
  76.1 21.6 %collective-permute-start.13 = (bf16[4,2,80,640]{3,2,1,0:T(8,128)(2,1)S(1)}, bf16[4,2,80,640]{3,2,1,0:T(8,128)(2,1)S(1)}, u32[]{:S(2)}, u32[]{:S(2)}) collective-permute-start(bf16[4,2,80,640]{3,2,1,0:T(8,128)(2,1)S(1)} %bitcast.171), channel_id=1, source_target_pairs={{0,1},{1,0},{2,3},{3,2},{4,5},{5,4},{6,7},{7,6},{8,9},{9,8},{10,11... | collective-permute-start | bytes 2457608 | tf_op jit(solution)/shard_map/u0_c/ppermute | solution.py:1011
  91.3 24.8 %collective-permute-start.14 = (bf16[4,2,80,640]{3,2,1,0:T(8,128)(2,1)}, bf16[4,2,80,640]{3,2,1,0:T(8,128)(2,1)}, u32[]{:S(2)}, u32[]{:S(2)}) collective-permute-start(bf16[4,2,80,640]{3,2,1,0:T(8,128)(2,1)} %collective-permute-done.12.refs_1_), channel_id=1, source_target_pairs={{0,1},{1,0},{2,3},{3,2},{4,5},{5,4},{6,7},{7,6},{8,9},{9,8},{10,11... | collective-permute-start | bytes 2457608 | tf_op jit(solution)/shard_map/u0_yc/ppermute | solution.py:1011
  96.7 22.4 %collective-permute-start.20 = (bf16[4,2,80,640]{3,2,1,0:T(8,128)(2,1)}, bf16[4,2,80,640]{3,2,1,0:T(8,128)(2,1)}, u32[]{:S(2)}, u32[]{:S(2)}) collective-permute-start(bf16[4,2,80,640]{3,2,1,0:T(8,128)(2,1)} %collective-permute-done.15.refs_4_.refs_2_), channel_id=1, source_target_pairs={{0,1},{1,0},{2,3},{3,2},{4,5},{5,4},{6,7},{7,6},{8,9},{9,8},{10,11... | collective-permute-start | bytes 2457608 | tf_op jit(solution)/shard_map/u0_xc/ppermute | solution.py:1011
  96.7 22.4 %collective-permute-start.21 = (bf16[4,2,80,640]{3,2,1,0:T(8,128)(2,1)}, bf16[4,2,80,640]{3,2,1,0:T(8,128)(2,1)}, u32[]{:S(2)}, u32[]{:S(2)}) collective-permute-start(bf16[4,2,80,640]{3,2,1,0:T(8,128)(2,1)} %collective-permute-done.16.refs_5_.refs_3_), channel_id=1, source_target_pairs={{0,1},{1,0},{2,3},{3,2},{4,5},{5,4},{6,7},{7,6},{8,9},{9,8},{10,11... | collective-permute-start | bytes 2457608 | tf_op jit(solution)/shard_map/u0_yxc/ppermute | solution.py:1011
  97.2 18.2 %collective-permute-start.26 = (bf16[2,2,80,640]{3,2,1,0:T(8,128)(2,1)S(1)}, bf16[2,2,80,640]{3,2,1,0:T(8,128)(2,1)S(1)}, u32[]{:S(2)}, u32[]{:S(2)}) collective-permute-start(bf16[2,2,80,640]{3,2,1,0:T(8,128)(2,1)S(1)} %maximum_select_fusion.8), channel_id=1, source_target_pairs={{0,8},{8,0},{16,24},{24,16},{1,9},{9,1},{17,25},{25,17},{2,10},{10... | collective-permute-start | bytes 1228808 | tf_op jit(solution)/shard_map/u1_near/ppermute | solution.py:1060
  97.7 15.2 %collective-permute-start.22 = (bf16[2,1,80,640]{3,2,0,1:T(8,128)(2,1)S(1)}, bf16[2,1,80,640]{3,2,0,1:T(8,128)(2,1)S(1)}, u32[]{:S(2)}, u32[]{:S(2)}) collective-permute-start(bf16[2,1,80,640]{3,2,0,1:T(8,128)(2,1)S(1)} %maximum_select_fusion.10), channel_id=1, source_target_pairs={{0,8},{8,0},{16,24},{24,16},{1,9},{9,1},{17,25},{25,17},{2,10},{10... | collective-permute-start | bytes 614408 | tf_op jit(solution)/shard_map/a1_near/ppermute | solution.py:1060
  113.0 25.8 %collective-permute-start.23 = (bf16[2,320,640]{2,1,0:T(8,128)(2,1)S(1)}, bf16[2,320,640]{2,1,0:T(8,128)(2,1)S(1)}, u32[]{:S(2)}, u32[]{:S(2)}) collective-permute-start(bf16[2,320,640]{2,1,0:T(8,128)(2,1)S(1)} %get-tuple-element.431.refs_0_.refs_4_), channel_id=1, source_target_pairs={{0,4},{4,0},{1,5},{5,1},{2,6},{6,2},{3,7},{7,3},{8,12},{12,8},{9,1... | collective-permute-start | bytes 2457608 | tf_op jit(solution)/shard_map/d0_y/ppermute | solution.py:1011
  115.4 35.2 %collective-permute-start.24 = (bf16[2,320,640]{2,1,0:T(8,128)(2,1)S(1)}, bf16[2,320,640]{2,1,0:T(8,128)(2,1)}, u32[]{:S(2)}, u32[]{:S(2)}) collective-permute-start(bf16[2,320,640]{2,1,0:T(8,128)(2,1)S(1)} %get-tuple-element.432.refs_1_.refs_5_), channel_id=1, source_target_pairs={{0,4},{4,0},{1,5},{5,1},{2,6},{6,2},{3,7},{7,3},{8,12},{12,8},{9,1... | collective-permute-start | bytes 2457608 | tf_op jit(solution)/shard_map/d0_y/ppermute | solution.py:1011
  116.1 20.2 %collective-permute-start.25 = (bf16[1,320,640]{2,1,0:T(8,128)(2,1)}, bf16[1,320,640]{2,1,0:T(8,128)(2,1)}, u32[]{:S(2)}, u32[]{:S(2)}) collective-permute-start(bf16[1,320,640]{2,1,0:T(8,128)(2,1)} %reshape.651), channel_id=1, source_target_pairs={{0,16},{8,24},{16,0},{24,8},{1,17},{9,25},{17,1},{25,9},{2,18},{10... | collective-permute-start | bytes 1228808 | tf_op jit(solution)/shard_map/d1_far/ppermute | solution.py:1060
  119.1 32.6 %collective-permute-start.27 = (bf16[2,320,640]{2,1,0:T(8,128)(2,1)S(1)}, bf16[2,320,640]{2,1,0:T(8,128)(2,1)}, u32[]{:S(2)}, u32[]{:S(2)}) collective-permute-start(bf16[2,320,640]{2,1,0:T(8,128)(2,1)S(1)} %get-tuple-element.431.refs_0_.refs_4_), channel_id=1, source_target_pairs={{0,1},{1,0},{2,3},{3,2},{4,5},{5,4},{6,7},{7,6},{8,9},{9,8},{10,11... | collective-permute-start | bytes 2457608 | tf_op jit(solution)/shard_map/d0_c/ppermute | solution.py:1011
  119.1 34.3 %collective-permute-start.28 = (bf16[2,320,640]{2,1,0:T(8,128)(2,1)S(1)}, bf16[2,320,640]{2,1,0:T(8,128)(2,1)}, u32[]{:S(2)}, u32[]{:S(2)}) collective-permute-start(bf16[2,320,640]{2,1,0:T(8,128)(2,1)S(1)} %get-tuple-element.432.refs_1_.refs_5_), channel_id=1, source_target_pairs={{0,1},{1,0},{2,3},{3,2},{4,5},{5,4},{6,7},{7,6},{8,9},{9,8},{10,11... | collective-permute-start | bytes 2457608 | tf_op jit(solution)/shard_map/d0_c/ppermute | solution.py:1011
  151.1 20.5 %collective-permute-start.36 = (bf16[2,1,320,640]{3,2,0,1:T(8,128)(2,1)}, bf16[2,1,320,640]{3,2,0,1:T(8,128)(2,1)}, u32[]{:S(2)}, u32[]{:S(2)}) collective-permute-start(bf16[2,1,320,640]{3,2,0,1:T(8,128)(2,1)} %maximum_select_fusion.5), channel_id=1, source_target_pairs={{0,8},{8,0},{16,24},{24,16},{1,9},{9,1},{17,25},{25,17},{2,10},{10... | collective-permute-start | bytes 2457608 | tf_op jit(solution)/shard_map/d1_near/ppermute | solution.py:1060
  151.7 15.2 %collective-permute-start.31 = (bf16[4,1,80,640]{3,2,1,0:T(8,128)(2,1)S(1)}, bf16[4,1,80,640]{3,2,1,0:T(8,128)(2,1)}, u32[]{:S(2)}, u32[]{:S(2)}) collective-permute-start(bf16[4,1,80,640]{3,2,1,0:T(8,128)(2,1)S(1)} %bitcast.184), channel_id=1, source_target_pairs={{0,4},{4,0},{1,5},{5,1},{2,6},{6,2},{3,7},{7,3},{8,12},{12,8},{9,1... | collective-permute-start | bytes 1228808 | tf_op jit(solution)/shard_map/a1_y/ppermute | solution.py:1011
  153.4 27.0 %collective-permute-start.39 = (bf16[4,2,80,640]{3,2,1,0:T(8,128)(2,1)S(1)}, bf16[4,2,80,640]{3,2,1,0:T(8,128)(2,1)}, u32[]{:S(2)}, u32[]{:S(2)}) collective-permute-start(bf16[4,2,80,640]{3,2,1,0:T(8,128)(2,1)S(1)} %bitcast.174), channel_id=1, source_target_pairs={{0,4},{4,0},{1,5},{5,1},{2,6},{6,2},{3,7},{7,3},{8,12},{12,8},{9,1... | collective-permute-start | bytes 2457608 | tf_op jit(solution)/shard_map/u1_y/ppermute | solution.py:1011
  154.9 27.1 %collective-permute-start.34 = (bf16[4,1,80,640]{3,2,1,0:T(8,128)(2,1)S(1)}, bf16[4,1,80,640]{3,2,1,0:T(8,128)(2,1)}, u32[]{:S(2)}, u32[]{:S(2)}) collective-permute-start(bf16[4,1,80,640]{3,2,1,0:T(8,128)(2,1)S(1)} %bitcast.185), channel_id=1, source_target_pairs={{0,2},{2,0},{1,3},{3,1},{4,6},{6,4},{5,7},{7,5},{8,10},{10,8},{9,1... | collective-permute-start | bytes 1228808 | tf_op jit(solution)/shard_map/a1_x/ppermute | solution.py:1011
  156.5 26.1 %collective-permute-start.32 = (bf16[4,1,80,640]{3,2,1,0:T(8,128)(2,1)S(1)}, bf16[4,1,80,640]{3,2,1,0:T(8,128)(2,1)}, u32[]{:S(2)}, u32[]{:S(2)}) collective-permute-start(bf16[4,1,80,640]{3,2,1,0:T(8,128)(2,1)S(1)} %bitcast.186), channel_id=1, source_target_pairs={{0,1},{1,0},{2,3},{3,2},{4,5},{5,4},{6,7},{7,6},{8,9},{9,8},{10,11... | collective-permute-start | bytes 1228808 | tf_op jit(solution)/shard_map/a1_c/ppermute | solution.py:1011
  166.9 15.6 %collective-permute-start.35 = (bf16[4,1,80,640]{3,2,1,0:T(8,128)(2,1)}, bf16[4,1,80,640]{3,2,1,0:T(8,128)(2,1)S(1)}, u32[]{:S(2)}, u32[]{:S(2)}) collective-permute-start(bf16[4,1,80,640]{3,2,1,0:T(8,128)(2,1)} %collective-permute-done.31.refs_1_), channel_id=1, source_target_pairs={{0,2},{2,0},{1,3},{3,1},{4,6},{6,4},{5,7},{7,5},{8,10},{10,8},{9,1... | collective-permute-start | bytes 1228808 | tf_op jit(solution)/shard_map/a1_yx/ppermute | solution.py:1011
  180.4 21.3 %collective-permute-start.42 = (bf16[4,2,80,640]{3,2,1,0:T(8,128)(2,1)S(1)}, bf16[4,2,80,640]{3,2,1,0:T(8,128)(2,1)}, u32[]{:S(2)}, u32[]{:S(2)}) collective-permute-start(bf16[4,2,80,640]{3,2,1,0:T(8,128)(2,1)S(1)} %bitcast.175), channel_id=1, source_target_pairs={{0,2},{2,0},{1,3},{3,1},{4,6},{6,4},{5,7},{7,5},{8,10},{10,8},{9,1... | collective-permute-start | bytes 2457608 | tf_op jit(solution)/shard_map/u1_x/ppermute | solution.py:1011
  182.0 35.1 %collective-permute-start.43 = (bf16[4,2,80,640]{3,2,1,0:T(8,128)(2,1)}, bf16[4,2,80,640]{3,2,1,0:T(8,128)(2,1)}, u32[]{:S(2)}, u32[]{:S(2)}) collective-permute-start(bf16[4,2,80,640]{3,2,1,0:T(8,128)(2,1)} %collective-permute-done.39.refs_1_), channel_id=1, source_target_pairs={{0,2},{2,0},{1,3},{3,1},{4,6},{6,4},{5,7},{7,5},{8,10},{10,8},{9,1... | collective-permute-start | bytes 2457608 | tf_op jit(solution)/shard_map/u1_yx/ppermute | solution.py:1011
  182.5 36.9 %collective-permute-start.40 = (bf16[4,2,80,640]{3,2,1,0:T(8,128)(2,1)S(1)}, bf16[4,2,80,640]{3,2,1,0:T(8,128)(2,1)}, u32[]{:S(2)}, u32[]{:S(2)}) collective-permute-start(bf16[4,2,80,640]{3,2,1,0:T(8,128)(2,1)S(1)} %bitcast.176), channel_id=1, source_target_pairs={{0,1},{1,0},{2,3},{3,2},{4,5},{5,4},{6,7},{7,6},{8,9},{9,8},{10,11... | collective-permute-start | bytes 2457608 | tf_op jit(solution)/shard_map/u1_c/ppermute | solution.py:1011
  186.0 34.3 %collective-permute-start.41 = (bf16[4,2,80,640]{3,2,1,0:T(8,128)(2,1)}, bf16[4,2,80,640]{3,2,1,0:T(8,128)(2,1)}, u32[]{:S(2)}, u32[]{:S(2)}) collective-permute-start(bf16[4,2,80,640]{3,2,1,0:T(8,128)(2,1)} %collective-permute-done.39.refs_1_), channel_id=1, source_target_pairs={{0,1},{1,0},{2,3},{3,2},{4,5},{5,4},{6,7},{7,6},{8,9},{9,8},{10,11... | collective-permute-start | bytes 2457608 | tf_op jit(solution)/shard_map/u1_yc/ppermute | solution.py:1011
  217.6 21.1 %collective-permute-start.46 = (bf16[2,320,640]{2,1,0:T(8,128)(2,1)S(1)}, bf16[2,320,640]{2,1,0:T(8,128)(2,1)S(1)}, u32[]{:S(2)}, u32[]{:S(2)}) collective-permute-start(bf16[2,320,640]{2,1,0:T(8,128)(2,1)S(1)} %get-tuple-element.473.refs_0_.refs_4_), channel_id=1, source_target_pairs={{0,4},{4,0},{1,5},{5,1},{2,6},{6,2},{3,7},{7,3},{8,12},{12,8},{9,1... | collective-permute-start | bytes 2457608 | tf_op jit(solution)/shard_map/d1_y/ppermute | solution.py:1011
  219.3 36.0 %collective-permute-start.47 = (bf16[2,320,640]{2,1,0:T(8,128)(2,1)S(1)}, bf16[2,320,640]{2,1,0:T(8,128)(2,1)S(1)}, u32[]{:S(2)}, u32[]{:S(2)}) collective-permute-start(bf16[2,320,640]{2,1,0:T(8,128)(2,1)S(1)} %get-tuple-element.474.refs_1_.refs_5_), channel_id=1, source_target_pairs={{0,4},{4,0},{1,5},{5,1},{2,6},{6,2},{3,7},{7,3},{8,12},{12,8},{9,1... | collective-permute-start | bytes 2457608 | tf_op jit(solution)/shard_map/d1_y/ppermute | solution.py:1011
  220.3 38.2 %collective-permute-start.48 = (bf16[2,320,640]{2,1,0:T(8,128)(2,1)S(1)}, bf16[2,320,640]{2,1,0:T(8,128)(2,1)}, u32[]{:S(2)}, u32[]{:S(2)}) collective-permute-start(bf16[2,320,640]{2,1,0:T(8,128)(2,1)S(1)} %get-tuple-element.473.refs_0_.refs_4_), channel_id=1, source_target_pairs={{0,1},{1,0},{2,3},{3,2},{4,5},{5,4},{6,7},{7,6},{8,9},{9,8},{10,11... | collective-permute-start | bytes 2457608 | tf_op jit(solution)/shard_map/d1_c/ppermute | solution.py:1011
  220.3 38.1 %collective-permute-start.49 = (bf16[2,320,640]{2,1,0:T(8,128)(2,1)S(1)}, bf16[2,320,640]{2,1,0:T(8,128)(2,1)}, u32[]{:S(2)}, u32[]{:S(2)}) collective-permute-start(bf16[2,320,640]{2,1,0:T(8,128)(2,1)S(1)} %get-tuple-element.474.refs_1_.refs_5_), channel_id=1, source_target_pairs={{0,1},{1,0},{2,3},{3,2},{4,5},{5,4},{6,7},{7,6},{8,9},{9,8},{10,11... | collective-permute-start | bytes 2457608 | tf_op jit(solution)/shard_map/d1_c/ppermute | solution.py:1011
  286.0 15.6 %collective-permute-start.60 = (bf16[320,640]{1,0:T(8,128)(2,1)}, bf16[320,640]{1,0:T(8,128)(2,1)S(1)}, u32[]{:S(2)}, u32[]{:S(2)}) collective-permute-start(bf16[320,640]{1,0:T(8,128)(2,1)} %get-tuple-element.494), channel_id=1, source_target_pairs={{0,1},{1,0},{2,3},{3,2},{4,5},{5,4},{6,7},{7,6},{8,9},{9,8},{10,11... | collective-permute-start | bytes 1228808 | tf_op jit(solution)/shard_map/d1_c/ppermute | solution.py:1011
  286.2 15.7 %collective-permute-start.61 = (bf16[320,640]{1,0:T(8,128)(2,1)}, bf16[320,640]{1,0:T(8,128)(2,1)S(1)}, u32[]{:S(2)}, u32[]{:S(2)}) collective-permute-start(bf16[320,640]{1,0:T(8,128)(2,1)} %get-tuple-element.508), channel_id=1, source_target_pairs={{0,1},{1,0},{2,3},{3,2},{4,5},{5,4},{6,7},{7,6},{8,9},{9,8},{10,11... | collective-permute-start | bytes 1228808 | tf_op jit(solution)/shard_map/d1_c/ppermute | solution.py:1011
  286.6 15.5 %collective-permute-start.62 = (bf16[320,640]{1,0:T(8,128)(2,1)}, bf16[320,640]{1,0:T(8,128)(2,1)S(1)}, u32[]{:S(2)}, u32[]{:S(2)}) collective-permute-start(bf16[320,640]{1,0:T(8,128)(2,1)} %get-tuple-element.509), channel_id=1, source_target_pairs={{0,1},{1,0},{2,3},{3,2},{4,5},{5,4},{6,7},{7,6},{8,9},{9,8},{10,11... | collective-permute-start | bytes 1228808 | tf_op jit(solution)/shard_map/d1_c/ppermute | solution.py:1011
  286.7 15.8 %collective-permute-start.63 = (bf16[320,640]{1,0:T(8,128)(2,1)}, bf16[320,640]{1,0:T(8,128)(2,1)S(1)}, u32[]{:S(2)}, u32[]{:S(2)}) collective-permute-start(bf16[320,640]{1,0:T(8,128)(2,1)} %get-tuple-element.510), channel_id=1, source_target_pairs={{0,1},{1,0},{2,3},{3,2},{4,5},{5,4},{6,7},{7,6},{8,9},{9,8},{10,11... | collective-permute-start | bytes 1228808 | tf_op jit(solution)/shard_map/d1_c/ppermute | solution.py:1011
  306.1 57.8 %collective-permute-start.68 = (bf16[4,320,640]{2,1,0:T(8,128)(2,1)}, bf16[4,320,640]{2,1,0:T(8,128)(2,1)S(1)}, u32[]{:S(2)}, u32[]{:S(2)}) collective-permute-start(bf16[4,320,640]{2,1,0:T(8,128)(2,1)} %shard_map.262), channel_id=1, source_target_pairs={{0,4},{4,0},{1,5},{5,1},{2,6},{6,2},{3,7},{7,3},{8,12},{12,8},{9,1... | collective-permute-start | bytes 4915208 | tf_op jit(solution)/shard_map/d1_y/ppermute | solution.py:1011
  309.8 36.7 %collective-permute-start.69 = (bf16[320,640]{1,0:T(8,128)(2,1)}, bf16[320,640]{1,0:T(8,128)(2,1)S(1)}, u32[]{:S(2)}, u32[]{:S(2)}) collective-permute-start(bf16[320,640]{1,0:T(8,128)(2,1)} %get-tuple-element.542), channel_id=1, source_target_pairs={{0,1},{1,0},{2,3},{3,2},{4,5},{5,4},{6,7},{7,6},{8,9},{9,8},{10,11... | collective-permute-start | bytes 1228808 | tf_op jit(solution)/shard_map/d1_c/ppermute | solution.py:1011
  347.6 16.4 %collective-permute-start.70 = (bf16[320,640]{1,0:T(8,128)(2,1)}, bf16[320,640]{1,0:T(8,128)(2,1)}, u32[]{:S(2)}, u32[]{:S(2)}) collective-permute-start(bf16[320,640]{1,0:T(8,128)(2,1)} %get-tuple-element.543), channel_id=1, source_target_pairs={{0,1},{1,0},{2,3},{3,2},{4,5},{5,4},{6,7},{7,6},{8,9},{9,8},{10,11... | collective-permute-start | bytes 1228808 | tf_op jit(solution)/shard_map/d1_c/ppermute | solution.py:1011
  348.2 15.8 %collective-permute-start.71 = (bf16[320,640]{1,0:T(8,128)(2,1)}, bf16[320,640]{1,0:T(8,128)(2,1)}, u32[]{:S(2)}, u32[]{:S(2)}) collective-permute-start(bf16[320,640]{1,0:T(8,128)(2,1)} %get-tuple-element.544), channel_id=1, source_target_pairs={{0,1},{1,0},{2,3},{3,2},{4,5},{5,4},{6,7},{7,6},{8,9},{9,8},{10,11... | collective-permute-start | bytes 1228808 | tf_op jit(solution)/shard_map/d1_c/ppermute | solution.py:1011
  348.8 15.2 %collective-permute-start.72 = (bf16[320,640]{1,0:T(8,128)(2,1)}, bf16[320,640]{1,0:T(8,128)(2,1)}, u32[]{:S(2)}, u32[]{:S(2)}) collective-permute-start(bf16[320,640]{1,0:T(8,128)(2,1)} %get-tuple-element.545), channel_id=1, source_target_pairs={{0,1},{1,0},{2,3},{3,2},{4,5},{5,4},{6,7},{7,6},{8,9},{9,8},{10,11... | collective-permute-start | bytes 1228808 | tf_op jit(solution)/shard_map/d1_c/ppermute | solution.py:1011
  349.5 56.0 %collective-permute-start.86 = (bf16[2,4,2,80,640]{4,3,2,1,0:T(8,128)(2,1)}, bf16[2,4,2,80,640]{4,3,2,1,0:T(8,128)(2,1)S(1)}, u32[]{:S(2)}, u32[]{:S(2)}) collective-permute-start(bf16[2,4,2,80,640]{4,3,2,1,0:T(8,128)(2,1)} %get-tuple-element.529), channel_id=1, source_target_pairs={{0,2},{2,0},{1,3},{3,1},{4,6},{6,4},{5,7},{7,5},{8,10},{10,8},{9,1... | collective-permute-start | bytes 4915208 | tf_op jit(solution)/shard_map/u1_x/ppermute | solution.py:1011
  368.7 177.4 %reduce-scatter.8.cloned.1.call-start = ((), (), s32[]{:S(2)}) async-start(), calls=%async_computation.5 | async-start | bytes 2048000 | tf_op jit(solution)/shard_map/reduce_scatter | solution.py:1111
  370.2 35.3 %collective-permute-start.85 = (bf16[2,4,80,640]{3,2,1,0:T(8,128)(2,1)}, bf16[2,4,80,640]{3,2,1,0:T(8,128)(2,1)}, u32[]{:S(2)}, u32[]{:S(2)}) collective-permute-start(bf16[2,4,80,640]{3,2,1,0:T(8,128)(2,1)} %get-tuple-element.559), channel_id=1, source_target_pairs={{0,2},{2,0},{1,3},{3,1},{4,6},{6,4},{5,7},{7,5},{8,10},{10,8},{9,1... | collective-permute-start | bytes 2457608 | tf_op jit(solution)/shard_map/a1_x/ppermute | solution.py:1011
  372.2 19.4 %collective-permute-start.88 = (bf16[320,640]{1,0:T(8,128)(2,1)}, bf16[320,640]{1,0:T(8,128)(2,1)}, u32[]{:S(2)}, u32[]{:S(2)}) collective-permute-start(bf16[320,640]{1,0:T(8,128)(2,1)} %get-tuple-element.602), channel_id=1, source_target_pairs={{0,1},{1,0},{2,3},{3,2},{4,5},{5,4},{6,7},{7,6},{8,9},{9,8},{10,11... | collective-permute-start | bytes 1228808 | tf_op jit(solution)/shard_map/d0_c/ppermute | solution.py:1011
  372.8 19.0 %collective-permute-start.89 = (bf16[320,640]{1,0:T(8,128)(2,1)}, bf16[320,640]{1,0:T(8,128)(2,1)}, u32[]{:S(2)}, u32[]{:S(2)}) collective-permute-start(bf16[320,640]{1,0:T(8,128)(2,1)} %get-tuple-element.603), channel_id=1, source_target_pairs={{0,1},{1,0},{2,3},{3,2},{4,5},{5,4},{6,7},{7,6},{8,9},{9,8},{10,11... | collective-permute-start | bytes 1228808 | tf_op jit(solution)/shard_map/d0_c/ppermute | solution.py:1011
  376.8 55.4 %collective-permute-start.87 = (bf16[4,320,640]{2,1,0:T(8,128)(2,1)}, bf16[4,320,640]{2,1,0:T(8,128)(2,1)}, u32[]{:S(2)}, u32[]{:S(2)}) collective-permute-start(bf16[4,320,640]{2,1,0:T(8,128)(2,1)} %shard_map.268), channel_id=1, source_target_pairs={{0,4},{4,0},{1,5},{5,1},{2,6},{6,2},{3,7},{7,3},{8,12},{12,8},{9,1... | collective-permute-start | bytes 4915208 | tf_op jit(solution)/shard_map/d0_y/ppermute | solution.py:1011
  409.8 42.9 %collective-permute-start.97 = (bf16[4,2,80,640]{3,2,1,0:T(8,128)(2,1)}, bf16[4,2,80,640]{3,2,1,0:T(8,128)(2,1)}, u32[]{:S(2)}, u32[]{:S(2)}) collective-permute-start(bf16[4,2,80,640]{3,2,1,0:T(8,128)(2,1)} %fusion.1), channel_id=1, source_target_pairs={{0,4},{4,0},{1,5},{5,1},{2,6},{6,2},{3,7},{7,3},{8,12},{12,8},{9,1... | collective-permute-start | bytes 2457608 | tf_op jit(solution)/shard_map/u1_y/ppermute | solution.py:1011
  410.1 20.5 %collective-permute-start.90 = (bf16[320,640]{1,0:T(8,128)(2,1)}, bf16[320,640]{1,0:T(8,128)(2,1)}, u32[]{:S(2)}, u32[]{:S(2)}) collective-permute-start(bf16[320,640]{1,0:T(8,128)(2,1)} %get-tuple-element.604), channel_id=1, source_target_pairs={{0,1},{1,0},{2,3},{3,2},{4,5},{5,4},{6,7},{7,6},{8,9},{9,8},{10,11... | collective-permute-start | bytes 1228808 | tf_op jit(solution)/shard_map/d0_c/ppermute | solution.py:1011
  410.1 22.1 %collective-permute-start.91 = (bf16[320,640]{1,0:T(8,128)(2,1)}, bf16[320,640]{1,0:T(8,128)(2,1)}, u32[]{:S(2)}, u32[]{:S(2)}) collective-permute-start(bf16[320,640]{1,0:T(8,128)(2,1)} %get-tuple-element.605), channel_id=1, source_target_pairs={{0,1},{1,0},{2,3},{3,2},{4,5},{5,4},{6,7},{7,6},{8,9},{9,8},{10,11... | collective-permute-start | bytes 1228808 | tf_op jit(solution)/shard_map/d0_c/ppermute | solution.py:1011
  413.2 39.5 %collective-permute-start.98 = (bf16[4,80,640]{2,1,0:T(8,128)(2,1)}, bf16[4,80,640]{2,1,0:T(8,128)(2,1)}, u32[]{:S(2)}, u32[]{:S(2)}) collective-permute-start(bf16[4,80,640]{2,1,0:T(8,128)(2,1)} %fusion.5), channel_id=1, source_target_pairs={{0,4},{4,0},{1,5},{5,1},{2,6},{6,2},{3,7},{7,3},{8,12},{12,8},{9,1... | collective-permute-start | bytes 1228808 | tf_op jit(solution)/shard_map/a1_y/ppermute | solution.py:1011
  430.6 38.8 %collective-permute-start.92 = (bf16[2,4,2,80,640]{4,3,2,1,0:T(8,128)(2,1)}, bf16[2,4,2,80,640]{4,3,2,1,0:T(8,128)(2,1)}, u32[]{:S(2)}, u32[]{:S(2)}) collective-permute-start(bf16[2,4,2,80,640]{4,3,2,1,0:T(8,128)(2,1)} %get-tuple-element.606), channel_id=1, source_target_pairs={{0,2},{2,0},{1,3},{3,1},{4,6},{6,4},{5,7},{7,5},{8,10},{10,8},{9,1... | collective-permute-start | bytes 4915208 | tf_op jit(solution)/shard_map/u0_x/ppermute | solution.py:1011
  455.1 96.1 %reduce-scatter.4.cloned.1.call-start = ((), (), s32[]{:S(2)}) async-start(), calls=%async_computation.3 | async-start | bytes 1024000 | tf_op jit(solution)/shard_map/reduce_scatter | solution.py:1111
  458.4 47.3 %collective-permute-start.103 = (bf16[2,3,80,640]{3,2,1,0:T(8,128)(2,1)}, bf16[2,3,80,640]{3,2,1,0:T(8,128)(2,1)S(1)}, u32[]{:S(2)}, u32[]{:S(2)}) collective-permute-start(bf16[2,3,80,640]{3,2,1,0:T(8,128)(2,1)} %get-tuple-element.777), channel_id=1, source_target_pairs={{0,8},{8,0},{16,24},{24,16},{1,9},{9,1},{17,25},{25,17},{2,10},{10... | collective-permute-start | bytes 1843208 | tf_op jit(solution)/shard_map/j1_near/ppermute | solution.py:1060
  464.7 43.7 %collective-permute-start.100 = (bf16[2,4,80,640]{3,2,1,0:T(8,128)(2,1)}, bf16[2,4,80,640]{3,2,1,0:T(8,128)(2,1)}, u32[]{:S(2)}, u32[]{:S(2)}) collective-permute-start(bf16[2,4,80,640]{3,2,1,0:T(8,128)(2,1)} %get-tuple-element.648), channel_id=1, source_target_pairs={{0,2},{2,0},{1,3},{3,1},{4,6},{6,4},{5,7},{7,5},{8,10},{10,8},{9,1... | collective-permute-start | bytes 2457608 | tf_op jit(solution)/shard_map/a0_x/ppermute | solution.py:1011
  471.6 40.3 %collective-permute-start.99 = (bf16[4,2,80,640]{3,2,1,0:T(8,128)(2,1)}, bf16[4,2,80,640]{3,2,1,0:T(8,128)(2,1)}, u32[]{:S(2)}, u32[]{:S(2)}) collective-permute-start(bf16[4,2,80,640]{3,2,1,0:T(8,128)(2,1)} %fusion.2), channel_id=1, source_target_pairs={{0,4},{4,0},{1,5},{5,1},{2,6},{6,2},{3,7},{7,3},{8,12},{12,8},{9,1... | collective-permute-start | bytes 2457608 | tf_op jit(solution)/shard_map/u0_y/ppermute | solution.py:1011
  472.8 33.8 %collective-permute-start.102 = (f32[88,640]{1,0:T(8,128)S(1)}, f32[88,640]{1,0:T(8,128)S(1)}, u32[]{:S(2)}, u32[]{:S(2)}) collective-permute-start(f32[88,640]{1,0:T(8,128)S(1)} %add.156), channel_id=1, source_target_pairs={{0,16},{8,24},{16,0},{24,8},{1,17},{9,25},{17,1},{25,9},{2,18},{10... | collective-permute-start | bytes 675848 | tf_op jit(solution)/shard_map/small_far/ppermute | solution.py:1060
  520.9 15.1 %collective-permute-start.114 = (bf16[3,80,640]{2,1,0:T(8,128)(2,1)S(1)}, bf16[3,80,640]{2,1,0:T(8,128)(2,1)S(1)}, u32[]{:S(2)}, u32[]{:S(2)}) collective-permute-start(bf16[3,80,640]{2,1,0:T(8,128)(2,1)S(1)} %add_convert_fusion.4.refs_1_), channel_id=1, source_target_pairs={{0,2},{2,0},{1,3},{3,1},{4,6},{6,4},{5,7},{7,5},{8,10},{10,8},{9,1... | collective-permute-start | bytes 921608 | tf_op jit(solution)/shard_map/j1_x/ppermute | solution.py:1011
  525.5 32.2 %collective-permute-start.113 = (bf16[3,80,640]{2,1,0:T(8,128)(2,1)S(1)}, bf16[3,80,640]{2,1,0:T(8,128)(2,1)S(1)}, u32[]{:S(2)}, u32[]{:S(2)}) collective-permute-start(bf16[3,80,640]{2,1,0:T(8,128)(2,1)S(1)} %add_convert_fusion.4.refs_1_), channel_id=1, source_target_pairs={{0,1},{1,0},{2,3},{3,2},{4,5},{5,4},{6,7},{7,6},{8,9},{9,8},{10,11... | collective-permute-start | bytes 921608 | tf_op jit(solution)/shard_map/j1_c/ppermute | solution.py:1011
  525.6 21.0 %collective-permute-start.117 = (bf16[320,640]{1,0:T(8,128)(2,1)}, bf16[320,640]{1,0:T(8,128)(2,1)S(1)}, u32[]{:S(2)}, u32[]{:S(2)}) collective-permute-start(bf16[320,640]{1,0:T(8,128)(2,1)} %bitcast.208), channel_id=1, source_target_pairs={{0,2},{2,0},{1,3},{3,1},{4,6},{6,4},{5,7},{7,5},{8,10},{10,8},{9,1... | collective-permute-start | bytes 1228808 | tf_op jit(solution)/shard_map/d1_x/ppermute | solution.py:1011
  536.0 26.2 %collective-permute-start.116 = (bf16[320,640]{1,0:T(8,128)(2,1)}, bf16[320,640]{1,0:T(8,128)(2,1)S(1)}, u32[]{:S(2)}, u32[]{:S(2)}) collective-permute-start(bf16[320,640]{1,0:T(8,128)(2,1)} %bitcast.209), channel_id=1, source_target_pairs={{0,1},{1,0},{2,3},{3,2},{4,5},{5,4},{6,7},{7,6},{8,9},{9,8},{10,11... | collective-permute-start | bytes 1228808 | tf_op jit(solution)/shard_map/d1_c/ppermute | solution.py:1011
  536.3 14.4 %collective-permute-start.109 = (bf16[80,640]{1,0:T(8,128)(2,1)S(1)}, bf16[80,640]{1,0:T(8,128)(2,1)S(1)}, u32[]{:S(2)}, u32[]{:S(2)}) collective-permute-start(bf16[80,640]{1,0:T(8,128)(2,1)S(1)} %get-tuple-element.801), channel_id=1, source_target_pairs={{0,16},{8,24},{16,0},{24,8},{1,17},{9,25},{17,1},{25,9},{2,18},{10... | collective-permute-start | bytes 307208 | tf_op jit(solution)/shard_map/a0_far/ppermute | solution.py:1060
  (154 other events, 1425.8 us)
Sparse Core Ops, SparseCore 0:
  368.8 35.4 reduce-scatter.5
  455.2 51.6 reduce-scatter.7
  525.7 25.3 reduce-scatter.3

commit v5 on v4

--- a/solution.py
+++ b/solution.py
@@ -110,6 +110,10 @@
         lanes = pl.ds(pl.multiple_of(quarter * D, 128), D)
         copies.append(copy(buffer.at[:, 0], held.at[:, y_at ^ dy, :, lanes], sems.at[number]))
     return copies
+
+
+def tiles_from(line):
+    return line.shape[1] - 2
 
 
 def square(values):
@@ -244,7 +248,7 @@
             at = (place_ref[0] ^ dx) * 2 + (place_ref[2] ^ dc)
             for half in range(2):
                 target = held.at[at, :, place_ref[1] ^ dy, :, half * TILE : (half + 1) * TILE]
-                copy(buffer.at[:, half], target, sems.at[at, dy, half]).start()
+                copy(buffer.at[:, tiles_from(buffer) + half], target, sems.at[at, dy, half]).start()
 
     for dy in range(2):
         for half in range(2):
@@ -524,7 +528,7 @@
         for dy in range(2):
             for half in range(2):
                 target = held_up.at[step, :, y_at ^ dy, :, half * TILE : (half + 1) * TILE]
-                source = ups[2 * dx + dy].at[:, half]
+                source = ups[2 * dx + dy].at[:, tiles_from(ups[0]) + half]
                 copy(source, target, up_sems.at[step, dy, half]).start()
 
 
@@ -1215,10 +1219,12 @@
         u0_near = moves.hop(u0, 1, "u0_near")
         (d0,) = run.hold(d0)
         d0_far = moves.hop(d0, 2, "d0_far")
-        a1 = run(moves.own_quarter, attn_weight[1])
         a0 = run(moves.low, a0, a0_near)
         a0_y, a0_x, a0_c = fan(a0, "a0")
-        u1 = run(moves.own_quarter, up_weight[1])
+        j1 = run(
+            lambda a, u: jnp.concatenate([moves.own_quarter(a), moves.own_quarter(u)]),
+            *(attn_weight[1], up_weight[1]),
+        )
         d1 = run(moves.own_half, down_weight[1])
         a0_y = run.hold(*a0_y)
         a0_yx, a0_yc = fan_y(a0_y, "a0")
@@ -1235,44 +1241,44 @@
         u0_yx, u0_yc = fan_y(u0_y, "u0")
         d0 = run(moves.low_halves, d0, d0_near)
         d0_y, d0_c = swaps(d0, "y", "d0_y"), swaps(d0, "c", "d0_c")
-        a1, u1, d1 = run.hold(a1, u1, d1)
-        a1_far = moves.hop(a1, 2, "a1_far")
-        u1_far = moves.hop(u1, 2, "u1_far")
-        a1 = run(moves.high, a1, a1_far)
-        a1_near = moves.hop(a1, 1, "a1_near")
-        u1 = run(moves.high, u1, u1_far)
-        u1_near = moves.hop(u1, 1, "u1_near")
-        u0_x, u0_yx = run.hold(u0_x, u0_yx)
-        u0_xc, u0_yxc = fan_x(u0_x, u0_yx, "u0")
-        a1 = run(moves.low, a1, a1_near)
-        a1_y, a1_x, a1_c = fan(a1, "a1")
-        d1_far = moves.hop(d1, 2, "d1_far")
+        j1, d1 = run.hold(j1, d1)
+        j1_far = moves.hop(j1, 2, "j1_far")
+        u0_x = run.hold(*u0_x)
+        u0_xc = swaps(u0_x, "c", "u0_xc")
+        j1 = run(moves.high, j1, j1_far)
+        j1_near = moves.hop(j1, 1, "j1_near")
+        d0_y[0:1] = run.hold(d0_y[0])
+        d0_yc = swaps(d0_y[:1], "c", "d0_yc")
+        u0_yx = run.hold(*u0_yx)
+        u0_yxc = swaps(u0_yx, "c", "u0_yxc")
+        j1 = run(moves.low, j1, j1_near)
+        j1_y, j1_x, j1_c = fan(j1, "j1")
+        d0_y[1:2] = run.hold(d0_y[1])
+        d0_yc += swaps(d0_y[1:], "c", "d0_yc")
         ups0 = in_place(u0, u0_y, u0_x, u0_c, u0_yx, u0_yc, u0_xc, u0_yxc)
         wide0 = run(up_on(0), mixed0[4], *ups0)
-        u1 = run(moves.low, u1, u1_near)
-        u1_y, u1_x, u1_c = fan(u1, "u1")
+        (d1,) = run.hold(d1)
+        d1_far = moves.hop(d1, 2, "d1_far")
+        downs0 = (*d0, *d0_y, *d0_c, *d0_yc)
+        residual1 = run(down_on(0), mixed0[3], wide0[0], *downs0)
+        j1_x = run.hold(*j1_x)
+        j1_xc = swaps(j1_x, "c", "j1_xc")
+        j1_y = run.hold(*j1_y)
+        j1_yx, j1_yc = fan_y(j1_y, "j1")
         d1 = run(moves.high, d1, d1_far)
         d1_near = moves.hop(d1, 1, "d1_near")
-        d0_y = run.hold(*d0_y)
-        d0_yc = swaps(d0_y, "c", "d0_yc")
-        downs0 = (*d0, *d0_y, *d0_c, *d0_yc)
-        residual1 = run(down_on(0), mixed0[3], wide0[0], *downs0)
-        a1_y = run.hold(*a1_y)
-        a1_yx, a1_yc = fan_y(a1_y, "a1")
         d1 = run(moves.low_halves, d1, d1_near)
         d1_y, d1_c = swaps(d1, "y", "d1_y"), swaps(d1, "c", "d1_c")
-        a1_x, a1_yx = run.hold(a1_x, a1_yx)
-        a1_xc, a1_yxc = fan_x(a1_x, a1_yx, "a1")
-        u1_y = run.hold(*u1_y)
-        u1_yx, u1_yc = fan_y(u1_y, "u1")
-        quarters1 = in_place(a1, a1_y, a1_x, a1_c, a1_yx, a1_yc, a1_xc, a1_yxc)
+        j1_yx = run.hold(*j1_yx)
+        j1_yxc = swaps(j1_yx, "c", "j1_yxc")
+        ups1 = in_place(j1, j1_y, j1_x, j1_c, j1_yx, j1_yc, j1_xc, j1_yxc)
+        quarters1 = ups1
         mixed1 = run(mix_on(1), residual1, *quarters1)
-        u1_x, u1_yx = run.hold(u1_x, u1_yx)
-        u1_xc, u1_yxc = fan_x(u1_x, u1_yx, "u1")
-        ups1 = in_place(u1, u1_y, u1_x, u1_c, u1_yx, u1_yc, u1_xc, u1_yxc)
+        d1_y[0:1] = run.hold(d1_y[0])
+        d1_yc = swaps(d1_y[:1], "c", "d1_yc")
         wide1 = run(up_on(1), mixed1[4], *ups1)
-        d1_y = run.hold(*d1_y)
-        d1_yc = swaps(d1_y, "c", "d1_yc")
+        d1_y[1:2] = run.hold(d1_y[1])
+        d1_yc += swaps(d1_y[1:], "c", "d1_yc")
         downs1 = (*d1, *d1_y, *d1_c, *d1_yc)
         residual = run(down_on(1), mixed1[3], wide1[0], *downs1)
         weights = [(quarters0, ups0, downs0), (quarters1, ups1, downs1)]

time: 591 us -> 571 us (0.966)
  waiting for transfers between devices: 207 us -> 188 us
    ppermute x105 -> x98, waiting for transfers between devices: 110 us -> 85.5 us  [swap(): return lax.ppermute(value, axis, [(0, 1), (1, 0)])]
    ppermute x18 -> x16, waiting for transfers between devices: 96.4 us -> 102 us  [hop(): lax.ppermute(value, 'z', [(at, at ^ reach) for at in range(self.z_size)])]
    ppermute x18 -> x16, starting transfers between devices: 21.4 us -> 17.1 us  [hop(): lax.ppermute(value, 'z', [(at, at ^ reach) for at in range(self.z_size)])]
    unnamed x197 -> x182, local copies, waits for them, and re-layouts: 14.5 us -> 16.3 us
    ppermute x105 -> x98, starting transfers between devices: 49.9 us -> 51.5 us  [swap(): return lax.ppermute(value, axis, [(0, 1), (1, 0)])]
  transfers between devices with their start and end apart: 126 -> 117, of which waited for: 45 -> 34; matrix products, arithmetic and copies ran while one was open for 8% -> 9% of each run, Pallas kernels for 32% -> 34%
where the time goes in v5:
time: 571 us; the launch traced here: 565 us
  Pallas kernels  220 us (39%)
  waiting for transfers between devices  188 us (33%)
  starting transfers between devices  69 us (12%)
  local copies, waits for them, and re-layouts  38.3 us (7%)
  other arithmetic  27.8 us (5%)
  between operations  22.7 us (4%)
    ppermute x16, waiting for transfers between devices, hop(): lax.ppermute(value, 'z', [(at, at ^ reach) for at in range(self.z_size)])  102 us
    ppermute x98, waiting for transfers between devices, swap(): return lax.ppermute(value, axis, [(0, 1), (1, 0)])  85.5 us
    ppermute x98, starting transfers between devices, swap(): return lax.ppermute(value, axis, [(0, 1), (1, 0)])  51.5 us
    pallas_call x2, Pallas kernels, mix_back(): pl.pallas_call(mix_back_kernel, out_shape=(part,) * 4 + (sds((ROWS, D), B...  33.8 us
    pallas_call x2, Pallas kernels, wide_back_last(): pl.pallas_call(wide_back_last_kernel, grid=(2,), in_specs=[SMEM_SPEC, ful...  31.3 us
    pallas_call x2, Pallas kernels, mix(): pl.pallas_call(mix_kernel, grid=(1,), out_shape=(sds((ROWS, 3 * D), BF),...  29.1 us
    pallas_call x2, Pallas kernels, wide_back_first(): pl.pallas_call(wide_back_first_kernel, grid=(2,), in_specs=[SMEM_SPEC, fu...  28.7 us
    pallas_call x2, Pallas kernels, up(): pl.pallas_call(up_kernel, grid=(STEPS,), out_shape=(out, out), in_specs=[...  22.1 us
  transfers between devices with their start and end apart: 117, of which 34 were waited for; matrix products, arithmetic and copies ran while one was open for 9% of the time, Pallas kernels for 34%

profile of v5, /device:TPU:0, one launch (start us, length us, event | category | flops | bytes accessed | tf_op | source)
XLA Modules:
  0.0 565.5 jit_solution(2822860237731501981)
XLA Ops:
  8.7 4.1 collective-permute-start
  17.9 5.3 collective-permute-start.1
  23.2 4.2 collective-permute-done.2
  28.9 3.5 collective-permute-start.8
  32.5 1.6 collective-permute-start.3
  39.7 9.4 %collective-permute-done.9 = bf16[2,2,80,640]{3,2,1,0:T(8,128)(2,1)} collective-permute-done((bf16[2,2,80,640]{3,2,1,0:T(8,128)(2,1)S(1)}, bf16[2,2,80,640]{3,2,1,0:T(8,128)(2,1)}, u32[]{:S(2)}, u32[]{:S(2)}) %collective-permute-start.9) | collective-permute-done | bytes 409632 | tf_op jit(solution)/shard_map/u0_near/ppermute | solution.py:1064
  52.0 1.6 maximum_select_fusion.4
  53.6 1.6 collective-permute-start.12
  55.2 4.7 collective-permute-done.7.refs_5_
  64.7 14.3 %shard_map.253 = (bf16[512,1920]{1,0:T(8,128)(2,1)}, f32[20,1,512]{2,1,0:T(1,128)}, bf16[512,640]{1,0:T(8,128)(2,1)}, f32[512,640]{1,0:T(8,128)}, bf16[512,640]{1,0:T(8,128)(2,1)}) custom-call(s32[3]{0:T(128)} %pad_add_fusion.place_ref.refs_0_, s32[4]{0:T(128)} %lengths_ref.7, bf16[512,640]{1,0:T(8,128)(2,1)} %residual_ref.2, ...), custom_call_target="tpu_custom_call" | custom-call | flops 400000000 | bytes 2097152 | tf_op jit(solution)/shard_map/pallas_call | solution.py:210
  79.7 1.7 maximum_select_fusion
  82.5 1.6 collective-permute-start.23
  84.1 14.4 %collective-permute-done.18 = bf16[3,80,640]{2,1,0:T(8,128)(2,1)S(1)} collective-permute-done((bf16[3,80,640]{2,1,0:T(8,128)(2,1)S(1)}, bf16[3,80,640]{2,1,0:T(8,128)(2,1)S(1)}, u32[]{:S(2)}, u32[]{:S(2)}) %collective-permute-start.18) | collective-permute-done | bytes 307232 | tf_op jit(solution)/shard_map/j1_far/ppermute | solution.py:1064
  100.8 14.9 %collective-permute-done.21 = bf16[2,3,80,640]{3,2,1,0:T(8,128)(2,1)S(1)} collective-permute-done((bf16[2,3,80,640]{3,2,1,0:T(8,128)(2,1)S(1)}, bf16[2,3,80,640]{3,2,1,0:T(8,128)(2,1)S(1)}, u32[]{:S(2)}, u32[]{:S(2)}) %collective-permute-start.21) | collective-permute-done | bytes 614432 | tf_op jit(solution)/shard_map/j1_near/ppermute | solution.py:1064
  116.7 4.0 collective-permute-done.22.refs_2_.refs_6_
  124.8 11.1 %shard_map.254 = (bf16[4,512,1280]{2,1,0:T(8,128)(2,1)}, bf16[4,512,1280]{2,1,0:T(8,128)(2,1)}) custom-call(s32[3]{0:T(128)} %pad_add_fusion.place_ref.refs_0_, bf16[512,640]{1,0:T(8,128)(2,1)} %get-tuple-element.402.second_ref, bf16[4,2,80,640]{3,2,1,0:T(8,128)(2,1)} %bitcast.169, bf16[4,2,80,640]{3,2,1,0:T(8,128)(2,1)} %collective-permute-done.12.refs_1_, ...), custom_call_target="tpu_custom_call" | custom-call | flops 400000000 | bytes 2097152 | tf_op jit(solution)/shard_map/pallas_call | solution.py:278
  135.9 2.7 collective-permute-start.33
  138.7 2.5 collective-permute-start.31
  141.2 10.4 %shard_map.255.residual_ref = f32[512,640]{1,0:T(8,128)} custom-call(s32[3]{0:T(128)} %pad_add_fusion.place_ref.refs_0_, f32[512,640]{1,0:T(8,128)} %get-tuple-element.414.middle_ref.refs_14_, bf16[4,512,1280]{2,1,0:T(8,128)(2,1)} %get-tuple-element.415.active_ref, bf16[2,320,640]{2,1,0:T(8,128)(2,1)} %get-tuple-element.416.refs_0_.refs_4_, ...), custom_call_target="tpu_custom_call" | custom-call | flops 400000000 | bytes 2097152 | tf_op jit(solution)/shard_map/pallas_call | solution.py:320
  151.6 5.7 %collective-permute-done.33 = bf16[1,320,640]{2,1,0:T(8,128)(2,1)} collective-permute-done((bf16[1,320,640]{2,1,0:T(8,128)(2,1)S(1)}, bf16[1,320,640]{2,1,0:T(8,128)(2,1)}, u32[]{:S(2)}, u32[]{:S(2)}) %collective-permute-start.33) | collective-permute-done | bytes 409632 | tf_op jit(solution)/shard_map/d1_far/ppermute | solution.py:1064
  158.7 2.5 collective-permute-start.32
  161.7 7.4 %collective-permute-done.31.refs_4_.refs_2_ = bf16[4,3,80,640]{3,2,1,0:T(8,128)(2,1)} collective-permute-done((bf16[4,3,80,640]{3,2,1,0:T(8,128)(2,1)S(1)}, bf16[4,3,80,640]{3,2,1,0:T(8,128)(2,1)}, u32[]{:S(2)}, u32[]{:S(2)}) %collective-permute-start.31) | collective-permute-done | bytes 1228832 | tf_op jit(solution)/shard_map/j1_x/ppermute | solution.py:1015
  169.1 9.0 %collective-permute-done.34 = bf16[2,1,320,640]{3,2,0,1:T(8,128)(2,1)S(1)} collective-permute-done((bf16[2,1,320,640]{3,2,0,1:T(8,128)(2,1)S(1)}, bf16[2,1,320,640]{3,2,0,1:T(8,128)(2,1)S(1)}, u32[]{:S(2)}, u32[]{:S(2)}) %collective-permute-start.34) | collective-permute-done | bytes 819232 | tf_op jit(solution)/shard_map/d1_near/ppermute | solution.py:1064
  179.4 15.2 %collective-permute-done.32.refs_5_.refs_3_ = bf16[4,3,80,640]{3,2,1,0:T(8,128)(2,1)} collective-permute-done((bf16[4,3,80,640]{3,2,1,0:T(8,128)(2,1)S(1)}, bf16[4,3,80,640]{3,2,1,0:T(8,128)(2,1)}, u32[]{:S(2)}, u32[]{:S(2)}) %collective-permute-start.32) | collective-permute-done | bytes 1228832 | tf_op jit(solution)/shard_map/j1_yx/ppermute | solution.py:1015
  199.4 14.8 %shard_map.256 = (bf16[512,1920]{1,0:T(8,128)(2,1)}, f32[20,1,512]{2,1,0:T(1,128)}, bf16[512,640]{1,0:T(8,128)(2,1)}, f32[512,640]{1,0:T(8,128)}, bf16[512,640]{1,0:T(8,128)(2,1)}) custom-call(s32[3]{0:T(128)} %pad_add_fusion.place_ref.refs_0_, s32[4]{0:T(128)} %lengths_ref.7, f32[512,640]{1,0:T(8,128)} %shard_map.255.residual_ref, ...), custom_call_target="tpu_custom_call" | custom-call | flops 400000000 | bytes 2097152 | tf_op jit(solution)/shard_map/pallas_call | solution.py:210
  214.3 11.0 %shard_map.257 = (bf16[4,512,1280]{2,1,0:T(8,128)(2,1)}, bf16[4,512,1280]{2,1,0:T(8,128)(2,1)}) custom-call(s32[3]{0:T(128)} %pad_add_fusion.place_ref.refs_0_, bf16[512,640]{1,0:T(8,128)(2,1)} %get-tuple-element.445.second_ref, bf16[4,3,80,640]{3,2,1,0:T(8,128)(2,1)} %bitcast.163, bf16[4,3,80,640]{3,2,1,0:T(8,128)(2,1)} %copy-done.1, ...), custom_call_target="tpu_custom_call" | custom-call | flops 400000000 | bytes 2097152 | tf_op jit(solution)/shard_map/pallas_call | solution.py:278
  226.0 6.9 %collective-permute-done.37.refs_2_.refs_6_ = bf16[2,320,640]{2,1,0:T(8,128)(2,1)S(1)} collective-permute-done((bf16[2,320,640]{2,1,0:T(8,128)(2,1)}, bf16[2,320,640]{2,1,0:T(8,128)(2,1)S(1)}, u32[]{:S(2)}, u32[]{:S(2)}) %collective-permute-start.37) | collective-permute-done | bytes 819232 | tf_op jit(solution)/shard_map/d1_y/ppermute | solution.py:1015
  236.7 10.4 %shard_map.258.residual_ref = f32[512,640]{1,0:T(8,128)} custom-call(s32[3]{0:T(128)} %pad_add_fusion.place_ref.refs_0_, f32[512,640]{1,0:T(8,128)} %get-tuple-element.457.middle_ref.refs_14_, bf16[4,512,1280]{2,1,0:T(8,128)(2,1)} %get-tuple-element.458.active_ref, bf16[2,320,640]{2,1,0:T(8,128)(2,1)} %get-tuple-element.459.refs_0_.refs_4_, ...), custom_call_target="tpu_custom_call" | custom-call | flops 400000000 | bytes 2097152 | tf_op jit(solution)/shard_map/pallas_call | solution.py:320
  248.8 6.7 %shard_map.259 = (bf16[512,640]{1,0:T(8,128)(2,1)}, f32[512,640]{1,0:T(8,128)}, bf16[512,640]{1,0:T(8,128)(2,1)}, f32[40,640]{1,0:T(8,128)}) custom-call(f32[512,640]{1,0:T(8,128)} %shard_map.258.residual_ref, s32[512,1]{1,0:T(8,128)} %copy.70.targets_ref, s32[512,1]{1,0:T(8,128)} %copy.71.masked_ref, bf16[640,128]{1,0:T(8,128)(2,1)} %pad.8.weight_ref, ...), custom_call_target="tpu_custom_call" | custom-call | flops 400000000 | bytes 2097152 | tf_op jit(solution)/shard_map/pallas_call | solution.py:397
  255.5 8.2 %shard_map.260 = (bf16[320,640]{1,0:T(8,128)(2,1)}, bf16[320,640]{1,0:T(8,128)(2,1)}, bf16[320,640]{1,0:T(8,128)(2,1)}, bf16[320,640]{1,0:T(8,128)(2,1)}, bf16[3...) custom-call(s32[3]{0:T(128)} %pad_add_fusion.place_ref.refs_0_, ...), custom_call_target="tpu_custom_call" | custom-call | flops 400000000 | bytes 2097152 | tf_op jit(solution)/shard_map/pallas_call | solution.py:449
  264.8 14.4 %shard_map.261 = (bf16[4,80,640]{2,1,0:T(8,128)(2,1)}, bf16[4,80,640]{2,1,0:T(8,128)(2,1)}, bf16[4,80,640]{2,1,0:T(8,128)(2,1)}, bf16[4,80,640]{2,1,0:T(8,128)(2...) custom-call(s32[3]{0:T(128)} %pad_add_fusion.place_ref.refs_0_, ...), custom_call_target="tpu_custom_call" | custom-call | flops 400000000 | bytes 2097152 | tf_op jit(solution)/shard_map/pallas_call | solution.py:604
  281.2 2.9 shard_map.262
  288.6 15.7 %shard_map.263 = (bf16[2,4,2,80,640]{4,3,2,1,0:T(8,128)(2,1)}, bf16[2,4,2,80,640]{4,3,2,1,0:T(8,128)(2,1)}, f32[2,1280]{1,0:T(2,128)}, f32[512,640]{1,0:T(8,128)...) custom-call(s32[3]{0:T(128)} %pad_add_fusion.place_ref.refs_0_, bf16[512,640]{1,0:T(8,128)(2,1)} %get-tuple-element.502.grad_ref.rounded_ref, ...), custom_call_target="tpu_custom_call" | custom-call | flops 400000000 | bytes 2097152 | tf_op jit(solution)/shard_map/pallas_call | solution.py:710
  304.3 17.0 %shard_map.264 = (bf16[4,80,640]{2,1,0:T(8,128)(2,1)}, bf16[4,80,640]{2,1,0:T(8,128)(2,1)}, bf16[4,80,640]{2,1,0:T(8,128)(2,1)}, bf16[4,80,640]{2,1,0:T(8,128)(2...) custom-call(s32[3]{0:T(128)} %pad_add_fusion.place_ref.refs_0_, ...), custom_call_target="tpu_custom_call" | custom-call | flops 400000000 | bytes 2097152 | tf_op jit(solution)/shard_map/pallas_call | solution.py:862
  325.7 1.7 collective-permute-start.77
  327.5 8.2 %shard_map.265 = (bf16[320,640]{1,0:T(8,128)(2,1)}, bf16[320,640]{1,0:T(8,128)(2,1)}, bf16[320,640]{1,0:T(8,128)(2,1)}, bf16[320,640]{1,0:T(8,128)(2,1)}, bf16[3...) custom-call(s32[3]{0:T(128)} %pad_add_fusion.place_ref.refs_0_, ...), custom_call_target="tpu_custom_call" | custom-call | flops 400000000 | bytes 2097152 | tf_op jit(solution)/shard_map/pallas_call | solution.py:449
  335.7 4.6 shard_map.266
  341.6 3.4 shard_map.267
  350.2 2.9 shard_map.268
  353.1 1.6 collective-permute-start.78
  354.7 14.3 %shard_map.269 = (bf16[4,80,640]{2,1,0:T(8,128)(2,1)}, bf16[4,80,640]{2,1,0:T(8,128)(2,1)}, bf16[4,80,640]{2,1,0:T(8,128)(2,1)}, bf16[4,80,640]{2,1,0:T(8,128)(2...) custom-call(s32[3]{0:T(128)} %pad_add_fusion.place_ref.refs_0_, ...), custom_call_target="tpu_custom_call" | custom-call | flops 400000000 | bytes 2097152 | tf_op jit(solution)/shard_map/pallas_call | solution.py:604
  369.7 12.0 %collective-permute-done.76 = bf16[2,4,80,640]{3,2,1,0:T(8,128)(2,1)} collective-permute-done((bf16[2,4,80,640]{3,2,1,0:T(8,128)(2,1)}, bf16[2,4,80,640]{3,2,1,0:T(8,128)(2,1)}, u32[]{:S(2)}, u32[]{:S(2)}) %collective-permute-start.76) | collective-permute-done | bytes 819232 | tf_op jit(solution)/shard_map/a1_x/ppermute | solution.py:1015
  382.7 1.6 collective-permute-done.70.refs_18_
  388.0 1.9 fusion.5
  391.2 15.6 %shard_map.270 = (bf16[2,4,2,80,640]{4,3,2,1,0:T(8,128)(2,1)}, bf16[2,4,2,80,640]{4,3,2,1,0:T(8,128)(2,1)}, f32[2,1280]{1,0:T(2,128)}, f32[512,640]{1,0:T(8,128)...) custom-call(s32[3]{0:T(128)} %pad_add_fusion.place_ref.refs_0_, bf16[512,640]{1,0:T(8,128)(2,1)} %get-tuple-element.575.grad_ref.rounded_ref, ...), custom_call_target="tpu_custom_call" | custom-call | flops 400000000 | bytes 2097152 | tf_op jit(solution)/shard_map/pallas_call | solution.py:710
  406.8 1.8 collective-permute-start.83
  408.6 3.4 shard_map.271
  412.0 16.8 %shard_map.272 = (bf16[4,80,640]{2,1,0:T(8,128)(2,1)}, bf16[4,80,640]{2,1,0:T(8,128)(2,1)}, bf16[4,80,640]{2,1,0:T(8,128)(2,1)}, bf16[4,80,640]{2,1,0:T(8,128)(2...) custom-call(s32[3]{0:T(128)} %pad_add_fusion.place_ref.refs_0_, ...), custom_call_target="tpu_custom_call" | custom-call | flops 400000000 | bytes 2097152 | tf_op jit(solution)/shard_map/pallas_call | solution.py:862
  435.0 4.8 shard_map.273
  440.7 5.1 collective-permute-done.83
  445.9 2.2 fusion.2
  450.6 31.3 %collective-permute-done.94 = bf16[2,3,80,640]{3,2,1,0:T(8,128)(2,1)S(1)} collective-permute-done((bf16[2,3,80,640]{3,2,1,0:T(8,128)(2,1)}, bf16[2,3,80,640]{3,2,1,0:T(8,128)(2,1)S(1)}, u32[]{:S(2)}, u32[]{:S(2)}) %collective-permute-start.94) | collective-permute-done | bytes 614432 | tf_op jit(solution)/shard_map/j1_near/ppermute | solution.py:1064
  483.9 1.9 fusion.6
  485.7 1.6 collective-permute-start.95
  487.3 2.6 fusion
  489.9 8.4 %collective-permute-done.97 = bf16[3,80,640]{2,1,0:T(8,128)(2,1)S(1)} collective-permute-done((bf16[3,80,640]{2,1,0:T(8,128)(2,1)}, bf16[3,80,640]{2,1,0:T(8,128)(2,1)S(1)}, u32[]{:S(2)}, u32[]{:S(2)}) %collective-permute-start.97) | collective-permute-done | bytes 307232 | tf_op jit(solution)/shard_map/j1_far/ppermute | solution.py:1064
  501.2 2.0 collective-permute-start.99
  504.9 10.2 %collective-permute-done.99 = f32[88,640]{1,0:T(8,128)S(1)} collective-permute-done((f32[88,640]{1,0:T(8,128)S(1)}, f32[88,640]{1,0:T(8,128)S(1)}, u32[]{:S(2)}, u32[]{:S(2)}) %collective-permute-start.99) | collective-permute-done | bytes 225312 | tf_op jit(solution)/shard_map/small_x/ppermute | solution.py:1015
  515.1 1.6 collective-permute-start.101
  516.9 6.2 %collective-permute-done.101 = f32[88,640]{1,0:T(8,128)S(1)} collective-permute-done((f32[88,640]{1,0:T(8,128)S(1)}, f32[88,640]{1,0:T(8,128)S(1)}, u32[]{:S(2)}, u32[]{:S(2)}) %collective-permute-start.101) | collective-permute-done | bytes 225312 | tf_op jit(solution)/shard_map/small_y/ppermute | solution.py:1015
  525.7 3.9 collective-permute-done.100
  530.7 5.8 %collective-permute-done.112.refs_7_ = bf16[320,640]{1,0:T(8,128)(2,1)S(1)} collective-permute-done((bf16[320,640]{1,0:T(8,128)(2,1)}, bf16[320,640]{1,0:T(8,128)(2,1)S(1)}, u32[]{:S(2)}, u32[]{:S(2)}) %collective-permute-start.112) | collective-permute-done | bytes 409632 | tf_op jit(solution)/shard_map/d0_x/ppermute | solution.py:1015
  542.9 4.6 shard_map.274
  550.5 4.6 shard_map.275
  (477 shorter events, 94.8 us)
Async XLA Ops:
  7.2 497.6 %reduce-scatter.6.cloned.1.call-start = ((), (), s32[]{:S(2)}) async-start(), calls=%async_computation.4 | async-start | bytes 2048000 | tf_op jit(solution)/shard_map/reduce_scatter | solution.py:1115
  28.8 20.3 %collective-permute-start.9 = (bf16[2,2,80,640]{3,2,1,0:T(8,128)(2,1)S(1)}, bf16[2,2,80,640]{3,2,1,0:T(8,128)(2,1)}, u32[]{:S(2)}, u32[]{:S(2)}) collective-permute-start(bf16[2,2,80,640]{3,2,1,0:T(8,128)(2,1)S(1)} %maximum_select_fusion.7), channel_id=1, source_target_pairs={{0,8},{8,0},{16,24},{24,16},{1,9},{9,1},{17,25},{25,17},{2,10},{10... | collective-permute-start | bytes 1228808 | tf_op jit(solution)/shard_map/u0_near/ppermute | solution.py:1064
  28.9 23.1 %collective-permute-start.8 = (bf16[1,320,640]{2,1,0:T(8,128)(2,1)S(1)}, bf16[1,320,640]{2,1,0:T(8,128)(2,1)}, u32[]{:S(2)}, u32[]{:S(2)}) collective-permute-start(bf16[1,320,640]{2,1,0:T(8,128)(2,1)S(1)} %reshape.541), channel_id=1, source_target_pairs={{0,16},{8,24},{16,0},{24,8},{1,17},{9,25},{17,1},{25,9},{2,18},{10... | collective-permute-start | bytes 1228808 | tf_op jit(solution)/shard_map/d0_far/ppermute | solution.py:1064
  32.5 16.6 %collective-permute-start.3 = (bf16[4,1,80,640]{3,2,1,0:T(8,128)(2,1)S(1)}, bf16[4,1,80,640]{3,2,1,0:T(8,128)(2,1)}, u32[]{:S(2)}, u32[]{:S(2)}) collective-permute-start(bf16[4,1,80,640]{3,2,1,0:T(8,128)(2,1)S(1)} %bitcast.171), channel_id=1, source_target_pairs={{0,4},{4,0},{1,5},{5,1},{2,6},{6,2},{3,7},{7,3},{8,12},{12,8},{9,1... | collective-permute-start | bytes 1228808 | tf_op jit(solution)/shard_map/a0_y/ppermute | solution.py:1015
  34.1 21.1 %collective-permute-start.6 = (bf16[4,1,80,640]{3,2,1,0:T(8,128)(2,1)S(1)}, bf16[4,1,80,640]{3,2,1,0:T(8,128)(2,1)}, u32[]{:S(2)}, u32[]{:S(2)}) collective-permute-start(bf16[4,1,80,640]{3,2,1,0:T(8,128)(2,1)S(1)} %bitcast.172), channel_id=1, source_target_pairs={{0,2},{2,0},{1,3},{3,1},{4,6},{6,4},{5,7},{7,5},{8,10},{10,8},{9,1... | collective-permute-start | bytes 1228808 | tf_op jit(solution)/shard_map/a0_x/ppermute | solution.py:1015
  35.6 24.3 %collective-permute-start.4 = (bf16[4,1,80,640]{3,2,1,0:T(8,128)(2,1)S(1)}, bf16[4,1,80,640]{3,2,1,0:T(8,128)(2,1)}, u32[]{:S(2)}, u32[]{:S(2)}) collective-permute-start(bf16[4,1,80,640]{3,2,1,0:T(8,128)(2,1)S(1)} %bitcast.173), channel_id=1, source_target_pairs={{0,1},{1,0},{2,3},{3,2},{4,5},{5,4},{6,7},{7,6},{8,9},{9,8},{10,11... | collective-permute-start | bytes 1228808 | tf_op jit(solution)/shard_map/a0_c/ppermute | solution.py:1015
  53.6 25.5 %collective-permute-start.16 = (bf16[2,1,320,640]{3,2,0,1:T(8,128)(2,1)S(1)}, bf16[2,1,320,640]{3,2,0,1:T(8,128)(2,1)}, u32[]{:S(2)}, u32[]{:S(2)}) collective-permute-start(bf16[2,1,320,640]{3,2,0,1:T(8,128)(2,1)S(1)} %maximum_select_fusion.4), channel_id=1, source_target_pairs={{0,8},{8,0},{16,24},{24,16},{1,9},{9,1},{17,25},{25,17},{2,10},{10... | collective-permute-start | bytes 2457608 | tf_op jit(solution)/shard_map/d0_near/ppermute | solution.py:1064
  53.6 25.4 %collective-permute-start.12 = (bf16[4,2,80,640]{3,2,1,0:T(8,128)(2,1)S(1)}, bf16[4,2,80,640]{3,2,1,0:T(8,128)(2,1)}, u32[]{:S(2)}, u32[]{:S(2)}) collective-permute-start(bf16[4,2,80,640]{3,2,1,0:T(8,128)(2,1)S(1)} %bitcast.166), channel_id=1, source_target_pairs={{0,4},{4,0},{1,5},{5,1},{2,6},{6,2},{3,7},{7,3},{8,12},{12,8},{9,1... | collective-permute-start | bytes 2457608 | tf_op jit(solution)/shard_map/u0_y/ppermute | solution.py:1015
  61.1 21.3 %collective-permute-start.15 = (bf16[4,2,80,640]{3,2,1,0:T(8,128)(2,1)S(1)}, bf16[4,2,80,640]{3,2,1,0:T(8,128)(2,1)}, u32[]{:S(2)}, u32[]{:S(2)}) collective-permute-start(bf16[4,2,80,640]{3,2,1,0:T(8,128)(2,1)S(1)} %bitcast.167), channel_id=1, source_target_pairs={{0,2},{2,0},{1,3},{3,1},{4,6},{6,4},{5,7},{7,5},{8,10},{10,8},{9,1... | collective-permute-start | bytes 2457608 | tf_op jit(solution)/shard_map/u0_x/ppermute | solution.py:1015
  63.8 36.4 %collective-permute-start.13 = (bf16[4,2,80,640]{3,2,1,0:T(8,128)(2,1)S(1)}, bf16[4,2,80,640]{3,2,1,0:T(8,128)(2,1)}, u32[]{:S(2)}, u32[]{:S(2)}) collective-permute-start(bf16[4,2,80,640]{3,2,1,0:T(8,128)(2,1)S(1)} %bitcast.168), channel_id=1, source_target_pairs={{0,1},{1,0},{2,3},{3,2},{4,5},{5,4},{6,7},{7,6},{8,9},{9,8},{10,11... | collective-permute-start | bytes 2457608 | tf_op jit(solution)/shard_map/u0_c/ppermute | solution.py:1015
  79.0 21.1 %collective-permute-start.17 = (bf16[4,2,80,640]{3,2,1,0:T(8,128)(2,1)}, bf16[4,2,80,640]{3,2,1,0:T(8,128)(2,1)S(1)}, u32[]{:S(2)}, u32[]{:S(2)}) collective-permute-start(bf16[4,2,80,640]{3,2,1,0:T(8,128)(2,1)} %collective-permute-done.12.refs_1_), channel_id=1, source_target_pairs={{0,2},{2,0},{1,3},{3,1},{4,6},{6,4},{5,7},{7,5},{8,10},{10,8},{9,1... | collective-permute-start | bytes 2457608 | tf_op jit(solution)/shard_map/u0_yx/ppermute | solution.py:1015
  82.4 17.9 %collective-permute-start.19 = (bf16[4,2,80,640]{3,2,1,0:T(8,128)(2,1)}, bf16[4,2,80,640]{3,2,1,0:T(8,128)(2,1)S(1)}, u32[]{:S(2)}, u32[]{:S(2)}) collective-permute-start(bf16[4,2,80,640]{3,2,1,0:T(8,128)(2,1)} %collective-permute-done.15.refs_4_.refs_2_), channel_id=1, source_target_pairs={{0,1},{1,0},{2,3},{3,2},{4,5},{5,4},{6,7},{7,6},{8,9},{9,8},{10,11... | collective-permute-start | bytes 2457608 | tf_op jit(solution)/shard_map/u0_xc/ppermute | solution.py:1015
  82.5 16.0 %collective-permute-start.18 = (bf16[3,80,640]{2,1,0:T(8,128)(2,1)S(1)}, bf16[3,80,640]{2,1,0:T(8,128)(2,1)S(1)}, u32[]{:S(2)}, u32[]{:S(2)}) collective-permute-start(bf16[3,80,640]{2,1,0:T(8,128)(2,1)S(1)} %copy-done.29), channel_id=1, source_target_pairs={{0,16},{8,24},{16,0},{24,8},{1,17},{9,25},{17,1},{25,9},{2,18},{10... | collective-permute-start | bytes 921608 | tf_op jit(solution)/shard_map/j1_far/ppermute | solution.py:1064
  82.5 33.3 %collective-permute-start.23 = (bf16[2,320,640]{2,1,0:T(8,128)(2,1)S(1)}, bf16[2,320,640]{2,1,0:T(8,128)(2,1)}, u32[]{:S(2)}, u32[]{:S(2)}) collective-permute-start(bf16[2,320,640]{2,1,0:T(8,128)(2,1)S(1)} %get-tuple-element.417.refs_1_.refs_5_), channel_id=1, source_target_pairs={{0,4},{4,0},{1,5},{5,1},{2,6},{6,2},{3,7},{7,3},{8,12},{12,8},{9,1... | collective-permute-start | bytes 2457608 | tf_op jit(solution)/shard_map/d0_y/ppermute | solution.py:1015
  98.5 22.3 %collective-permute-start.22 = (bf16[2,320,640]{2,1,0:T(8,128)(2,1)}, bf16[2,320,640]{2,1,0:T(8,128)(2,1)}, u32[]{:S(2)}, u32[]{:S(2)}) collective-permute-start(bf16[2,320,640]{2,1,0:T(8,128)(2,1)} %get-tuple-element.416.refs_0_.refs_4_), channel_id=1, source_target_pairs={{0,4},{4,0},{1,5},{5,1},{2,6},{6,2},{3,7},{7,3},{8,12},{12,8},{9,1... | collective-permute-start | bytes 2457608 | tf_op jit(solution)/shard_map/d0_y/ppermute | solution.py:1015
  100.1 15.6 %collective-permute-start.21 = (bf16[2,3,80,640]{3,2,1,0:T(8,128)(2,1)S(1)}, bf16[2,3,80,640]{3,2,1,0:T(8,128)(2,1)S(1)}, u32[]{:S(2)}, u32[]{:S(2)}) collective-permute-start(bf16[2,3,80,640]{3,2,1,0:T(8,128)(2,1)S(1)} %maximum_select_fusion.6), channel_id=1, source_target_pairs={{0,8},{8,0},{16,24},{24,16},{1,9},{9,1},{17,25},{25,17},{2,10},{10... | collective-permute-start | bytes 1843208 | tf_op jit(solution)/shard_map/j1_near/ppermute | solution.py:1064
  100.2 22.0 %collective-permute-start.14 = (bf16[4,2,80,640]{3,2,1,0:T(8,128)(2,1)}, bf16[4,2,80,640]{3,2,1,0:T(8,128)(2,1)S(1)}, u32[]{:S(2)}, u32[]{:S(2)}) collective-permute-start(bf16[4,2,80,640]{3,2,1,0:T(8,128)(2,1)} %collective-permute-done.12.refs_1_), channel_id=1, source_target_pairs={{0,1},{1,0},{2,3},{3,2},{4,5},{5,4},{6,7},{7,6},{8,9},{9,8},{10,11... | collective-permute-start | bytes 2457608 | tf_op jit(solution)/shard_map/u0_yc/ppermute | solution.py:1015
  100.3 21.9 %collective-permute-start.20 = (bf16[4,2,80,640]{3,2,1,0:T(8,128)(2,1)S(1)}, bf16[4,2,80,640]{3,2,1,0:T(8,128)(2,1)S(1)}, u32[]{:S(2)}, u32[]{:S(2)}) collective-permute-start(bf16[4,2,80,640]{3,2,1,0:T(8,128)(2,1)S(1)} %collective-permute-done.17.refs_5_.refs_3_), channel_id=1, source_target_pairs={{0,1},{1,0},{2,3},{3,2},{4,5},{5,4},{6,7},{7,6},{8,9},{9,8},{10,11... | collective-permute-start | bytes 2457608 | tf_op jit(solution)/shard_map/u0_yxc/ppermute | solution.py:1015
  115.7 20.2 %collective-permute-start.24 = (bf16[2,320,640]{2,1,0:T(8,128)(2,1)}, bf16[2,320,640]{2,1,0:T(8,128)(2,1)}, u32[]{:S(2)}, u32[]{:S(2)}) collective-permute-start(bf16[2,320,640]{2,1,0:T(8,128)(2,1)} %get-tuple-element.416.refs_0_.refs_4_), channel_id=1, source_target_pairs={{0,1},{1,0},{2,3},{3,2},{4,5},{5,4},{6,7},{7,6},{8,9},{9,8},{10,11... | collective-permute-start | bytes 2457608 | tf_op jit(solution)/shard_map/d0_c/ppermute | solution.py:1015
  115.7 22.9 %collective-permute-start.25 = (bf16[2,320,640]{2,1,0:T(8,128)(2,1)S(1)}, bf16[2,320,640]{2,1,0:T(8,128)(2,1)}, u32[]{:S(2)}, u32[]{:S(2)}) collective-permute-start(bf16[2,320,640]{2,1,0:T(8,128)(2,1)S(1)} %get-tuple-element.417.refs_1_.refs_5_), channel_id=1, source_target_pairs={{0,1},{1,0},{2,3},{3,2},{4,5},{5,4},{6,7},{7,6},{8,9},{9,8},{10,11... | collective-permute-start | bytes 2457608 | tf_op jit(solution)/shard_map/d0_c/ppermute | solution.py:1015
  120.7 37.9 %collective-permute-start.28 = (bf16[4,3,80,640]{3,2,1,0:T(8,128)(2,1)S(1)}, bf16[4,3,80,640]{3,2,1,0:T(8,128)(2,1)S(1)}, u32[]{:S(2)}, u32[]{:S(2)}) collective-permute-start(bf16[4,3,80,640]{3,2,1,0:T(8,128)(2,1)S(1)} %bitcast.159), channel_id=1, source_target_pairs={{0,4},{4,0},{1,5},{5,1},{2,6},{6,2},{3,7},{7,3},{8,12},{12,8},{9,1... | collective-permute-start | bytes 3686408 | tf_op jit(solution)/shard_map/j1_y/ppermute | solution.py:1015
  122.2 18.9 %collective-permute-start.26 = (bf16[2,320,640]{2,1,0:T(8,128)(2,1)}, bf16[2,320,640]{2,1,0:T(8,128)(2,1)}, u32[]{:S(2)}, u32[]{:S(2)}) collective-permute-start(bf16[2,320,640]{2,1,0:T(8,128)(2,1)} %collective-permute-done.22.refs_2_.refs_6_), channel_id=1, source_target_pairs={{0,1},{1,0},{2,3},{3,2},{4,5},{5,4},{6,7},{7,6},{8,9},{9,8},{10,11... | collective-permute-start | bytes 2457608 | tf_op jit(solution)/shard_map/d0_yc/ppermute | solution.py:1015
  123.1 18.0 %collective-permute-start.27 = (bf16[2,320,640]{2,1,0:T(8,128)(2,1)}, bf16[2,320,640]{2,1,0:T(8,128)(2,1)}, u32[]{:S(2)}, u32[]{:S(2)}) collective-permute-start(bf16[2,320,640]{2,1,0:T(8,128)(2,1)} %collective-permute-done.23.refs_3_.refs_7_), channel_id=1, source_target_pairs={{0,1},{1,0},{2,3},{3,2},{4,5},{5,4},{6,7},{7,6},{8,9},{9,8},{10,11... | collective-permute-start | bytes 2457608 | tf_op jit(solution)/shard_map/d0_yc/ppermute | solution.py:1015
  135.9 21.4 %collective-permute-start.33 = (bf16[1,320,640]{2,1,0:T(8,128)(2,1)S(1)}, bf16[1,320,640]{2,1,0:T(8,128)(2,1)}, u32[]{:S(2)}, u32[]{:S(2)}) collective-permute-start(bf16[1,320,640]{2,1,0:T(8,128)(2,1)S(1)} %copy-done.16), channel_id=1, source_target_pairs={{0,16},{8,24},{16,0},{24,8},{1,17},{9,25},{17,1},{25,9},{2,18},{10... | collective-permute-start | bytes 1228808 | tf_op jit(solution)/shard_map/d1_far/ppermute | solution.py:1064
  138.7 30.4 %collective-permute-start.31 = (bf16[4,3,80,640]{3,2,1,0:T(8,128)(2,1)S(1)}, bf16[4,3,80,640]{3,2,1,0:T(8,128)(2,1)}, u32[]{:S(2)}, u32[]{:S(2)}) collective-permute-start(bf16[4,3,80,640]{3,2,1,0:T(8,128)(2,1)S(1)} %bitcast.160), channel_id=1, source_target_pairs={{0,2},{2,0},{1,3},{3,1},{4,6},{6,4},{5,7},{7,5},{8,10},{10,8},{9,1... | collective-permute-start | bytes 3686408 | tf_op jit(solution)/shard_map/j1_x/ppermute | solution.py:1015
  158.6 19.5 %collective-permute-start.34 = (bf16[2,1,320,640]{3,2,0,1:T(8,128)(2,1)S(1)}, bf16[2,1,320,640]{3,2,0,1:T(8,128)(2,1)S(1)}, u32[]{:S(2)}, u32[]{:S(2)}) collective-permute-start(bf16[2,1,320,640]{3,2,0,1:T(8,128)(2,1)S(1)} %maximum_select_fusion.5), channel_id=1, source_target_pairs={{0,8},{8,0},{16,24},{24,16},{1,9},{9,1},{17,25},{25,17},{2,10},{10... | collective-permute-start | bytes 2457608 | tf_op jit(solution)/shard_map/d1_near/ppermute | solution.py:1064
  158.7 35.9 %collective-permute-start.32 = (bf16[4,3,80,640]{3,2,1,0:T(8,128)(2,1)S(1)}, bf16[4,3,80,640]{3,2,1,0:T(8,128)(2,1)}, u32[]{:S(2)}, u32[]{:S(2)}) collective-permute-start(bf16[4,3,80,640]{3,2,1,0:T(8,128)(2,1)S(1)} %collective-permute-done.28.refs_1_), channel_id=1, source_target_pairs={{0,2},{2,0},{1,3},{3,1},{4,6},{6,4},{5,7},{7,5},{8,10},{10,8},{9,1... | collective-permute-start | bytes 3686408 | tf_op jit(solution)/shard_map/j1_yx/ppermute | solution.py:1015
  161.2 33.9 %collective-permute-start.29 = (bf16[4,3,80,640]{3,2,1,0:T(8,128)(2,1)S(1)}, bf16[4,3,80,640]{3,2,1,0:T(8,128)(2,1)S(1)}, u32[]{:S(2)}, u32[]{:S(2)}) collective-permute-start(bf16[4,3,80,640]{3,2,1,0:T(8,128)(2,1)S(1)} %bitcast.161), channel_id=1, source_target_pairs={{0,1},{1,0},{2,3},{3,2},{4,5},{5,4},{6,7},{7,6},{8,9},{9,8},{10,11... | collective-permute-start | bytes 3686408 | tf_op jit(solution)/shard_map/j1_c/ppermute | solution.py:1015
  161.2 37.7 %collective-permute-start.30 = (bf16[4,3,80,640]{3,2,1,0:T(8,128)(2,1)S(1)}, bf16[4,3,80,640]{3,2,1,0:T(8,128)(2,1)}, u32[]{:S(2)}, u32[]{:S(2)}) collective-permute-start(bf16[4,3,80,640]{3,2,1,0:T(8,128)(2,1)S(1)} %collective-permute-done.28.refs_1_), channel_id=1, source_target_pairs={{0,1},{1,0},{2,3},{3,2},{4,5},{5,4},{6,7},{7,6},{8,9},{9,8},{10,11... | collective-permute-start | bytes 3686408 | tf_op jit(solution)/shard_map/j1_yc/ppermute | solution.py:1015
  169.1 29.8 %collective-permute-start.35 = (bf16[4,3,80,640]{3,2,1,0:T(8,128)(2,1)}, bf16[4,3,80,640]{3,2,1,0:T(8,128)(2,1)}, u32[]{:S(2)}, u32[]{:S(2)}) collective-permute-start(bf16[4,3,80,640]{3,2,1,0:T(8,128)(2,1)} %collective-permute-done.31.refs_4_.refs_2_), channel_id=1, source_target_pairs={{0,1},{1,0},{2,3},{3,2},{4,5},{5,4},{6,7},{7,6},{8,9},{9,8},{10,11... | collective-permute-start | bytes 3686408 | tf_op jit(solution)/shard_map/j1_xc/ppermute | solution.py:1015
  194.6 30.7 %collective-permute-start.38 = (bf16[2,320,640]{2,1,0:T(8,128)(2,1)S(1)}, bf16[2,320,640]{2,1,0:T(8,128)(2,1)}, u32[]{:S(2)}, u32[]{:S(2)}) collective-permute-start(bf16[2,320,640]{2,1,0:T(8,128)(2,1)S(1)} %get-tuple-element.460.refs_1_.refs_5_), channel_id=1, source_target_pairs={{0,4},{4,0},{1,5},{5,1},{2,6},{6,2},{3,7},{7,3},{8,12},{12,8},{9,1... | collective-permute-start | bytes 2457608 | tf_op jit(solution)/shard_map/d1_y/ppermute | solution.py:1015
  196.2 36.7 %collective-permute-start.37 = (bf16[2,320,640]{2,1,0:T(8,128)(2,1)}, bf16[2,320,640]{2,1,0:T(8,128)(2,1)S(1)}, u32[]{:S(2)}, u32[]{:S(2)}) collective-permute-start(bf16[2,320,640]{2,1,0:T(8,128)(2,1)} %get-tuple-element.459.refs_0_.refs_4_), channel_id=1, source_target_pairs={{0,4},{4,0},{1,5},{5,1},{2,6},{6,2},{3,7},{7,3},{8,12},{12,8},{9,1... | collective-permute-start | bytes 2457608 | tf_op jit(solution)/shard_map/d1_y/ppermute | solution.py:1015
  198.9 36.6 %collective-permute-start.39 = (bf16[2,320,640]{2,1,0:T(8,128)(2,1)}, bf16[2,320,640]{2,1,0:T(8,128)(2,1)}, u32[]{:S(2)}, u32[]{:S(2)}) collective-permute-start(bf16[2,320,640]{2,1,0:T(8,128)(2,1)} %get-tuple-element.459.refs_0_.refs_4_), channel_id=1, source_target_pairs={{0,1},{1,0},{2,3},{3,2},{4,5},{5,4},{6,7},{7,6},{8,9},{9,8},{10,11... | collective-permute-start | bytes 2457608 | tf_op jit(solution)/shard_map/d1_c/ppermute | solution.py:1015
  198.9 36.6 %collective-permute-start.40 = (bf16[2,320,640]{2,1,0:T(8,128)(2,1)S(1)}, bf16[2,320,640]{2,1,0:T(8,128)(2,1)S(1)}, u32[]{:S(2)}, u32[]{:S(2)}) collective-permute-start(bf16[2,320,640]{2,1,0:T(8,128)(2,1)S(1)} %get-tuple-element.460.refs_1_.refs_5_), channel_id=1, source_target_pairs={{0,1},{1,0},{2,3},{3,2},{4,5},{5,4},{6,7},{7,6},{8,9},{9,8},{10,11... | collective-permute-start | bytes 2457608 | tf_op jit(solution)/shard_map/d1_c/ppermute | solution.py:1015
  263.7 16.0 %collective-permute-start.51 = (bf16[320,640]{1,0:T(8,128)(2,1)}, bf16[320,640]{1,0:T(8,128)(2,1)S(1)}, u32[]{:S(2)}, u32[]{:S(2)}) collective-permute-start(bf16[320,640]{1,0:T(8,128)(2,1)} %get-tuple-element.480), channel_id=1, source_target_pairs={{0,1},{1,0},{2,3},{3,2},{4,5},{5,4},{6,7},{7,6},{8,9},{9,8},{10,11... | collective-permute-start | bytes 1228808 | tf_op jit(solution)/shard_map/d1_c/ppermute | solution.py:1015
  264.2 15.6 %collective-permute-start.52 = (bf16[320,640]{1,0:T(8,128)(2,1)}, bf16[320,640]{1,0:T(8,128)(2,1)S(1)}, u32[]{:S(2)}, u32[]{:S(2)}) collective-permute-start(bf16[320,640]{1,0:T(8,128)(2,1)} %get-tuple-element.494), channel_id=1, source_target_pairs={{0,1},{1,0},{2,3},{3,2},{4,5},{5,4},{6,7},{7,6},{8,9},{9,8},{10,11... | collective-permute-start | bytes 1228808 | tf_op jit(solution)/shard_map/d1_c/ppermute | solution.py:1015
  264.3 15.9 %collective-permute-start.53 = (bf16[320,640]{1,0:T(8,128)(2,1)}, bf16[320,640]{1,0:T(8,128)(2,1)S(1)}, u32[]{:S(2)}, u32[]{:S(2)}) collective-permute-start(bf16[320,640]{1,0:T(8,128)(2,1)} %get-tuple-element.495), channel_id=1, source_target_pairs={{0,1},{1,0},{2,3},{3,2},{4,5},{5,4},{6,7},{7,6},{8,9},{9,8},{10,11... | collective-permute-start | bytes 1228808 | tf_op jit(solution)/shard_map/d1_c/ppermute | solution.py:1015
  264.8 15.6 %collective-permute-start.54 = (bf16[320,640]{1,0:T(8,128)(2,1)}, bf16[320,640]{1,0:T(8,128)(2,1)S(1)}, u32[]{:S(2)}, u32[]{:S(2)}) collective-permute-start(bf16[320,640]{1,0:T(8,128)(2,1)} %get-tuple-element.496), channel_id=1, source_target_pairs={{0,1},{1,0},{2,3},{3,2},{4,5},{5,4},{6,7},{7,6},{8,9},{9,8},{10,11... | collective-permute-start | bytes 1228808 | tf_op jit(solution)/shard_map/d1_c/ppermute | solution.py:1015
  284.0 56.3 %collective-permute-start.59 = (bf16[4,320,640]{2,1,0:T(8,128)(2,1)}, bf16[4,320,640]{2,1,0:T(8,128)(2,1)S(1)}, u32[]{:S(2)}, u32[]{:S(2)}) collective-permute-start(bf16[4,320,640]{2,1,0:T(8,128)(2,1)} %shard_map.262), channel_id=1, source_target_pairs={{0,4},{4,0},{1,5},{5,1},{2,6},{6,2},{3,7},{7,3},{8,12},{12,8},{9,1... | collective-permute-start | bytes 4915208 | tf_op jit(solution)/shard_map/d1_y/ppermute | solution.py:1015
  286.6 36.1 %collective-permute-start.60 = (bf16[320,640]{1,0:T(8,128)(2,1)}, bf16[320,640]{1,0:T(8,128)(2,1)}, u32[]{:S(2)}, u32[]{:S(2)}) collective-permute-start(bf16[320,640]{1,0:T(8,128)(2,1)} %get-tuple-element.528), channel_id=1, source_target_pairs={{0,1},{1,0},{2,3},{3,2},{4,5},{5,4},{6,7},{7,6},{8,9},{9,8},{10,11... | collective-permute-start | bytes 1228808 | tf_op jit(solution)/shard_map/d1_c/ppermute | solution.py:1015
  323.8 16.5 %collective-permute-start.61 = (bf16[320,640]{1,0:T(8,128)(2,1)}, bf16[320,640]{1,0:T(8,128)(2,1)}, u32[]{:S(2)}, u32[]{:S(2)}) collective-permute-start(bf16[320,640]{1,0:T(8,128)(2,1)} %get-tuple-element.529), channel_id=1, source_target_pairs={{0,1},{1,0},{2,3},{3,2},{4,5},{5,4},{6,7},{7,6},{8,9},{9,8},{10,11... | collective-permute-start | bytes 1228808 | tf_op jit(solution)/shard_map/d1_c/ppermute | solution.py:1015
  324.4 16.0 %collective-permute-start.62 = (bf16[320,640]{1,0:T(8,128)(2,1)}, bf16[320,640]{1,0:T(8,128)(2,1)}, u32[]{:S(2)}, u32[]{:S(2)}) collective-permute-start(bf16[320,640]{1,0:T(8,128)(2,1)} %get-tuple-element.530), channel_id=1, source_target_pairs={{0,1},{1,0},{2,3},{3,2},{4,5},{5,4},{6,7},{7,6},{8,9},{9,8},{10,11... | collective-permute-start | bytes 1228808 | tf_op jit(solution)/shard_map/d1_c/ppermute | solution.py:1015
  325.7 56.0 %collective-permute-start.77 = (bf16[2,4,2,80,640]{4,3,2,1,0:T(8,128)(2,1)}, bf16[2,4,2,80,640]{4,3,2,1,0:T(8,128)(2,1)S(1)}, u32[]{:S(2)}, u32[]{:S(2)}) collective-permute-start(bf16[2,4,2,80,640]{4,3,2,1,0:T(8,128)(2,1)} %get-tuple-element.515), channel_id=1, source_target_pairs={{0,2},{2,0},{1,3},{3,1},{4,6},{6,4},{5,7},{7,5},{8,10},{10,8},{9,1... | collective-permute-start | bytes 4915208 | tf_op jit(solution)/shard_map/u1_x/ppermute | solution.py:1015
  345.0 180.1 %reduce-scatter.8.cloned.1.call-start = ((), (), s32[]{:S(2)}) async-start(), calls=%async_computation.5 | async-start | bytes 2048000 | tf_op jit(solution)/shard_map/reduce_scatter | solution.py:1115
  346.6 35.1 %collective-permute-start.76 = (bf16[2,4,80,640]{3,2,1,0:T(8,128)(2,1)}, bf16[2,4,80,640]{3,2,1,0:T(8,128)(2,1)}, u32[]{:S(2)}, u32[]{:S(2)}) collective-permute-start(bf16[2,4,80,640]{3,2,1,0:T(8,128)(2,1)} %get-tuple-element.545), channel_id=1, source_target_pairs={{0,2},{2,0},{1,3},{3,1},{4,6},{6,4},{5,7},{7,5},{8,10},{10,8},{9,1... | collective-permute-start | bytes 2457608 | tf_op jit(solution)/shard_map/a1_x/ppermute | solution.py:1015
  348.5 20.6 %collective-permute-start.79 = (bf16[320,640]{1,0:T(8,128)(2,1)}, bf16[320,640]{1,0:T(8,128)(2,1)}, u32[]{:S(2)}, u32[]{:S(2)}) collective-permute-start(bf16[320,640]{1,0:T(8,128)(2,1)} %get-tuple-element.588), channel_id=1, source_target_pairs={{0,1},{1,0},{2,3},{3,2},{4,5},{5,4},{6,7},{7,6},{8,9},{9,8},{10,11... | collective-permute-start | bytes 1228808 | tf_op jit(solution)/shard_map/d0_c/ppermute | solution.py:1015
  349.1 20.1 %collective-permute-start.80 = (bf16[320,640]{1,0:T(8,128)(2,1)}, bf16[320,640]{1,0:T(8,128)(2,1)}, u32[]{:S(2)}, u32[]{:S(2)}) collective-permute-start(bf16[320,640]{1,0:T(8,128)(2,1)} %get-tuple-element.589), channel_id=1, source_target_pairs={{0,1},{1,0},{2,3},{3,2},{4,5},{5,4},{6,7},{7,6},{8,9},{9,8},{10,11... | collective-permute-start | bytes 1228808 | tf_op jit(solution)/shard_map/d0_c/ppermute | solution.py:1015
  353.1 55.5 %collective-permute-start.78 = (bf16[4,320,640]{2,1,0:T(8,128)(2,1)}, bf16[4,320,640]{2,1,0:T(8,128)(2,1)}, u32[]{:S(2)}, u32[]{:S(2)}) collective-permute-start(bf16[4,320,640]{2,1,0:T(8,128)(2,1)} %shard_map.268), channel_id=1, source_target_pairs={{0,4},{4,0},{1,5},{5,1},{2,6},{6,2},{3,7},{7,3},{8,12},{12,8},{9,1... | collective-permute-start | bytes 4915208 | tf_op jit(solution)/shard_map/d0_y/ppermute | solution.py:1015
  386.0 43.1 %collective-permute-start.88 = (bf16[4,2,80,640]{3,2,1,0:T(8,128)(2,1)}, bf16[4,2,80,640]{3,2,1,0:T(8,128)(2,1)}, u32[]{:S(2)}, u32[]{:S(2)}) collective-permute-start(bf16[4,2,80,640]{3,2,1,0:T(8,128)(2,1)} %fusion.1), channel_id=1, source_target_pairs={{0,4},{4,0},{1,5},{5,1},{2,6},{6,2},{3,7},{7,3},{8,12},{12,8},{9,1... | collective-permute-start | bytes 2457608 | tf_op jit(solution)/shard_map/u1_y/ppermute | solution.py:1015
  387.5 19.3 %collective-permute-start.81 = (bf16[320,640]{1,0:T(8,128)(2,1)}, bf16[320,640]{1,0:T(8,128)(2,1)}, u32[]{:S(2)}, u32[]{:S(2)}) collective-permute-start(bf16[320,640]{1,0:T(8,128)(2,1)} %get-tuple-element.590), channel_id=1, source_target_pairs={{0,1},{1,0},{2,3},{3,2},{4,5},{5,4},{6,7},{7,6},{8,9},{9,8},{10,11... | collective-permute-start | bytes 1228808 | tf_op jit(solution)/shard_map/d0_c/ppermute | solution.py:1015
  387.5 21.1 %collective-permute-start.82 = (bf16[320,640]{1,0:T(8,128)(2,1)}, bf16[320,640]{1,0:T(8,128)(2,1)}, u32[]{:S(2)}, u32[]{:S(2)}) collective-permute-start(bf16[320,640]{1,0:T(8,128)(2,1)} %get-tuple-element.591), channel_id=1, source_target_pairs={{0,1},{1,0},{2,3},{3,2},{4,5},{5,4},{6,7},{7,6},{8,9},{9,8},{10,11... | collective-permute-start | bytes 1228808 | tf_op jit(solution)/shard_map/d0_c/ppermute | solution.py:1015
  390.6 38.5 %collective-permute-start.89 = (bf16[4,80,640]{2,1,0:T(8,128)(2,1)}, bf16[4,80,640]{2,1,0:T(8,128)(2,1)}, u32[]{:S(2)}, u32[]{:S(2)}) collective-permute-start(bf16[4,80,640]{2,1,0:T(8,128)(2,1)} %fusion.5), channel_id=1, source_target_pairs={{0,4},{4,0},{1,5},{5,1},{2,6},{6,2},{3,7},{7,3},{8,12},{12,8},{9,1... | collective-permute-start | bytes 1228808 | tf_op jit(solution)/shard_map/a1_y/ppermute | solution.py:1015
  406.8 39.1 %collective-permute-start.83 = (bf16[2,4,2,80,640]{4,3,2,1,0:T(8,128)(2,1)}, bf16[2,4,2,80,640]{4,3,2,1,0:T(8,128)(2,1)}, u32[]{:S(2)}, u32[]{:S(2)}) collective-permute-start(bf16[2,4,2,80,640]{4,3,2,1,0:T(8,128)(2,1)} %get-tuple-element.592), channel_id=1, source_target_pairs={{0,2},{2,0},{1,3},{3,1},{4,6},{6,4},{5,7},{7,5},{8,10},{10,8},{9,1... | collective-permute-start | bytes 4915208 | tf_op jit(solution)/shard_map/u0_x/ppermute | solution.py:1015
  431.5 98.2 %reduce-scatter.4.cloned.1.call-start = ((), (), s32[]{:S(2)}) async-start(), calls=%async_computation.3 | async-start | bytes 1024000 | tf_op jit(solution)/shard_map/reduce_scatter | solution.py:1115
  434.8 47.1 %collective-permute-start.94 = (bf16[2,3,80,640]{3,2,1,0:T(8,128)(2,1)}, bf16[2,3,80,640]{3,2,1,0:T(8,128)(2,1)S(1)}, u32[]{:S(2)}, u32[]{:S(2)}) collective-permute-start(bf16[2,3,80,640]{3,2,1,0:T(8,128)(2,1)} %get-tuple-element.763), channel_id=1, source_target_pairs={{0,8},{8,0},{16,24},{24,16},{1,9},{9,1},{17,25},{25,17},{2,10},{10... | collective-permute-start | bytes 1843208 | tf_op jit(solution)/shard_map/j1_near/ppermute | solution.py:1064
  439.8 44.1 %collective-permute-start.91 = (bf16[2,4,80,640]{3,2,1,0:T(8,128)(2,1)}, bf16[2,4,80,640]{3,2,1,0:T(8,128)(2,1)}, u32[]{:S(2)}, u32[]{:S(2)}) collective-permute-start(bf16[2,4,80,640]{3,2,1,0:T(8,128)(2,1)} %get-tuple-element.634), channel_id=1, source_target_pairs={{0,2},{2,0},{1,3},{3,1},{4,6},{6,4},{5,7},{7,5},{8,10},{10,8},{9,1... | collective-permute-start | bytes 2457608 | tf_op jit(solution)/shard_map/a0_x/ppermute | solution.py:1015
  448.1 39.2 %collective-permute-start.90 = (bf16[4,2,80,640]{3,2,1,0:T(8,128)(2,1)}, bf16[4,2,80,640]{3,2,1,0:T(8,128)(2,1)}, u32[]{:S(2)}, u32[]{:S(2)}) collective-permute-start(bf16[4,2,80,640]{3,2,1,0:T(8,128)(2,1)} %fusion.2), channel_id=1, source_target_pairs={{0,4},{4,0},{1,5},{5,1},{2,6},{6,2},{3,7},{7,3},{8,12},{12,8},{9,1... | collective-permute-start | bytes 2457608 | tf_op jit(solution)/shard_map/u0_y/ppermute | solution.py:1015
  450.6 32.3 %collective-permute-start.93 = (f32[88,640]{1,0:T(8,128)S(1)}, f32[88,640]{1,0:T(8,128)S(1)}, u32[]{:S(2)}, u32[]{:S(2)}) collective-permute-start(f32[88,640]{1,0:T(8,128)S(1)} %add.155), channel_id=1, source_target_pairs={{0,16},{8,24},{16,0},{24,8},{1,17},{9,25},{17,1},{25,9},{2,18},{10... | collective-permute-start | bytes 675848 | tf_op jit(solution)/shard_map/small_far/ppermute | solution.py:1064
  482.9 15.4 %collective-permute-start.97 = (bf16[3,80,640]{2,1,0:T(8,128)(2,1)}, bf16[3,80,640]{2,1,0:T(8,128)(2,1)S(1)}, u32[]{:S(2)}, u32[]{:S(2)}) collective-permute-start(bf16[3,80,640]{2,1,0:T(8,128)(2,1)} %get-tuple-element.767), channel_id=1, source_target_pairs={{0,16},{8,24},{16,0},{24,8},{1,17},{9,25},{17,1},{25,9},{2,18},{10... | collective-permute-start | bytes 921608 | tf_op jit(solution)/shard_map/j1_far/ppermute | solution.py:1064
  482.9 17.2 %collective-permute-start.96 = (f32[88,640]{1,0:T(8,128)S(1)}, f32[88,640]{1,0:T(8,128)}, u32[]{:S(2)}, u32[]{:S(2)}) collective-permute-start(f32[88,640]{1,0:T(8,128)S(1)} %add.159), channel_id=1, source_target_pairs={{0,8},{8,0},{16,24},{24,16},{1,9},{9,1},{17,25},{25,17},{2,10},{10... | collective-permute-start | bytes 675848 | tf_op jit(solution)/shard_map/small_near/ppermute | solution.py:1064
  485.7 17.5 %collective-permute-start.95 = (bf16[4,80,640]{2,1,0:T(8,128)(2,1)}, bf16[4,80,640]{2,1,0:T(8,128)(2,1)}, u32[]{:S(2)}, u32[]{:S(2)}) collective-permute-start(bf16[4,80,640]{2,1,0:T(8,128)(2,1)} %fusion.6), channel_id=1, source_target_pairs={{0,4},{4,0},{1,5},{5,1},{2,6},{6,2},{3,7},{7,3},{8,12},{12,8},{9,1... | collective-permute-start | bytes 1228808 | tf_op jit(solution)/shard_map/a0_y/ppermute | solution.py:1015
  504.6 32.2 %collective-permute-start.104 = (bf16[3,80,640]{2,1,0:T(8,128)(2,1)S(1)}, bf16[3,80,640]{2,1,0:T(8,128)(2,1)S(1)}, u32[]{:S(2)}, u32[]{:S(2)}) collective-permute-start(bf16[3,80,640]{2,1,0:T(8,128)(2,1)S(1)} %add_convert_fusion.4.refs_1_), channel_id=1, source_target_pairs={{0,1},{1,0},{2,3},{3,2},{4,5},{5,4},{6,7},{7,6},{8,9},{9,8},{10,11... | collective-permute-start | bytes 921608 | tf_op jit(solution)/shard_map/j1_c/ppermute | solution.py:1015
  504.8 20.9 %collective-permute-start.108 = (bf16[320,640]{1,0:T(8,128)(2,1)}, bf16[320,640]{1,0:T(8,128)(2,1)S(1)}, u32[]{:S(2)}, u32[]{:S(2)}) collective-permute-start(bf16[320,640]{1,0:T(8,128)(2,1)} %bitcast.195), channel_id=1, source_target_pairs={{0,2},{2,0},{1,3},{3,1},{4,6},{6,4},{5,7},{7,5},{8,10},{10,8},{9,1... | collective-permute-start | bytes 1228808 | tf_op jit(solution)/shard_map/d1_x/ppermute | solution.py:1015
  515.1 26.3 %collective-permute-start.107 = (bf16[320,640]{1,0:T(8,128)(2,1)}, bf16[320,640]{1,0:T(8,128)(2,1)S(1)}, u32[]{:S(2)}, u32[]{:S(2)}) collective-permute-start(bf16[320,640]{1,0:T(8,128)(2,1)} %bitcast.196), channel_id=1, source_target_pairs={{0,1},{1,0},{2,3},{3,2},{4,5},{5,4},{6,7},{7,6},{8,9},{9,8},{10,11... | collective-permute-start | bytes 1228808 | tf_op jit(solution)/shard_map/d1_c/ppermute | solution.py:1015
  (137 other events, 1013.2 us)
Sparse Core Ops, SparseCore 0:
  345.1 34.6 reduce-scatter.5
  431.6 51.1 reduce-scatter.7
  504.9 24.8 reduce-scatter.3

commit v6 on v5

--- a/solution.py
+++ b/solution.py
@@ -971,7 +971,7 @@
                     tile, :, block * 128 : (block + 1) * 128
                 ].astype(F32)
     copies = [
-        copy(target, out.at[layer], sems.at[number])
+        copy(target.at[: out.shape[1], :], out.at[layer], sems.at[number])
         for number, (target, out) in enumerate(zip((attn, ups, downs), outs))
     ]
     copies[0].start()
@@ -1004,7 +1004,8 @@
         + [ANY_SPEC] * len(old),
         out_specs=(ANY_SPEC,) * 3,
         out_shape=tuple(sds((LAYERS, *shape), F32) for shape in (attn, wide, wide)),
-        scratch_shapes=[pltpu.VMEM(shape, F32) for shape in (attn, wide, wide)] + [semaphores(3)],
+        scratch_shapes=[pltpu.VMEM((shape[0] + 40, 128), F32) for shape in (attn, wide, wide)]
+        + [semaphores(3)],
         input_output_aliases={9 + number: number for number in range(len(old))},
         **KERNEL,
     )(place, *quarters, *halves, *old)

time: 571 us -> 571 us (level)
  no operation moved by 1% of the time
where the time goes in v6:
time: 571 us; the launch traced here: 565 us
  Pallas kernels  220 us (39%)
  waiting for transfers between devices  188 us (33%)
  starting transfers between devices  69 us (12%)
  local copies, waits for them, and re-layouts  38.3 us (7%)
  other arithmetic  27.8 us (5%)
  between operations  22.7 us (4%)
    ppermute x16, waiting for transfers between devices, hop(): lax.ppermute(value, 'z', [(at, at ^ reach) for at in range(self.z_size)])  102 us
    ppermute x98, waiting for transfers between devices, swap(): return lax.ppermute(value, axis, [(0, 1), (1, 0)])  85.5 us
    ppermute x98, starting transfers between devices, swap(): return lax.ppermute(value, axis, [(0, 1), (1, 0)])  51.5 us
    pallas_call x2, Pallas kernels, mix_back(): pl.pallas_call(mix_back_kernel, out_shape=(part,) * 4 + (sds((ROWS, D), B...  33.8 us
    pallas_call x2, Pallas kernels, wide_back_last(): pl.pallas_call(wide_back_last_kernel, grid=(2,), in_specs=[SMEM_SPEC, ful...  31.3 us
    pallas_call x2, Pallas kernels, mix(): pl.pallas_call(mix_kernel, grid=(1,), out_shape=(sds((ROWS, 3 * D), BF),...  29.1 us
    pallas_call x2, Pallas kernels, wide_back_first(): pl.pallas_call(wide_back_first_kernel, grid=(2,), in_specs=[SMEM_SPEC, fu...  28.7 us
    pallas_call x2, Pallas kernels, up(): pl.pallas_call(up_kernel, grid=(STEPS,), out_shape=(out, out), in_specs=[...  22.1 us
  transfers between devices with their start and end apart: 117, of which 34 were waited for; matrix products, arithmetic and copies ran while one was open for 9% of the time, Pallas kernels for 34%

profile of v6, /device:TPU:0, one launch (start us, length us, event | category | flops | bytes accessed | tf_op | source)
XLA Modules:
  0.0 565.5 jit_solution(2762074615683227979)
XLA Ops:
  8.7 4.1 collective-permute-start
  17.9 5.3 collective-permute-start.1
  23.2 4.2 collective-permute-done.2
  28.9 3.5 collective-permute-start.8
  32.5 1.6 collective-permute-start.3
  39.7 9.4 %collective-permute-done.9 = bf16[2,2,80,640]{3,2,1,0:T(8,128)(2,1)} collective-permute-done((bf16[2,2,80,640]{3,2,1,0:T(8,128)(2,1)S(1)}, bf16[2,2,80,640]{3,2,1,0:T(8,128)(2,1)}, u32[]{:S(2)}, u32[]{:S(2)}) %collective-permute-start.9) | collective-permute-done | bytes 409632 | tf_op jit(solution)/shard_map/u0_near/ppermute | solution.py:1065
  52.0 1.6 maximum_select_fusion.4
  53.6 1.6 collective-permute-start.12
  55.2 4.7 collective-permute-done.7.refs_5_
  64.7 14.3 %shard_map.253 = (bf16[512,1920]{1,0:T(8,128)(2,1)}, f32[20,1,512]{2,1,0:T(1,128)}, bf16[512,640]{1,0:T(8,128)(2,1)}, f32[512,640]{1,0:T(8,128)}, bf16[512,640]{1,0:T(8,128)(2,1)}) custom-call(s32[3]{0:T(128)} %pad_add_fusion.place_ref.refs_0_, s32[4]{0:T(128)} %lengths_ref.7, bf16[512,640]{1,0:T(8,128)(2,1)} %residual_ref.2, ...), custom_call_target="tpu_custom_call" | custom-call | flops 400000000 | bytes 2097152 | tf_op jit(solution)/shard_map/pallas_call | solution.py:210
  79.7 1.7 maximum_select_fusion
  82.5 1.6 collective-permute-start.23
  84.1 14.4 %collective-permute-done.18 = bf16[3,80,640]{2,1,0:T(8,128)(2,1)S(1)} collective-permute-done((bf16[3,80,640]{2,1,0:T(8,128)(2,1)S(1)}, bf16[3,80,640]{2,1,0:T(8,128)(2,1)S(1)}, u32[]{:S(2)}, u32[]{:S(2)}) %collective-permute-start.18) | collective-permute-done | bytes 307232 | tf_op jit(solution)/shard_map/j1_far/ppermute | solution.py:1065
  100.8 14.9 %collective-permute-done.21 = bf16[2,3,80,640]{3,2,1,0:T(8,128)(2,1)S(1)} collective-permute-done((bf16[2,3,80,640]{3,2,1,0:T(8,128)(2,1)S(1)}, bf16[2,3,80,640]{3,2,1,0:T(8,128)(2,1)S(1)}, u32[]{:S(2)}, u32[]{:S(2)}) %collective-permute-start.21) | collective-permute-done | bytes 614432 | tf_op jit(solution)/shard_map/j1_near/ppermute | solution.py:1065
  116.7 4.0 collective-permute-done.22.refs_2_.refs_6_
  124.8 11.1 %shard_map.254 = (bf16[4,512,1280]{2,1,0:T(8,128)(2,1)}, bf16[4,512,1280]{2,1,0:T(8,128)(2,1)}) custom-call(s32[3]{0:T(128)} %pad_add_fusion.place_ref.refs_0_, bf16[512,640]{1,0:T(8,128)(2,1)} %get-tuple-element.402.second_ref, bf16[4,2,80,640]{3,2,1,0:T(8,128)(2,1)} %bitcast.169, bf16[4,2,80,640]{3,2,1,0:T(8,128)(2,1)} %collective-permute-done.12.refs_1_, ...), custom_call_target="tpu_custom_call" | custom-call | flops 400000000 | bytes 2097152 | tf_op jit(solution)/shard_map/pallas_call | solution.py:278
  135.9 2.7 collective-permute-start.33
  138.7 2.5 collective-permute-start.31
  141.2 10.4 %shard_map.255.residual_ref = f32[512,640]{1,0:T(8,128)} custom-call(s32[3]{0:T(128)} %pad_add_fusion.place_ref.refs_0_, f32[512,640]{1,0:T(8,128)} %get-tuple-element.414.middle_ref.refs_14_, bf16[4,512,1280]{2,1,0:T(8,128)(2,1)} %get-tuple-element.415.active_ref, bf16[2,320,640]{2,1,0:T(8,128)(2,1)} %get-tuple-element.416.refs_0_.refs_4_, ...), custom_call_target="tpu_custom_call" | custom-call | flops 400000000 | bytes 2097152 | tf_op jit(solution)/shard_map/pallas_call | solution.py:320
  151.6 5.7 %collective-permute-done.33 = bf16[1,320,640]{2,1,0:T(8,128)(2,1)} collective-permute-done((bf16[1,320,640]{2,1,0:T(8,128)(2,1)S(1)}, bf16[1,320,640]{2,1,0:T(8,128)(2,1)}, u32[]{:S(2)}, u32[]{:S(2)}) %collective-permute-start.33) | collective-permute-done | bytes 409632 | tf_op jit(solution)/shard_map/d1_far/ppermute | solution.py:1065
  158.7 2.5 collective-permute-start.32
  161.7 7.4 %collective-permute-done.31.refs_4_.refs_2_ = bf16[4,3,80,640]{3,2,1,0:T(8,128)(2,1)} collective-permute-done((bf16[4,3,80,640]{3,2,1,0:T(8,128)(2,1)S(1)}, bf16[4,3,80,640]{3,2,1,0:T(8,128)(2,1)}, u32[]{:S(2)}, u32[]{:S(2)}) %collective-permute-start.31) | collective-permute-done | bytes 1228832 | tf_op jit(solution)/shard_map/j1_x/ppermute | solution.py:1016
  169.1 9.0 %collective-permute-done.34 = bf16[2,1,320,640]{3,2,0,1:T(8,128)(2,1)S(1)} collective-permute-done((bf16[2,1,320,640]{3,2,0,1:T(8,128)(2,1)S(1)}, bf16[2,1,320,640]{3,2,0,1:T(8,128)(2,1)S(1)}, u32[]{:S(2)}, u32[]{:S(2)}) %collective-permute-start.34) | collective-permute-done | bytes 819232 | tf_op jit(solution)/shard_map/d1_near/ppermute | solution.py:1065
  179.4 15.2 %collective-permute-done.32.refs_5_.refs_3_ = bf16[4,3,80,640]{3,2,1,0:T(8,128)(2,1)} collective-permute-done((bf16[4,3,80,640]{3,2,1,0:T(8,128)(2,1)S(1)}, bf16[4,3,80,640]{3,2,1,0:T(8,128)(2,1)}, u32[]{:S(2)}, u32[]{:S(2)}) %collective-permute-start.32) | collective-permute-done | bytes 1228832 | tf_op jit(solution)/shard_map/j1_yx/ppermute | solution.py:1016
  199.4 14.8 %shard_map.256 = (bf16[512,1920]{1,0:T(8,128)(2,1)}, f32[20,1,512]{2,1,0:T(1,128)}, bf16[512,640]{1,0:T(8,128)(2,1)}, f32[512,640]{1,0:T(8,128)}, bf16[512,640]{1,0:T(8,128)(2,1)}) custom-call(s32[3]{0:T(128)} %pad_add_fusion.place_ref.refs_0_, s32[4]{0:T(128)} %lengths_ref.7, f32[512,640]{1,0:T(8,128)} %shard_map.255.residual_ref, ...), custom_call_target="tpu_custom_call" | custom-call | flops 400000000 | bytes 2097152 | tf_op jit(solution)/shard_map/pallas_call | solution.py:210
  214.3 11.0 %shard_map.257 = (bf16[4,512,1280]{2,1,0:T(8,128)(2,1)}, bf16[4,512,1280]{2,1,0:T(8,128)(2,1)}) custom-call(s32[3]{0:T(128)} %pad_add_fusion.place_ref.refs_0_, bf16[512,640]{1,0:T(8,128)(2,1)} %get-tuple-element.445.second_ref, bf16[4,3,80,640]{3,2,1,0:T(8,128)(2,1)} %bitcast.163, bf16[4,3,80,640]{3,2,1,0:T(8,128)(2,1)} %copy-done.1, ...), custom_call_target="tpu_custom_call" | custom-call | flops 400000000 | bytes 2097152 | tf_op jit(solution)/shard_map/pallas_call | solution.py:278
  226.0 6.9 %collective-permute-done.37.refs_2_.refs_6_ = bf16[2,320,640]{2,1,0:T(8,128)(2,1)S(1)} collective-permute-done((bf16[2,320,640]{2,1,0:T(8,128)(2,1)}, bf16[2,320,640]{2,1,0:T(8,128)(2,1)S(1)}, u32[]{:S(2)}, u32[]{:S(2)}) %collective-permute-start.37) | collective-permute-done | bytes 819232 | tf_op jit(solution)/shard_map/d1_y/ppermute | solution.py:1016
  236.7 10.4 %shard_map.258.residual_ref = f32[512,640]{1,0:T(8,128)} custom-call(s32[3]{0:T(128)} %pad_add_fusion.place_ref.refs_0_, f32[512,640]{1,0:T(8,128)} %get-tuple-element.457.middle_ref.refs_14_, bf16[4,512,1280]{2,1,0:T(8,128)(2,1)} %get-tuple-element.458.active_ref, bf16[2,320,640]{2,1,0:T(8,128)(2,1)} %get-tuple-element.459.refs_0_.refs_4_, ...), custom_call_target="tpu_custom_call" | custom-call | flops 400000000 | bytes 2097152 | tf_op jit(solution)/shard_map/pallas_call | solution.py:320
  248.8 6.7 %shard_map.259 = (bf16[512,640]{1,0:T(8,128)(2,1)}, f32[512,640]{1,0:T(8,128)}, bf16[512,640]{1,0:T(8,128)(2,1)}, f32[40,640]{1,0:T(8,128)}) custom-call(f32[512,640]{1,0:T(8,128)} %shard_map.258.residual_ref, s32[512,1]{1,0:T(8,128)} %copy.70.targets_ref, s32[512,1]{1,0:T(8,128)} %copy.71.masked_ref, bf16[640,128]{1,0:T(8,128)(2,1)} %pad.8.weight_ref, ...), custom_call_target="tpu_custom_call" | custom-call | flops 400000000 | bytes 2097152 | tf_op jit(solution)/shard_map/pallas_call | solution.py:397
  255.5 8.2 %shard_map.260 = (bf16[320,640]{1,0:T(8,128)(2,1)}, bf16[320,640]{1,0:T(8,128)(2,1)}, bf16[320,640]{1,0:T(8,128)(2,1)}, bf16[320,640]{1,0:T(8,128)(2,1)}, bf16[3...) custom-call(s32[3]{0:T(128)} %pad_add_fusion.place_ref.refs_0_, ...), custom_call_target="tpu_custom_call" | custom-call | flops 400000000 | bytes 2097152 | tf_op jit(solution)/shard_map/pallas_call | solution.py:449
  264.8 14.4 %shard_map.261 = (bf16[4,80,640]{2,1,0:T(8,128)(2,1)}, bf16[4,80,640]{2,1,0:T(8,128)(2,1)}, bf16[4,80,640]{2,1,0:T(8,128)(2,1)}, bf16[4,80,640]{2,1,0:T(8,128)(2...) custom-call(s32[3]{0:T(128)} %pad_add_fusion.place_ref.refs_0_, ...), custom_call_target="tpu_custom_call" | custom-call | flops 400000000 | bytes 2097152 | tf_op jit(solution)/shard_map/pallas_call | solution.py:604
  281.2 2.9 shard_map.262
  288.6 15.7 %shard_map.263 = (bf16[2,4,2,80,640]{4,3,2,1,0:T(8,128)(2,1)}, bf16[2,4,2,80,640]{4,3,2,1,0:T(8,128)(2,1)}, f32[2,1280]{1,0:T(2,128)}, f32[512,640]{1,0:T(8,128)...) custom-call(s32[3]{0:T(128)} %pad_add_fusion.place_ref.refs_0_, bf16[512,640]{1,0:T(8,128)(2,1)} %get-tuple-element.502.grad_ref.rounded_ref, ...), custom_call_target="tpu_custom_call" | custom-call | flops 400000000 | bytes 2097152 | tf_op jit(solution)/shard_map/pallas_call | solution.py:710
  304.3 17.0 %shard_map.264 = (bf16[4,80,640]{2,1,0:T(8,128)(2,1)}, bf16[4,80,640]{2,1,0:T(8,128)(2,1)}, bf16[4,80,640]{2,1,0:T(8,128)(2,1)}, bf16[4,80,640]{2,1,0:T(8,128)(2...) custom-call(s32[3]{0:T(128)} %pad_add_fusion.place_ref.refs_0_, ...), custom_call_target="tpu_custom_call" | custom-call | flops 400000000 | bytes 2097152 | tf_op jit(solution)/shard_map/pallas_call | solution.py:862
  325.7 1.7 collective-permute-start.77
  327.5 8.2 %shard_map.265 = (bf16[320,640]{1,0:T(8,128)(2,1)}, bf16[320,640]{1,0:T(8,128)(2,1)}, bf16[320,640]{1,0:T(8,128)(2,1)}, bf16[320,640]{1,0:T(8,128)(2,1)}, bf16[3...) custom-call(s32[3]{0:T(128)} %pad_add_fusion.place_ref.refs_0_, ...), custom_call_target="tpu_custom_call" | custom-call | flops 400000000 | bytes 2097152 | tf_op jit(solution)/shard_map/pallas_call | solution.py:449
  335.7 4.6 shard_map.266
  341.6 3.4 shard_map.267
  350.2 2.9 shard_map.268
  353.1 1.6 collective-permute-start.78
  354.7 14.3 %shard_map.269 = (bf16[4,80,640]{2,1,0:T(8,128)(2,1)}, bf16[4,80,640]{2,1,0:T(8,128)(2,1)}, bf16[4,80,640]{2,1,0:T(8,128)(2,1)}, bf16[4,80,640]{2,1,0:T(8,128)(2...) custom-call(s32[3]{0:T(128)} %pad_add_fusion.place_ref.refs_0_, ...), custom_call_target="tpu_custom_call" | custom-call | flops 400000000 | bytes 2097152 | tf_op jit(solution)/shard_map/pallas_call | solution.py:604
  369.7 12.0 %collective-permute-done.76 = bf16[2,4,80,640]{3,2,1,0:T(8,128)(2,1)} collective-permute-done((bf16[2,4,80,640]{3,2,1,0:T(8,128)(2,1)}, bf16[2,4,80,640]{3,2,1,0:T(8,128)(2,1)}, u32[]{:S(2)}, u32[]{:S(2)}) %collective-permute-start.76) | collective-permute-done | bytes 819232 | tf_op jit(solution)/shard_map/a1_x/ppermute | solution.py:1016
  382.7 1.6 collective-permute-done.70.refs_18_
  388.0 1.9 fusion.5
  391.2 15.6 %shard_map.270 = (bf16[2,4,2,80,640]{4,3,2,1,0:T(8,128)(2,1)}, bf16[2,4,2,80,640]{4,3,2,1,0:T(8,128)(2,1)}, f32[2,1280]{1,0:T(2,128)}, f32[512,640]{1,0:T(8,128)...) custom-call(s32[3]{0:T(128)} %pad_add_fusion.place_ref.refs_0_, bf16[512,640]{1,0:T(8,128)(2,1)} %get-tuple-element.575.grad_ref.rounded_ref, ...), custom_call_target="tpu_custom_call" | custom-call | flops 400000000 | bytes 2097152 | tf_op jit(solution)/shard_map/pallas_call | solution.py:710
  406.8 1.8 collective-permute-start.83
  408.6 3.4 shard_map.271
  412.0 16.8 %shard_map.272 = (bf16[4,80,640]{2,1,0:T(8,128)(2,1)}, bf16[4,80,640]{2,1,0:T(8,128)(2,1)}, bf16[4,80,640]{2,1,0:T(8,128)(2,1)}, bf16[4,80,640]{2,1,0:T(8,128)(2...) custom-call(s32[3]{0:T(128)} %pad_add_fusion.place_ref.refs_0_, ...), custom_call_target="tpu_custom_call" | custom-call | flops 400000000 | bytes 2097152 | tf_op jit(solution)/shard_map/pallas_call | solution.py:862
  435.0 4.8 shard_map.273
  440.7 5.1 collective-permute-done.83
  445.9 2.2 fusion.2
  450.6 31.3 %collective-permute-done.94 = bf16[2,3,80,640]{3,2,1,0:T(8,128)(2,1)S(1)} collective-permute-done((bf16[2,3,80,640]{3,2,1,0:T(8,128)(2,1)}, bf16[2,3,80,640]{3,2,1,0:T(8,128)(2,1)S(1)}, u32[]{:S(2)}, u32[]{:S(2)}) %collective-permute-start.94) | collective-permute-done | bytes 614432 | tf_op jit(solution)/shard_map/j1_near/ppermute | solution.py:1065
  483.9 1.9 fusion.6
  485.7 1.6 collective-permute-start.95
  487.3 2.6 fusion
  489.9 8.4 %collective-permute-done.97 = bf16[3,80,640]{2,1,0:T(8,128)(2,1)S(1)} collective-permute-done((bf16[3,80,640]{2,1,0:T(8,128)(2,1)}, bf16[3,80,640]{2,1,0:T(8,128)(2,1)S(1)}, u32[]{:S(2)}, u32[]{:S(2)}) %collective-permute-start.97) | collective-permute-done | bytes 307232 | tf_op jit(solution)/shard_map/j1_far/ppermute | solution.py:1065
  501.2 2.0 collective-permute-start.99
  504.9 10.2 %collective-permute-done.99 = f32[88,640]{1,0:T(8,128)S(1)} collective-permute-done((f32[88,640]{1,0:T(8,128)S(1)}, f32[88,640]{1,0:T(8,128)S(1)}, u32[]{:S(2)}, u32[]{:S(2)}) %collective-permute-start.99) | collective-permute-done | bytes 225312 | tf_op jit(solution)/shard_map/small_x/ppermute | solution.py:1016
  515.1 1.6 collective-permute-start.101
  516.9 6.2 %collective-permute-done.101 = f32[88,640]{1,0:T(8,128)S(1)} collective-permute-done((f32[88,640]{1,0:T(8,128)S(1)}, f32[88,640]{1,0:T(8,128)S(1)}, u32[]{:S(2)}, u32[]{:S(2)}) %collective-permute-start.101) | collective-permute-done | bytes 225312 | tf_op jit(solution)/shard_map/small_y/ppermute | solution.py:1016
  525.7 3.9 collective-permute-done.100
  530.7 5.8 %collective-permute-done.112.refs_7_ = bf16[320,640]{1,0:T(8,128)(2,1)S(1)} collective-permute-done((bf16[320,640]{1,0:T(8,128)(2,1)}, bf16[320,640]{1,0:T(8,128)(2,1)S(1)}, u32[]{:S(2)}, u32[]{:S(2)}) %collective-permute-start.112) | collective-permute-done | bytes 409632 | tf_op jit(solution)/shard_map/d0_x/ppermute | solution.py:1016
  542.9 4.6 shard_map.274
  550.5 4.6 shard_map.275
  (477 shorter events, 94.8 us)
Async XLA Ops:
  7.2 497.6 %reduce-scatter.6.cloned.1.call-start = ((), (), s32[]{:S(2)}) async-start(), calls=%async_computation.4 | async-start | bytes 2048000 | tf_op jit(solution)/shard_map/reduce_scatter | solution.py:1116
  28.8 20.3 %collective-permute-start.9 = (bf16[2,2,80,640]{3,2,1,0:T(8,128)(2,1)S(1)}, bf16[2,2,80,640]{3,2,1,0:T(8,128)(2,1)}, u32[]{:S(2)}, u32[]{:S(2)}) collective-permute-start(bf16[2,2,80,640]{3,2,1,0:T(8,128)(2,1)S(1)} %maximum_select_fusion.7), channel_id=1, source_target_pairs={{0,8},{8,0},{16,24},{24,16},{1,9},{9,1},{17,25},{25,17},{2,10},{10... | collective-permute-start | bytes 1228808 | tf_op jit(solution)/shard_map/u0_near/ppermute | solution.py:1065
  28.9 23.1 %collective-permute-start.8 = (bf16[1,320,640]{2,1,0:T(8,128)(2,1)S(1)}, bf16[1,320,640]{2,1,0:T(8,128)(2,1)}, u32[]{:S(2)}, u32[]{:S(2)}) collective-permute-start(bf16[1,320,640]{2,1,0:T(8,128)(2,1)S(1)} %reshape.541), channel_id=1, source_target_pairs={{0,16},{8,24},{16,0},{24,8},{1,17},{9,25},{17,1},{25,9},{2,18},{10... | collective-permute-start | bytes 1228808 | tf_op jit(solution)/shard_map/d0_far/ppermute | solution.py:1065
  32.5 16.6 %collective-permute-start.3 = (bf16[4,1,80,640]{3,2,1,0:T(8,128)(2,1)S(1)}, bf16[4,1,80,640]{3,2,1,0:T(8,128)(2,1)}, u32[]{:S(2)}, u32[]{:S(2)}) collective-permute-start(bf16[4,1,80,640]{3,2,1,0:T(8,128)(2,1)S(1)} %bitcast.171), channel_id=1, source_target_pairs={{0,4},{4,0},{1,5},{5,1},{2,6},{6,2},{3,7},{7,3},{8,12},{12,8},{9,1... | collective-permute-start | bytes 1228808 | tf_op jit(solution)/shard_map/a0_y/ppermute | solution.py:1016
  34.1 21.1 %collective-permute-start.6 = (bf16[4,1,80,640]{3,2,1,0:T(8,128)(2,1)S(1)}, bf16[4,1,80,640]{3,2,1,0:T(8,128)(2,1)}, u32[]{:S(2)}, u32[]{:S(2)}) collective-permute-start(bf16[4,1,80,640]{3,2,1,0:T(8,128)(2,1)S(1)} %bitcast.172), channel_id=1, source_target_pairs={{0,2},{2,0},{1,3},{3,1},{4,6},{6,4},{5,7},{7,5},{8,10},{10,8},{9,1... | collective-permute-start | bytes 1228808 | tf_op jit(solution)/shard_map/a0_x/ppermute | solution.py:1016
  35.6 24.3 %collective-permute-start.4 = (bf16[4,1,80,640]{3,2,1,0:T(8,128)(2,1)S(1)}, bf16[4,1,80,640]{3,2,1,0:T(8,128)(2,1)}, u32[]{:S(2)}, u32[]{:S(2)}) collective-permute-start(bf16[4,1,80,640]{3,2,1,0:T(8,128)(2,1)S(1)} %bitcast.173), channel_id=1, source_target_pairs={{0,1},{1,0},{2,3},{3,2},{4,5},{5,4},{6,7},{7,6},{8,9},{9,8},{10,11... | collective-permute-start | bytes 1228808 | tf_op jit(solution)/shard_map/a0_c/ppermute | solution.py:1016
  53.6 25.5 %collective-permute-start.16 = (bf16[2,1,320,640]{3,2,0,1:T(8,128)(2,1)S(1)}, bf16[2,1,320,640]{3,2,0,1:T(8,128)(2,1)}, u32[]{:S(2)}, u32[]{:S(2)}) collective-permute-start(bf16[2,1,320,640]{3,2,0,1:T(8,128)(2,1)S(1)} %maximum_select_fusion.4), channel_id=1, source_target_pairs={{0,8},{8,0},{16,24},{24,16},{1,9},{9,1},{17,25},{25,17},{2,10},{10... | collective-permute-start | bytes 2457608 | tf_op jit(solution)/shard_map/d0_near/ppermute | solution.py:1065
  53.6 25.4 %collective-permute-start.12 = (bf16[4,2,80,640]{3,2,1,0:T(8,128)(2,1)S(1)}, bf16[4,2,80,640]{3,2,1,0:T(8,128)(2,1)}, u32[]{:S(2)}, u32[]{:S(2)}) collective-permute-start(bf16[4,2,80,640]{3,2,1,0:T(8,128)(2,1)S(1)} %bitcast.166), channel_id=1, source_target_pairs={{0,4},{4,0},{1,5},{5,1},{2,6},{6,2},{3,7},{7,3},{8,12},{12,8},{9,1... | collective-permute-start | bytes 2457608 | tf_op jit(solution)/shard_map/u0_y/ppermute | solution.py:1016
  61.1 21.3 %collective-permute-start.15 = (bf16[4,2,80,640]{3,2,1,0:T(8,128)(2,1)S(1)}, bf16[4,2,80,640]{3,2,1,0:T(8,128)(2,1)}, u32[]{:S(2)}, u32[]{:S(2)}) collective-permute-start(bf16[4,2,80,640]{3,2,1,0:T(8,128)(2,1)S(1)} %bitcast.167), channel_id=1, source_target_pairs={{0,2},{2,0},{1,3},{3,1},{4,6},{6,4},{5,7},{7,5},{8,10},{10,8},{9,1... | collective-permute-start | bytes 2457608 | tf_op jit(solution)/shard_map/u0_x/ppermute | solution.py:1016
  63.8 36.4 %collective-permute-start.13 = (bf16[4,2,80,640]{3,2,1,0:T(8,128)(2,1)S(1)}, bf16[4,2,80,640]{3,2,1,0:T(8,128)(2,1)}, u32[]{:S(2)}, u32[]{:S(2)}) collective-permute-start(bf16[4,2,80,640]{3,2,1,0:T(8,128)(2,1)S(1)} %bitcast.168), channel_id=1, source_target_pairs={{0,1},{1,0},{2,3},{3,2},{4,5},{5,4},{6,7},{7,6},{8,9},{9,8},{10,11... | collective-permute-start | bytes 2457608 | tf_op jit(solution)/shard_map/u0_c/ppermute | solution.py:1016
  79.0 21.1 %collective-permute-start.17 = (bf16[4,2,80,640]{3,2,1,0:T(8,128)(2,1)}, bf16[4,2,80,640]{3,2,1,0:T(8,128)(2,1)S(1)}, u32[]{:S(2)}, u32[]{:S(2)}) collective-permute-start(bf16[4,2,80,640]{3,2,1,0:T(8,128)(2,1)} %collective-permute-done.12.refs_1_), channel_id=1, source_target_pairs={{0,2},{2,0},{1,3},{3,1},{4,6},{6,4},{5,7},{7,5},{8,10},{10,8},{9,1... | collective-permute-start | bytes 2457608 | tf_op jit(solution)/shard_map/u0_yx/ppermute | solution.py:1016
  82.4 17.9 %collective-permute-start.19 = (bf16[4,2,80,640]{3,2,1,0:T(8,128)(2,1)}, bf16[4,2,80,640]{3,2,1,0:T(8,128)(2,1)S(1)}, u32[]{:S(2)}, u32[]{:S(2)}) collective-permute-start(bf16[4,2,80,640]{3,2,1,0:T(8,128)(2,1)} %collective-permute-done.15.refs_4_.refs_2_), channel_id=1, source_target_pairs={{0,1},{1,0},{2,3},{3,2},{4,5},{5,4},{6,7},{7,6},{8,9},{9,8},{10,11... | collective-permute-start | bytes 2457608 | tf_op jit(solution)/shard_map/u0_xc/ppermute | solution.py:1016
  82.5 16.0 %collective-permute-start.18 = (bf16[3,80,640]{2,1,0:T(8,128)(2,1)S(1)}, bf16[3,80,640]{2,1,0:T(8,128)(2,1)S(1)}, u32[]{:S(2)}, u32[]{:S(2)}) collective-permute-start(bf16[3,80,640]{2,1,0:T(8,128)(2,1)S(1)} %copy-done.29), channel_id=1, source_target_pairs={{0,16},{8,24},{16,0},{24,8},{1,17},{9,25},{17,1},{25,9},{2,18},{10... | collective-permute-start | bytes 921608 | tf_op jit(solution)/shard_map/j1_far/ppermute | solution.py:1065
  82.5 33.3 %collective-permute-start.23 = (bf16[2,320,640]{2,1,0:T(8,128)(2,1)S(1)}, bf16[2,320,640]{2,1,0:T(8,128)(2,1)}, u32[]{:S(2)}, u32[]{:S(2)}) collective-permute-start(bf16[2,320,640]{2,1,0:T(8,128)(2,1)S(1)} %get-tuple-element.417.refs_1_.refs_5_), channel_id=1, source_target_pairs={{0,4},{4,0},{1,5},{5,1},{2,6},{6,2},{3,7},{7,3},{8,12},{12,8},{9,1... | collective-permute-start | bytes 2457608 | tf_op jit(solution)/shard_map/d0_y/ppermute | solution.py:1016
  98.5 22.3 %collective-permute-start.22 = (bf16[2,320,640]{2,1,0:T(8,128)(2,1)}, bf16[2,320,640]{2,1,0:T(8,128)(2,1)}, u32[]{:S(2)}, u32[]{:S(2)}) collective-permute-start(bf16[2,320,640]{2,1,0:T(8,128)(2,1)} %get-tuple-element.416.refs_0_.refs_4_), channel_id=1, source_target_pairs={{0,4},{4,0},{1,5},{5,1},{2,6},{6,2},{3,7},{7,3},{8,12},{12,8},{9,1... | collective-permute-start | bytes 2457608 | tf_op jit(solution)/shard_map/d0_y/ppermute | solution.py:1016
  100.1 15.6 %collective-permute-start.21 = (bf16[2,3,80,640]{3,2,1,0:T(8,128)(2,1)S(1)}, bf16[2,3,80,640]{3,2,1,0:T(8,128)(2,1)S(1)}, u32[]{:S(2)}, u32[]{:S(2)}) collective-permute-start(bf16[2,3,80,640]{3,2,1,0:T(8,128)(2,1)S(1)} %maximum_select_fusion.6), channel_id=1, source_target_pairs={{0,8},{8,0},{16,24},{24,16},{1,9},{9,1},{17,25},{25,17},{2,10},{10... | collective-permute-start | bytes 1843208 | tf_op jit(solution)/shard_map/j1_near/ppermute | solution.py:1065
  100.2 22.0 %collective-permute-start.14 = (bf16[4,2,80,640]{3,2,1,0:T(8,128)(2,1)}, bf16[4,2,80,640]{3,2,1,0:T(8,128)(2,1)S(1)}, u32[]{:S(2)}, u32[]{:S(2)}) collective-permute-start(bf16[4,2,80,640]{3,2,1,0:T(8,128)(2,1)} %collective-permute-done.12.refs_1_), channel_id=1, source_target_pairs={{0,1},{1,0},{2,3},{3,2},{4,5},{5,4},{6,7},{7,6},{8,9},{9,8},{10,11... | collective-permute-start | bytes 2457608 | tf_op jit(solution)/shard_map/u0_yc/ppermute | solution.py:1016
  100.3 21.9 %collective-permute-start.20 = (bf16[4,2,80,640]{3,2,1,0:T(8,128)(2,1)S(1)}, bf16[4,2,80,640]{3,2,1,0:T(8,128)(2,1)S(1)}, u32[]{:S(2)}, u32[]{:S(2)}) collective-permute-start(bf16[4,2,80,640]{3,2,1,0:T(8,128)(2,1)S(1)} %collective-permute-done.17.refs_5_.refs_3_), channel_id=1, source_target_pairs={{0,1},{1,0},{2,3},{3,2},{4,5},{5,4},{6,7},{7,6},{8,9},{9,8},{10,11... | collective-permute-start | bytes 2457608 | tf_op jit(solution)/shard_map/u0_yxc/ppermute | solution.py:1016
  115.7 20.2 %collective-permute-start.24 = (bf16[2,320,640]{2,1,0:T(8,128)(2,1)}, bf16[2,320,640]{2,1,0:T(8,128)(2,1)}, u32[]{:S(2)}, u32[]{:S(2)}) collective-permute-start(bf16[2,320,640]{2,1,0:T(8,128)(2,1)} %get-tuple-element.416.refs_0_.refs_4_), channel_id=1, source_target_pairs={{0,1},{1,0},{2,3},{3,2},{4,5},{5,4},{6,7},{7,6},{8,9},{9,8},{10,11... | collective-permute-start | bytes 2457608 | tf_op jit(solution)/shard_map/d0_c/ppermute | solution.py:1016
  115.7 22.9 %collective-permute-start.25 = (bf16[2,320,640]{2,1,0:T(8,128)(2,1)S(1)}, bf16[2,320,640]{2,1,0:T(8,128)(2,1)}, u32[]{:S(2)}, u32[]{:S(2)}) collective-permute-start(bf16[2,320,640]{2,1,0:T(8,128)(2,1)S(1)} %get-tuple-element.417.refs_1_.refs_5_), channel_id=1, source_target_pairs={{0,1},{1,0},{2,3},{3,2},{4,5},{5,4},{6,7},{7,6},{8,9},{9,8},{10,11... | collective-permute-start | bytes 2457608 | tf_op jit(solution)/shard_map/d0_c/ppermute | solution.py:1016
  120.7 37.9 %collective-permute-start.28 = (bf16[4,3,80,640]{3,2,1,0:T(8,128)(2,1)S(1)}, bf16[4,3,80,640]{3,2,1,0:T(8,128)(2,1)S(1)}, u32[]{:S(2)}, u32[]{:S(2)}) collective-permute-start(bf16[4,3,80,640]{3,2,1,0:T(8,128)(2,1)S(1)} %bitcast.159), channel_id=1, source_target_pairs={{0,4},{4,0},{1,5},{5,1},{2,6},{6,2},{3,7},{7,3},{8,12},{12,8},{9,1... | collective-permute-start | bytes 3686408 | tf_op jit(solution)/shard_map/j1_y/ppermute | solution.py:1016
  122.2 18.9 %collective-permute-start.26 = (bf16[2,320,640]{2,1,0:T(8,128)(2,1)}, bf16[2,320,640]{2,1,0:T(8,128)(2,1)}, u32[]{:S(2)}, u32[]{:S(2)}) collective-permute-start(bf16[2,320,640]{2,1,0:T(8,128)(2,1)} %collective-permute-done.22.refs_2_.refs_6_), channel_id=1, source_target_pairs={{0,1},{1,0},{2,3},{3,2},{4,5},{5,4},{6,7},{7,6},{8,9},{9,8},{10,11... | collective-permute-start | bytes 2457608 | tf_op jit(solution)/shard_map/d0_yc/ppermute | solution.py:1016
  123.1 18.0 %collective-permute-start.27 = (bf16[2,320,640]{2,1,0:T(8,128)(2,1)}, bf16[2,320,640]{2,1,0:T(8,128)(2,1)}, u32[]{:S(2)}, u32[]{:S(2)}) collective-permute-start(bf16[2,320,640]{2,1,0:T(8,128)(2,1)} %collective-permute-done.23.refs_3_.refs_7_), channel_id=1, source_target_pairs={{0,1},{1,0},{2,3},{3,2},{4,5},{5,4},{6,7},{7,6},{8,9},{9,8},{10,11... | collective-permute-start | bytes 2457608 | tf_op jit(solution)/shard_map/d0_yc/ppermute | solution.py:1016
  135.9 21.4 %collective-permute-start.33 = (bf16[1,320,640]{2,1,0:T(8,128)(2,1)S(1)}, bf16[1,320,640]{2,1,0:T(8,128)(2,1)}, u32[]{:S(2)}, u32[]{:S(2)}) collective-permute-start(bf16[1,320,640]{2,1,0:T(8,128)(2,1)S(1)} %copy-done.16), channel_id=1, source_target_pairs={{0,16},{8,24},{16,0},{24,8},{1,17},{9,25},{17,1},{25,9},{2,18},{10... | collective-permute-start | bytes 1228808 | tf_op jit(solution)/shard_map/d1_far/ppermute | solution.py:1065
  138.7 30.4 %collective-permute-start.31 = (bf16[4,3,80,640]{3,2,1,0:T(8,128)(2,1)S(1)}, bf16[4,3,80,640]{3,2,1,0:T(8,128)(2,1)}, u32[]{:S(2)}, u32[]{:S(2)}) collective-permute-start(bf16[4,3,80,640]{3,2,1,0:T(8,128)(2,1)S(1)} %bitcast.160), channel_id=1, source_target_pairs={{0,2},{2,0},{1,3},{3,1},{4,6},{6,4},{5,7},{7,5},{8,10},{10,8},{9,1... | collective-permute-start | bytes 3686408 | tf_op jit(solution)/shard_map/j1_x/ppermute | solution.py:1016
  158.6 19.5 %collective-permute-start.34 = (bf16[2,1,320,640]{3,2,0,1:T(8,128)(2,1)S(1)}, bf16[2,1,320,640]{3,2,0,1:T(8,128)(2,1)S(1)}, u32[]{:S(2)}, u32[]{:S(2)}) collective-permute-start(bf16[2,1,320,640]{3,2,0,1:T(8,128)(2,1)S(1)} %maximum_select_fusion.5), channel_id=1, source_target_pairs={{0,8},{8,0},{16,24},{24,16},{1,9},{9,1},{17,25},{25,17},{2,10},{10... | collective-permute-start | bytes 2457608 | tf_op jit(solution)/shard_map/d1_near/ppermute | solution.py:1065
  158.7 35.9 %collective-permute-start.32 = (bf16[4,3,80,640]{3,2,1,0:T(8,128)(2,1)S(1)}, bf16[4,3,80,640]{3,2,1,0:T(8,128)(2,1)}, u32[]{:S(2)}, u32[]{:S(2)}) collective-permute-start(bf16[4,3,80,640]{3,2,1,0:T(8,128)(2,1)S(1)} %collective-permute-done.28.refs_1_), channel_id=1, source_target_pairs={{0,2},{2,0},{1,3},{3,1},{4,6},{6,4},{5,7},{7,5},{8,10},{10,8},{9,1... | collective-permute-start | bytes 3686408 | tf_op jit(solution)/shard_map/j1_yx/ppermute | solution.py:1016
  161.2 33.9 %collective-permute-start.29 = (bf16[4,3,80,640]{3,2,1,0:T(8,128)(2,1)S(1)}, bf16[4,3,80,640]{3,2,1,0:T(8,128)(2,1)S(1)}, u32[]{:S(2)}, u32[]{:S(2)}) collective-permute-start(bf16[4,3,80,640]{3,2,1,0:T(8,128)(2,1)S(1)} %bitcast.161), channel_id=1, source_target_pairs={{0,1},{1,0},{2,3},{3,2},{4,5},{5,4},{6,7},{7,6},{8,9},{9,8},{10,11... | collective-permute-start | bytes 3686408 | tf_op jit(solution)/shard_map/j1_c/ppermute | solution.py:1016
  161.2 37.7 %collective-permute-start.30 = (bf16[4,3,80,640]{3,2,1,0:T(8,128)(2,1)S(1)}, bf16[4,3,80,640]{3,2,1,0:T(8,128)(2,1)}, u32[]{:S(2)}, u32[]{:S(2)}) collective-permute-start(bf16[4,3,80,640]{3,2,1,0:T(8,128)(2,1)S(1)} %collective-permute-done.28.refs_1_), channel_id=1, source_target_pairs={{0,1},{1,0},{2,3},{3,2},{4,5},{5,4},{6,7},{7,6},{8,9},{9,8},{10,11... | collective-permute-start | bytes 3686408 | tf_op jit(solution)/shard_map/j1_yc/ppermute | solution.py:1016
  169.1 29.8 %collective-permute-start.35 = (bf16[4,3,80,640]{3,2,1,0:T(8,128)(2,1)}, bf16[4,3,80,640]{3,2,1,0:T(8,128)(2,1)}, u32[]{:S(2)}, u32[]{:S(2)}) collective-permute-start(bf16[4,3,80,640]{3,2,1,0:T(8,128)(2,1)} %collective-permute-done.31.refs_4_.refs_2_), channel_id=1, source_target_pairs={{0,1},{1,0},{2,3},{3,2},{4,5},{5,4},{6,7},{7,6},{8,9},{9,8},{10,11... | collective-permute-start | bytes 3686408 | tf_op jit(solution)/shard_map/j1_xc/ppermute | solution.py:1016
  194.6 30.7 %collective-permute-start.38 = (bf16[2,320,640]{2,1,0:T(8,128)(2,1)S(1)}, bf16[2,320,640]{2,1,0:T(8,128)(2,1)}, u32[]{:S(2)}, u32[]{:S(2)}) collective-permute-start(bf16[2,320,640]{2,1,0:T(8,128)(2,1)S(1)} %get-tuple-element.460.refs_1_.refs_5_), channel_id=1, source_target_pairs={{0,4},{4,0},{1,5},{5,1},{2,6},{6,2},{3,7},{7,3},{8,12},{12,8},{9,1... | collective-permute-start | bytes 2457608 | tf_op jit(solution)/shard_map/d1_y/ppermute | solution.py:1016
  196.2 36.7 %collective-permute-start.37 = (bf16[2,320,640]{2,1,0:T(8,128)(2,1)}, bf16[2,320,640]{2,1,0:T(8,128)(2,1)S(1)}, u32[]{:S(2)}, u32[]{:S(2)}) collective-permute-start(bf16[2,320,640]{2,1,0:T(8,128)(2,1)} %get-tuple-element.459.refs_0_.refs_4_), channel_id=1, source_target_pairs={{0,4},{4,0},{1,5},{5,1},{2,6},{6,2},{3,7},{7,3},{8,12},{12,8},{9,1... | collective-permute-start | bytes 2457608 | tf_op jit(solution)/shard_map/d1_y/ppermute | solution.py:1016
  198.9 36.6 %collective-permute-start.39 = (bf16[2,320,640]{2,1,0:T(8,128)(2,1)}, bf16[2,320,640]{2,1,0:T(8,128)(2,1)}, u32[]{:S(2)}, u32[]{:S(2)}) collective-permute-start(bf16[2,320,640]{2,1,0:T(8,128)(2,1)} %get-tuple-element.459.refs_0_.refs_4_), channel_id=1, source_target_pairs={{0,1},{1,0},{2,3},{3,2},{4,5},{5,4},{6,7},{7,6},{8,9},{9,8},{10,11... | collective-permute-start | bytes 2457608 | tf_op jit(solution)/shard_map/d1_c/ppermute | solution.py:1016
  198.9 36.6 %collective-permute-start.40 = (bf16[2,320,640]{2,1,0:T(8,128)(2,1)S(1)}, bf16[2,320,640]{2,1,0:T(8,128)(2,1)S(1)}, u32[]{:S(2)}, u32[]{:S(2)}) collective-permute-start(bf16[2,320,640]{2,1,0:T(8,128)(2,1)S(1)} %get-tuple-element.460.refs_1_.refs_5_), channel_id=1, source_target_pairs={{0,1},{1,0},{2,3},{3,2},{4,5},{5,4},{6,7},{7,6},{8,9},{9,8},{10,11... | collective-permute-start | bytes 2457608 | tf_op jit(solution)/shard_map/d1_c/ppermute | solution.py:1016
  263.7 16.0 %collective-permute-start.51 = (bf16[320,640]{1,0:T(8,128)(2,1)}, bf16[320,640]{1,0:T(8,128)(2,1)S(1)}, u32[]{:S(2)}, u32[]{:S(2)}) collective-permute-start(bf16[320,640]{1,0:T(8,128)(2,1)} %get-tuple-element.480), channel_id=1, source_target_pairs={{0,1},{1,0},{2,3},{3,2},{4,5},{5,4},{6,7},{7,6},{8,9},{9,8},{10,11... | collective-permute-start | bytes 1228808 | tf_op jit(solution)/shard_map/d1_c/ppermute | solution.py:1016
  264.2 15.6 %collective-permute-start.52 = (bf16[320,640]{1,0:T(8,128)(2,1)}, bf16[320,640]{1,0:T(8,128)(2,1)S(1)}, u32[]{:S(2)}, u32[]{:S(2)}) collective-permute-start(bf16[320,640]{1,0:T(8,128)(2,1)} %get-tuple-element.494), channel_id=1, source_target_pairs={{0,1},{1,0},{2,3},{3,2},{4,5},{5,4},{6,7},{7,6},{8,9},{9,8},{10,11... | collective-permute-start | bytes 1228808 | tf_op jit(solution)/shard_map/d1_c/ppermute | solution.py:1016
  264.3 15.9 %collective-permute-start.53 = (bf16[320,640]{1,0:T(8,128)(2,1)}, bf16[320,640]{1,0:T(8,128)(2,1)S(1)}, u32[]{:S(2)}, u32[]{:S(2)}) collective-permute-start(bf16[320,640]{1,0:T(8,128)(2,1)} %get-tuple-element.495), channel_id=1, source_target_pairs={{0,1},{1,0},{2,3},{3,2},{4,5},{5,4},{6,7},{7,6},{8,9},{9,8},{10,11... | collective-permute-start | bytes 1228808 | tf_op jit(solution)/shard_map/d1_c/ppermute | solution.py:1016
  264.8 15.6 %collective-permute-start.54 = (bf16[320,640]{1,0:T(8,128)(2,1)}, bf16[320,640]{1,0:T(8,128)(2,1)S(1)}, u32[]{:S(2)}, u32[]{:S(2)}) collective-permute-start(bf16[320,640]{1,0:T(8,128)(2,1)} %get-tuple-element.496), channel_id=1, source_target_pairs={{0,1},{1,0},{2,3},{3,2},{4,5},{5,4},{6,7},{7,6},{8,9},{9,8},{10,11... | collective-permute-start | bytes 1228808 | tf_op jit(solution)/shard_map/d1_c/ppermute | solution.py:1016
  284.0 56.3 %collective-permute-start.59 = (bf16[4,320,640]{2,1,0:T(8,128)(2,1)}, bf16[4,320,640]{2,1,0:T(8,128)(2,1)S(1)}, u32[]{:S(2)}, u32[]{:S(2)}) collective-permute-start(bf16[4,320,640]{2,1,0:T(8,128)(2,1)} %shard_map.262), channel_id=1, source_target_pairs={{0,4},{4,0},{1,5},{5,1},{2,6},{6,2},{3,7},{7,3},{8,12},{12,8},{9,1... | collective-permute-start | bytes 4915208 | tf_op jit(solution)/shard_map/d1_y/ppermute | solution.py:1016
  286.6 36.1 %collective-permute-start.60 = (bf16[320,640]{1,0:T(8,128)(2,1)}, bf16[320,640]{1,0:T(8,128)(2,1)}, u32[]{:S(2)}, u32[]{:S(2)}) collective-permute-start(bf16[320,640]{1,0:T(8,128)(2,1)} %get-tuple-element.528), channel_id=1, source_target_pairs={{0,1},{1,0},{2,3},{3,2},{4,5},{5,4},{6,7},{7,6},{8,9},{9,8},{10,11... | collective-permute-start | bytes 1228808 | tf_op jit(solution)/shard_map/d1_c/ppermute | solution.py:1016
  323.8 16.5 %collective-permute-start.61 = (bf16[320,640]{1,0:T(8,128)(2,1)}, bf16[320,640]{1,0:T(8,128)(2,1)}, u32[]{:S(2)}, u32[]{:S(2)}) collective-permute-start(bf16[320,640]{1,0:T(8,128)(2,1)} %get-tuple-element.529), channel_id=1, source_target_pairs={{0,1},{1,0},{2,3},{3,2},{4,5},{5,4},{6,7},{7,6},{8,9},{9,8},{10,11... | collective-permute-start | bytes 1228808 | tf_op jit(solution)/shard_map/d1_c/ppermute | solution.py:1016
  324.4 16.0 %collective-permute-start.62 = (bf16[320,640]{1,0:T(8,128)(2,1)}, bf16[320,640]{1,0:T(8,128)(2,1)}, u32[]{:S(2)}, u32[]{:S(2)}) collective-permute-start(bf16[320,640]{1,0:T(8,128)(2,1)} %get-tuple-element.530), channel_id=1, source_target_pairs={{0,1},{1,0},{2,3},{3,2},{4,5},{5,4},{6,7},{7,6},{8,9},{9,8},{10,11... | collective-permute-start | bytes 1228808 | tf_op jit(solution)/shard_map/d1_c/ppermute | solution.py:1016
  325.7 56.0 %collective-permute-start.77 = (bf16[2,4,2,80,640]{4,3,2,1,0:T(8,128)(2,1)}, bf16[2,4,2,80,640]{4,3,2,1,0:T(8,128)(2,1)S(1)}, u32[]{:S(2)}, u32[]{:S(2)}) collective-permute-start(bf16[2,4,2,80,640]{4,3,2,1,0:T(8,128)(2,1)} %get-tuple-element.515), channel_id=1, source_target_pairs={{0,2},{2,0},{1,3},{3,1},{4,6},{6,4},{5,7},{7,5},{8,10},{10,8},{9,1... | collective-permute-start | bytes 4915208 | tf_op jit(solution)/shard_map/u1_x/ppermute | solution.py:1016
  345.0 180.1 %reduce-scatter.8.cloned.1.call-start = ((), (), s32[]{:S(2)}) async-start(), calls=%async_computation.5 | async-start | bytes 2048000 | tf_op jit(solution)/shard_map/reduce_scatter | solution.py:1116
  346.6 35.1 %collective-permute-start.76 = (bf16[2,4,80,640]{3,2,1,0:T(8,128)(2,1)}, bf16[2,4,80,640]{3,2,1,0:T(8,128)(2,1)}, u32[]{:S(2)}, u32[]{:S(2)}) collective-permute-start(bf16[2,4,80,640]{3,2,1,0:T(8,128)(2,1)} %get-tuple-element.545), channel_id=1, source_target_pairs={{0,2},{2,0},{1,3},{3,1},{4,6},{6,4},{5,7},{7,5},{8,10},{10,8},{9,1... | collective-permute-start | bytes 2457608 | tf_op jit(solution)/shard_map/a1_x/ppermute | solution.py:1016
  348.5 20.6 %collective-permute-start.79 = (bf16[320,640]{1,0:T(8,128)(2,1)}, bf16[320,640]{1,0:T(8,128)(2,1)}, u32[]{:S(2)}, u32[]{:S(2)}) collective-permute-start(bf16[320,640]{1,0:T(8,128)(2,1)} %get-tuple-element.588), channel_id=1, source_target_pairs={{0,1},{1,0},{2,3},{3,2},{4,5},{5,4},{6,7},{7,6},{8,9},{9,8},{10,11... | collective-permute-start | bytes 1228808 | tf_op jit(solution)/shard_map/d0_c/ppermute | solution.py:1016
  349.1 20.1 %collective-permute-start.80 = (bf16[320,640]{1,0:T(8,128)(2,1)}, bf16[320,640]{1,0:T(8,128)(2,1)}, u32[]{:S(2)}, u32[]{:S(2)}) collective-permute-start(bf16[320,640]{1,0:T(8,128)(2,1)} %get-tuple-element.589), channel_id=1, source_target_pairs={{0,1},{1,0},{2,3},{3,2},{4,5},{5,4},{6,7},{7,6},{8,9},{9,8},{10,11... | collective-permute-start | bytes 1228808 | tf_op jit(solution)/shard_map/d0_c/ppermute | solution.py:1016
  353.1 55.5 %collective-permute-start.78 = (bf16[4,320,640]{2,1,0:T(8,128)(2,1)}, bf16[4,320,640]{2,1,0:T(8,128)(2,1)}, u32[]{:S(2)}, u32[]{:S(2)}) collective-permute-start(bf16[4,320,640]{2,1,0:T(8,128)(2,1)} %shard_map.268), channel_id=1, source_target_pairs={{0,4},{4,0},{1,5},{5,1},{2,6},{6,2},{3,7},{7,3},{8,12},{12,8},{9,1... | collective-permute-start | bytes 4915208 | tf_op jit(solution)/shard_map/d0_y/ppermute | solution.py:1016
  386.0 43.1 %collective-permute-start.88 = (bf16[4,2,80,640]{3,2,1,0:T(8,128)(2,1)}, bf16[4,2,80,640]{3,2,1,0:T(8,128)(2,1)}, u32[]{:S(2)}, u32[]{:S(2)}) collective-permute-start(bf16[4,2,80,640]{3,2,1,0:T(8,128)(2,1)} %fusion.1), channel_id=1, source_target_pairs={{0,4},{4,0},{1,5},{5,1},{2,6},{6,2},{3,7},{7,3},{8,12},{12,8},{9,1... | collective-permute-start | bytes 2457608 | tf_op jit(solution)/shard_map/u1_y/ppermute | solution.py:1016
  387.5 19.3 %collective-permute-start.81 = (bf16[320,640]{1,0:T(8,128)(2,1)}, bf16[320,640]{1,0:T(8,128)(2,1)}, u32[]{:S(2)}, u32[]{:S(2)}) collective-permute-start(bf16[320,640]{1,0:T(8,128)(2,1)} %get-tuple-element.590), channel_id=1, source_target_pairs={{0,1},{1,0},{2,3},{3,2},{4,5},{5,4},{6,7},{7,6},{8,9},{9,8},{10,11... | collective-permute-start | bytes 1228808 | tf_op jit(solution)/shard_map/d0_c/ppermute | solution.py:1016
  387.5 21.1 %collective-permute-start.82 = (bf16[320,640]{1,0:T(8,128)(2,1)}, bf16[320,640]{1,0:T(8,128)(2,1)}, u32[]{:S(2)}, u32[]{:S(2)}) collective-permute-start(bf16[320,640]{1,0:T(8,128)(2,1)} %get-tuple-element.591), channel_id=1, source_target_pairs={{0,1},{1,0},{2,3},{3,2},{4,5},{5,4},{6,7},{7,6},{8,9},{9,8},{10,11... | collective-permute-start | bytes 1228808 | tf_op jit(solution)/shard_map/d0_c/ppermute | solution.py:1016
  390.6 38.5 %collective-permute-start.89 = (bf16[4,80,640]{2,1,0:T(8,128)(2,1)}, bf16[4,80,640]{2,1,0:T(8,128)(2,1)}, u32[]{:S(2)}, u32[]{:S(2)}) collective-permute-start(bf16[4,80,640]{2,1,0:T(8,128)(2,1)} %fusion.5), channel_id=1, source_target_pairs={{0,4},{4,0},{1,5},{5,1},{2,6},{6,2},{3,7},{7,3},{8,12},{12,8},{9,1... | collective-permute-start | bytes 1228808 | tf_op jit(solution)/shard_map/a1_y/ppermute | solution.py:1016
  406.8 39.1 %collective-permute-start.83 = (bf16[2,4,2,80,640]{4,3,2,1,0:T(8,128)(2,1)}, bf16[2,4,2,80,640]{4,3,2,1,0:T(8,128)(2,1)}, u32[]{:S(2)}, u32[]{:S(2)}) collective-permute-start(bf16[2,4,2,80,640]{4,3,2,1,0:T(8,128)(2,1)} %get-tuple-element.592), channel_id=1, source_target_pairs={{0,2},{2,0},{1,3},{3,1},{4,6},{6,4},{5,7},{7,5},{8,10},{10,8},{9,1... | collective-permute-start | bytes 4915208 | tf_op jit(solution)/shard_map/u0_x/ppermute | solution.py:1016
  431.5 98.2 %reduce-scatter.4.cloned.1.call-start = ((), (), s32[]{:S(2)}) async-start(), calls=%async_computation.3 | async-start | bytes 1024000 | tf_op jit(solution)/shard_map/reduce_scatter | solution.py:1116
  434.8 47.1 %collective-permute-start.94 = (bf16[2,3,80,640]{3,2,1,0:T(8,128)(2,1)}, bf16[2,3,80,640]{3,2,1,0:T(8,128)(2,1)S(1)}, u32[]{:S(2)}, u32[]{:S(2)}) collective-permute-start(bf16[2,3,80,640]{3,2,1,0:T(8,128)(2,1)} %get-tuple-element.763), channel_id=1, source_target_pairs={{0,8},{8,0},{16,24},{24,16},{1,9},{9,1},{17,25},{25,17},{2,10},{10... | collective-permute-start | bytes 1843208 | tf_op jit(solution)/shard_map/j1_near/ppermute | solution.py:1065
  439.8 44.1 %collective-permute-start.91 = (bf16[2,4,80,640]{3,2,1,0:T(8,128)(2,1)}, bf16[2,4,80,640]{3,2,1,0:T(8,128)(2,1)}, u32[]{:S(2)}, u32[]{:S(2)}) collective-permute-start(bf16[2,4,80,640]{3,2,1,0:T(8,128)(2,1)} %get-tuple-element.634), channel_id=1, source_target_pairs={{0,2},{2,0},{1,3},{3,1},{4,6},{6,4},{5,7},{7,5},{8,10},{10,8},{9,1... | collective-permute-start | bytes 2457608 | tf_op jit(solution)/shard_map/a0_x/ppermute | solution.py:1016
  448.1 39.2 %collective-permute-start.90 = (bf16[4,2,80,640]{3,2,1,0:T(8,128)(2,1)}, bf16[4,2,80,640]{3,2,1,0:T(8,128)(2,1)}, u32[]{:S(2)}, u32[]{:S(2)}) collective-permute-start(bf16[4,2,80,640]{3,2,1,0:T(8,128)(2,1)} %fusion.2), channel_id=1, source_target_pairs={{0,4},{4,0},{1,5},{5,1},{2,6},{6,2},{3,7},{7,3},{8,12},{12,8},{9,1... | collective-permute-start | bytes 2457608 | tf_op jit(solution)/shard_map/u0_y/ppermute | solution.py:1016
  450.6 32.3 %collective-permute-start.93 = (f32[88,640]{1,0:T(8,128)S(1)}, f32[88,640]{1,0:T(8,128)S(1)}, u32[]{:S(2)}, u32[]{:S(2)}) collective-permute-start(f32[88,640]{1,0:T(8,128)S(1)} %add.155), channel_id=1, source_target_pairs={{0,16},{8,24},{16,0},{24,8},{1,17},{9,25},{17,1},{25,9},{2,18},{10... | collective-permute-start | bytes 675848 | tf_op jit(solution)/shard_map/small_far/ppermute | solution.py:1065
  482.9 15.4 %collective-permute-start.97 = (bf16[3,80,640]{2,1,0:T(8,128)(2,1)}, bf16[3,80,640]{2,1,0:T(8,128)(2,1)S(1)}, u32[]{:S(2)}, u32[]{:S(2)}) collective-permute-start(bf16[3,80,640]{2,1,0:T(8,128)(2,1)} %get-tuple-element.767), channel_id=1, source_target_pairs={{0,16},{8,24},{16,0},{24,8},{1,17},{9,25},{17,1},{25,9},{2,18},{10... | collective-permute-start | bytes 921608 | tf_op jit(solution)/shard_map/j1_far/ppermute | solution.py:1065
  482.9 17.2 %collective-permute-start.96 = (f32[88,640]{1,0:T(8,128)S(1)}, f32[88,640]{1,0:T(8,128)}, u32[]{:S(2)}, u32[]{:S(2)}) collective-permute-start(f32[88,640]{1,0:T(8,128)S(1)} %add.159), channel_id=1, source_target_pairs={{0,8},{8,0},{16,24},{24,16},{1,9},{9,1},{17,25},{25,17},{2,10},{10... | collective-permute-start | bytes 675848 | tf_op jit(solution)/shard_map/small_near/ppermute | solution.py:1065
  485.7 17.5 %collective-permute-start.95 = (bf16[4,80,640]{2,1,0:T(8,128)(2,1)}, bf16[4,80,640]{2,1,0:T(8,128)(2,1)}, u32[]{:S(2)}, u32[]{:S(2)}) collective-permute-start(bf16[4,80,640]{2,1,0:T(8,128)(2,1)} %fusion.6), channel_id=1, source_target_pairs={{0,4},{4,0},{1,5},{5,1},{2,6},{6,2},{3,7},{7,3},{8,12},{12,8},{9,1... | collective-permute-start | bytes 1228808 | tf_op jit(solution)/shard_map/a0_y/ppermute | solution.py:1016
  504.6 32.2 %collective-permute-start.104 = (bf16[3,80,640]{2,1,0:T(8,128)(2,1)S(1)}, bf16[3,80,640]{2,1,0:T(8,128)(2,1)S(1)}, u32[]{:S(2)}, u32[]{:S(2)}) collective-permute-start(bf16[3,80,640]{2,1,0:T(8,128)(2,1)S(1)} %add_convert_fusion.4.refs_1_), channel_id=1, source_target_pairs={{0,1},{1,0},{2,3},{3,2},{4,5},{5,4},{6,7},{7,6},{8,9},{9,8},{10,11... | collective-permute-start | bytes 921608 | tf_op jit(solution)/shard_map/j1_c/ppermute | solution.py:1016
  504.8 20.9 %collective-permute-start.108 = (bf16[320,640]{1,0:T(8,128)(2,1)}, bf16[320,640]{1,0:T(8,128)(2,1)S(1)}, u32[]{:S(2)}, u32[]{:S(2)}) collective-permute-start(bf16[320,640]{1,0:T(8,128)(2,1)} %bitcast.195), channel_id=1, source_target_pairs={{0,2},{2,0},{1,3},{3,1},{4,6},{6,4},{5,7},{7,5},{8,10},{10,8},{9,1... | collective-permute-start | bytes 1228808 | tf_op jit(solution)/shard_map/d1_x/ppermute | solution.py:1016
  515.1 26.3 %collective-permute-start.107 = (bf16[320,640]{1,0:T(8,128)(2,1)}, bf16[320,640]{1,0:T(8,128)(2,1)S(1)}, u32[]{:S(2)}, u32[]{:S(2)}) collective-permute-start(bf16[320,640]{1,0:T(8,128)(2,1)} %bitcast.196), channel_id=1, source_target_pairs={{0,1},{1,0},{2,3},{3,2},{4,5},{5,4},{6,7},{7,6},{8,9},{9,8},{10,11... | collective-permute-start | bytes 1228808 | tf_op jit(solution)/shard_map/d1_c/ppermute | solution.py:1016
  (137 other events, 1013.2 us)
Sparse Core Ops, SparseCore 0:
  345.1 34.6 reduce-scatter.5
  431.6 51.1 reduce-scatter.7
  504.9 24.8 reduce-scatter.3
